TPU v7x, 32 devices: a whole 2x2x4 slice. The times are simulated.
32 devices in a mesh: dp: 4 (over z), tensor: 8 (over y, x, core).
Axes of the slice: x: 2, y: 2, z: 4, core: 2. Of those that a mesh axis runs over, the one named last changes fastest.
Arguments:
- inputs: bfloat16 [8, 2048, 2048], P('dp', 'tensor'), may hold values from -6 to 6
- cotangent: bfloat16 [8, 2048, 2048], P('dp', 'tensor'), may hold values from -6 to 6
- documents: int32 [8, 2048], P('dp'), may hold values from 0 to 7, as said below
- padding: int32 [8, 2048], P('dp'), may hold values from 0 to 1, as said below
- attn_gain: float32 [2048], replicated, may hold values from 0.5 to 1.5
- attn_shift: float32 [2048], replicated, may hold values from -1.75 to 1.75
- query_matrix: bfloat16 [2048, 2048], P(None, 'tensor'), may hold values from -0.25 to 0.25
- query_bias: float32 [2048], P('tensor'), may hold values from -1.75 to 1.75
- shared_matrix: bfloat16 [2048, 256], replicated, may hold values from -0.125 to 0.125
- value_bias: float32 [128], replicated, may hold values from -1.75 to 1.75
- output_matrix: bfloat16 [2048, 2048], P('tensor'), may hold values from -0.5 to 0.5
- output_bias: float32 [2048], replicated, may hold values from -1.75 to 1.75
- mlp_gain: float32 [2048], replicated, may hold values from 0.5 to 1.5
- mlp_shift: float32 [2048], replicated, may hold values from -1.75 to 1.75
- expansion_weights: bfloat16 [2048, 8192], P(None, 'tensor'), may hold values from -0.125 to 0.125
- up_bias: float32 [8192], P('tensor'), may hold values from -1.75 to 1.75
- down_matrix: bfloat16 [8192, 2048], P('tensor'), may hold values from -0.0625 to 0.0625
- down_bias: float32 [2048], replicated, may hold values from -1.75 to 1.75
Outputs:
- block_out: bfloat16 [8, 2048, 2048], P('dp', 'tensor')
- input_grad: float32 [8, 2048, 2048], P('dp', 'tensor')
- focus_scale_derivative: float32 [2048], replicated
- focus_offset_derivative: float32 [2048], replicated
- query_weight_grad: float32 [2048, 2048], P(None, 'tensor')
- query_bias_grad: float32 [2048], P('tensor')
- shared_weight_grad: float32 [2048, 256], replicated
- value_bias_grad: float32 [128], replicated
- output_weight_grad: float32 [2048, 2048], P('tensor')
- output_bias_grad: float32 [2048], replicated
- mlp_gain_grad: float32 [2048], replicated
- mlp_shift_grad: float32 [2048], replicated
- up_weight_grad: float32 [2048, 8192], P(None, 'tensor')
- up_bias_grad: float32 [8192], P('tensor')
- down_weight_grad: float32 [8192, 2048], P('tensor')
- down_bias_grad: float32 [2048], replicated
Inputs may be any that keep to these rules, and one draw needn't show every extreme that they name: Along each row the ids start at 0 and never fall, rising by at most one from a position to the next; in each group of 2 consecutive rows one row, drawn from the seed, is a single document, and every other row holds exactly 8 documents. Each row is real on a leading run of at least 1792 positions and padded after it; the single-document row of each group has no padding.
All inputs are finite; a program needn't handle non-finite values.
Results may differ from a plain program's by a relative error of at most 0.015.
Values may be sent and summed in bfloat16 or wider, within the bound.
A program may use at most 384 MiB of HBM per device.

v0:
```python
import jax
import jax.numpy as jnp
from jax import lax
from jax.sharding import PartitionSpec as P

EPSILON = 1e-05


def layer_norm(values, gain, shift):
    center = values - jnp.mean(values, axis=-1, keepdims=True)
    spread = jnp.mean(center * center, axis=-1, keepdims=True)
    return center * lax.rsqrt(spread + EPSILON) * gain + shift


def smooth_gate(values):
    return jax.nn.gelu(values, approximate=True)


def block_mask(start, rows, doc_seq, pad_seq):
    length = doc_seq.shape[0]
    place_key = jnp.arange(length, dtype=jnp.int32)
    place_query = start + jnp.arange(rows, dtype=jnp.int32)
    doc_query = lax.dynamic_slice_in_dim(doc_seq, start, rows, 0)
    causal = place_key[None, :] <= place_query[:, None]
    same_doc = doc_seq[None, :] == doc_query[:, None]
    visible = (pad_seq[None, :] == 1) | (place_key[None, :] == place_query[:, None])
    return causal & same_doc & visible


def attention_forward(query, keys, values, documents, padding, head_size):
    seqs_here, length, width = query.shape
    local_heads = width // head_size
    rows = min(512, length)
    blocks = length // rows
    scale = head_size ** (-0.5)
    starts = jnp.arange(blocks, dtype=jnp.int32) * rows

    def one_sequence(pack):
        query_seq, keys_seq, values_seq, doc_seq, pad_seq = pack
        query_blocks = query_seq.reshape(blocks, rows, local_heads, head_size)

        def one_block(item):
            query_block, start = item
            scores = (
                jnp.einsum("qhd,kd->hqk", query_block, keys_seq, preferred_element_type=jnp.float32)
                * scale
            )
            allowed = block_mask(start, rows, doc_seq, pad_seq)
            scores = jnp.where(allowed[None], scores, -1e30)
            highest = jnp.max(scores, axis=-1, keepdims=True)
            expo = jnp.exp(scores - highest)
            total = jnp.sum(expo, axis=-1, keepdims=True)
            probs = (expo / total).astype(jnp.bfloat16)
            result = jnp.einsum(
                "hqk,kd->qhd", probs, values_seq, preferred_element_type=jnp.float32
            ).astype(jnp.bfloat16)
            return (result, (highest + jnp.log(total))[..., 0])

        results, log_totals = lax.map(one_block, (query_blocks, starts))
        return (results.reshape(length, width), log_totals)

    return lax.map(one_sequence, (query, keys, values, documents, padding))


def attention_backward(query, keys, values, documents, padding, log_totals, grad_out, head_size):
    seqs_here, length, width = query.shape
    local_heads = width // head_size
    rows = min(512, length)
    blocks = length // rows
    scale = head_size ** (-0.5)
    starts = jnp.arange(blocks, dtype=jnp.int32) * rows

    def one_sequence(pack):
        query_seq, keys_seq, values_seq, doc_seq, pad_seq, lse_seq, grad_seq = pack
        query_blocks = query_seq.reshape(blocks, rows, local_heads, head_size)
        grad_blocks = grad_seq.reshape(blocks, rows, local_heads, head_size)

        def one_block(carry, item):
            key_acc, value_acc = carry
            query_block, grad_block, lse_block, start = item
            scores = (
                jnp.einsum("qhd,kd->hqk", query_block, keys_seq, preferred_element_type=jnp.float32)
                * scale
            )
            allowed = block_mask(start, rows, doc_seq, pad_seq)
            scores = jnp.where(allowed[None], scores, -1e30)
            probs = jnp.where(allowed[None], jnp.exp(scores - lse_block[..., None]), 0.0)
            grad_probs = jnp.einsum(
                "qhd,kd->hqk", grad_block, values_seq, preferred_element_type=jnp.float32
            )
            inner = jnp.sum(grad_probs * probs, axis=-1, keepdims=True)
            grad_scores = (probs * (grad_probs - inner)).astype(jnp.bfloat16)
            query_gradient = (
                jnp.einsum("hqk,kd->qhd", grad_scores, keys_seq, preferred_element_type=jnp.float32)
                * scale
            )
            key_acc = (
                key_acc
                + jnp.einsum(
                    "hqk,qhd->kd", grad_scores, query_block, preferred_element_type=jnp.float32
                )
                * scale
            )
            value_acc = value_acc + jnp.einsum(
                "hqk,qhd->kd",
                probs.astype(jnp.bfloat16),
                grad_block,
                preferred_element_type=jnp.float32,
            )
            return ((key_acc, value_acc), query_gradient)

        empty = jnp.zeros((length, head_size), jnp.float32)
        (key_acc, value_acc), grad_queries = lax.scan(
            one_block, (empty, empty), (query_blocks, grad_blocks, lse_seq, starts)
        )
        return (grad_queries.reshape(length, width), jnp.concatenate([key_acc, value_acc], axis=-1))

    return lax.map(one_sequence, (query, keys, values, documents, padding, log_totals, grad_out))


def body(
    inputs,
    cotangent,
    documents,
    padding,
    attn_gain,
    attn_shift,
    query_matrix,
    query_bias,
    shared_matrix,
    value_bias,
    output_matrix,
    output_bias,
    mlp_gain,
    mlp_shift,
    expansion_weights,
    up_bias,
    down_matrix,
    down_bias,
):
    head_size = value_bias.shape[0]
    inputs_wide = inputs.astype(jnp.float32)
    hidden_local = layer_norm(inputs_wide, attn_gain, attn_shift).astype(jnp.bfloat16)
    hidden_every = lax.all_gather(hidden_local, "tensor", axis=1, tiled=True)
    query = (
        jnp.einsum("nif,ft->nit", hidden_every, query_matrix, preferred_element_type=jnp.float32)
        + query_bias
    ).astype(jnp.bfloat16)
    shared = jnp.einsum(
        "nif,ft->nit", hidden_every, shared_matrix, preferred_element_type=jnp.float32
    )
    keys = shared[..., :head_size].astype(jnp.bfloat16)
    values = (shared[..., head_size:] + value_bias).astype(jnp.bfloat16)
    attended_rows, log_totals = attention_forward(
        query, keys, values, documents, padding, head_size
    )
    partial_out = jnp.einsum(
        "tkw,wu->tku", attended_rows, output_matrix, preferred_element_type=jnp.float32
    )
    attn_branch = lax.psum_scatter(partial_out, "tensor", scatter_dimension=1, tiled=True)
    mixed = inputs_wide + attn_branch + output_bias
    normed_own = layer_norm(mixed, mlp_gain, mlp_shift).astype(jnp.bfloat16)
    standardized_whole = lax.all_gather(normed_own, "tensor", axis=1, tiled=True)
    raised = (
        jnp.einsum(
            "rfu,ux->rfx", standardized_whole, expansion_weights, preferred_element_type=jnp.float32
        )
        + up_bias
    )
    active_values = smooth_gate(raised).astype(jnp.bfloat16)
    partial_feedforward = jnp.einsum(
        "nau,ui->nai", active_values, down_matrix, preferred_element_type=jnp.float32
    )
    mlp_branch = lax.psum_scatter(
        partial_feedforward.astype(jnp.bfloat16), "tensor", scatter_dimension=1, tiled=True
    ).astype(jnp.float32)
    block_out = (mixed + mlp_branch + down_bias).astype(jnp.bfloat16)
    cot_wide = cotangent.astype(jnp.float32)
    cotangent_every = lax.all_gather(cotangent, "tensor", axis=1, tiled=True)
    down_gradient = jnp.einsum(
        "jti,jtv->iv", active_values, cotangent_every, preferred_element_type=jnp.float32
    )
    down_bias_grad = jnp.sum(cot_wide, axis=(0, 1))
    grad_active = jnp.einsum(
        "ony,vy->onv", cotangent_every, down_matrix, preferred_element_type=jnp.float32
    )
    gate_value, gate_back = jax.vjp(smooth_gate, raised)
    raised_gradient = gate_back(grad_active)[0].astype(jnp.bfloat16)
    up_bias_part = jnp.sum(raised_gradient.astype(jnp.float32), axis=(0, 1))
    up_gradient = jnp.einsum(
        "nyq,nyz->qz", standardized_whole, raised_gradient, preferred_element_type=jnp.float32
    )
    grad_normed_part = jnp.einsum(
        "pjw,ow->pjo", raised_gradient, expansion_weights, preferred_element_type=jnp.float32
    )
    derivative_standardized = lax.psum_scatter(
        grad_normed_part, "tensor", scatter_dimension=1, tiled=True
    )
    norm_value, norm_back = jax.vjp(layer_norm, mixed, mlp_gain, mlp_shift)
    grad_mix_norm, mlp_gain_part, mlp_shift_part = norm_back(derivative_standardized)
    grad_mixed = cot_wide + grad_mix_norm
    output_bias_part = jnp.sum(grad_mixed, axis=(0, 1))
    grad_mixed_low = grad_mixed.astype(jnp.bfloat16)
    gradient_rows = lax.all_gather(grad_mixed_low, "tensor", axis=1, tiled=True)
    output_gradient = jnp.einsum(
        "xup,xun->pn", attended_rows, gradient_rows, preferred_element_type=jnp.float32
    )
    grad_attended = jnp.einsum(
        "wia,fa->wif", gradient_rows, output_matrix, preferred_element_type=jnp.float32
    ).astype(jnp.bfloat16)
    grad_query_wide, shared_part = attention_backward(
        query, keys, values, documents, padding, log_totals, grad_attended, head_size
    )
    query_gradient = grad_query_wide.astype(jnp.bfloat16)
    query_bias_part = jnp.sum(query_gradient.astype(jnp.float32), axis=(0, 1))
    query_grad = jnp.einsum(
        "rvm,rvw->mw", hidden_every, query_gradient, preferred_element_type=jnp.float32
    )
    grad_hidden_part = jnp.einsum(
        "ogq,iq->ogi", query_gradient, query_matrix, preferred_element_type=jnp.float32
    )
    grad_hidden_q, shared_own = (
        lax.psum_scatter(
            grad_hidden_part.astype(jnp.bfloat16), "tensor", scatter_dimension=1, tiled=True
        ).astype(jnp.float32),
        lax.psum_scatter(
            shared_part.astype(jnp.bfloat16), "tensor", scatter_dimension=1, tiled=True
        ).astype(jnp.float32),
    )
    shared_reduced = shared_own.astype(jnp.bfloat16)
    shared_grad = jnp.einsum(
        "rvm,rvw->mw", hidden_local, shared_reduced, preferred_element_type=jnp.float32
    )
    value_bias_part = jnp.sum(shared_reduced[..., head_size:].astype(jnp.float32), axis=(0, 1))
    grad_hidden = grad_hidden_q + jnp.einsum(
        "ogq,iq->ogi", shared_reduced, shared_matrix, preferred_element_type=jnp.float32
    )
    first_value, first_back = jax.vjp(layer_norm, inputs_wide, attn_gain, attn_shift)
    grad_in_norm, attn_gain_part, attn_shift_part = first_back(grad_hidden)
    input_grad = grad_mixed + grad_in_norm
    query_grad, query_bias_part, output_gradient, up_gradient, up_bias_part, down_gradient = (
        lax.psum(query_grad.astype(jnp.bfloat16), "dp").astype(jnp.float32),
        lax.psum(query_bias_part.astype(jnp.bfloat16), "dp").astype(jnp.float32),
        lax.psum(output_gradient.astype(jnp.bfloat16), "dp").astype(jnp.float32),
        lax.psum(up_gradient.astype(jnp.bfloat16), "dp").astype(jnp.float32),
        lax.psum(up_bias_part.astype(jnp.bfloat16), "dp").astype(jnp.float32),
        lax.psum(down_gradient.astype(jnp.bfloat16), "dp").astype(jnp.float32),
    )
    (
        shared_grad,
        value_bias_part,
        attn_gain_part,
        attn_shift_part,
        mlp_gain_part,
        mlp_shift_part,
        output_bias_part,
        down_bias_grad,
    ) = lax.psum(
        (
            shared_grad,
            value_bias_part,
            attn_gain_part,
            attn_shift_part,
            mlp_gain_part,
            mlp_shift_part,
            output_bias_part,
            down_bias_grad,
        ),
        ("dp", "tensor"),
    )
    return (
        block_out,
        input_grad,
        attn_gain_part,
        attn_shift_part,
        query_grad,
        query_bias_part,
        shared_grad,
        value_bias_part,
        output_gradient,
        output_bias_part,
        mlp_gain_part,
        mlp_shift_part,
        up_gradient,
        up_bias_part,
        down_gradient,
        down_bias_grad,
    )


def solution(mesh):
    placed = (
        P("dp", "tensor", None),
        P("dp", "tensor", None),
        P("dp", None),
        P("dp", None),
        P(),
        P(),
        P(None, "tensor"),
        P("tensor"),
        P(),
        P(),
        P("tensor", None),
        P(),
        P(),
        P(),
        P(None, "tensor"),
        P("tensor"),
        P("tensor", None),
        P(),
    )
    return jax.shard_map(
        body,
        mesh=mesh,
        in_specs=placed,
        out_specs=(
            P("dp", "tensor", None),
            P("dp", "tensor", None),
            P(),
            P(),
            P(None, "tensor"),
            P("tensor"),
            P(),
            P(),
            P("tensor", None),
            P(),
            P(),
            P(),
            P(None, "tensor"),
            P("tensor"),
            P("tensor", None),
            P(),
        ),
        check_vma=False,
    )
```

profile of v0, /device:TPU:0, one launch (start us, length us, event | category | flops | bytes accessed | tf_op | source)
XLA Modules:
  0.0 2110.7 jit_solution(17325909140800629212)
XLA Ops:
  15.1 92.6 %all-gather.5.cloned.1.call-done = bf16[2,2048,2048]{2,1,0:T(8,128)(2,1)} async-done(((bf16[2,256,2048]{2,1,0:T(8,128)(2,1)}), bf16[2,2048,2048]{2,1,0:T(8,128)(2,1)}) %all-gather.5.cloned.1.call-update) | async-done | bytes 16777232 | tf_op jit(solution)/shard_map/all_gather | solution.py:144
  107.7 8.8 fusion.76
  119.8 6.0 add_convert_fusion.2
  125.8 125.2 %while.56 = (s32[]{:T(128)}, bf16[2,2048,256]{2,1,0:T(8,128)(2,1)}, f32[2,4,2,512]{3,2,1,0:T(2,128)S(1)}, bf16[2,2048,256]{2,1,0:T(8,128)(2,1)}, bf16[2,2048,128...) while((s32[]{:T(128)}, bf16[2,2048,256]{2,1,0:T(8,128)(2,1)}, ...), condition=%wide.region_7.8_spmd.clone, body=%wide.region_2.7_spmd.clone.sunk | while | flops 1105331712 | bytes 44693992 | solution.py:62
  129.7 56.9 %while.59 = (s32[]{:T(128)}, bf16[4,512,2,128]{3,2,1,0:T(2,128)(2,1)S(1)}, f32[4,2,512]{2,1,0:T(2,128)S(1)}, s32[4]{0:T(128)S(1)}, s32[2048]{0:T(1024)S(1)}, /*i...) while((s32[]{:T(128)}, ...), condition=%wide.region_6.6_spmd, body=%wide.region_3.5_spmd.sunk | while | flops 1105331712 | bytes 34142424 | solution.py:59
  192.3 56.9 %while.59 = (s32[]{:T(128)}, bf16[4,512,2,128]{3,2,1,0:T(2,128)(2,1)S(1)}, f32[4,2,512]{2,1,0:T(2,128)S(1)}, s32[4]{0:T(128)S(1)}, s32[2048]{0:T(1024)S(1)}, /*i...) while((s32[]{:T(128)}, ...), condition=%wide.region_6.6_spmd, body=%wide.region_3.5_spmd.sunk | while | flops 1105331712 | bytes 34142424 | solution.py:59
  251.0 15.0 fusion.73
  266.0 205.4 %reduce-scatter.6.cloned.1.call-done = f32[2,256,2048]{2,1,0:T(8,128)} async-done(((f32[2,2048,2048]{2,1,0:T(8,128)}), f32[2,256,2048]{2,1,0:T(8,128)}) %reduce-scatter.6.cloned.1.call-update) | async-done | bytes 4194320 | tf_op jit(solution)/shard_map/reduce_scatter | solution.py:160
  479.6 89.4 %all-gather.7.cloned.1.call-done = bf16[2,2048,2048]{2,1,0:T(8,128)(2,1)} async-done(((bf16[2,256,2048]{2,1,0:T(8,128)(2,1)}), bf16[2,2048,2048]{2,1,0:T(8,128)(2,1)}) %all-gather.7.cloned.1.call-update) | async-done | bytes 16777232 | tf_op jit(solution)/shard_map/all_gather | solution.py:163
  568.9 23.4 %fusion.64 = f32[2,2048,1024]{2,1,0:T(8,128)} fusion(bf16[2,2048,2048]{2,1,0:T(8,128)(2,1)} %all-gather.7.cloned.1.call-done, bf16[2048,1024]{1,0:T(8,128)(2,1)} %param.40), kind=kOutput, calls=%fused_computation.117 | convolution fusion | flops 17179869184 | bytes 37748736 | tf_op jit(solution)/shard_map/rfu,ux->rfx/dot_general | solution.py:165
  592.4 68.4 %all-gather.9.cloned.1.call-done = bf16[2,2048,2048]{2,1,0:T(8,128)(2,1)} async-done(((bf16[2,256,2048]{2,1,0:T(8,128)(2,1)}), bf16[2,2048,2048]{2,1,0:T(8,128)(2,1)}) %all-gather.9.cloned.1.call-update) | async-done | bytes 16777232 | tf_op jit(solution)/shard_map/all_gather | solution.py:179
  660.8 36.9 %fusion.88 = (bf16[1024]{0:T(1024)(128)(2,1)}, bf16[2,2048,1024]{2,1,0:T(8,128)(2,1)}) fusion(f32[2,2048,1024]{2,1,0:T(8,128)} %fusion.64, f32[1024]{0:T(1024)S(1)} %copy-done.58, bf16[2,2048,2048]{2,1,0:T(8,128)(2,1)} %all-gather.9.cloned.1.call-done, bf16[1024,2048]{1,0:T(8,128)(2,1)} %param.42), kind=kOutput, calls=%fused_computation.164 | convolution fusion | flops 17272143872 | bytes 46143488 | tf_op jit(solution)/shard_map/ony,vy->onv/dot_general | solution.py:184
  697.7 24.4 %fusion.62 = f32[2,2048,2048]{2,1,0:T(8,128)} fusion(bf16[2,2048,1024]{2,1,0:T(8,128)(2,1)} %get-tuple-element.475, bf16[2048,1024]{1,0:T(8,128)(2,1)S(1)} %copy-done.57), kind=kOutput, calls=%fused_computation.115 | convolution fusion | flops 17179869184 | bytes 46137344 | tf_op jit(solution)/shard_map/pjw,ow->pjo/dot_general | solution.py:193
  722.2 27.2 %convolution_convert_fusion.1 = bf16[2,2048,2048]{2,1,0:T(8,128)(2,1)} fusion(bf16[1024,2048]{1,0:T(8,128)(2,1)} %param.42, f32[2,2048,1024]{2,1,0:T(8,128)} %fusion.64, f32[1024]{0:T(1024)S(1)} %copy-done.58), kind=kOutput, calls=%fused_computation.91 | convolution fusion | flops 17230200832 | bytes 37752832 | tf_op jit(solution)/shard_map/nau,ui->nai/dot_general | solution.py:171
  749.5 178.1 %reduce-scatter.10.cloned.1.call-done = f32[2,256,2048]{2,1,0:T(8,128)} async-done(((f32[2,2048,2048]{2,1,0:T(8,128)}), f32[2,256,2048]{2,1,0:T(8,128)}) %reduce-scatter.10.cloned.1.call-update) | async-done | bytes 4194320 | tf_op jit(solution)/shard_map/reduce_scatter | solution.py:196
  932.7 114.4 %reduce-scatter.8.cloned.1.call-done = bf16[2,256,2048]{2,1,0:T(8,128)(2,1)} async-done(((bf16[2,2048,2048]{2,1,0:T(8,128)(2,1)}), bf16[2,256,2048]{2,1,0:T(8,128)(2,1)}) %reduce-scatter.8.cloned.1.call-update) | async-done | bytes 2097168 | tf_op jit(solution)/shard_map/reduce_scatter | solution.py:174
  1047.1 5.8 fusion.85
  1056.9 23.7 %bitcast_convert_fusion.1 = bf16[2048,1024]{1,0:T(8,128)(2,1)} fusion(bf16[2,2048,2048]{2,1,0:T(8,128)(2,1)} %all-gather.7.cloned.1.call-done, bf16[2,2048,1024]{2,1,0:T(8,128)(2,1)} %get-tuple-element.475), kind=kOutput, calls=%fused_computation.93 | convolution fusion | flops 17181966336 | bytes 29360128 | tf_op jit(solution)/shard_map/nyq,nyz->qz/dot_general | solution.py:190
  1080.6 66.2 %all-gather.11.cloned.1.call-done = bf16[2,2048,2048]{2,1,0:T(8,128)(2,1)} async-done(((bf16[2,256,2048]{2,1,0:T(8,128)(2,1)}), bf16[2,2048,2048]{2,1,0:T(8,128)(2,1)}) %all-gather.11.cloned.1.call-update) | async-done | bytes 16777232 | tf_op jit(solution)/shard_map/all_gather | solution.py:204
  1146.8 9.8 convolution_convert_fusion.2
  1156.6 278.6 %while.58 = (s32[]{:T(128)}, bf16[2,2048,256]{2,1,0:T(8,128)(2,1)}, bf16[2,2048,256]{2,1,0:T(8,128)(2,1)}, bf16[2,2048,256]{2,1,0:T(8,128)(2,1)}, bf16[2,2048,25...) while((s32[]{:T(128)}, bf16[2,2048,256]{2,1,0:T(8,128)(2,1)}, ...), condition=%wide.region_19.20_spmd.clone, body=%wide.region_15.19_spmd.clone.sunk | while | flops 2715289088 | bytes 144034416 | solution.py:118
  1164.9 127.9 %while.60 = (s32[]{:T(128)}, f32[2048,128]{1,0:T(8,128)S(1)}, f32[2048,128]{1,0:T(8,128)S(1)}, bf16[4,512,2,128]{3,2,1,0:T(2,128)(2,1)}, s32[4]{0:T(128)S(1)}, /...) while((s32[]{:T(128)}, f32[2048,128]{1,0:T(8,128)S(1)}, ...), condition=%wide.region_18.18_spmd.clone, body=%wide.region_16.17_spmd.clone.sunk | while | flops 2713191936 | bytes 126142768 | solution.py:113
  1172.8 6.3 fusion.134
  1179.0 8.6 fusion.135
  1204.7 6.3 fusion.134
  1211.0 8.6 fusion.135
  1236.7 6.3 fusion.134
  1243.0 8.6 fusion.135
  1268.7 6.3 fusion.134
  1275.0 8.6 fusion.135
  1304.0 127.9 %while.60 = (s32[]{:T(128)}, f32[2048,128]{1,0:T(8,128)S(1)}, f32[2048,128]{1,0:T(8,128)S(1)}, bf16[4,512,2,128]{3,2,1,0:T(2,128)(2,1)}, s32[4]{0:T(128)S(1)}, /...) while((s32[]{:T(128)}, f32[2048,128]{1,0:T(8,128)S(1)}, ...), condition=%wide.region_18.18_spmd.clone, body=%wide.region_16.17_spmd.clone.sunk | while | flops 2713191936 | bytes 126142768 | solution.py:113
  1311.8 6.3 fusion.134
  1318.1 8.6 fusion.135
  1343.8 6.3 fusion.134
  1350.1 8.6 fusion.135
  1375.8 6.3 fusion.134
  1382.1 8.6 fusion.135
  1407.8 6.3 fusion.134
  1414.1 8.6 fusion.135
  1435.4 27.6 %bitcast_convert_fusion = bf16[1024,2048]{1,0:T(8,128)(2,1)} fusion(bf16[2,2048,2048]{2,1,0:T(8,128)(2,1)} %all-gather.9.cloned.1.call-done, f32[2,2048,1024]{2,1,0:T(8,128)} %fusion.64, f32[1024]{0:T(1024)S(1)} %copy-done.59), kind=kOutput, calls=%fused_computation.92 | convolution fusion | flops 17223909376 | bytes 37752832 | tf_op jit(solution)/shard_map/jti,jtv->iv/dot_general | solution.py:180
  1468.5 9.6 fusion.66
  1479.9 8.9 convolution_convert_fusion
  1489.5 11.9 all-reduce.1
  1506.4 335.4 %all-reduce.8.cloned.1.call-done = (bf16[2048,256]{1,0:T(8,128)(2,1)}, bf16[256,2048]{1,0:T(8,128)(2,1)}, bf16[2048,1024]{1,0:T(8,128)(2,1)}, bf16[1024,2048]{1,0:T(8,128)(2,1)}) async-done(((bf16[2048,256]{1,0:T(8,128)(2,1)}, bf16[256,2048]{1,0:T(8,128)(2,1)}, bf16[2048,1024]{1,0:T(8,128)(2,1)}, bf16[1024,2048]{1,0:T(8,128)(2,1)}), (bf16[2048,256]{1,0:T(8,128)(2,1)}, bf16[256,2048]{1,0:T(8,128)(2,1)}, ...) | async-done | bytes 10485776 | tf_op jit(solution)/shard_map/psum | solution.py:242
  1852.6 5.6 convert_element_type.133
  1858.2 102.2 %reduce-scatter.12.cloned.1.call-done = bf16[2,256,2048]{2,1,0:T(8,128)(2,1)} async-done(((bf16[2,2048,2048]{2,1,0:T(8,128)(2,1)}), bf16[2,256,2048]{2,1,0:T(8,128)(2,1)}) %reduce-scatter.12.cloned.1.call-update) | async-done | bytes 2097168 | tf_op jit(solution)/shard_map/reduce_scatter | solution.py:223
  1970.1 40.8 %all-reduce = (f32[2048]{0:T(1024)}, f32[2048]{0:T(1024)}, f32[128]{0:T(128)}, f32[2048]{0:T(1024)}, f32[2048]{0:T(1024)}, /*index=5*/f32[2048]{0:T(1024)}, f32[2048]{0:T(1024)}) all-reduce(f32[2048]{0:T(1024)S(1)} %get-tuple-element.357, f32[2048]{0:T(1024)S(1)} %get-tuple-element.360, ...), channel_id=1, replica_groups=mesh['dp'=4,'tensor'=8] {'dp','tensor'}, use_global_device_ids=true, to_apply=%region_25.26 | all-reduce | flops 12416 | bytes 99328 | tf_op jit(solution)/shard_map/psum | solution.py:258
  2010.9 90.1 %all-reduce.6.cloned.1.call-done = f32[2048,256]{1,0:T(8,128)} async-done(((f32[2048,256]{1,0:T(8,128)}), f32[2048,256]{1,0:T(8,128)}) %all-reduce.6.cloned.1.call-update) | async-done | bytes 2097168 | tf_op jit(solution)/shard_map/psum | solution.py:258
  (470 shorter events, 316.8 us)
Async XLA Ops:
  7.2 243.8 %copy-start = (bf16[256,2048]{1,0:T(8,128)(2,1)S(1)}, bf16[256,2048]{1,0:T(8,128)(2,1)}, u32[]{:S(2)}) copy-start(bf16[256,2048]{1,0:T(8,128)(2,1)} %param.36) | copy-start | bytes 3145732
  7.2 100.5 %all-gather.5.cloned.1.call-start = ((), (), s32[]{:S(2)}) async-start(), calls=%async_computation.5 | async-start | bytes 18874368 | tf_op jit(solution)/shard_map/all_gather | solution.py:144
  15.0 456.4 %reduce-scatter.6.cloned.1.call-start = ((), (), s32[]{:S(2)}) async-start(), calls=%async_computation.6 | async-start | bytes 37748736 | tf_op jit(solution)/shard_map/reduce_scatter | solution.py:160
  15.1 102.6 %copy-start.55 = (f32[128]{0:T(128)S(1)}, f32[128]{0:T(128)}, u32[]{:S(2)}) copy-start(f32[128]{0:T(128)} %param.35) | copy-start | bytes 1540
  107.7 11.4 copy-start.56
  119.8 6.0 copy-start.24
  119.8 6.0 copy-start.26
  251.0 15.0 copy-start.30
  266.0 205.4 %copy-start.6 = (bf16[2,256,2048]{2,1,0:T(8,128)(2,1)S(1)}, bf16[2,256,2048]{2,1,0:T(8,128)(2,1)}, u32[]{:S(2)}) copy-start(bf16[2,256,2048]{2,1,0:T(8,128)(2,1)} %param.26) | copy-start | bytes 6291460
  266.0 205.4 %copy-start.51 = (f32[2048]{0:T(1024)S(1)}, f32[2048]{0:T(1024)}, u32[]{:S(2)}) copy-start(f32[2048]{0:T(1024)} %param.37) | copy-start | bytes 24580
  266.0 303.0 %all-gather.7.cloned.1.call-start = ((), (), s32[]{:S(2)}) async-start(), calls=%async_computation.7 | async-start | bytes 18874368 | tf_op jit(solution)/shard_map/all_gather | solution.py:163
  478.9 181.8 %all-gather.9.cloned.1.call-start = ((), (), s32[]{:S(2)}) async-start(), calls=%async_computation.9 | async-start | bytes 18874368 | tf_op jit(solution)/shard_map/all_gather | solution.py:179
  479.5 181.2 %copy-start.58 = (f32[1024]{0:T(1024)S(1)}, f32[1024]{0:T(1024)}, u32[]{:S(2)}) copy-start(f32[1024]{0:T(1024)} %param.41) | copy-start | bytes 12292
  479.5 448.1 %reduce-scatter.10.cloned.1.call-start = ((), (), s32[]{:S(2)}) async-start(), calls=%async_computation.10 | async-start | bytes 37748736 | tf_op jit(solution)/shard_map/reduce_scatter | solution.py:196
  660.8 37.0 %copy-start.57 = (bf16[2048,1024]{1,0:T(8,128)(2,1)S(1)}, bf16[2048,1024]{1,0:T(8,128)(2,1)}, u32[]{:S(2)}) copy-start(bf16[2048,1024]{1,0:T(8,128)(2,1)} %param.40) | copy-start | bytes 12582916
  722.2 324.9 %reduce-scatter.8.cloned.1.call-start = ((), (), s32[]{:S(2)}) async-start(), calls=%async_computation.8 | async-start | bytes 18874368 | tf_op jit(solution)/shard_map/reduce_scatter | solution.py:174
  749.4 178.2 %copy-start.35 = (f32[2048]{0:T(1024)S(1)}, f32[2048]{0:T(1024)}, u32[]{:S(2)}) copy-start(f32[2048]{0:T(1024)} %param.38) | copy-start | bytes 24580
  749.4 178.2 %copy-start.37 = (f32[2,256]{1,0:T(2,128)S(1)}, f32[2,256]{1,0:T(2,128)}, u32[]{:S(2)}) copy-start(f32[2,256]{1,0:T(2,128)} %copy-done.36) | copy-start | bytes 6148
  749.4 178.2 %copy-start.41 = (f32[2,256]{1,0:T(2,128)S(1)}, f32[2,256]{1,0:T(2,128)}, u32[]{:S(2)}) copy-start(f32[2,256]{1,0:T(2,128)} %copy-done.40) | copy-start | bytes 6148
  749.4 183.2 %copy-start.45 = (f32[2,256]{1,0:T(2,128)S(1)}, f32[2,256]{1,0:T(2,128)}, u32[]{:S(2)}) copy-start(f32[2,256]{1,0:T(2,128)} %copy-done.44) | copy-start | bytes 6148
  749.4 297.6 %copy-start.53 = (f32[2048]{0:T(1024)S(1)}, f32[2048]{0:T(1024)}, u32[]{:S(2)}) copy-start(f32[2048]{0:T(1024)} %param.43) | copy-start | bytes 24580
  749.4 397.4 %all-gather.11.cloned.1.call-start = ((), (), s32[]{:S(2)}) async-start(), calls=%async_computation.11 | async-start | bytes 18874368 | tf_op jit(solution)/shard_map/all_gather | solution.py:204
  932.7 122.2 %copy-start.11 = (bf16[2,256,2048]{2,1,0:T(8,128)(2,1)S(1)}, bf16[2,256,2048]{2,1,0:T(8,128)(2,1)}, u32[]{:S(2)}) copy-start(bf16[2,256,2048]{2,1,0:T(8,128)(2,1)} %param.27) | copy-start | bytes 6291460
  1056.8 445.7 %reduce-scatter.14.cloned.1.call-start = ((), (), s32[]{:S(2)}) async-start(), calls=%async_computation.13 | async-start | bytes 2359296 | tf_op jit(solution)/shard_map/reduce_scatter | solution.py:226
  1080.6 76.0 %copy-start.25 = (s32[2,2048]{1,0:T(2,128)S(1)}, s32[2,2048]{1,0:T(2,128)}, u32[]{:S(2)}) copy-start(s32[2,2048]{1,0:T(2,128)} %param.28) | copy-start | bytes 49156
  1080.6 76.0 %copy-start.27 = (s32[2,2048]{1,0:T(2,128)S(1)}, s32[2,2048]{1,0:T(2,128)}, u32[]{:S(2)}) copy-start(s32[2,2048]{1,0:T(2,128)} %param.29) | copy-start | bytes 49156
  1080.6 76.0 %copy-start.31 = (f32[2,4,2,512]{3,2,1,0:T(2,128)S(1)}, f32[2,4,2,512]{3,2,1,0:T(2,128)}, u32[]{:S(2)}) copy-start(f32[2,4,2,512]{3,2,1,0:T(2,128)} %copy-done.30) | copy-start | bytes 98308
  1156.6 278.7 %copy-start.59 = (f32[1024]{0:T(1024)S(1)}, f32[1024]{0:T(1024)}, u32[]{:S(2)}) copy-start(f32[1024]{0:T(1024)} %param.41) | copy-start | bytes 12292
  1172.7 6.3 copy-start.2
  1204.7 6.3 copy-start.2
  1236.7 6.3 copy-start.2
  1268.7 6.3 copy-start.2
  1311.8 6.3 copy-start.2
  1343.8 6.3 copy-start.2
  1375.8 6.3 copy-start.2
  1407.8 6.3 copy-start.2
  1435.3 27.6 %copy-start.13 = (bf16[2,2048,256]{2,1,0:T(8,128)(2,1)S(1)}, bf16[2,2048,256]{2,1,0:T(8,128)(2,1)}, u32[]{:S(2)}) copy-start(bf16[2,2048,256]{2,1,0:T(8,128)(2,1)} %get-tuple-element.234) | copy-start | bytes 6291460
  1435.3 406.5 %all-reduce.8.cloned.1.call-start = ((), (), s32[]{:S(2)}) async-start(), calls=%async_computation.15 | async-start | bytes 20971520 | tf_op jit(solution)/shard_map/psum | solution.py:242
  1435.4 27.6 %copy-start.10 = (bf16[2,2048,2048]{2,1,0:T(8,128)(2,1)S(1)}, bf16[2,2048,2048]{2,1,0:T(8,128)(2,1)}, u32[]{:S(2)}) copy-start(bf16[2,2048,2048]{2,1,0:T(8,128)(2,1)} %all-gather.11.cloned.1.call-done) | copy-start | bytes 50331652
  1478.1 482.3 %reduce-scatter.12.cloned.1.call-start = ((), (), s32[]{:S(2)}) async-start(), calls=%async_computation.12 | async-start | bytes 18874368 | tf_op jit(solution)/shard_map/reduce_scatter | solution.py:223
  1488.9 612.1 %all-reduce.6.cloned.1.call-start = ((), (), s32[]{:S(2)}) async-start(), calls=%async_computation.14 | async-start | bytes 4194304 | tf_op jit(solution)/shard_map/psum | solution.py:258
  1852.6 107.8 %copy-start.7 = (bf16[2,256,2048]{2,1,0:T(8,128)(2,1)S(1)}, bf16[2,256,2048]{2,1,0:T(8,128)(2,1)}, u32[]{:S(2)}) copy-start(bf16[2,256,2048]{2,1,0:T(8,128)(2,1)} %param.26) | copy-start | bytes 6291460
  1852.6 107.8 %copy-start.22 = (bf16[2048,256]{1,0:T(8,128)(2,1)S(1)}, bf16[2048,256]{1,0:T(8,128)(2,1)}, u32[]{:S(2)}) copy-start(bf16[2048,256]{1,0:T(8,128)(2,1)} %param.34) | copy-start | bytes 3145732
  1852.6 107.8 %copy-start.29 = (f32[2048]{0:T(1024)S(1)}, f32[2048]{0:T(1024)}, u32[]{:S(2)}) copy-start(f32[2048]{0:T(1024)} %param.30) | copy-start | bytes 24580
  1852.6 107.8 %copy-start.33 = (f32[2,256]{1,0:T(2,128)S(1)}, f32[2,256]{1,0:T(2,128)}, u32[]{:S(2)}) copy-start(f32[2,256]{1,0:T(2,128)} %copy-done.32) | copy-start | bytes 6148
  1858.2 105.3 %copy-start.49 = (f32[2,256]{1,0:T(2,128)S(1)}, f32[2,256]{1,0:T(2,128)}, u32[]{:S(2)}) copy-start(f32[2,256]{1,0:T(2,128)} %copy-done.48) | copy-start | bytes 6148
  1858.2 105.3 %copy-start.39 = (f32[2,256]{1,0:T(2,128)S(1)}, f32[2,256]{1,0:T(2,128)}, u32[]{:S(2)}) copy-start(f32[2,256]{1,0:T(2,128)} %copy-done.38) | copy-start | bytes 6148
  1966.4 137.6 %copy-start.1 = (bf16[256,2048]{1,0:T(8,128)(2,1)S(1)}, bf16[256,2048]{1,0:T(8,128)(2,1)}, u32[]{:S(2)}) copy-start(bf16[256,2048]{1,0:T(8,128)(2,1)} %param.36) | copy-start | bytes 3145732
  (52 other events, 154.0 us)
Sparse Core Ops, SparseCore 0:
  15.1 92.5 all-gather.4
  266.1 205.2 reduce-scatter.5
  479.1 89.8 all-gather.6
  570.9 89.8 all-gather.8
  722.3 205.2 reduce-scatter.9
  931.0 115.9 reduce-scatter.7
  1057.0 89.8 all-gather.10
  1435.4 41.2 reduce-scatter.13
  1481.0 360.7 all-reduce.7
  1845.6 114.8 reduce-scatter.11
  1966.7 134.2 all-reduce.5
where the time goes:
time: 2120 us; the launch traced here: 2110 us
  waiting for transfers between devices  1340 us (63%)
  matrix products  408 us (19%)
  other arithmetic  182 us (9%)
  local copies, waits for them, and re-layouts  77.3 us (4%)
  blocking collectives  52.7 us (2%)
  loops' own time  32.9 us (2%)
    psum x1, waiting for transfers between devices, body(): lax.psum(query_grad.astype(jnp.bfloat16), 'dp').astype(jnp.float32)  335 us
    reduce_scatter x1, waiting for transfers between devices, body(): lax.psum_scatter(partial_out, 'tensor', scatter_dimension=1, tiled=True)  205 us
    reduce_scatter x1, waiting for transfers between devices, body(): lax.psum_scatter(grad_normed_part, 'tensor', scatter_dimension=1, tiled=T...  178 us
    reduce_scatter x1, waiting for transfers between devices, body(): lax.psum_scatter(partial_feedforward.astype(jnp.bfloat16), 'tensor', scat...  114 us
    reduce_scatter x1, waiting for transfers between devices, body(): lax.psum_scatter(grad_hidden_part.astype(jnp.bfloat16), 'tensor', scatter...  102 us
    all_gather x1, waiting for transfers between devices, body(): hidden_every = lax.all_gather(hidden_local, 'tensor', axis=1, tiled=True)  92.6 us
    psum x1, waiting for transfers between devices, body(): lax.psum((shared_grad, value_bias_part, attn_gain_part, attn_shift_part,...  90.1 us
    all_gather x1, waiting for transfers between devices, body(): lax.all_gather(normed_own, 'tensor', axis=1, tiled=True)  89.4 us
  transfers between devices with their start and end apart: 11, of which 10 were waited for; matrix products, arithmetic and copies ran while one was open for 8% of the time, Pallas kernels for 0%

commit v1 on v0

v1 whole, which is shorter than its diff:
```python
import functools

import jax
import jax.numpy as jnp
from jax import lax
from jax.experimental import pallas as pl
from jax.experimental.pallas import tpu as pltpu
from jax.sharding import PartitionSpec as P

EPSILON = 1e-05
LOG2E = 1.4426950408889634
LN2 = 0.6931471805599453
BF = jnp.bfloat16
F32 = jnp.float32
NEG = -1e30
MIB = 1024 * 1024


def dot(a, b):
    return lax.dot_general(a, b, (((1,), (0,)), ((), ())), preferred_element_type=F32)


def dot_nt(a, b):
    return lax.dot_general(a, b, (((1,), (1,)), ((), ())), preferred_element_type=F32)


def dot_tn(a, b):
    return lax.dot_general(a, b, (((0,), (0,)), ((), ())), preferred_element_type=F32)


def swap(x, bit, axis="tensor"):
    n = lax.axis_size(axis)
    return lax.ppermute(x, axis, [(i, i ^ (1 << bit)) for i in range(n)])


def bit_orders(n):
    bits = list(range(1, n.bit_length() - 1))
    return bits, bits[::-1]


def gather_slots(block, order):
    held = {0: block}
    for bit in list(order) + [0]:
        held.update({k | (1 << bit): swap(v, bit) for k, v in list(held.items())})
    return [held[k] for k in range(len(held))]


def scatter_slots(slots, order):
    held = dict(enumerate(slots))
    for bit in [0] + list(order)[::-1]:
        for k in sorted(held, reverse=True):
            if k & (1 << bit):
                arrived = swap(held.pop(k).astype(BF), bit)
                low = k ^ (1 << bit)
                held[low] = held[low].astype(F32) + arrived.astype(F32)
        held = {k: (v if len(held) == 1 else v.astype(BF)) for k, v in held.items()}
    return held[0].astype(F32)


def xor_order(x, me):
    n = x.shape[0]
    rest = x.shape[1:]
    for bit in range(n.bit_length() - 1):
        pairs = x.reshape((n >> (bit + 1), 2, 1 << bit) + rest)
        x = jnp.where((me >> bit) & 1 == 1, jnp.flip(pairs, 1), pairs).reshape((n,) + rest)
    return x


def stack_heads(block, heads, hd):
    return jnp.concatenate([block[:, i * hd : (i + 1) * hd] for i in range(heads)], axis=0)


def diagonal_mask(rows, cols, same):
    key_at = lax.broadcasted_iota(jnp.int32, (rows, cols), 0)
    query_at = lax.broadcasted_iota(jnp.int32, (rows, cols), 1) % rows
    return (same & (key_at < query_at)) | (key_at == query_at)


def below_blocks(low, at, step, carry):
    even = at - at % 2
    carry = lax.fori_loop(jnp.maximum(low, even), at, lambda b, c: step(b ^ at, 1, c), carry)
    return lax.fori_loop(low // 2, at // 2, lambda p, c: step((p ^ (at // 2)) * 2, 2, c), carry)


def attention_fwd_kernel(low_ref, at_ref, q_ref, k_ref, vt_ref, dock_ref, docq_ref, o_ref, lse_ref, *, heads, hd):
    row = pl.program_id(0)
    span = q_ref.shape[1]
    at = at_ref[0]
    q2 = stack_heads(q_ref[0], heads, hd)
    docq = docq_ref[0]

    def scores(slot, count):
        here = pl.ds(pl.multiple_of(slot * span, count * span), count * span)
        s = dot_nt(k_ref[0, here, :], q2)
        same = dock_ref[0, here, :] == docq
        return s, same, here

    s, same, here = scores(0, 1)
    s = jnp.where(diagonal_mask(span, heads * span, same), s, NEG)
    top = jnp.max(s, axis=0, keepdims=True)
    p = jnp.exp2(s - top)
    total = jnp.sum(p, axis=0, keepdims=True)
    acc = dot(vt_ref[0, :, here], p.astype(BF))

    def step(slot, count, carry):
        top, total, acc = carry
        s, same, here = scores(slot, count)
        s = jnp.where(same, s, NEG)
        new = jnp.maximum(top, jnp.max(s, axis=0, keepdims=True))
        shrink = jnp.exp2(top - new)
        p = jnp.exp2(s - new)
        total = total * shrink + jnp.sum(p, axis=0, keepdims=True)
        acc = acc * shrink + dot(vt_ref[0, :, here], p.astype(BF))
        return new, total, acc

    carry = below_blocks(low_ref[row], at, step, (top, total, acc))
    top, total, acc = carry
    out = (acc / total).T.astype(BF)
    for i in range(heads):
        o_ref[0, :, i * hd : (i + 1) * hd] = out[i * span : (i + 1) * span]
    lse_ref[0, 0] = top + jnp.log2(total)


def attention_bwd_kernel(
    low_ref, at_ref, q_ref, do_ref, o_ref, lse_ref, k_ref, kt_ref, v_ref, dock_ref, docq_ref,
    dq_ref, dk_ref, dv_ref, *, heads, hd, scale,
):
    row = pl.program_id(0)
    span = q_ref.shape[1]
    at = at_ref[0]

    @pl.when(pl.program_id(1) == 0)
    def _():
        dk_ref[...] = jnp.zeros_like(dk_ref)
        dv_ref[...] = jnp.zeros_like(dv_ref)

    q2 = stack_heads(q_ref[0], heads, hd)
    do2 = stack_heads(do_ref[0], heads, hd)
    o2 = stack_heads(o_ref[0], heads, hd)
    delta = jnp.sum((do2.astype(F32) * o2.astype(F32)).T, axis=0, keepdims=True)
    lse = lse_ref[0, 0]
    docq = docq_ref[0]

    def one(slot, count, dqt, diagonal=False):
        here = pl.ds(pl.multiple_of(slot * span, count * span), count * span)
        s = dot_nt(k_ref[0, here, :], q2)
        same = dock_ref[0, here, :] == docq
        if diagonal:
            same = diagonal_mask(span, heads * span, same)
        p = jnp.where(same, jnp.exp2(s - lse), 0.0)
        dp = dot_nt(v_ref[0, here, :], do2)
        ds = (p * (dp - delta)).astype(BF)
        dk_ref[0, here, :] += dot(ds, q2)
        dv_ref[0, here, :] += dot(p.astype(BF), do2)
        return dqt + dot(kt_ref[0, :, here], ds)

    dqt = one(0, 1, jnp.zeros((hd, heads * span), F32), True)
    dqt = below_blocks(low_ref[row], at, one, dqt)
    dq = (dqt * scale).T.astype(BF)
    for i in range(heads):
        dq_ref[0, :, i * hd : (i + 1) * hd] = dq[i * span : (i + 1) * span]


def attention_fwd(q, k, vt, low, at, dock, docq, heads, hd):
    rows, span, width = q.shape
    length = k.shape[1]
    groups = width // (heads * hd)
    gw = heads * hd
    return pl.pallas_call(
        functools.partial(attention_fwd_kernel, heads=heads, hd=hd),
        grid_spec=pltpu.PrefetchScalarGridSpec(
            num_scalar_prefetch=2,
            grid=(rows, groups),
            in_specs=[
                pl.BlockSpec((1, span, gw), lambda r, g, *_: (r, 0, g)),
                pl.BlockSpec((1, length, hd), lambda r, g, *_: (r, 0, 0)),
                pl.BlockSpec((1, hd, length), lambda r, g, *_: (r, 0, 0)),
                pl.BlockSpec((1, length, 1), lambda r, g, *_: (r, 0, 0)),
                pl.BlockSpec((1, 1, heads * span), lambda r, g, *_: (r, 0, 0)),
            ],
            out_specs=[
                pl.BlockSpec((1, span, gw), lambda r, g, *_: (r, 0, g)),
                pl.BlockSpec((1, 1, 1, heads * span), lambda r, g, *_: (r, g, 0, 0)),
            ],
        ),
        out_shape=[
            jax.ShapeDtypeStruct((rows, span, width), BF),
            jax.ShapeDtypeStruct((rows, groups, 1, heads * span), F32),
        ],
        compiler_params=pltpu.CompilerParams(vmem_limit_bytes=24 * MIB),
        cost_estimate=pl.CostEstimate(
            flops=2 * rows * span * width * length, bytes_accessed=8 * MIB, transcendentals=rows * span * length
        ),
    )(low, at, q, k, vt, dock, docq)


def attention_bwd(q, do, o, lse, k, kt, v, low, at, dock, docq, heads, hd, scale):
    rows, span, width = q.shape
    length = k.shape[1]
    groups = width // (heads * hd)
    gw = heads * hd
    blk = pl.BlockSpec((1, span, gw), lambda r, g, *_: (r, 0, g))
    full = pl.BlockSpec((1, length, hd), lambda r, g, *_: (r, 0, 0))
    return pl.pallas_call(
        functools.partial(attention_bwd_kernel, heads=heads, hd=hd, scale=scale),
        grid_spec=pltpu.PrefetchScalarGridSpec(
            num_scalar_prefetch=2,
            grid=(rows, groups),
            in_specs=[
                blk,
                blk,
                blk,
                pl.BlockSpec((1, 1, 1, heads * span), lambda r, g, *_: (r, g, 0, 0)),
                full,
                pl.BlockSpec((1, hd, length), lambda r, g, *_: (r, 0, 0)),
                full,
                pl.BlockSpec((1, length, 1), lambda r, g, *_: (r, 0, 0)),
                pl.BlockSpec((1, 1, heads * span), lambda r, g, *_: (r, 0, 0)),
            ],
            out_specs=[blk, full, full],
        ),
        out_shape=[
            jax.ShapeDtypeStruct((rows, span, width), BF),
            jax.ShapeDtypeStruct((rows, length, hd), F32),
            jax.ShapeDtypeStruct((rows, length, hd), F32),
        ],
        compiler_params=pltpu.CompilerParams(vmem_limit_bytes=32 * MIB),
        cost_estimate=pl.CostEstimate(
            flops=5 * rows * span * width * length, bytes_accessed=16 * MIB, transcendentals=rows * span * length
        ),
    )(low, at, q, do, o, lse, k, kt, v, dock, docq)


def fill(whole_ref, parts, axis):
    for i, slots in enumerate(parts):
        for k, part in enumerate(slots):
            rows, cols = part.shape
            if axis == 1:
                whole_ref[i * rows : (i + 1) * rows, k * cols : (k + 1) * cols] = part[...]
            else:
                whole_ref[k * rows : (k + 1) * rows, i * cols : (i + 1) * cols] = part[...]


def split_parts(refs):
    count = len(refs) // 2
    return [refs[:count], refs[count:]]


def q_kernel(x_ref, b_ref, *refs, factor):
    *parts, o_ref, w_s = refs

    @pl.when(pl.program_id(0) == 0)
    def _():
        fill(w_s, split_parts(parts), 1)

    o_ref[...] = ((dot(x_ref[...], w_s[...]) + b_ref[...]) * factor).astype(BF)


def o_kernel(a_ref, x_ref, b_ref, gain_ref, shift_ref, *refs):
    *parts, mixed_ref, normed_ref, w_s = refs

    @pl.when(pl.program_id(0) == 0)
    def _():
        fill(w_s, split_parts(parts), 0)

    mixed = x_ref[...].astype(F32) + dot(a_ref[...], w_s[...]) + b_ref[...]
    mixed_ref[...] = mixed
    unit, _ = norm_parts(mixed)
    normed_ref[...] = (unit * gain_ref[...] + shift_ref[...]).astype(BF)


def do_kernel(g_ref, *refs):
    *parts, o_ref, w_s = refs

    @pl.when(pl.program_id(0) == 0)
    def _():
        fill(w_s, split_parts(parts), 0)

    o_ref[...] = dot_nt(g_ref[...], w_s[...]).astype(BF)


def dh_kernel(g_ref, kv_ref, shared_ref, *refs):
    *parts, o_ref, w_s = refs

    @pl.when(pl.program_id(0) == 0)
    def _():
        fill(w_s, split_parts(parts), 1)

    o_ref[...] = dot_nt(g_ref[...], w_s[...]) + dot_nt(kv_ref[...], shared_ref[...])


def slot_product(kernel, tiled, fixed, parts, outs, shape):
    flat = parts[0] + parts[1]
    tokens = tiled[0].shape[0]
    tile = tokens // 2
    still = lambda a: pl.BlockSpec(a.shape, lambda i: (0, 0), pipeline_mode=pl.Buffered(1))
    flow = lambda a: pl.BlockSpec((tile, a.shape[1]), lambda i: (i, 0))
    result = pl.pallas_call(
        kernel,
        grid=(2,),
        in_specs=[flow(a) for a in tiled] + [still(a) for a in fixed] + [still(a) for a in flat],
        out_specs=[flow(o) for o in outs],
        out_shape=outs,
        scratch_shapes=[pltpu.VMEM(shape, BF)],
        compiler_params=pltpu.CompilerParams(vmem_limit_bytes=48 * MIB),
        cost_estimate=pl.CostEstimate(
            flops=2 * tokens * shape[0] * shape[1], bytes_accessed=2 * shape[0] * shape[1] + 8 * MIB, transcendentals=0
        ),
    )(*tiled, *fixed, *flat)
    return result


def weight_grad_kernel(*refs, units):
    count = sum(len(a) + len(b) for a, b in units)
    ins = refs[:count]
    o_ref, a_s, b_s, acc, sem = refs[count:]
    steps = len(units)
    wide = a_s.shape[2]
    tile = min(256, wide)

    def copies(u):
        slot, at, out = u % 2, sum(len(a) + len(b) for a, b in units[:u]), []
        for which, (buf, rows) in enumerate(((a_s, units[u][0]), (b_s, units[u][1]))):
            begin = 0
            for j, size in enumerate(rows):
                out.append(
                    pltpu.make_async_copy(ins[at], buf.at[slot, pl.ds(begin, size)], sem.at[slot, which, j])
                )
                begin += size
                at += 1
        return out

    for c in copies(0):
        c.start()
    for u in range(steps):
        if u + 1 < steps:
            for c in copies(u + 1):
                c.start()
        for c in copies(u):
            c.wait()

        @pl.loop(0, wide // tile)
        def _(i, u=u):
            here = pl.ds(pl.multiple_of(i * tile, tile), tile)
            term = dot_tn(a_s[u % 2, :, here], b_s[u % 2])
            if u == 0:
                acc[here, :] = term
            elif u + 1 < steps:
                acc[here, :] += term
            else:
                o_ref[here, :] = (acc[here, :] + term).astype(BF)


def weight_grad(a_units, b_units):
    units = [([x.shape[0] for x in a], [x.shape[0] for x in b]) for a, b in zip(a_units, b_units)]
    flat = [x for a, b in zip(a_units, b_units) for x in list(a) + list(b)]
    tokens = sum(units[0][0])
    wide, cols = a_units[0][0].shape[1], b_units[0][0].shape[1]
    most = max(max(len(a), len(b)) for a, b in units)
    return pl.pallas_call(
        functools.partial(weight_grad_kernel, units=units),
        in_specs=[pl.BlockSpec(memory_space=pl.ANY)] * len(flat),
        out_specs=pl.BlockSpec(memory_space=pltpu.VMEM),
        out_shape=jax.ShapeDtypeStruct((wide, cols), BF),
        scratch_shapes=[
            pltpu.VMEM((2, tokens, wide), BF),
            pltpu.VMEM((2, tokens, cols), BF),
            pltpu.VMEM((wide, cols), F32),
            pltpu.SemaphoreType.DMA((2, 2, most)),
        ],
        compiler_params=pltpu.CompilerParams(vmem_limit_bytes=48 * MIB),
        cost_estimate=pl.CostEstimate(
            flops=2 * tokens * len(units) * wide * cols, bytes_accessed=32 * MIB, transcendentals=0
        ),
    )(*flat)


def sum_all(x, axes):
    for axis in axes:
        for bit in range(lax.axis_size(axis).bit_length() - 1):
            x = x + swap(x, bit, axis)
    return x


def sum_line(x):
    if lax.axis_size("dp") != 4:
        return lax.psum(x, "dp")
    inner = lax.axis_index("dp") % 3 != 0
    pair = (x.astype(F32) + lax.ppermute(x, "dp", [(0, 1), (3, 2)]).astype(F32)).astype(BF)
    both = (pair.astype(F32) + lax.ppermute(pair, "dp", [(1, 2), (2, 1)]).astype(F32)).astype(BF)
    return jnp.where(inner, both, lax.ppermute(both, "dp", [(1, 0), (2, 3)]))


def mlp_kernel(xa_ref, xb_ref, ca_ref, cb_ref, up_ref, bias_ref, down_ref,
               ffa_ref, ffb_ref, gna_ref, gnb_ref, act_ref, gr_ref, gb_ref, x_s, c_s, ff_s, gn_s):
    step = pl.program_id(0)
    half = xa_ref.shape[0]

    @pl.when(step == 0)
    def _():
        x_s[:half] = xa_ref[...]
        x_s[half:] = xb_ref[...]
        c_s[:half] = ca_ref[...]
        c_s[half:] = cb_ref[...]

    raised = dot(x_s[...], up_ref[...]) + bias_ref[...]
    square = raised * raised
    th = jnp.tanh(0.7978845608028654 * raised * (1.0 + 0.044715 * square))
    act = (0.5 * raised * (1.0 + th)).astype(BF)
    act_ref[...] = act
    ff = dot(act, down_ref[...])
    slope = 0.5 * (1.0 + th) + 0.5 * raised * (1.0 - th * th) * (
        0.7978845608028654 * (1.0 + 3 * 0.044715 * square)
    )
    gr32 = dot_nt(c_s[...], down_ref[...]) * slope
    gr = gr32.astype(BF)
    gr_ref[...] = gr
    gb_ref[...] = jnp.sum(gr.astype(F32), axis=0, keepdims=True)
    gn = dot_nt(gr, up_ref[...])

    @pl.when(step == 0)
    def _():
        ff_s[...] = ff
        gn_s[...] = gn

    @pl.when(step != 0)
    def _():
        ff_s[...] += ff
        gn_s[...] += gn

    @pl.when(step == pl.num_programs(0) - 1)
    def _():
        ffa_ref[...] = ff_s[:half].astype(BF)
        ffb_ref[...] = ff_s[half:].astype(BF)
        gna_ref[...] = gn_s[:half].astype(BF)
        gnb_ref[...] = gn_s[half:].astype(BF)


def mlp_unit(xa, xb, ca, cb, up, bias, down):
    half, d = xa.shape
    ff = up.shape[1]
    tile = min(512, ff)
    tokens = 2 * half
    whole = pl.BlockSpec((half, d), lambda j: (0, 0))
    return pl.pallas_call(
        mlp_kernel,
        grid=(ff // tile,),
        in_specs=[
            whole, whole, whole, whole,
            pl.BlockSpec((d, tile), lambda j: (0, j)),
            pl.BlockSpec((1, tile), lambda j: (0, j)),
            pl.BlockSpec((tile, d), lambda j: (j, 0)),
        ],
        out_specs=[
            whole, whole, whole, whole,
            pl.BlockSpec((tokens, tile), lambda j: (0, j)),
            pl.BlockSpec((tokens, tile), lambda j: (0, j)),
            pl.BlockSpec((1, tile), lambda j: (0, j)),
        ],
        out_shape=[jax.ShapeDtypeStruct((half, d), BF)] * 4
        + [jax.ShapeDtypeStruct((tokens, ff), BF)] * 2
        + [jax.ShapeDtypeStruct((1, ff), F32)],
        scratch_shapes=[
            pltpu.VMEM((tokens, d), BF),
            pltpu.VMEM((tokens, d), BF),
            pltpu.VMEM((tokens, d), F32),
            pltpu.VMEM((tokens, d), F32),
        ],
        compiler_params=pltpu.CompilerParams(vmem_limit_bytes=56 * MIB),
        cost_estimate=pl.CostEstimate(
            flops=8 * tokens * d * ff, bytes_accessed=20 * MIB, transcendentals=tokens * ff
        ),
    )(xa, xb, ca, cb, up, bias, down)


def norm_parts(values):
    center = values - jnp.mean(values, axis=-1, keepdims=True)
    scale = lax.rsqrt(jnp.mean(center * center, axis=-1, keepdims=True) + EPSILON)
    return center * scale, scale


def norm_back(unit, scale, gain, grad):
    e = gain * grad
    back = scale * (e - jnp.mean(e, axis=-1, keepdims=True) - unit * jnp.mean(e * unit, axis=-1, keepdims=True))
    return back, jnp.sum(grad * unit, axis=(0, 1)), jnp.sum(grad, axis=(0, 1))


def body(
    inputs, cotangent, documents, padding, attn_gain, attn_shift, query_matrix, query_bias, shared_matrix,
    value_bias, output_matrix, output_bias, mlp_gain, mlp_shift, expansion_weights, up_bias, down_matrix, down_bias,
):
    n = lax.axis_size("tensor")
    me = lax.axis_index("tensor")
    hd = value_bias.shape[0]
    seqs, span, d = inputs.shape
    length = documents.shape[1]
    qw = query_matrix.shape[1]
    heads = qw // hd
    scale = hd**-0.5
    paths = bit_orders(n)
    tokens = seqs * span

    x32 = inputs.astype(F32)
    unit1, scale1 = norm_parts(x32)
    hidden = (unit1 * attn_gain + attn_shift).astype(BF)
    h2 = hidden.reshape(tokens, d)
    shared = dot(h2, shared_matrix)
    kv_own = jnp.concatenate([shared[:, :hd], shared[:, hd:] + value_bias], axis=1).astype(BF)
    kv_own = kv_own.reshape(seqs, span, 2 * hd)
    kv = jnp.concatenate(gather_slots(kv_own, paths[0]), axis=1)
    keys, values = kv[..., :hd], kv[..., hd:]
    keys_t, values_t = keys.swapaxes(1, 2), values.swapaxes(1, 2)

    half = d // 2
    wq = [gather_slots(query_matrix[i * half : (i + 1) * half], paths[i]) for i in range(2)]
    wo = [gather_slots(output_matrix[:, i * half : (i + 1) * half], paths[i]) for i in range(2)]
    bq = jnp.concatenate(gather_slots(query_bias[None], paths[0]), axis=1)

    like = lambda t, cols: jax.ShapeDtypeStruct((tokens, cols), t)
    (query,) = slot_product(
        functools.partial(q_kernel, factor=scale * LOG2E), [h2], [bq], wq, [like(BF, n * qw)], (d, n * qw)
    )
    query = query.reshape(seqs, span, n * qw)
    first = lax.dynamic_slice_in_dim(documents, me * span, 1, 1)
    low = (jnp.sum((documents < first).astype(jnp.int32), axis=1) // span).astype(jnp.int32)
    low = jnp.minimum(low, me)
    at = me.reshape(1).astype(jnp.int32)
    dock = jnp.where(padding == 1, documents, -1)
    dock = xor_order(dock.reshape(seqs, n, span).swapaxes(0, 1), me).swapaxes(0, 1).reshape(seqs, length, 1)
    docq = lax.dynamic_slice_in_dim(documents, me * span, span, 1)
    docq = jnp.concatenate([docq] * heads, axis=1)[:, None, :]
    attended, lse = attention_fwd(query, keys, values_t, low, at, dock, docq, heads, hd)
    a2 = attended.reshape(tokens, n * qw)
    mixed, normed = slot_product(
        o_kernel, [a2, inputs.reshape(tokens, d)], [output_bias[None], mlp_gain[None], mlp_shift[None]], wo,
        [like(F32, d), like(BF, d)], (n * qw, d),
    )
    mixed, normed = mixed.reshape(seqs, span, d), normed.reshape(seqs, span, d)
    unit2, scale2 = norm_parts(mixed)

    cot_slots = [gather_slots(cotangent[r], paths[r % 2]) for r in range(seqs)]
    normed_slots = [gather_slots(normed[r], paths[r % 2]) for r in range(seqs)]
    ff_slots = [[None] * n for _ in range(seqs)]
    gn_slots = [[None] * n for _ in range(seqs)]
    acts, grs, xs, cs = [], [], [], []
    up_bias_part = jnp.zeros((1, up_bias.shape[0]), F32)
    for k in range(0, n, 2):
        for r in range(seqs):
            xa, xb, ca, cb = normed_slots[r][k], normed_slots[r][k + 1], cot_slots[r][k], cot_slots[r][k + 1]
            ffa, ffb, gna, gnb, act, gr, gb = mlp_unit(
                xa, xb, ca, cb, expansion_weights, up_bias[None], down_matrix
            )
            ff_slots[r][k], ff_slots[r][k + 1] = ffa, ffb
            gn_slots[r][k], gn_slots[r][k + 1] = gna, gnb
            acts.append(act)
            grs.append(gr)
            xs.append([xa, xb])
            cs.append([ca, cb])
            up_bias_part = up_bias_part + gb
    grad_normed = jnp.stack([scatter_slots(gn_slots[r], paths[r % 2]) for r in range(seqs)])
    down_gradient = weight_grad([[a] for a in acts], cs)
    up_gradient = weight_grad(xs, [[g] for g in grs])
    mlp_branch = jnp.stack([scatter_slots(ff_slots[r], paths[r % 2]) for r in range(seqs)])
    block_out = (mixed + mlp_branch + down_bias).astype(BF)

    cot_wide = cotangent.astype(F32)
    back2, mlp_gain_part, mlp_shift_part = norm_back(unit2, scale2, mlp_gain, grad_normed)
    grad_mixed = cot_wide + back2
    gm2 = grad_mixed.astype(BF).reshape(tokens, d)
    (grad_attended,) = slot_product(do_kernel, [gm2], [], wo, [like(BF, n * qw)], (n * qw, d))
    grad_attended = grad_attended.reshape(seqs, span, n * qw)
    dq, dk, dv = attention_bwd(
        query, grad_attended, attended, lse, keys, keys_t, values, low, at, dock, docq, heads, hd, scale
    )
    dq2 = dq.reshape(tokens, n * qw)

    wo_grads = [
        scatter_slots(
            [dot_tn(a2[:, k * qw : (k + 1) * qw], gm2[:, i * half : (i + 1) * half]) for k in range(n)], paths[i]
        )
        for i in range(2)
    ]
    dkv = jnp.concatenate([dk * LN2, dv], axis=-1).astype(BF)
    dkv_own = scatter_slots([dkv[:, k * span : (k + 1) * span] for k in range(n)], paths[0]).astype(BF)
    wq_grads = [
        scatter_slots(
            [dot_tn(h2[:, i * half : (i + 1) * half], dq2[:, k * qw : (k + 1) * qw]) for k in range(n)], paths[i]
        )
        for i in range(2)
    ]
    (grad_hidden,) = slot_product(
        dh_kernel, [dq2, dkv_own.reshape(tokens, 2 * hd)], [shared_matrix], wq, [like(F32, d)], (d, n * qw)
    )
    grad_hidden = grad_hidden.reshape(seqs, span, d)
    back1, attn_gain_part, attn_shift_part = norm_back(unit1, scale1, attn_gain, grad_hidden)
    input_grad = grad_mixed + back1
    shared_part = dot_tn(h2, dkv_own.reshape(tokens, 2 * hd))
    value_bias_part = jnp.sum(dkv_own[..., hd:].astype(F32), axis=(0, 1))
    query_bias_part = xor_order(jnp.sum(dq2.astype(F32), axis=0).reshape(n, qw), me).reshape(-1)

    everywhere = ("tensor", "dp")
    down_gradient, up_gradient = lax.psum((down_gradient, up_gradient), "dp")
    output_gradient = jnp.concatenate([sum_line(g.astype(BF)) for g in wo_grads], axis=1)
    query_gradient = jnp.concatenate([sum_line(g.astype(BF)) for g in wq_grads], axis=0)
    up_bias_grad = sum_all(up_bias_part, ("dp",))[0]
    early = sum_all(
        jnp.stack([mlp_gain_part, mlp_shift_part, jnp.sum(grad_mixed, axis=(0, 1)), jnp.sum(cot_wide, axis=(0, 1))]),
        everywhere,
    )
    mlp_gain_grad, mlp_shift_grad, output_bias_grad, down_bias_grad = early
    late = sum_all(
        jnp.concatenate([attn_gain_part, attn_shift_part, query_bias_part, value_bias_part])[None], everywhere
    )[0]
    attn_gain_grad, attn_shift_grad = late[:d], late[d : 2 * d]
    query_bias_grad = lax.dynamic_slice_in_dim(late, 2 * d + me * qw, qw, 0)
    value_bias_grad = late[2 * d + n * qw :]
    piece = d // n
    shared_slots = [
        lax.dynamic_slice_in_dim(shared_part, (me ^ k) * piece, piece, 0).astype(BF) for k in range(n)
    ]
    shared_sum = sum_all(scatter_slots(shared_slots, paths[0]), ("dp",)).astype(BF)
    shared_slots = jnp.concatenate(gather_slots(shared_sum, paths[0]), axis=0)
    shared_grad = xor_order(shared_slots.reshape(n, piece, 2 * hd), me).reshape(d, 2 * hd).astype(F32)
    output_gradient, query_gradient, up_gradient, down_gradient = (
        g.astype(F32) for g in (output_gradient, query_gradient, up_gradient, down_gradient)
    )
    return (
        block_out, input_grad, attn_gain_grad, attn_shift_grad, query_gradient, query_bias_grad, shared_grad,
        value_bias_grad, output_gradient, output_bias_grad, mlp_gain_grad, mlp_shift_grad, up_gradient, up_bias_grad,
        down_gradient, down_bias_grad,
    )


def solution(mesh):
    act = P("dp", "tensor", None)
    cols, rows, vec, rep = P(None, "tensor"), P("tensor", None), P("tensor"), P()
    ids = P("dp", None)
    return jax.shard_map(
        body,
        mesh=mesh,
        in_specs=(act, act, ids, ids, rep, rep, cols, vec, rep, rep, rows, rep, rep, rep, cols, vec, rows, rep),
        out_specs=(act, act, rep, rep, cols, vec, rep, rep, rows, rep, rep, rep, cols, vec, rows, rep),
        check_vma=False,
    )
```

time: 2120 us -> 1030 us (0.49)
  waiting for transfers between devices: 1340 us -> 380 us
  matrix products: 408 us -> 44.7 us
  Pallas kernels: 0 us -> 270 us
  starting transfers between devices: 0.45 us -> 171 us
  other arithmetic: 182 us -> 79.9 us
  blocking collectives: 52.7 us -> 0 us
  loops' own time: 32.9 us -> 0 us
    reduce_scatter x5 -> x0, waiting for transfers between devices: 600 us -> none  [the longest x1 205 us: body(): lax.psum_scatter(partial_out, 'tensor', scatter_dimension=1, tiled=True)]
    psum x2 -> x1, waiting for transfers between devices: 425 us -> 0.01 us  [body(): down_gradient, up_gradient = lax.psum((down_gradient, up_gradient), 'dp')]
    ppermute x0 -> x173, waiting for transfers between devices: none -> 380 us  [the longest x161 324 us: swap(): return lax.ppermute(x, axis, [(i, i ^ 1 << bit) for i in range(n)])]
    dot_general x71 -> x34, matrix products: 408 us -> 44.7 us  [the longest x33 43.9 us: dot_tn(): lax.dot_general(a, b, (((0,), (0,)), ((), ())), preferred_element_type=F32)]
    all_gather x4 -> x0, waiting for transfers between devices: 317 us -> none  [the longest x1 92.6 us: body(): hidden_every = lax.all_gather(hidden_local, 'tensor', axis=1, tiled=True)]
    pallas_call x0 -> x16, Pallas kernels: none -> 270 us  [the longest x8 142 us: mlp_unit(): pl.pallas_call(mlp_kernel, grid=(ff // tile,), in_specs=[whole, whole, wh...]
    ppermute x0 -> x173, starting transfers between devices: none -> 171 us  [the longest x161 156 us: swap(): return lax.ppermute(x, axis, [(i, i ^ 1 << bit) for i in range(n)])]
    convert_element_type x18 -> x40, other arithmetic: 93.7 us -> 40.2 us  [the longest x20 19.3 us: scatter_slots(): held = {k: v if len(held) == 1 else v.astype(BF) for k, v in held.items()}]
  transfers between devices with their start and end apart: 11 -> 174, of which waited for: 10 -> 57; matrix products, arithmetic and copies ran while one was open for 8% -> 14% of each run, Pallas kernels for 0% -> 26%
where the time goes in v1:
time: 1030 us; the launch traced here: 1020 us
  waiting for transfers between devices  380 us (37%)
  Pallas kernels  270 us (26%)
  starting transfers between devices  171 us (17%)
  other arithmetic  79.9 us (8%)
  local copies, waits for them, and re-layouts  62.1 us (6%)
  matrix products  44.7 us (4%)
  between operations  17.1 us (2%)
    ppermute x161, waiting for transfers between devices, swap(): return lax.ppermute(x, axis, [(i, i ^ 1 << bit) for i in range(n)])  324 us
    ppermute x161, starting transfers between devices, swap(): return lax.ppermute(x, axis, [(i, i ^ 1 << bit) for i in range(n)])  156 us
    pallas_call x8, Pallas kernels, mlp_unit(): pl.pallas_call(mlp_kernel, grid=(ff // tile,), in_specs=[whole, whole, wh...  142 us
    pallas_call x2, Pallas kernels, weight_grad(): pl.pallas_call(functools.partial(weight_grad_kernel, units=units), in_spe...  60.7 us
    dot_general x33, matrix products, dot_tn(): lax.dot_general(a, b, (((0,), (0,)), ((), ())), preferred_element_type=F32)  43.9 us
    ppermute x4, waiting for transfers between devices, sum_line(): return jnp.where(inner, both, lax.ppermute(both, 'dp', [(1, 0), (2, 3)]))  41 us
    pallas_call x4, Pallas kernels, slot_product(): pl.pallas_call(kernel, grid=(2,), in_specs=[flow(a) for a in tiled] + [st...  40.9 us
    unnamed x361, local copies, waits for them, and re-layouts  40.1 us
  transfers between devices with their start and end apart: 174, of which 57 were waited for; matrix products, arithmetic and copies ran while one was open for 14% of the time, Pallas kernels for 26%

profile of v1, /device:TPU:0, one launch (start us, length us, event | category | flops | bytes accessed | tf_op | source)
XLA Modules:
  0.0 1023.9 jit_solution(15228987323092666423)
XLA Ops:
  21.0 6.6 collective-permute-done.5
  30.8 6.5 collective-permute-done.22
  42.9 9.2 collective-permute-done.10.refs_4_
  54.8 8.7 collective-permute-done.38.refs_12_
  67.5 7.2 collective-permute-done.31.refs_4_
  82.2 5.8 collective-permute-done.19.refs_14_
  117.5 12.8 %collective-permute-done.53.ca_ref.refs_7_ = bf16[256,2048]{1,0:T(8,128)(2,1)} collective-permute-done((bf16[256,2048]{1,0:T(8,128)(2,1)}, bf16[256,2048]{1,0:T(8,128)(2,1)}, u32[]{:S(2)}, u32[]{:S(2)}) %collective-permute-start.53) | collective-permute-done | bytes 1048608 | tf_op jit(solution)/shard_map/ppermute | solution.py:33
  138.7 9.3 shard_map.297
  150.2 11.2 %shard_map.298 = (bf16[2,256,2048]{2,1,0:T(8,128)(2,1)S(1)}, f32[2,8,1,512]{3,2,1,0:T(1,128)S(1)}) custom-call(s32[2]{0:T(128)S(1)} %fusion.130.low_ref, s32[1]{0:T(128)} %bitcast.at_ref, bf16[2,256,2048]{2,1,0:T(8,128)(2,1)S(1)} %bitcast.135, bf16[2,2048,128]{2,1,0:T(8,128)(2,1)S(1)} %copy-done.7, bf16[2,128,2048]{2,1,0:T(8,128)(2,1)S(1)} %copy-done.5, ...), custom_call_target="tpu_custom_call" | custom-call | flops 4294967296 | bytes 8388608 | tf_op jit(solution)/shard_map/pallas_call | solution.py:169
  162.9 11.3 %shard_map.299 = (f32[512,2048]{1,0:T(8,128)}, bf16[512,2048]{1,0:T(8,128)(2,1)}) custom-call(bf16[512,2048]{1,0:T(8,128)(2,1)} %bitcast.115, bf16[512,2048]{1,0:T(8,128)(2,1)} %bitcast.139, f32[1,2048]{1,0:T(1,128)S(1)} %bitcast.133, f32[1,2048]{1,0:T(1,128)S(1)} %bitcast.132, f32[1,2048]{1,0:T(1,128)S(1)} %bitcast.134, bf16[256,1024]{1,0:T(8,128)(2,1)S(1)} %copy-done.39, ...), custom_call_target="tpu_custom_call" | custom-call | flops 4294967296 | bytes 16777216 | tf_op jit(solution)/shard_map/pallas_call | solution.py:298
  174.2 16.9 %collective-permute-start.58 = (bf16[256,2048]{1,0:T(8,128)(2,1)}, bf16[256,2048]{1,0:T(8,128)(2,1)}, u32[]{:S(2)}, u32[]{:S(2)}) collective-permute-start(bf16[256,2048]{1,0:T(8,128)(2,1)} %collective-permute-done.53.ca_ref.refs_7_), channel_id=1, source_target_pairs={{0,4},{1,5},{2,6},{3,7},{4,0},{5,1},{6,2},{7,3},{8,12},{9,13},{10,... | collective-permute-start | bytes 3145736 | tf_op jit(solution)/shard_map/ppermute | solution.py:33
  191.1 8.5 collective-permute-start.48
  217.5 10.4 %collective-permute-done.79.ca_ref.refs_22_ = bf16[256,2048]{1,0:T(8,128)(2,1)} collective-permute-done((bf16[256,2048]{1,0:T(8,128)(2,1)}, bf16[256,2048]{1,0:T(8,128)(2,1)}, u32[]{:S(2)}, u32[]{:S(2)}) %collective-permute-start.79) | collective-permute-done | bytes 1048608 | tf_op jit(solution)/shard_map/ppermute | solution.py:33
  230.7 19.4 %collective-permute-done.66.xa_ref.refs_9_ = bf16[256,2048]{1,0:T(8,128)(2,1)} collective-permute-done((bf16[256,2048]{1,0:T(8,128)(2,1)S(1)}, bf16[256,2048]{1,0:T(8,128)(2,1)}, u32[]{:S(2)}, u32[]{:S(2)}) %collective-permute-start.66) | collective-permute-done | bytes 1048608 | tf_op jit(solution)/shard_map/ppermute | solution.py:33
  250.3 17.6 %shard_map.304 = (bf16[256,2048]{1,0:T(8,128)(2,1)}, bf16[256,2048]{1,0:T(8,128)(2,1)}, bf16[256,2048]{1,0:T(8,128)(2,1)}, bf16[256,2048]{1,0:T(8,128)(2,1)}, bf...) custom-call(bf16[256,2048]{1,0:T(8,128)(2,1)} %copy-done.14, ...), custom_call_target="tpu_custom_call" | custom-call | flops 8589934592 | bytes 20971520 | tf_op jit(solution)/shard_map/pallas_call | solution.py:445
  270.2 18.0 %shard_map.300 = (bf16[256,2048]{1,0:T(8,128)(2,1)}, bf16[256,2048]{1,0:T(8,128)(2,1)}, bf16[256,2048]{1,0:T(8,128)(2,1)}, bf16[256,2048]{1,0:T(8,128)(2,1)}, bf...) custom-call(bf16[256,2048]{1,0:T(8,128)(2,1)} %copy-done.12, ...), custom_call_target="tpu_custom_call" | custom-call | flops 8589934592 | bytes 20971520 | tf_op jit(solution)/shard_map/pallas_call | solution.py:445
  289.5 17.6 %shard_map.305 = (bf16[256,2048]{1,0:T(8,128)(2,1)}, bf16[256,2048]{1,0:T(8,128)(2,1)}, bf16[256,2048]{1,0:T(8,128)(2,1)}, bf16[256,2048]{1,0:T(8,128)(2,1)}, bf...) custom-call(bf16[256,2048]{1,0:T(8,128)(2,1)} %collective-permute-done.66.xa_ref.refs_9_, ...), custom_call_target="tpu_custom_call" | custom-call | flops 8589934592 | bytes 20971520 | tf_op jit(solution)/shard_map/pallas_call | solution.py:445
  310.4 17.8 %shard_map.306 = (bf16[256,2048]{1,0:T(8,128)(2,1)}, bf16[256,2048]{1,0:T(8,128)(2,1)}, bf16[256,2048]{1,0:T(8,128)(2,1)}, bf16[256,2048]{1,0:T(8,128)(2,1)}, bf...) custom-call(bf16[256,2048]{1,0:T(8,128)(2,1)} %collective-permute-done.72.xa_ref.refs_15_, ...), custom_call_target="tpu_custom_call" | custom-call | flops 8589934592 | bytes 20971520 | tf_op jit(solution)/shard_map/pallas_call | solution.py:445
  328.8 17.6 %shard_map.301 = (bf16[256,2048]{1,0:T(8,128)(2,1)}, bf16[256,2048]{1,0:T(8,128)(2,1)}, bf16[256,2048]{1,0:T(8,128)(2,1)}, bf16[256,2048]{1,0:T(8,128)(2,1)}, bf...) custom-call(bf16[256,2048]{1,0:T(8,128)(2,1)} %copy-done.135, ...), custom_call_target="tpu_custom_call" | custom-call | flops 8589934592 | bytes 20971520 | tf_op jit(solution)/shard_map/pallas_call | solution.py:445
  348.0 18.0 %shard_map.302 = (bf16[256,2048]{1,0:T(8,128)(2,1)}, bf16[256,2048]{1,0:T(8,128)(2,1)}, bf16[256,2048]{1,0:T(8,128)(2,1)}, bf16[256,2048]{1,0:T(8,128)(2,1)}, bf...) custom-call(bf16[256,2048]{1,0:T(8,128)(2,1)} %copy-done.137, ...), custom_call_target="tpu_custom_call" | custom-call | flops 8589934592 | bytes 20971520 | tf_op jit(solution)/shard_map/pallas_call | solution.py:445
  367.4 17.7 %shard_map.307 = (bf16[256,2048]{1,0:T(8,128)(2,1)}, bf16[256,2048]{1,0:T(8,128)(2,1)}, bf16[256,2048]{1,0:T(8,128)(2,1)}, bf16[256,2048]{1,0:T(8,128)(2,1)}, bf...) custom-call(bf16[256,2048]{1,0:T(8,128)(2,1)} %collective-permute-done.77.xa_ref.refs_21_, ...), custom_call_target="tpu_custom_call" | custom-call | flops 8589934592 | bytes 20971520 | tf_op jit(solution)/shard_map/pallas_call | solution.py:445
  387.4 18.0 %shard_map.303 = (bf16[256,2048]{1,0:T(8,128)(2,1)}, bf16[256,2048]{1,0:T(8,128)(2,1)}, bf16[256,2048]{1,0:T(8,128)(2,1)}, bf16[256,2048]{1,0:T(8,128)(2,1)}, bf...) custom-call(bf16[256,2048]{1,0:T(8,128)(2,1)} %copy-done.143, ...), custom_call_target="tpu_custom_call" | custom-call | flops 8589934592 | bytes 20971520 | tf_op jit(solution)/shard_map/pallas_call | solution.py:445
  405.5 26.4 %shard_map.312 = bf16[1024,2048]{1,0:T(8,128)(2,1)} custom-call(bf16[512,1024]{1,0:T(8,128)(2,1)S(1)} %copy-done.60, bf16[256,2048]{1,0:T(8,128)(2,1)S(1)} %copy-done.9, bf16[256,2048]{1,0:T(8,128)(2,1)S(1)} %copy-done.43, bf16[512,1024]{1,0:T(8,128)(2,1)S(1)} %copy-done.58, bf16[256,2048]{1,0:T(8,128)(2,1)S(1)} %copy-done.11, ...), custom_call_target="tpu_custom_call" | custom-call | flops 17179869184 | bytes 33554432 | tf_op jit(solution)/shard_map/pallas_call | solution.py:360
  431.9 34.3 %shard_map.311 = bf16[2048,1024]{1,0:T(8,128)(2,1)} custom-call(bf16[256,2048]{1,0:T(8,128)(2,1)S(1)} %copy-done.13, bf16[256,2048]{1,0:T(8,128)(2,1)} %collective-permute-done.42.xb_ref.refs_1_, bf16[512,1024]{1,0:T(8,128)(2,1)S(1)} %copy-done.59, bf16[256,2048]{1,0:T(8,128)(2,1)S(1)} %copy-done.15, ...), custom_call_target="tpu_custom_call" | custom-call | flops 17179869184 | bytes 33554432 | tf_op jit(solution)/shard_map/pallas_call | solution.py:360
  489.2 20.1 %collective-permute-done.96 = bf16[256,2048]{1,0:T(8,128)(2,1)S(1)} collective-permute-done((bf16[256,2048]{1,0:T(8,128)(2,1)S(1)}, bf16[256,2048]{1,0:T(8,128)(2,1)S(1)}, u32[]{:S(2)}, u32[]{:S(2)}) %collective-permute-start.96) | collective-permute-done | bytes 1048608 | tf_op jit(solution)/shard_map/ppermute | solution.py:33
  517.4 18.0 %collective-permute-done.82 = bf16[256,2048]{1,0:T(8,128)(2,1)S(1)} collective-permute-done((bf16[256,2048]{1,0:T(8,128)(2,1)S(1)}, bf16[256,2048]{1,0:T(8,128)(2,1)S(1)}, u32[]{:S(2)}, u32[]{:S(2)}) %collective-permute-start.82) | collective-permute-done | bytes 1048608 | tf_op jit(solution)/shard_map/ppermute | solution.py:33
  541.4 16.5 %collective-permute-done.93 = bf16[256,2048]{1,0:T(8,128)(2,1)S(1)} collective-permute-done((bf16[256,2048]{1,0:T(8,128)(2,1)S(1)}, bf16[256,2048]{1,0:T(8,128)(2,1)S(1)}, u32[]{:S(2)}, u32[]{:S(2)}) %collective-permute-start.93) | collective-permute-done | bytes 1048608 | tf_op jit(solution)/shard_map/ppermute | solution.py:33
  557.9 22.3 %collective-permute-done.97 = bf16[256,2048]{1,0:T(8,128)(2,1)S(1)} collective-permute-done((bf16[256,2048]{1,0:T(8,128)(2,1)S(1)}, bf16[256,2048]{1,0:T(8,128)(2,1)S(1)}, u32[]{:S(2)}, u32[]{:S(2)}) %collective-permute-start.97) | collective-permute-done | bytes 1048608 | tf_op jit(solution)/shard_map/ppermute | solution.py:33
  590.2 16.9 %collective-permute-done.71 = bf16[256,2048]{1,0:T(8,128)(2,1)} collective-permute-done((bf16[256,2048]{1,0:T(8,128)(2,1)S(1)}, bf16[256,2048]{1,0:T(8,128)(2,1)}, u32[]{:S(2)}, u32[]{:S(2)}) %collective-permute-start.71) | collective-permute-done | bytes 1048608 | tf_op jit(solution)/shard_map/ppermute | solution.py:33
  607.1 23.2 %collective-permute-done.83 = bf16[256,2048]{1,0:T(8,128)(2,1)} collective-permute-done((bf16[256,2048]{1,0:T(8,128)(2,1)}, bf16[256,2048]{1,0:T(8,128)(2,1)}, u32[]{:S(2)}, u32[]{:S(2)}) %collective-permute-start.83) | collective-permute-done | bytes 1048608 | tf_op jit(solution)/shard_map/ppermute | solution.py:33
  645.3 9.4 shard_map.308
  657.9 14.6 %shard_map.309 = (bf16[2,256,2048]{2,1,0:T(8,128)(2,1)S(1)}, f32[2,2048,128]{2,1,0:T(8,128)S(1)}, f32[2,2048,128]{2,1,0:T(8,128)S(1)}) custom-call(s32[2]{0:T(128)S(1)} %fusion.130.low_ref, s32[1]{0:T(128)} %bitcast.at_ref, bf16[2,256,2048]{2,1,0:T(8,128)(2,1)S(1)} %bitcast.136, bf16[2,256,2048]{2,1,0:T(8,128)(2,1)S(1)} %bitcast.137, ...), custom_call_target="tpu_custom_call" | custom-call | flops 10737418240 | bytes 16777216 | tf_op jit(solution)/shard_map/pallas_call | solution.py:204
  706.0 9.2 collective-permute-start.166
  717.3 7.2 collective-permute-start.167
  726.5 17.7 %collective-permute-start.168 = (f32[4,2048]{1,0:T(4,128)S(1)}, f32[4,2048]{1,0:T(4,128)S(1)}, u32[]{:S(2)}, u32[]{:S(2)}) collective-permute-start(f32[4,2048]{1,0:T(4,128)S(1)} %fusion.145), channel_id=1, source_target_pairs={{0,4},{1,5},{2,6},{3,7},{4,0},{5,1},{6,2},{7,3},{8,12},{9,13},{10,... | collective-permute-start | bytes 98312 | tf_op jit(solution)/shard_map/ppermute | solution.py:33
  791.5 10.9 %shard_map.310 = f32[512,2048]{1,0:T(8,128)} custom-call(bf16[512,2048]{1,0:T(8,128)(2,1)} %bitcast.113, bf16[512,256]{1,0:T(8,128)(2,1)S(1)} %bitcast.114, bf16[2048,256]{1,0:T(8,128)(2,1)} %shared_ref.1, bf16[1024,256]{1,0:T(8,128)(2,1)S(1)} %get-tuple-element.185.refs_0_, bf16[1024,256]{1,0:T(8,128)(2,1)} %collective-permute-done.7.refs_1_, ...), custom_call_target="tpu_custom_call" | custom-call | flops 4294967296 | bytes 16777216 | tf_op jit(solution)/shard_map/pallas_call | solution.py:298
  835.2 11.8 %collective-permute-done.135 = bf16[256,256]{1,0:T(8,128)(2,1)S(1)} collective-permute-done((bf16[256,256]{1,0:T(8,128)(2,1)S(1)}, bf16[256,256]{1,0:T(8,128)(2,1)S(1)}, u32[]{:S(2)}, u32[]{:S(2)}) %collective-permute-start.135) | collective-permute-done | bytes 131104 | tf_op jit(solution)/shard_map/ppermute | solution.py:33
  863.8 8.6 collective-permute-done.161
  875.3 8.2 collective-permute-done.122
  887.2 7.6 collective-permute-done.116
  896.6 9.4 collective-permute-done.158
  924.3 5.8 collective-permute-done.142
  937.9 8.5 collective-permute-done.163
  961.3 10.0 collective-permute-done.129
  971.4 11.2 %collective-permute-done.119 = bf16[1024,256]{1,0:T(8,128)(2,1)S(1)} collective-permute-done((bf16[1024,256]{1,0:T(8,128)(2,1)S(1)}, bf16[1024,256]{1,0:T(8,128)(2,1)S(1)}, u32[]{:S(2)}, u32[]{:S(2)}) %collective-permute-start.119) | collective-permute-done | bytes 524320 | tf_op jit(solution)/shard_map/ppermute | solution.py:391
  982.6 11.2 %collective-permute-done.165 = bf16[256,1024]{1,0:T(8,128)(2,1)S(1)} collective-permute-done((bf16[256,1024]{1,0:T(8,128)(2,1)S(1)}, bf16[256,1024]{1,0:T(8,128)(2,1)S(1)}, u32[]{:S(2)}, u32[]{:S(2)}) %collective-permute-start.165) | collective-permute-done | bytes 524320 | tf_op jit(solution)/shard_map/ppermute | solution.py:391
  993.9 8.6 collective-permute-done.155
  1005.6 6.8 convert_element_type.1010
  (848 shorter events, 366.3 us)
Async XLA Ops:
  7.2 998.4 %all-reduce.3.cloned.1.call-start = ((), (), s32[]{:S(2)}) async-start(), calls=%async_computation | async-start | bytes 16777216 | tf_op jit(solution)/shard_map/psum | solution.py:602
  110.1 37.9 %collective-permute-start.41 = (bf16[256,1024]{1,0:T(8,128)(2,1)}, bf16[256,1024]{1,0:T(8,128)(2,1)}, u32[]{:S(2)}, u32[]{:S(2)}) collective-permute-start(bf16[256,1024]{1,0:T(8,128)(2,1)} %collective-permute-done.40.refs_14_), channel_id=1, source_target_pairs={{0,1},{1,0},{2,3},{3,2},{4,5},{5,4},{6,7},{7,6},{8,9},{9,8},{10,11... | collective-permute-start | bytes 1572872 | tf_op jit(solution)/shard_map/ppermute | solution.py:33
  111.1 37.4 %collective-permute-start.34 = (bf16[256,1024]{1,0:T(8,128)(2,1)}, bf16[256,1024]{1,0:T(8,128)(2,1)}, u32[]{:S(2)}, u32[]{:S(2)}) collective-permute-start(bf16[256,1024]{1,0:T(8,128)(2,1)} %collective-permute-done.33.refs_6_), channel_id=1, source_target_pairs={{0,1},{1,0},{2,3},{3,2},{4,5},{5,4},{6,7},{7,6},{8,9},{9,8},{10,11... | collective-permute-start | bytes 1572872 | tf_op jit(solution)/shard_map/ppermute | solution.py:33
  130.3 43.9 %collective-permute-start.47 = (bf16[256,2048]{1,0:T(8,128)(2,1)}, bf16[256,2048]{1,0:T(8,128)(2,1)}, u32[]{:S(2)}, u32[]{:S(2)}) collective-permute-start(bf16[256,2048]{1,0:T(8,128)(2,1)} %get-tuple-element.172.ca_ref.refs_1_), channel_id=1, source_target_pairs={{0,4},{1,5},{2,6},{3,7},{4,0},{5,1},{6,2},{7,3},{8,12},{9,13},{10,... | collective-permute-start | bytes 3145736 | tf_op jit(solution)/shard_map/ppermute | solution.py:33
  130.8 60.3 %collective-permute-start.43 = (bf16[256,2048]{1,0:T(8,128)(2,1)}, bf16[256,2048]{1,0:T(8,128)(2,1)S(1)}, u32[]{:S(2)}, u32[]{:S(2)}) collective-permute-start(bf16[256,2048]{1,0:T(8,128)(2,1)} %get-tuple-element.172.ca_ref.refs_1_), channel_id=1, source_target_pairs={{0,1},{1,0},{2,3},{3,2},{4,5},{5,4},{6,7},{7,6},{8,9},{9,8},{10,11... | collective-permute-start | bytes 3145736 | tf_op jit(solution)/shard_map/ppermute | solution.py:33
  130.8 68.8 %collective-permute-start.74 = (bf16[256,2048]{1,0:T(8,128)(2,1)}, bf16[256,2048]{1,0:T(8,128)(2,1)}, u32[]{:S(2)}, u32[]{:S(2)}) collective-permute-start(bf16[256,2048]{1,0:T(8,128)(2,1)} %get-tuple-element.173.ca_ref.refs_4_), channel_id=1, source_target_pairs={{0,4},{1,5},{2,6},{3,7},{4,0},{5,1},{6,2},{7,3},{8,12},{9,13},{10,... | collective-permute-start | bytes 3145736 | tf_op jit(solution)/shard_map/ppermute | solution.py:33
  148.0 57.4 %collective-permute-start.68 = (bf16[256,2048]{1,0:T(8,128)(2,1)S(1)}, bf16[256,2048]{1,0:T(8,128)(2,1)S(1)}, u32[]{:S(2)}, u32[]{:S(2)}) collective-permute-start(bf16[256,2048]{1,0:T(8,128)(2,1)S(1)} %copy-done.10), channel_id=1, source_target_pairs={{0,2},{1,3},{2,0},{3,1},{4,6},{5,7},{6,4},{7,5},{8,10},{9,11},{10,... | collective-permute-start | bytes 3145736 | tf_op jit(solution)/shard_map/ppermute | solution.py:33
  148.6 57.2 %collective-permute-start.64 = (bf16[256,2048]{1,0:T(8,128)(2,1)S(1)}, bf16[256,2048]{1,0:T(8,128)(2,1)}, u32[]{:S(2)}, u32[]{:S(2)}) collective-permute-start(bf16[256,2048]{1,0:T(8,128)(2,1)S(1)} %copy-done.10), channel_id=1, source_target_pairs={{0,1},{1,0},{2,3},{3,2},{4,5},{5,4},{6,7},{7,6},{8,9},{9,8},{10,11... | collective-permute-start | bytes 3145736 | tf_op jit(solution)/shard_map/ppermute | solution.py:33
  174.2 37.1 %collective-permute-start.58 = (bf16[256,2048]{1,0:T(8,128)(2,1)}, bf16[256,2048]{1,0:T(8,128)(2,1)}, u32[]{:S(2)}, u32[]{:S(2)}) collective-permute-start(bf16[256,2048]{1,0:T(8,128)(2,1)} %collective-permute-done.53.ca_ref.refs_7_), channel_id=1, source_target_pairs={{0,4},{1,5},{2,6},{3,7},{4,0},{5,1},{6,2},{7,3},{8,12},{9,13},{10,... | collective-permute-start | bytes 3145736 | tf_op jit(solution)/shard_map/ppermute | solution.py:33
  205.4 44.8 %collective-permute-start.66 = (bf16[256,2048]{1,0:T(8,128)(2,1)S(1)}, bf16[256,2048]{1,0:T(8,128)(2,1)}, u32[]{:S(2)}, u32[]{:S(2)}) collective-permute-start(bf16[256,2048]{1,0:T(8,128)(2,1)S(1)} %get-tuple-element.175.xa_ref.refs_3_), channel_id=1, source_target_pairs={{0,2},{1,3},{2,0},{3,1},{4,6},{5,7},{6,4},{7,5},{8,10},{9,11},{10,... | collective-permute-start | bytes 3145736 | tf_op jit(solution)/shard_map/ppermute | solution.py:33
  206.4 43.9 %collective-permute-start.63 = (bf16[256,2048]{1,0:T(8,128)(2,1)S(1)}, bf16[256,2048]{1,0:T(8,128)(2,1)}, u32[]{:S(2)}, u32[]{:S(2)}) collective-permute-start(bf16[256,2048]{1,0:T(8,128)(2,1)S(1)} %get-tuple-element.175.xa_ref.refs_3_), channel_id=1, source_target_pairs={{0,1},{1,0},{2,3},{3,2},{4,5},{5,4},{6,7},{7,6},{8,9},{9,8},{10,11... | collective-permute-start | bytes 3145736 | tf_op jit(solution)/shard_map/ppermute | solution.py:33
  211.3 56.5 %collective-permute-start.69 = (bf16[256,2048]{1,0:T(8,128)(2,1)}, bf16[256,2048]{1,0:T(8,128)(2,1)}, u32[]{:S(2)}, u32[]{:S(2)}) collective-permute-start(bf16[256,2048]{1,0:T(8,128)(2,1)} %copy-done.132), channel_id=1, source_target_pairs={{0,1},{1,0},{2,3},{3,2},{4,5},{5,4},{6,7},{7,6},{8,9},{9,8},{10,11... | collective-permute-start | bytes 3145736 | tf_op jit(solution)/shard_map/ppermute | solution.py:33
  215.5 54.6 %collective-permute-start.72 = (bf16[256,2048]{1,0:T(8,128)(2,1)S(1)}, bf16[256,2048]{1,0:T(8,128)(2,1)}, u32[]{:S(2)}, u32[]{:S(2)}) collective-permute-start(bf16[256,2048]{1,0:T(8,128)(2,1)S(1)} %get-tuple-element.175.xa_ref.refs_3_), channel_id=1, source_target_pairs={{0,4},{1,5},{2,6},{3,7},{4,0},{5,1},{6,2},{7,3},{8,12},{9,13},{10,... | collective-permute-start | bytes 3145736 | tf_op jit(solution)/shard_map/ppermute | solution.py:33
  228.0 40.4 %collective-permute-start.42 = (bf16[256,2048]{1,0:T(8,128)(2,1)S(1)}, bf16[256,2048]{1,0:T(8,128)(2,1)}, u32[]{:S(2)}, u32[]{:S(2)}) collective-permute-start(bf16[256,2048]{1,0:T(8,128)(2,1)S(1)} %get-tuple-element.174.xa_ref.refs_0_), channel_id=1, source_target_pairs={{0,1},{1,0},{2,3},{3,2},{4,5},{5,4},{6,7},{7,6},{8,9},{9,8},{10,11... | collective-permute-start | bytes 3145736 | tf_op jit(solution)/shard_map/ppermute | solution.py:33
  250.2 38.0 %collective-permute-start.45 = (bf16[256,2048]{1,0:T(8,128)(2,1)S(1)}, bf16[256,2048]{1,0:T(8,128)(2,1)S(1)}, u32[]{:S(2)}, u32[]{:S(2)}) collective-permute-start(bf16[256,2048]{1,0:T(8,128)(2,1)S(1)} %get-tuple-element.174.xa_ref.refs_0_), channel_id=1, source_target_pairs={{0,4},{1,5},{2,6},{3,7},{4,0},{5,1},{6,2},{7,3},{8,12},{9,13},{10,... | collective-permute-start | bytes 3145736 | tf_op jit(solution)/shard_map/ppermute | solution.py:33
  250.3 38.3 %collective-permute-start.67 = (bf16[256,2048]{1,0:T(8,128)(2,1)}, bf16[256,2048]{1,0:T(8,128)(2,1)S(1)}, u32[]{:S(2)}, u32[]{:S(2)}) collective-permute-start(bf16[256,2048]{1,0:T(8,128)(2,1)} %collective-permute-done.66.xa_ref.refs_9_), channel_id=1, source_target_pairs={{0,1},{1,0},{2,3},{3,2},{4,5},{5,4},{6,7},{7,6},{8,9},{9,8},{10,11... | collective-permute-start | bytes 3145736 | tf_op jit(solution)/shard_map/ppermute | solution.py:33
  267.8 39.2 %collective-permute-start.75 = (bf16[256,2048]{1,0:T(8,128)(2,1)}, bf16[256,2048]{1,0:T(8,128)(2,1)S(1)}, u32[]{:S(2)}, u32[]{:S(2)}) collective-permute-start(bf16[256,2048]{1,0:T(8,128)(2,1)} %collective-permute-done.74.ca_ref.refs_16_), channel_id=1, source_target_pairs={{0,1},{1,0},{2,3},{3,2},{4,5},{5,4},{6,7},{7,6},{8,9},{9,8},{10,11... | collective-permute-start | bytes 3145736 | tf_op jit(solution)/shard_map/ppermute | solution.py:33
  268.4 39.1 %collective-permute-start.51 = (bf16[256,2048]{1,0:T(8,128)(2,1)S(1)}, bf16[256,2048]{1,0:T(8,128)(2,1)S(1)}, u32[]{:S(2)}, u32[]{:S(2)}) collective-permute-start(bf16[256,2048]{1,0:T(8,128)(2,1)S(1)} %get-tuple-element.174.xa_ref.refs_0_), channel_id=1, source_target_pairs={{0,2},{1,3},{2,0},{3,1},{4,6},{5,7},{6,4},{7,5},{8,10},{9,11},{10,... | collective-permute-start | bytes 3145736 | tf_op jit(solution)/shard_map/ppermute | solution.py:33
  270.2 39.3 %collective-permute-start.73 = (bf16[256,2048]{1,0:T(8,128)(2,1)}, bf16[256,2048]{1,0:T(8,128)(2,1)S(1)}, u32[]{:S(2)}, u32[]{:S(2)}) collective-permute-start(bf16[256,2048]{1,0:T(8,128)(2,1)} %collective-permute-done.72.xa_ref.refs_15_), channel_id=1, source_target_pairs={{0,1},{1,0},{2,3},{3,2},{4,5},{5,4},{6,7},{7,6},{8,9},{9,8},{10,11... | collective-permute-start | bytes 3145736 | tf_op jit(solution)/shard_map/ppermute | solution.py:33
  288.2 40.1 %collective-permute-start.77 = (bf16[256,2048]{1,0:T(8,128)(2,1)}, bf16[256,2048]{1,0:T(8,128)(2,1)}, u32[]{:S(2)}, u32[]{:S(2)}) collective-permute-start(bf16[256,2048]{1,0:T(8,128)(2,1)} %collective-permute-done.72.xa_ref.refs_15_), channel_id=1, source_target_pairs={{0,2},{1,3},{2,0},{3,1},{4,6},{5,7},{6,4},{7,5},{8,10},{9,11},{10,... | collective-permute-start | bytes 3145736 | tf_op jit(solution)/shard_map/ppermute | solution.py:33
  288.5 39.7 %collective-permute-start.46 = (bf16[256,2048]{1,0:T(8,128)(2,1)S(1)}, bf16[256,2048]{1,0:T(8,128)(2,1)}, u32[]{:S(2)}, u32[]{:S(2)}) collective-permute-start(bf16[256,2048]{1,0:T(8,128)(2,1)S(1)} %collective-permute-done.45.xa_ref.refs_12_), channel_id=1, source_target_pairs={{0,1},{1,0},{2,3},{3,2},{4,5},{5,4},{6,7},{7,6},{8,9},{9,8},{10,11... | collective-permute-start | bytes 3145736 | tf_op jit(solution)/shard_map/ppermute | solution.py:33
  307.1 39.3 %collective-permute-start.54 = (bf16[256,2048]{1,0:T(8,128)(2,1)}, bf16[256,2048]{1,0:T(8,128)(2,1)}, u32[]{:S(2)}, u32[]{:S(2)}) collective-permute-start(bf16[256,2048]{1,0:T(8,128)(2,1)} %collective-permute-done.53.ca_ref.refs_7_), channel_id=1, source_target_pairs={{0,1},{1,0},{2,3},{3,2},{4,5},{5,4},{6,7},{7,6},{8,9},{9,8},{10,11... | collective-permute-start | bytes 3145736 | tf_op jit(solution)/shard_map/ppermute | solution.py:33
  307.5 39.0 %collective-permute-start.56 = (bf16[256,2048]{1,0:T(8,128)(2,1)S(1)}, bf16[256,2048]{1,0:T(8,128)(2,1)S(1)}, u32[]{:S(2)}, u32[]{:S(2)}) collective-permute-start(bf16[256,2048]{1,0:T(8,128)(2,1)S(1)} %collective-permute-done.51.xa_ref.refs_6_), channel_id=1, source_target_pairs={{0,4},{1,5},{2,6},{3,7},{4,0},{5,1},{6,2},{7,3},{8,12},{9,13},{10,... | collective-permute-start | bytes 3145736 | tf_op jit(solution)/shard_map/ppermute | solution.py:33
  309.5 37.5 %collective-permute-start.52 = (bf16[256,2048]{1,0:T(8,128)(2,1)S(1)}, bf16[256,2048]{1,0:T(8,128)(2,1)S(1)}, u32[]{:S(2)}, u32[]{:S(2)}) collective-permute-start(bf16[256,2048]{1,0:T(8,128)(2,1)S(1)} %collective-permute-done.51.xa_ref.refs_6_), channel_id=1, source_target_pairs={{0,1},{1,0},{2,3},{3,2},{4,5},{5,4},{6,7},{7,6},{8,9},{9,8},{10,11... | collective-permute-start | bytes 3145736 | tf_op jit(solution)/shard_map/ppermute | solution.py:33
  328.2 37.8 %collective-permute-start.80 = (bf16[256,2048]{1,0:T(8,128)(2,1)}, bf16[256,2048]{1,0:T(8,128)(2,1)S(1)}, u32[]{:S(2)}, u32[]{:S(2)}) collective-permute-start(bf16[256,2048]{1,0:T(8,128)(2,1)} %collective-permute-done.79.ca_ref.refs_22_), channel_id=1, source_target_pairs={{0,1},{1,0},{2,3},{3,2},{4,5},{5,4},{6,7},{7,6},{8,9},{9,8},{10,11... | collective-permute-start | bytes 3145736 | tf_op jit(solution)/shard_map/ppermute | solution.py:33
  328.3 38.0 %collective-permute-start.78 = (bf16[256,2048]{1,0:T(8,128)(2,1)}, bf16[256,2048]{1,0:T(8,128)(2,1)S(1)}, u32[]{:S(2)}, u32[]{:S(2)}) collective-permute-start(bf16[256,2048]{1,0:T(8,128)(2,1)} %collective-permute-done.77.xa_ref.refs_21_), channel_id=1, source_target_pairs={{0,1},{1,0},{2,3},{3,2},{4,5},{5,4},{6,7},{7,6},{8,9},{9,8},{10,11... | collective-permute-start | bytes 3145736 | tf_op jit(solution)/shard_map/ppermute | solution.py:33
  346.4 38.6 %collective-permute-start.59 = (bf16[256,2048]{1,0:T(8,128)(2,1)}, bf16[256,2048]{1,0:T(8,128)(2,1)S(1)}, u32[]{:S(2)}, u32[]{:S(2)}) collective-permute-start(bf16[256,2048]{1,0:T(8,128)(2,1)} %collective-permute-done.58.ca_ref.refs_19_), channel_id=1, source_target_pairs={{0,1},{1,0},{2,3},{3,2},{4,5},{5,4},{6,7},{7,6},{8,9},{9,8},{10,11... | collective-permute-start | bytes 3145736 | tf_op jit(solution)/shard_map/ppermute | solution.py:33
  346.6 120.5 %collective-permute-start.70 = (bf16[256,2048]{1,0:T(8,128)(2,1)}, bf16[256,2048]{1,0:T(8,128)(2,1)}, u32[]{:S(2)}, u32[]{:S(2)}) collective-permute-start(bf16[256,2048]{1,0:T(8,128)(2,1)} %get-tuple-element.93), channel_id=1, source_target_pairs={{0,1},{1,0},{2,3},{3,2},{4,5},{5,4},{6,7},{7,6},{8,9},{9,8},{10,11... | collective-permute-start | bytes 3145736 | tf_op jit(solution)/shard_map/ppermute | solution.py:33
  347.0 38.4 %collective-permute-start.57 = (bf16[256,2048]{1,0:T(8,128)(2,1)S(1)}, bf16[256,2048]{1,0:T(8,128)(2,1)S(1)}, u32[]{:S(2)}, u32[]{:S(2)}) collective-permute-start(bf16[256,2048]{1,0:T(8,128)(2,1)S(1)} %collective-permute-done.56.xa_ref.refs_18_), channel_id=1, source_target_pairs={{0,1},{1,0},{2,3},{3,2},{4,5},{5,4},{6,7},{7,6},{8,9},{9,8},{10,11... | collective-permute-start | bytes 3145736 | tf_op jit(solution)/shard_map/ppermute | solution.py:33
  366.0 103.3 %collective-permute-start.92 = (bf16[256,2048]{1,0:T(8,128)(2,1)}, bf16[256,2048]{1,0:T(8,128)(2,1)}, u32[]{:S(2)}, u32[]{:S(2)}) collective-permute-start(bf16[256,2048]{1,0:T(8,128)(2,1)} %get-tuple-element.109), channel_id=1, source_target_pairs={{0,1},{1,0},{2,3},{3,2},{4,5},{5,4},{6,7},{7,6},{8,9},{9,8},{10,11... | collective-permute-start | bytes 3145736 | tf_op jit(solution)/shard_map/ppermute | solution.py:33
  366.3 122.0 %collective-permute-start.94 = (bf16[256,2048]{1,0:T(8,128)(2,1)}, bf16[256,2048]{1,0:T(8,128)(2,1)}, u32[]{:S(2)}, u32[]{:S(2)}) collective-permute-start(bf16[256,2048]{1,0:T(8,128)(2,1)} %get-tuple-element.111), channel_id=1, source_target_pairs={{0,1},{1,0},{2,3},{3,2},{4,5},{5,4},{6,7},{7,6},{8,9},{9,8},{10,11... | collective-permute-start | bytes 3145736 | tf_op jit(solution)/shard_map/ppermute | solution.py:33
  385.0 86.3 %collective-permute-start.49 = (bf16[256,2048]{1,0:T(8,128)(2,1)}, bf16[256,2048]{1,0:T(8,128)(2,1)}, u32[]{:S(2)}, u32[]{:S(2)}) collective-permute-start(bf16[256,2048]{1,0:T(8,128)(2,1)} %get-tuple-element.85), channel_id=1, source_target_pairs={{0,1},{1,0},{2,3},{3,2},{4,5},{5,4},{6,7},{7,6},{8,9},{9,8},{10,11... | collective-permute-start | bytes 3145736 | tf_op jit(solution)/shard_map/ppermute | solution.py:33
  387.1 90.8 %collective-permute-start.85 = (bf16[256,2048]{1,0:T(8,128)(2,1)}, bf16[256,2048]{1,0:T(8,128)(2,1)}, u32[]{:S(2)}, u32[]{:S(2)}) collective-permute-start(bf16[256,2048]{1,0:T(8,128)(2,1)} %get-tuple-element.101), channel_id=1, source_target_pairs={{0,1},{1,0},{2,3},{3,2},{4,5},{5,4},{6,7},{7,6},{8,9},{9,8},{10,11... | collective-permute-start | bytes 3145736 | tf_op jit(solution)/shard_map/ppermute | solution.py:33
  514.8 66.1 %collective-permute-start.84 = (bf16[256,2048]{1,0:T(8,128)(2,1)S(1)}, bf16[256,2048]{1,0:T(8,128)(2,1)S(1)}, u32[]{:S(2)}, u32[]{:S(2)}) collective-permute-start(bf16[256,2048]{1,0:T(8,128)(2,1)S(1)} %copy-done.130), channel_id=1, source_target_pairs={{0,1},{1,0},{2,3},{3,2},{4,5},{5,4},{6,7},{7,6},{8,9},{9,8},{10,11... | collective-permute-start | bytes 3145736 | tf_op jit(solution)/shard_map/ppermute | solution.py:33
  514.8 43.0 %collective-permute-start.93 = (bf16[256,2048]{1,0:T(8,128)(2,1)S(1)}, bf16[256,2048]{1,0:T(8,128)(2,1)S(1)}, u32[]{:S(2)}, u32[]{:S(2)}) collective-permute-start(bf16[256,2048]{1,0:T(8,128)(2,1)S(1)} %add_convert_fusion.4), channel_id=1, source_target_pairs={{0,2},{1,3},{2,0},{3,1},{4,6},{5,7},{6,4},{7,5},{8,10},{9,11},{10,... | collective-permute-start | bytes 3145736 | tf_op jit(solution)/shard_map/ppermute | solution.py:33
  515.8 66.6 %collective-permute-start.86 = (bf16[256,2048]{1,0:T(8,128)(2,1)S(1)}, bf16[256,2048]{1,0:T(8,128)(2,1)S(1)}, u32[]{:S(2)}, u32[]{:S(2)}) collective-permute-start(bf16[256,2048]{1,0:T(8,128)(2,1)S(1)} %add_convert_fusion.10), channel_id=1, source_target_pairs={{0,4},{1,5},{2,6},{3,7},{4,0},{5,1},{6,2},{7,3},{8,12},{9,13},{10,... | collective-permute-start | bytes 3145736 | tf_op jit(solution)/shard_map/ppermute | solution.py:33
  535.4 44.8 %collective-permute-start.97 = (bf16[256,2048]{1,0:T(8,128)(2,1)S(1)}, bf16[256,2048]{1,0:T(8,128)(2,1)S(1)}, u32[]{:S(2)}, u32[]{:S(2)}) collective-permute-start(bf16[256,2048]{1,0:T(8,128)(2,1)S(1)} %add_convert_fusion), channel_id=1, source_target_pairs={{0,4},{1,5},{2,6},{3,7},{4,0},{5,1},{6,2},{7,3},{8,12},{9,13},{10,... | collective-permute-start | bytes 3145736 | tf_op jit(solution)/shard_map/ppermute | solution.py:33
  537.3 45.6 %collective-permute-start.90 = (bf16[256,2048]{1,0:T(8,128)(2,1)S(1)}, bf16[256,2048]{1,0:T(8,128)(2,1)S(1)}, u32[]{:S(2)}, u32[]{:S(2)}) collective-permute-start(bf16[256,2048]{1,0:T(8,128)(2,1)S(1)} %add_convert_fusion.6), channel_id=1, source_target_pairs={{0,2},{1,3},{2,0},{3,1},{4,6},{5,7},{6,4},{7,5},{8,10},{9,11},{10,... | collective-permute-start | bytes 3145736 | tf_op jit(solution)/shard_map/ppermute | solution.py:33
  557.9 31.7 %collective-permute-start.65 = (bf16[256,2048]{1,0:T(8,128)(2,1)S(1)}, bf16[256,2048]{1,0:T(8,128)(2,1)}, u32[]{:S(2)}, u32[]{:S(2)}) collective-permute-start(bf16[256,2048]{1,0:T(8,128)(2,1)S(1)} %copy-done.129), channel_id=1, source_target_pairs={{0,1},{1,0},{2,3},{3,2},{4,5},{5,4},{6,7},{7,6},{8,9},{9,8},{10,11... | collective-permute-start | bytes 3145736 | tf_op jit(solution)/shard_map/ppermute | solution.py:33
  580.2 53.2 %collective-permute-start.44 = (bf16[256,2048]{1,0:T(8,128)(2,1)}, bf16[256,2048]{1,0:T(8,128)(2,1)}, u32[]{:S(2)}, u32[]{:S(2)}) collective-permute-start(bf16[256,2048]{1,0:T(8,128)(2,1)} %get-tuple-element.83), channel_id=1, source_target_pairs={{0,1},{1,0},{2,3},{3,2},{4,5},{5,4},{6,7},{7,6},{8,9},{9,8},{10,11... | collective-permute-start | bytes 3145736 | tf_op jit(solution)/shard_map/ppermute | solution.py:33
  582.4 50.9 %collective-permute-start.50 = (bf16[256,2048]{1,0:T(8,128)(2,1)S(1)}, bf16[256,2048]{1,0:T(8,128)(2,1)}, u32[]{:S(2)}, u32[]{:S(2)}) collective-permute-start(bf16[256,2048]{1,0:T(8,128)(2,1)S(1)} %add_convert_fusion.22), channel_id=1, source_target_pairs={{0,4},{1,5},{2,6},{3,7},{4,0},{5,1},{6,2},{7,3},{8,12},{9,13},{10,... | collective-permute-start | bytes 3145736 | tf_op jit(solution)/shard_map/ppermute | solution.py:33
  582.9 47.4 %collective-permute-start.83 = (bf16[256,2048]{1,0:T(8,128)(2,1)}, bf16[256,2048]{1,0:T(8,128)(2,1)}, u32[]{:S(2)}, u32[]{:S(2)}) collective-permute-start(bf16[256,2048]{1,0:T(8,128)(2,1)} %add_convert_fusion.12), channel_id=1, source_target_pairs={{0,4},{1,5},{2,6},{3,7},{4,0},{5,1},{6,2},{7,3},{8,12},{9,13},{10,... | collective-permute-start | bytes 3145736 | tf_op jit(solution)/shard_map/ppermute | solution.py:33
  589.6 43.8 %collective-permute-start.62 = (bf16[256,2048]{1,0:T(8,128)(2,1)}, bf16[256,2048]{1,0:T(8,128)(2,1)}, u32[]{:S(2)}, u32[]{:S(2)}) collective-permute-start(bf16[256,2048]{1,0:T(8,128)(2,1)} %add_convert_fusion.18), channel_id=1, source_target_pairs={{0,2},{1,3},{2,0},{3,1},{4,6},{5,7},{6,4},{7,5},{8,10},{9,11},{10,... | collective-permute-start | bytes 3145736 | tf_op jit(solution)/shard_map/ppermute | solution.py:33
  750.5 109.4 %collective-permute-start.159 = (bf16[256,1024]{1,0:T(8,128)(2,1)}, bf16[256,1024]{1,0:T(8,128)(2,1)}, u32[]{:S(2)}, u32[]{:S(2)}) collective-permute-start(bf16[256,1024]{1,0:T(8,128)(2,1)} %convolution_convert_fusion.1), channel_id=1, source_target_pairs={{0,1},{1,0},{2,3},{3,2},{4,5},{5,4},{6,7},{7,6},{8,9},{9,8},{10,11... | collective-permute-start | bytes 1572872 | tf_op jit(solution)/shard_map/ppermute | solution.py:33
  773.4 58.2 %collective-permute-start.123 = (bf16[1024,256]{1,0:T(8,128)(2,1)}, bf16[1024,256]{1,0:T(8,128)(2,1)}, u32[]{:S(2)}, u32[]{:S(2)}) collective-permute-start(bf16[1024,256]{1,0:T(8,128)(2,1)} %convolution_convert_fusion.9), channel_id=1, source_target_pairs={{0,1},{1,0},{2,3},{3,2},{4,5},{5,4},{6,7},{7,6},{8,9},{9,8},{10,11... | collective-permute-start | bytes 1572872 | tf_op jit(solution)/shard_map/ppermute | solution.py:33
  785.0 46.8 %collective-permute-start.125 = (bf16[1024,256]{1,0:T(8,128)(2,1)}, bf16[1024,256]{1,0:T(8,128)(2,1)}, u32[]{:S(2)}, u32[]{:S(2)}) collective-permute-start(bf16[1024,256]{1,0:T(8,128)(2,1)} %add_convert_fusion.46), channel_id=1, source_target_pairs={{0,2},{1,3},{2,0},{3,1},{4,6},{5,7},{6,4},{7,5},{8,10},{9,11},{10,... | collective-permute-start | bytes 1572872 | tf_op jit(solution)/shard_map/ppermute | solution.py:33
  958.5 35.3 %collective-permute-start.165 = (bf16[256,1024]{1,0:T(8,128)(2,1)S(1)}, bf16[256,1024]{1,0:T(8,128)(2,1)S(1)}, u32[]{:S(2)}, u32[]{:S(2)}) collective-permute-start(bf16[256,1024]{1,0:T(8,128)(2,1)S(1)} %add_convert_fusion.24), channel_id=1, source_target_pairs={{8,0},{16,24},{9,1},{17,25},{10,2},{18,26},{11,3},{19,27},{12,4},{... | collective-permute-start | bytes 1572872 | tf_op jit(solution)/shard_map/ppermute | solution.py:391
  960.0 42.5 %collective-permute-start.155 = (bf16[256,1024]{1,0:T(8,128)(2,1)S(1)}, bf16[256,1024]{1,0:T(8,128)(2,1)S(1)}, u32[]{:S(2)}, u32[]{:S(2)}) collective-permute-start(bf16[256,1024]{1,0:T(8,128)(2,1)S(1)} %add_convert_fusion.33), channel_id=1, source_target_pairs={{8,0},{16,24},{9,1},{17,25},{10,2},{18,26},{11,3},{19,27},{12,4},{... | collective-permute-start | bytes 1572872 | tf_op jit(solution)/shard_map/ppermute | solution.py:391
  (296 other events, 3495.2 us)
Sparse Core Ops, SparseCore 0:
  466.5 293.7 all-reduce.2

commit v2 on v1

--- a/solution.py
+++ b/solution.py
@@ -382,13 +382,233 @@
     return x
 
 
-def sum_line(x):
-    if lax.axis_size("dp") != 4:
-        return lax.psum(x, "dp")
-    inner = lax.axis_index("dp") % 3 != 0
-    pair = (x.astype(F32) + lax.ppermute(x, "dp", [(0, 1), (3, 2)]).astype(F32)).astype(BF)
-    both = (pair.astype(F32) + lax.ppermute(pair, "dp", [(1, 2), (2, 1)]).astype(F32)).astype(BF)
-    return jnp.where(inner, both, lax.ppermute(both, "dp", [(1, 0), (2, 3)]))
+MESH = pl.DeviceIdType.MESH
+
+
+def greet(bits, line):
+    me, z = lax.axis_index("tensor"), lax.axis_index("dp")
+    barrier = pltpu.get_barrier_semaphore()
+    for bit in bits:
+        pl.semaphore_signal(barrier, inc=1, device_id={"tensor": me ^ (1 << bit)}, device_id_type=MESH)
+    count = len(bits)
+    if line:
+        inner = (z == 1) | (z == 2)
+        pl.semaphore_signal(barrier, inc=1, device_id={"dp": z ^ 1}, device_id_type=MESH)
+
+        @pl.when(inner)
+        def _():
+            pl.semaphore_signal(barrier, inc=1, device_id={"dp": 3 - z}, device_id_type=MESH)
+
+        count = count + 1 + inner.astype(jnp.int32)
+    pl.semaphore_wait(barrier, count)
+
+
+class Scatter:
+    def __init__(self, bits, send, recv, send_sem, recv_sem):
+        self.bits, self.send, self.recv, self.send_sem, self.recv_sem = bits, send, recv, send_sem, recv_sem
+        self.me = lax.axis_index("tensor")
+
+    def stage(self, k):
+        return next((i for i, b in enumerate(self.bits) if k >> b & 1), len(self.bits))
+
+    def copy(self, k):
+        bit = self.bits[self.stage(k)]
+        return pltpu.make_async_remote_copy(
+            src_ref=self.send.at[k],
+            dst_ref=self.recv.at[k - 1],
+            send_sem=self.send_sem.at[k],
+            recv_sem=self.recv_sem.at[k],
+            device_id={"tensor": self.me ^ (1 << bit)},
+            device_id_type=MESH,
+        )
+
+    def put(self, k, value):
+        self.send[k] = value.astype(BF)
+        if self.stage(k) == 0:
+            self.copy(k).start()
+
+    def total(self, k):
+        value = self.send[k].astype(F32)
+        for bit in self.bits[: self.stage(k)]:
+            self.copy(k | (1 << bit)).wait_recv()
+            value = value + self.recv[(k | (1 << bit)) - 1].astype(F32)
+        return value
+
+    def forward(self, k):
+        self.send[k] = self.total(k).astype(BF)
+        self.copy(k).start()
+
+    def drain(self):
+        for k in range(1, 1 << len(self.bits)):
+            self.copy(k).wait_send()
+
+
+def scatter_order(bits):
+    n = 1 << len(bits)
+    rank = lambda k: next(i for i, b in enumerate(bits) if k >> b & 1)
+    return sorted(range(2, n, 2), key=lambda k: (rank(k), -k))
+
+
+def attention_grads_kernel(a_ref, gm_ref, dq_ref, h_ref, dkv_ref, wo_ref, wq_ref, kv_ref,
+                           send, recv, ksend, krecv, zbuf, ssem, rsem, ksem, krsem, zsem, *, orders, line, qw):
+    bits_of = [[0] + list(o)[::-1] for o in orders]
+    count = len(bits_of[0])
+    n = 1 << count
+    half = gm_ref.shape[1] // 2
+    greet(range(count), line)
+    z = lax.axis_index("dp")
+
+    kv = Scatter(bits_of[0], ksend, krecv, ksem, krsem)
+    for k in list(range(1, n, 2)) + list(range(0, n, 2)):
+        kv.put(k, dkv_ref[k])
+
+    pairs = ((a_ref, gm_ref, wo_ref), (dq_ref, h_ref, wq_ref))
+    work = [
+        [Scatter(bits_of[p], send.at[m, p], recv.at[m, p], ssem.at[m, p], rsem.at[m, p]) for p in range(2)]
+        for m in range(2)
+    ]
+    sequence = [scatter_order(b) for b in bits_of]
+
+    def compute(m, p, k):
+        x, y, _ = pairs[m]
+        work[m][p].put(k, dot_tn(x[:, k * qw : (k + 1) * qw], y[:, p * half : (p + 1) * half]))
+
+    def products(m):
+        for i in range(n // 2):
+            for p in range(2):
+                k = (sequence[p] + [0])[i]
+                compute(m, p, k + 1)
+                compute(m, p, k)
+
+    def stage(m, i):
+        for at in range(n // 2 - 1):
+            for p in range(2):
+                k = sequence[p][at]
+                if work[m][p].stage(k) == i:
+                    work[m][p].forward(k)
+
+    def z_copy(m, p, hop, to):
+        return pltpu.make_async_remote_copy(
+            src_ref=zbuf.at[m, p, hop % 2],
+            dst_ref=zbuf.at[m, p, 2 + hop % 2],
+            send_sem=zsem.at[m, p, hop],
+            recv_sem=zsem.at[m, p, 3 + hop],
+            device_id={"dp": to},
+            device_id_type=MESH,
+        )
+
+    inner = (z == 1) | (z == 2)
+    outer = jnp.logical_not(inner)
+
+    def finish(m, p):
+        value = work[m][p].total(0)
+        if not line:
+            pairs[m][2][:, p * half : (p + 1) * half] = value
+            return
+        zbuf[m, p, 0] = value.astype(BF)
+
+        @pl.when(outer)
+        def _():
+            z_copy(m, p, 0, z ^ 1).start()
+
+    def middle(m, p):
+        @pl.when(inner)
+        def _():
+            z_copy(m, p, 0, z ^ 1).wait_recv()
+            zbuf[m, p, 1] = (zbuf[m, p, 0].astype(F32) + zbuf[m, p, 2].astype(F32)).astype(BF)
+            z_copy(m, p, 1, 3 - z).start()
+
+    def back(m, p):
+        here = pairs[m][2].at[:, p * half : (p + 1) * half]
+
+        @pl.when(inner)
+        def _():
+            z_copy(m, p, 1, 3 - z).wait_recv()
+            both = (zbuf[m, p, 1].astype(F32) + zbuf[m, p, 3].astype(F32)).astype(BF)
+            zbuf[m, p, 0] = both
+            z_copy(m, p, 2, z ^ 1).start()
+            here[...] = both.astype(F32)
+
+    def close(m, p):
+        here = pairs[m][2].at[:, p * half : (p + 1) * half]
+
+        @pl.when(outer)
+        def _():
+            z_copy(m, p, 0, z ^ 1).wait_send()
+            z_copy(m, p, 2, z ^ 1).wait_recv()
+            here[...] = zbuf[m, p, 2].astype(F32)
+
+        @pl.when(inner)
+        def _():
+            z_copy(m, p, 1, 3 - z).wait_send()
+            z_copy(m, p, 2, z ^ 1).wait_send()
+
+    def kv_stage(i):
+        for k in scatter_order(bits_of[0]):
+            if kv.stage(k) == i:
+                kv.forward(k)
+
+    def both(step, m):
+        for p in range(2):
+            step(m, p)
+
+    products(0)
+    stage(0, 1)
+    products(1)
+    for i in range(1, count):
+        kv_stage(i)
+        if i + 1 < count:
+            stage(0, i + 1)
+        else:
+            both(finish, 0)
+        stage(1, i)
+    kv_ref[...] = kv.total(0).astype(BF)
+    if line:
+        both(middle, 0)
+    both(finish, 1)
+    if line:
+        both(back, 0)
+        both(middle, 1)
+        both(close, 0)
+        both(back, 1)
+        both(close, 1)
+    kv.drain()
+    for m in range(2):
+        for p in range(2):
+            work[m][p].drain()
+
+
+def attention_grads(a, gm, dq, h, dkv, orders):
+    n, line = lax.axis_size("tensor"), lax.axis_size("dp") == 4
+    tokens, d = gm.shape
+    qw = a.shape[1] // n
+    slot = dkv.shape[1:]
+    dma = pltpu.SemaphoreType.DMA
+    vmem = pl.BlockSpec(memory_space=pltpu.VMEM)
+    return pl.pallas_call(
+        functools.partial(attention_grads_kernel, orders=orders, line=line, qw=qw),
+        in_specs=[vmem] * 5,
+        out_specs=[vmem] * 3,
+        out_shape=[
+            jax.ShapeDtypeStruct((qw, d), F32),
+            jax.ShapeDtypeStruct((qw, d), F32),
+            jax.ShapeDtypeStruct(slot, BF),
+        ],
+        scratch_shapes=[
+            pltpu.VMEM((2, 2, n, qw, d // 2), BF),
+            pltpu.VMEM((2, 2, n - 1, qw, d // 2), BF),
+            pltpu.VMEM((n,) + slot, BF),
+            pltpu.VMEM((n - 1,) + slot, BF),
+            pltpu.VMEM((2, 2, 4, qw, d // 2), BF),
+            dma((2, 2, n)), dma((2, 2, n)), dma((n,)), dma((n,)), dma((2, 2, 6)),
+        ],
+        compiler_params=pltpu.CompilerParams(
+            collective_id=1, has_side_effects=True, vmem_limit_bytes=60 * MIB
+        ),
+        cost_estimate=pl.CostEstimate(
+            flops=4 * tokens * n * qw * d, bytes_accessed=64 * MIB, transcendentals=0
+        ),
+    )(a, gm, dq, h, dkv)
 
 
 def mlp_kernel(xa_ref, xb_ref, ca_ref, cb_ref, up_ref, bias_ref, down_ref,
@@ -574,20 +794,14 @@
     )
     dq2 = dq.reshape(tokens, n * qw)
 
-    wo_grads = [
-        scatter_slots(
-            [dot_tn(a2[:, k * qw : (k + 1) * qw], gm2[:, i * half : (i + 1) * half]) for k in range(n)], paths[i]
-        )
-        for i in range(2)
-    ]
-    dkv = jnp.concatenate([dk * LN2, dv], axis=-1).astype(BF)
-    dkv_own = scatter_slots([dkv[:, k * span : (k + 1) * span] for k in range(n)], paths[0]).astype(BF)
-    wq_grads = [
-        scatter_slots(
-            [dot_tn(h2[:, i * half : (i + 1) * half], dq2[:, k * qw : (k + 1) * qw]) for k in range(n)], paths[i]
-        )
-        for i in range(2)
-    ]
+    dkv = jnp.concatenate([dk * LN2, dv], axis=-1).astype(BF).reshape(seqs, n, span, 2 * hd).swapaxes(0, 1)
+    output_gradient, query_gradient, dkv_own = attention_grads(
+        a2, gm2, dq2, h2, dkv.reshape(n, tokens, 2 * hd), paths
+    )
+    if lax.axis_size("dp") != 4:
+        output_gradient, query_gradient = lax.psum((output_gradient.astype(BF), query_gradient.astype(BF)), "dp")
+    dkv_own = dkv_own.reshape(seqs, span, 2 * hd)
+
     (grad_hidden,) = slot_product(
         dh_kernel, [dq2, dkv_own.reshape(tokens, 2 * hd)], [shared_matrix], wq, [like(F32, d)], (d, n * qw)
     )
@@ -600,8 +814,6 @@
 
     everywhere = ("tensor", "dp")
     down_gradient, up_gradient = lax.psum((down_gradient, up_gradient), "dp")
-    output_gradient = jnp.concatenate([sum_line(g.astype(BF)) for g in wo_grads], axis=1)
-    query_gradient = jnp.concatenate([sum_line(g.astype(BF)) for g in wq_grads], axis=0)
     up_bias_grad = sum_all(up_bias_part, ("dp",))[0]
     early = sum_all(
         jnp.stack([mlp_gain_part, mlp_shift_part, jnp.sum(grad_mixed, axis=(0, 1)), jnp.sum(cot_wide, axis=(0, 1))]),
@@ -622,7 +834,7 @@
     shared_slots = jnp.concatenate(gather_slots(shared_sum, paths[0]), axis=0)
     shared_grad = xor_order(shared_slots.reshape(n, piece, 2 * hd), me).reshape(d, 2 * hd).astype(F32)
     output_gradient, query_gradient, up_gradient, down_gradient = (
-        g.astype(F32) for g in (output_gradient, query_gradient, up_gradient, down_gradient)
+        g.astype(F32) for g in (output_gradient, query_gradient.T, up_gradient, down_gradient)
     )
     return (
         block_out, input_grad, attn_gain_grad, attn_shift_grad, query_gradient, query_bias_grad, shared_grad,

time: 1030 us -> 965 us (0.937)
  Pallas kernels: 270 us -> 441 us
  waiting for transfers between devices: 380 us -> 252 us
  starting transfers between devices: 171 us -> 108 us
  matrix products: 44.7 us -> 1.47 us
    pallas_call x0 -> x1, Pallas kernels: none -> 172 us  [attention_grads(): pl.pallas_call(functools.partial(attention_grads_kernel, orders=orders, l...]
    ppermute x161 -> x126, waiting for transfers between devices: 324 us -> 252 us  [swap(): return lax.ppermute(x, axis, [(i, i ^ 1 << bit) for i in range(n)])]
    ppermute x12 -> x0, waiting for transfers between devices: 55.4 us -> none  [the longest x4 41 us: sum_line(): return jnp.where(inner, both, lax.ppermute(both, 'dp', [(1, 0), (2, 3)]))]
    ppermute x161 -> x126, starting transfers between devices: 156 us -> 107 us  [swap(): return lax.ppermute(x, axis, [(i, i ^ 1 << bit) for i in range(n)])]
    dot_general x33 -> x1, matrix products: 43.9 us -> 0.76 us  [dot_tn(): lax.dot_general(a, b, (((0,), (0,)), ((), ())), preferred_element_type=F32)]
    ppermute x12 -> x0, starting transfers between devices: 14.6 us -> none  [the longest x4 6.39 us: sum_line(): lax.ppermute(x, 'dp', [(0, 1), (3, 2)]).astype(F32)]
    unnamed x361 -> x305, local copies, waits for them, and re-layouts: 40.1 us -> 48.8 us
  transfers between devices with their start and end apart: 174 -> 127, of which waited for: 57 -> 35; matrix products, arithmetic and copies ran while one was open for 14% -> 10% of each run, Pallas kernels for 26% -> 46%
where the time goes in v2:
time: 965 us; the launch traced here: 960 us
  Pallas kernels  441 us (46%)
  waiting for transfers between devices  252 us (26%)
  starting transfers between devices  108 us (11%)
  local copies, waits for them, and re-layouts  70.7 us (7%)
  other arithmetic  69.9 us (7%)
  between operations  16.3 us (2%)
    ppermute x126, waiting for transfers between devices, swap(): return lax.ppermute(x, axis, [(i, i ^ 1 << bit) for i in range(n)])  252 us
    pallas_call x1, Pallas kernels, attention_grads(): pl.pallas_call(functools.partial(attention_grads_kernel, orders=orders, l...  172 us
    pallas_call x8, Pallas kernels, mlp_unit(): pl.pallas_call(mlp_kernel, grid=(ff // tile,), in_specs=[whole, whole, wh...  143 us
    ppermute x126, starting transfers between devices, swap(): return lax.ppermute(x, axis, [(i, i ^ 1 << bit) for i in range(n)])  107 us
    pallas_call x2, Pallas kernels, weight_grad(): pl.pallas_call(functools.partial(weight_grad_kernel, units=units), in_spe...  60.5 us
    unnamed x305, local copies, waits for them, and re-layouts  48.8 us
    pallas_call x4, Pallas kernels, slot_product(): pl.pallas_call(kernel, grid=(2,), in_specs=[flow(a) for a in tiled] + [st...  40.7 us
  transfers between devices with their start and end apart: 127, of which 35 were waited for; matrix products, arithmetic and copies ran while one was open for 10% of the time, Pallas kernels for 46%

profile of v2, /device:TPU:0, one launch (start us, length us, event | category | flops | bytes accessed | tf_op | source)
XLA Modules:
  0.0 959.9 jit_solution(2872567102864749169)
XLA Ops:
  21.0 6.6 collective-permute-done.5
  30.7 6.6 collective-permute-done.22
  42.9 9.2 collective-permute-done.10.refs_4_
  54.8 8.7 collective-permute-done.38.refs_12_
  67.5 7.2 collective-permute-done.31.refs_4_
  75.8 4.0 collective-permute-done.26
  82.2 5.8 collective-permute-done.19.refs_14_
  97.3 5.4 collective-permute-done.40.refs_14_
  111.4 3.8 fusion.31
  117.5 12.8 %collective-permute-done.53.ca_ref.refs_7_ = bf16[256,2048]{1,0:T(8,128)(2,1)} collective-permute-done((bf16[256,2048]{1,0:T(8,128)(2,1)}, bf16[256,2048]{1,0:T(8,128)(2,1)}, u32[]{:S(2)}, u32[]{:S(2)}) %collective-permute-start.53) | collective-permute-done | bytes 1048608 | tf_op jit(solution)/shard_map/ppermute | solution.py:33
  138.7 9.3 shard_map.297
  150.2 11.2 %shard_map.298 = (bf16[2,256,2048]{2,1,0:T(8,128)(2,1)S(1)}, f32[2,8,1,512]{3,2,1,0:T(1,128)S(1)}) custom-call(s32[2]{0:T(128)S(1)} %fusion.27.low_ref, s32[1]{0:T(128)} %bitcast.at_ref, bf16[2,256,2048]{2,1,0:T(8,128)(2,1)S(1)} %bitcast.109, bf16[2,2048,128]{2,1,0:T(8,128)(2,1)S(1)} %copy-done.7, bf16[2,128,2048]{2,1,0:T(8,128)(2,1)S(1)} %copy-done.5, ...), custom_call_target="tpu_custom_call" | custom-call | flops 4294967296 | bytes 8388608 | tf_op jit(solution)/shard_map/pallas_call | solution.py:169
  162.9 11.3 %shard_map.299 = (f32[512,2048]{1,0:T(8,128)}, bf16[512,2048]{1,0:T(8,128)(2,1)}) custom-call(bf16[512,2048]{1,0:T(8,128)(2,1)} %bitcast.107, bf16[512,2048]{1,0:T(8,128)(2,1)} %bitcast.113, f32[1,2048]{1,0:T(1,128)S(1)} %bitcast.105, f32[1,2048]{1,0:T(1,128)S(1)} %bitcast.104, f32[1,2048]{1,0:T(1,128)S(1)} %bitcast.106, bf16[256,1024]{1,0:T(8,128)(2,1)S(1)} %copy-done.37, ...), custom_call_target="tpu_custom_call" | custom-call | flops 4294967296 | bytes 16777216 | tf_op jit(solution)/shard_map/pallas_call | solution.py:298
  174.1 16.9 %collective-permute-start.58 = (bf16[256,2048]{1,0:T(8,128)(2,1)}, bf16[256,2048]{1,0:T(8,128)(2,1)}, u32[]{:S(2)}, u32[]{:S(2)}) collective-permute-start(bf16[256,2048]{1,0:T(8,128)(2,1)} %collective-permute-done.53.ca_ref.refs_7_), channel_id=1, source_target_pairs={{0,4},{1,5},{2,6},{3,7},{4,0},{5,1},{6,2},{7,3},{8,12},{9,13},{10,... | collective-permute-start | bytes 3145736 | tf_op jit(solution)/shard_map/ppermute | solution.py:33
  194.1 7.1 collective-permute-start.79
  208.7 4.0 collective-permute-done.58.ca_ref.refs_19_
  217.5 7.9 collective-permute-done.79.ca_ref.refs_22_
  228.2 19.1 %collective-permute-done.66.xa_ref.refs_9_ = bf16[256,2048]{1,0:T(8,128)(2,1)} collective-permute-done((bf16[256,2048]{1,0:T(8,128)(2,1)S(1)}, bf16[256,2048]{1,0:T(8,128)(2,1)}, u32[]{:S(2)}, u32[]{:S(2)}) %collective-permute-start.66) | collective-permute-done | bytes 1048608 | tf_op jit(solution)/shard_map/ppermute | solution.py:33
  247.8 17.6 %shard_map.304 = (bf16[256,2048]{1,0:T(8,128)(2,1)}, bf16[256,2048]{1,0:T(8,128)(2,1)}, bf16[256,2048]{1,0:T(8,128)(2,1)}, bf16[256,2048]{1,0:T(8,128)(2,1)}, bf...) custom-call(bf16[256,2048]{1,0:T(8,128)(2,1)} %copy-done.14, ...), custom_call_target="tpu_custom_call" | custom-call | flops 8589934592 | bytes 20971520 | tf_op jit(solution)/shard_map/pallas_call | solution.py:665
  267.7 18.0 %shard_map.300 = (bf16[256,2048]{1,0:T(8,128)(2,1)}, bf16[256,2048]{1,0:T(8,128)(2,1)}, bf16[256,2048]{1,0:T(8,128)(2,1)}, bf16[256,2048]{1,0:T(8,128)(2,1)}, bf...) custom-call(bf16[256,2048]{1,0:T(8,128)(2,1)} %copy-done.12, ...), custom_call_target="tpu_custom_call" | custom-call | flops 8589934592 | bytes 20971520 | tf_op jit(solution)/shard_map/pallas_call | solution.py:665
  287.1 17.6 %shard_map.305 = (bf16[256,2048]{1,0:T(8,128)(2,1)}, bf16[256,2048]{1,0:T(8,128)(2,1)}, bf16[256,2048]{1,0:T(8,128)(2,1)}, bf16[256,2048]{1,0:T(8,128)(2,1)}, bf...) custom-call(bf16[256,2048]{1,0:T(8,128)(2,1)} %collective-permute-done.66.xa_ref.refs_9_, ...), custom_call_target="tpu_custom_call" | custom-call | flops 8589934592 | bytes 20971520 | tf_op jit(solution)/shard_map/pallas_call | solution.py:665
  307.7 17.8 %shard_map.306 = (bf16[256,2048]{1,0:T(8,128)(2,1)}, bf16[256,2048]{1,0:T(8,128)(2,1)}, bf16[256,2048]{1,0:T(8,128)(2,1)}, bf16[256,2048]{1,0:T(8,128)(2,1)}, bf...) custom-call(bf16[256,2048]{1,0:T(8,128)(2,1)} %collective-permute-done.72.xa_ref.refs_15_, ...), custom_call_target="tpu_custom_call" | custom-call | flops 8589934592 | bytes 20971520 | tf_op jit(solution)/shard_map/pallas_call | solution.py:665
  326.1 17.6 %shard_map.301 = (bf16[256,2048]{1,0:T(8,128)(2,1)}, bf16[256,2048]{1,0:T(8,128)(2,1)}, bf16[256,2048]{1,0:T(8,128)(2,1)}, bf16[256,2048]{1,0:T(8,128)(2,1)}, bf...) custom-call(bf16[256,2048]{1,0:T(8,128)(2,1)} %copy-done.124, ...), custom_call_target="tpu_custom_call" | custom-call | flops 8589934592 | bytes 20971520 | tf_op jit(solution)/shard_map/pallas_call | solution.py:665
  345.4 18.1 %shard_map.302 = (bf16[256,2048]{1,0:T(8,128)(2,1)}, bf16[256,2048]{1,0:T(8,128)(2,1)}, bf16[256,2048]{1,0:T(8,128)(2,1)}, bf16[256,2048]{1,0:T(8,128)(2,1)}, bf...) custom-call(bf16[256,2048]{1,0:T(8,128)(2,1)} %copy-done.126, ...), custom_call_target="tpu_custom_call" | custom-call | flops 8589934592 | bytes 20971520 | tf_op jit(solution)/shard_map/pallas_call | solution.py:665
  364.8 17.7 %shard_map.307 = (bf16[256,2048]{1,0:T(8,128)(2,1)}, bf16[256,2048]{1,0:T(8,128)(2,1)}, bf16[256,2048]{1,0:T(8,128)(2,1)}, bf16[256,2048]{1,0:T(8,128)(2,1)}, bf...) custom-call(bf16[256,2048]{1,0:T(8,128)(2,1)} %collective-permute-done.77.xa_ref.refs_21_, ...), custom_call_target="tpu_custom_call" | custom-call | flops 8589934592 | bytes 20971520 | tf_op jit(solution)/shard_map/pallas_call | solution.py:665
  383.8 18.3 %shard_map.303 = (bf16[256,2048]{1,0:T(8,128)(2,1)}, bf16[256,2048]{1,0:T(8,128)(2,1)}, bf16[256,2048]{1,0:T(8,128)(2,1)}, bf16[256,2048]{1,0:T(8,128)(2,1)}, bf...) custom-call(bf16[256,2048]{1,0:T(8,128)(2,1)} %copy-done.132, ...), custom_call_target="tpu_custom_call" | custom-call | flops 8589934592 | bytes 20971520 | tf_op jit(solution)/shard_map/pallas_call | solution.py:665
  403.4 26.3 %shard_map.313 = bf16[1024,2048]{1,0:T(8,128)(2,1)} custom-call(bf16[512,1024]{1,0:T(8,128)(2,1)S(1)} %copy-done.60, bf16[256,2048]{1,0:T(8,128)(2,1)S(1)} %copy-done.9, bf16[256,2048]{1,0:T(8,128)(2,1)S(1)} %copy-done.41, bf16[512,1024]{1,0:T(8,128)(2,1)S(1)} %copy-done.58, bf16[256,2048]{1,0:T(8,128)(2,1)S(1)} %copy-done.11, ...), custom_call_target="tpu_custom_call" | custom-call | flops 17179869184 | bytes 33554432 | tf_op jit(solution)/shard_map/pallas_call | solution.py:360
  429.8 34.1 %shard_map.312 = bf16[2048,1024]{1,0:T(8,128)(2,1)} custom-call(bf16[256,2048]{1,0:T(8,128)(2,1)S(1)} %copy-done.13, bf16[256,2048]{1,0:T(8,128)(2,1)} %collective-permute-done.42.xb_ref.refs_1_, bf16[512,1024]{1,0:T(8,128)(2,1)S(1)} %copy-done.59, bf16[256,2048]{1,0:T(8,128)(2,1)S(1)} %copy-done.15, ...), custom_call_target="tpu_custom_call" | custom-call | flops 17179869184 | bytes 33554432 | tf_op jit(solution)/shard_map/pallas_call | solution.py:360
  469.8 7.6 collective-permute-start.124
  482.1 4.3 collective-permute-done.125
  493.4 19.8 %collective-permute-done.96 = bf16[256,2048]{1,0:T(8,128)(2,1)S(1)} collective-permute-done((bf16[256,2048]{1,0:T(8,128)(2,1)S(1)}, bf16[256,2048]{1,0:T(8,128)(2,1)S(1)}, u32[]{:S(2)}, u32[]{:S(2)}) %collective-permute-start.96) | collective-permute-done | bytes 1048608 | tf_op jit(solution)/shard_map/ppermute | solution.py:33
  520.8 18.4 %collective-permute-done.82 = bf16[256,2048]{1,0:T(8,128)(2,1)S(1)} collective-permute-done((bf16[256,2048]{1,0:T(8,128)(2,1)S(1)}, bf16[256,2048]{1,0:T(8,128)(2,1)S(1)}, u32[]{:S(2)}, u32[]{:S(2)}) %collective-permute-start.82) | collective-permute-done | bytes 1048608 | tf_op jit(solution)/shard_map/ppermute | solution.py:33
  545.2 16.6 %collective-permute-done.93 = bf16[256,2048]{1,0:T(8,128)(2,1)S(1)} collective-permute-done((bf16[256,2048]{1,0:T(8,128)(2,1)S(1)}, bf16[256,2048]{1,0:T(8,128)(2,1)S(1)}, u32[]{:S(2)}, u32[]{:S(2)}) %collective-permute-start.93) | collective-permute-done | bytes 1048608 | tf_op jit(solution)/shard_map/ppermute | solution.py:33
  561.8 22.2 %collective-permute-done.97 = bf16[256,2048]{1,0:T(8,128)(2,1)S(1)} collective-permute-done((bf16[256,2048]{1,0:T(8,128)(2,1)S(1)}, bf16[256,2048]{1,0:T(8,128)(2,1)S(1)}, u32[]{:S(2)}, u32[]{:S(2)}) %collective-permute-start.97) | collective-permute-done | bytes 1048608 | tf_op jit(solution)/shard_map/ppermute | solution.py:33
  593.9 17.1 %collective-permute-done.71 = bf16[256,2048]{1,0:T(8,128)(2,1)} collective-permute-done((bf16[256,2048]{1,0:T(8,128)(2,1)}, bf16[256,2048]{1,0:T(8,128)(2,1)}, u32[]{:S(2)}, u32[]{:S(2)}) %collective-permute-start.71) | collective-permute-done | bytes 1048608 | tf_op jit(solution)/shard_map/ppermute | solution.py:33
  611.0 23.0 %collective-permute-done.83 = bf16[256,2048]{1,0:T(8,128)(2,1)} collective-permute-done((bf16[256,2048]{1,0:T(8,128)(2,1)}, bf16[256,2048]{1,0:T(8,128)(2,1)}, u32[]{:S(2)}, u32[]{:S(2)}) %collective-permute-start.83) | collective-permute-done | bytes 1048608 | tf_op jit(solution)/shard_map/ppermute | solution.py:33
  640.9 4.3 fusion.30
  648.9 9.4 shard_map.308
  663.2 14.6 %shard_map.309 = (bf16[2,256,2048]{2,1,0:T(8,128)(2,1)S(1)}, f32[2,2048,128]{2,1,0:T(8,128)S(1)}, f32[2,2048,128]{2,1,0:T(8,128)S(1)}) custom-call(s32[2]{0:T(128)S(1)} %fusion.27.low_ref, s32[1]{0:T(128)} %bitcast.at_ref, bf16[2,256,2048]{2,1,0:T(8,128)(2,1)S(1)} %bitcast.110, bf16[2,256,2048]{2,1,0:T(8,128)(2,1)S(1)} %bitcast.111, ...), custom_call_target="tpu_custom_call" | custom-call | flops 10737418240 | bytes 16777216 | tf_op jit(solution)/shard_map/pallas_call | solution.py:204
  684.9 171.8 %shard_map.310 = (f32[256,2048]{1,0:T(8,128)}, f32[256,2048]{1,0:T(8,128)}, bf16[512,256]{1,0:T(8,128)(2,1)}) custom-call(bf16[512,2048]{1,0:T(8,128)(2,1)} %bitcast.108, bf16[512,2048]{1,0:T(8,128)(2,1)} %bitcast.119, bf16[512,2048]{1,0:T(8,128)(2,1)} %bitcast.101, bf16[512,2048]{1,0:T(8,128)(2,1)} %bitcast.122, bf16[8,512,256]{2,1,0:T(8,128)(2,1)} %bitcast.125), custom_call_target="tpu_custom_call" | custom-call | flops 8589934592 | bytes 67108864 | tf_op jit(solution)/shard_map/pallas_call | solution.py:588
  859.7 10.7 %shard_map.311 = f32[512,2048]{1,0:T(8,128)} custom-call(bf16[512,2048]{1,0:T(8,128)(2,1)} %bitcast.102, bf16[512,256]{1,0:T(8,128)(2,1)S(1)} %copy-done.16, bf16[2048,256]{1,0:T(8,128)(2,1)} %shared_ref.1, bf16[1024,256]{1,0:T(8,128)(2,1)S(1)} %get-tuple-element.217.refs_0_, bf16[1024,256]{1,0:T(8,128)(2,1)} %collective-permute-done.7.refs_1_, ...), custom_call_target="tpu_custom_call" | custom-call | flops 4294967296 | bytes 16777216 | tf_op jit(solution)/shard_map/pallas_call | solution.py:298
  876.7 3.3 collective-permute-start.99
  882.1 3.8 collective-permute-done.100
  895.2 5.5 fusion.11
  908.0 6.1 collective-permute-done.110
  918.3 7.6 collective-permute-done.123
  940.2 6.8 convert_element_type.487
  947.0 4.4 convert_element_type.488
  (643 shorter events, 205.8 us)
Async XLA Ops:
  7.2 933.1 %all-reduce.3.cloned.1.call-start = ((), (), s32[]{:S(2)}) async-start(), calls=%async_computation | async-start | bytes 16777216 | tf_op jit(solution)/shard_map/psum | solution.py:816
  110.1 37.9 %collective-permute-start.41 = (bf16[256,1024]{1,0:T(8,128)(2,1)}, bf16[256,1024]{1,0:T(8,128)(2,1)}, u32[]{:S(2)}, u32[]{:S(2)}) collective-permute-start(bf16[256,1024]{1,0:T(8,128)(2,1)} %collective-permute-done.40.refs_14_), channel_id=1, source_target_pairs={{0,1},{1,0},{2,3},{3,2},{4,5},{5,4},{6,7},{7,6},{8,9},{9,8},{10,11... | collective-permute-start | bytes 1572872 | tf_op jit(solution)/shard_map/ppermute | solution.py:33
  111.1 37.4 %collective-permute-start.34 = (bf16[256,1024]{1,0:T(8,128)(2,1)}, bf16[256,1024]{1,0:T(8,128)(2,1)}, u32[]{:S(2)}, u32[]{:S(2)}) collective-permute-start(bf16[256,1024]{1,0:T(8,128)(2,1)} %collective-permute-done.33.refs_6_), channel_id=1, source_target_pairs={{0,1},{1,0},{2,3},{3,2},{4,5},{5,4},{6,7},{7,6},{8,9},{9,8},{10,11... | collective-permute-start | bytes 1572872 | tf_op jit(solution)/shard_map/ppermute | solution.py:33
  130.3 43.9 %collective-permute-start.47 = (bf16[256,2048]{1,0:T(8,128)(2,1)}, bf16[256,2048]{1,0:T(8,128)(2,1)}, u32[]{:S(2)}, u32[]{:S(2)}) collective-permute-start(bf16[256,2048]{1,0:T(8,128)(2,1)} %get-tuple-element.204.ca_ref.refs_1_), channel_id=1, source_target_pairs={{0,4},{1,5},{2,6},{3,7},{4,0},{5,1},{6,2},{7,3},{8,12},{9,13},{10,... | collective-permute-start | bytes 3145736 | tf_op jit(solution)/shard_map/ppermute | solution.py:33
  130.8 60.3 %collective-permute-start.43 = (bf16[256,2048]{1,0:T(8,128)(2,1)}, bf16[256,2048]{1,0:T(8,128)(2,1)S(1)}, u32[]{:S(2)}, u32[]{:S(2)}) collective-permute-start(bf16[256,2048]{1,0:T(8,128)(2,1)} %get-tuple-element.204.ca_ref.refs_1_), channel_id=1, source_target_pairs={{0,1},{1,0},{2,3},{3,2},{4,5},{5,4},{6,7},{7,6},{8,9},{9,8},{10,11... | collective-permute-start | bytes 3145736 | tf_op jit(solution)/shard_map/ppermute | solution.py:33
  130.8 63.2 %collective-permute-start.74 = (bf16[256,2048]{1,0:T(8,128)(2,1)}, bf16[256,2048]{1,0:T(8,128)(2,1)}, u32[]{:S(2)}, u32[]{:S(2)}) collective-permute-start(bf16[256,2048]{1,0:T(8,128)(2,1)} %get-tuple-element.205.ca_ref.refs_4_), channel_id=1, source_target_pairs={{0,4},{1,5},{2,6},{3,7},{4,0},{5,1},{6,2},{7,3},{8,12},{9,13},{10,... | collective-permute-start | bytes 3145736 | tf_op jit(solution)/shard_map/ppermute | solution.py:33
  148.0 54.9 %collective-permute-start.68 = (bf16[256,2048]{1,0:T(8,128)(2,1)S(1)}, bf16[256,2048]{1,0:T(8,128)(2,1)S(1)}, u32[]{:S(2)}, u32[]{:S(2)}) collective-permute-start(bf16[256,2048]{1,0:T(8,128)(2,1)S(1)} %copy-done.10), channel_id=1, source_target_pairs={{0,2},{1,3},{2,0},{3,1},{4,6},{5,7},{6,4},{7,5},{8,10},{9,11},{10,... | collective-permute-start | bytes 3145736 | tf_op jit(solution)/shard_map/ppermute | solution.py:33
  148.6 54.4 %collective-permute-start.64 = (bf16[256,2048]{1,0:T(8,128)(2,1)S(1)}, bf16[256,2048]{1,0:T(8,128)(2,1)}, u32[]{:S(2)}, u32[]{:S(2)}) collective-permute-start(bf16[256,2048]{1,0:T(8,128)(2,1)S(1)} %copy-done.10), channel_id=1, source_target_pairs={{0,1},{1,0},{2,3},{3,2},{4,5},{5,4},{6,7},{7,6},{8,9},{9,8},{10,11... | collective-permute-start | bytes 3145736 | tf_op jit(solution)/shard_map/ppermute | solution.py:33
  174.1 38.6 %collective-permute-start.58 = (bf16[256,2048]{1,0:T(8,128)(2,1)}, bf16[256,2048]{1,0:T(8,128)(2,1)}, u32[]{:S(2)}, u32[]{:S(2)}) collective-permute-start(bf16[256,2048]{1,0:T(8,128)(2,1)} %collective-permute-done.53.ca_ref.refs_7_), channel_id=1, source_target_pairs={{0,4},{1,5},{2,6},{3,7},{4,0},{5,1},{6,2},{7,3},{8,12},{9,13},{10,... | collective-permute-start | bytes 3145736 | tf_op jit(solution)/shard_map/ppermute | solution.py:33
  194.1 31.4 %collective-permute-start.79 = (bf16[256,2048]{1,0:T(8,128)(2,1)}, bf16[256,2048]{1,0:T(8,128)(2,1)}, u32[]{:S(2)}, u32[]{:S(2)}) collective-permute-start(bf16[256,2048]{1,0:T(8,128)(2,1)} %collective-permute-done.74.ca_ref.refs_16_), channel_id=1, source_target_pairs={{0,2},{1,3},{2,0},{3,1},{4,6},{5,7},{6,4},{7,5},{8,10},{9,11},{10,... | collective-permute-start | bytes 3145736 | tf_op jit(solution)/shard_map/ppermute | solution.py:33
  202.9 44.5 %collective-permute-start.66 = (bf16[256,2048]{1,0:T(8,128)(2,1)S(1)}, bf16[256,2048]{1,0:T(8,128)(2,1)}, u32[]{:S(2)}, u32[]{:S(2)}) collective-permute-start(bf16[256,2048]{1,0:T(8,128)(2,1)S(1)} %get-tuple-element.207.xa_ref.refs_3_), channel_id=1, source_target_pairs={{0,2},{1,3},{2,0},{3,1},{4,6},{5,7},{6,4},{7,5},{8,10},{9,11},{10,... | collective-permute-start | bytes 3145736 | tf_op jit(solution)/shard_map/ppermute | solution.py:33
  204.0 43.8 %collective-permute-start.63 = (bf16[256,2048]{1,0:T(8,128)(2,1)S(1)}, bf16[256,2048]{1,0:T(8,128)(2,1)}, u32[]{:S(2)}, u32[]{:S(2)}) collective-permute-start(bf16[256,2048]{1,0:T(8,128)(2,1)S(1)} %get-tuple-element.207.xa_ref.refs_3_), channel_id=1, source_target_pairs={{0,1},{1,0},{2,3},{3,2},{4,5},{5,4},{6,7},{7,6},{8,9},{9,8},{10,11... | collective-permute-start | bytes 3145736 | tf_op jit(solution)/shard_map/ppermute | solution.py:33
  212.7 52.7 %collective-permute-start.69 = (bf16[256,2048]{1,0:T(8,128)(2,1)}, bf16[256,2048]{1,0:T(8,128)(2,1)}, u32[]{:S(2)}, u32[]{:S(2)}) collective-permute-start(bf16[256,2048]{1,0:T(8,128)(2,1)} %copy-done.121), channel_id=1, source_target_pairs={{0,1},{1,0},{2,3},{3,2},{4,5},{5,4},{6,7},{7,6},{8,9},{9,8},{10,11... | collective-permute-start | bytes 3145736 | tf_op jit(solution)/shard_map/ppermute | solution.py:33
  215.5 52.2 %collective-permute-start.72 = (bf16[256,2048]{1,0:T(8,128)(2,1)S(1)}, bf16[256,2048]{1,0:T(8,128)(2,1)}, u32[]{:S(2)}, u32[]{:S(2)}) collective-permute-start(bf16[256,2048]{1,0:T(8,128)(2,1)S(1)} %get-tuple-element.207.xa_ref.refs_3_), channel_id=1, source_target_pairs={{0,4},{1,5},{2,6},{3,7},{4,0},{5,1},{6,2},{7,3},{8,12},{9,13},{10,... | collective-permute-start | bytes 3145736 | tf_op jit(solution)/shard_map/ppermute | solution.py:33
  225.5 40.5 %collective-permute-start.42 = (bf16[256,2048]{1,0:T(8,128)(2,1)S(1)}, bf16[256,2048]{1,0:T(8,128)(2,1)}, u32[]{:S(2)}, u32[]{:S(2)}) collective-permute-start(bf16[256,2048]{1,0:T(8,128)(2,1)S(1)} %get-tuple-element.206.xa_ref.refs_0_), channel_id=1, source_target_pairs={{0,1},{1,0},{2,3},{3,2},{4,5},{5,4},{6,7},{7,6},{8,9},{9,8},{10,11... | collective-permute-start | bytes 3145736 | tf_op jit(solution)/shard_map/ppermute | solution.py:33
  247.4 38.3 %collective-permute-start.45 = (bf16[256,2048]{1,0:T(8,128)(2,1)S(1)}, bf16[256,2048]{1,0:T(8,128)(2,1)S(1)}, u32[]{:S(2)}, u32[]{:S(2)}) collective-permute-start(bf16[256,2048]{1,0:T(8,128)(2,1)S(1)} %get-tuple-element.206.xa_ref.refs_0_), channel_id=1, source_target_pairs={{0,4},{1,5},{2,6},{3,7},{4,0},{5,1},{6,2},{7,3},{8,12},{9,13},{10,... | collective-permute-start | bytes 3145736 | tf_op jit(solution)/shard_map/ppermute | solution.py:33
  247.8 38.3 %collective-permute-start.67 = (bf16[256,2048]{1,0:T(8,128)(2,1)}, bf16[256,2048]{1,0:T(8,128)(2,1)S(1)}, u32[]{:S(2)}, u32[]{:S(2)}) collective-permute-start(bf16[256,2048]{1,0:T(8,128)(2,1)} %collective-permute-done.66.xa_ref.refs_9_), channel_id=1, source_target_pairs={{0,1},{1,0},{2,3},{3,2},{4,5},{5,4},{6,7},{7,6},{8,9},{9,8},{10,11... | collective-permute-start | bytes 3145736 | tf_op jit(solution)/shard_map/ppermute | solution.py:33
  265.4 39.3 %collective-permute-start.75 = (bf16[256,2048]{1,0:T(8,128)(2,1)}, bf16[256,2048]{1,0:T(8,128)(2,1)S(1)}, u32[]{:S(2)}, u32[]{:S(2)}) collective-permute-start(bf16[256,2048]{1,0:T(8,128)(2,1)} %collective-permute-done.74.ca_ref.refs_16_), channel_id=1, source_target_pairs={{0,1},{1,0},{2,3},{3,2},{4,5},{5,4},{6,7},{7,6},{8,9},{9,8},{10,11... | collective-permute-start | bytes 3145736 | tf_op jit(solution)/shard_map/ppermute | solution.py:33
  266.0 39.1 %collective-permute-start.51 = (bf16[256,2048]{1,0:T(8,128)(2,1)S(1)}, bf16[256,2048]{1,0:T(8,128)(2,1)S(1)}, u32[]{:S(2)}, u32[]{:S(2)}) collective-permute-start(bf16[256,2048]{1,0:T(8,128)(2,1)S(1)} %get-tuple-element.206.xa_ref.refs_0_), channel_id=1, source_target_pairs={{0,2},{1,3},{2,0},{3,1},{4,6},{5,7},{6,4},{7,5},{8,10},{9,11},{10,... | collective-permute-start | bytes 3145736 | tf_op jit(solution)/shard_map/ppermute | solution.py:33
  267.7 39.0 %collective-permute-start.73 = (bf16[256,2048]{1,0:T(8,128)(2,1)}, bf16[256,2048]{1,0:T(8,128)(2,1)S(1)}, u32[]{:S(2)}, u32[]{:S(2)}) collective-permute-start(bf16[256,2048]{1,0:T(8,128)(2,1)} %collective-permute-done.72.xa_ref.refs_15_), channel_id=1, source_target_pairs={{0,1},{1,0},{2,3},{3,2},{4,5},{5,4},{6,7},{7,6},{8,9},{9,8},{10,11... | collective-permute-start | bytes 3145736 | tf_op jit(solution)/shard_map/ppermute | solution.py:33
  285.7 39.9 %collective-permute-start.77 = (bf16[256,2048]{1,0:T(8,128)(2,1)}, bf16[256,2048]{1,0:T(8,128)(2,1)}, u32[]{:S(2)}, u32[]{:S(2)}) collective-permute-start(bf16[256,2048]{1,0:T(8,128)(2,1)} %collective-permute-done.72.xa_ref.refs_15_), channel_id=1, source_target_pairs={{0,2},{1,3},{2,0},{3,1},{4,6},{5,7},{6,4},{7,5},{8,10},{9,11},{10,... | collective-permute-start | bytes 3145736 | tf_op jit(solution)/shard_map/ppermute | solution.py:33
  286.1 39.5 %collective-permute-start.46 = (bf16[256,2048]{1,0:T(8,128)(2,1)S(1)}, bf16[256,2048]{1,0:T(8,128)(2,1)}, u32[]{:S(2)}, u32[]{:S(2)}) collective-permute-start(bf16[256,2048]{1,0:T(8,128)(2,1)S(1)} %collective-permute-done.45.xa_ref.refs_12_), channel_id=1, source_target_pairs={{0,1},{1,0},{2,3},{3,2},{4,5},{5,4},{6,7},{7,6},{8,9},{9,8},{10,11... | collective-permute-start | bytes 3145736 | tf_op jit(solution)/shard_map/ppermute | solution.py:33
  304.7 39.0 %collective-permute-start.54 = (bf16[256,2048]{1,0:T(8,128)(2,1)}, bf16[256,2048]{1,0:T(8,128)(2,1)}, u32[]{:S(2)}, u32[]{:S(2)}) collective-permute-start(bf16[256,2048]{1,0:T(8,128)(2,1)} %collective-permute-done.53.ca_ref.refs_7_), channel_id=1, source_target_pairs={{0,1},{1,0},{2,3},{3,2},{4,5},{5,4},{6,7},{7,6},{8,9},{9,8},{10,11... | collective-permute-start | bytes 3145736 | tf_op jit(solution)/shard_map/ppermute | solution.py:33
  305.1 38.8 %collective-permute-start.56 = (bf16[256,2048]{1,0:T(8,128)(2,1)S(1)}, bf16[256,2048]{1,0:T(8,128)(2,1)S(1)}, u32[]{:S(2)}, u32[]{:S(2)}) collective-permute-start(bf16[256,2048]{1,0:T(8,128)(2,1)S(1)} %collective-permute-done.51.xa_ref.refs_6_), channel_id=1, source_target_pairs={{0,4},{1,5},{2,6},{3,7},{4,0},{5,1},{6,2},{7,3},{8,12},{9,13},{10,... | collective-permute-start | bytes 3145736 | tf_op jit(solution)/shard_map/ppermute | solution.py:33
  306.7 37.6 %collective-permute-start.52 = (bf16[256,2048]{1,0:T(8,128)(2,1)S(1)}, bf16[256,2048]{1,0:T(8,128)(2,1)S(1)}, u32[]{:S(2)}, u32[]{:S(2)}) collective-permute-start(bf16[256,2048]{1,0:T(8,128)(2,1)S(1)} %collective-permute-done.51.xa_ref.refs_6_), channel_id=1, source_target_pairs={{0,1},{1,0},{2,3},{3,2},{4,5},{5,4},{6,7},{7,6},{8,9},{9,8},{10,11... | collective-permute-start | bytes 3145736 | tf_op jit(solution)/shard_map/ppermute | solution.py:33
  325.5 37.9 %collective-permute-start.80 = (bf16[256,2048]{1,0:T(8,128)(2,1)}, bf16[256,2048]{1,0:T(8,128)(2,1)S(1)}, u32[]{:S(2)}, u32[]{:S(2)}) collective-permute-start(bf16[256,2048]{1,0:T(8,128)(2,1)} %collective-permute-done.79.ca_ref.refs_22_), channel_id=1, source_target_pairs={{0,1},{1,0},{2,3},{3,2},{4,5},{5,4},{6,7},{7,6},{8,9},{9,8},{10,11... | collective-permute-start | bytes 3145736 | tf_op jit(solution)/shard_map/ppermute | solution.py:33
  325.6 38.1 %collective-permute-start.78 = (bf16[256,2048]{1,0:T(8,128)(2,1)}, bf16[256,2048]{1,0:T(8,128)(2,1)S(1)}, u32[]{:S(2)}, u32[]{:S(2)}) collective-permute-start(bf16[256,2048]{1,0:T(8,128)(2,1)} %collective-permute-done.77.xa_ref.refs_21_), channel_id=1, source_target_pairs={{0,1},{1,0},{2,3},{3,2},{4,5},{5,4},{6,7},{7,6},{8,9},{9,8},{10,11... | collective-permute-start | bytes 3145736 | tf_op jit(solution)/shard_map/ppermute | solution.py:33
  343.8 38.7 %collective-permute-start.59 = (bf16[256,2048]{1,0:T(8,128)(2,1)}, bf16[256,2048]{1,0:T(8,128)(2,1)S(1)}, u32[]{:S(2)}, u32[]{:S(2)}) collective-permute-start(bf16[256,2048]{1,0:T(8,128)(2,1)} %collective-permute-done.58.ca_ref.refs_19_), channel_id=1, source_target_pairs={{0,1},{1,0},{2,3},{3,2},{4,5},{5,4},{6,7},{7,6},{8,9},{9,8},{10,11... | collective-permute-start | bytes 3145736 | tf_op jit(solution)/shard_map/ppermute | solution.py:33
  343.9 120.8 %collective-permute-start.70 = (bf16[256,2048]{1,0:T(8,128)(2,1)}, bf16[256,2048]{1,0:T(8,128)(2,1)}, u32[]{:S(2)}, u32[]{:S(2)}) collective-permute-start(bf16[256,2048]{1,0:T(8,128)(2,1)} %get-tuple-element.96), channel_id=1, source_target_pairs={{0,1},{1,0},{2,3},{3,2},{4,5},{5,4},{6,7},{7,6},{8,9},{9,8},{10,11... | collective-permute-start | bytes 3145736 | tf_op jit(solution)/shard_map/ppermute | solution.py:33
  344.3 38.5 %collective-permute-start.57 = (bf16[256,2048]{1,0:T(8,128)(2,1)S(1)}, bf16[256,2048]{1,0:T(8,128)(2,1)S(1)}, u32[]{:S(2)}, u32[]{:S(2)}) collective-permute-start(bf16[256,2048]{1,0:T(8,128)(2,1)S(1)} %collective-permute-done.56.xa_ref.refs_18_), channel_id=1, source_target_pairs={{0,1},{1,0},{2,3},{3,2},{4,5},{5,4},{6,7},{7,6},{8,9},{9,8},{10,11... | collective-permute-start | bytes 3145736 | tf_op jit(solution)/shard_map/ppermute | solution.py:33
  363.5 104.4 %collective-permute-start.92 = (bf16[256,2048]{1,0:T(8,128)(2,1)}, bf16[256,2048]{1,0:T(8,128)(2,1)}, u32[]{:S(2)}, u32[]{:S(2)}) collective-permute-start(bf16[256,2048]{1,0:T(8,128)(2,1)} %get-tuple-element.112), channel_id=1, source_target_pairs={{0,1},{1,0},{2,3},{3,2},{4,5},{5,4},{6,7},{7,6},{8,9},{9,8},{10,11... | collective-permute-start | bytes 3145736 | tf_op jit(solution)/shard_map/ppermute | solution.py:33
  363.8 128.4 %collective-permute-start.94 = (bf16[256,2048]{1,0:T(8,128)(2,1)}, bf16[256,2048]{1,0:T(8,128)(2,1)}, u32[]{:S(2)}, u32[]{:S(2)}) collective-permute-start(bf16[256,2048]{1,0:T(8,128)(2,1)} %get-tuple-element.114), channel_id=1, source_target_pairs={{0,1},{1,0},{2,3},{3,2},{4,5},{5,4},{6,7},{7,6},{8,9},{9,8},{10,11... | collective-permute-start | bytes 3145736 | tf_op jit(solution)/shard_map/ppermute | solution.py:33
  382.5 87.3 %collective-permute-start.49 = (bf16[256,2048]{1,0:T(8,128)(2,1)}, bf16[256,2048]{1,0:T(8,128)(2,1)}, u32[]{:S(2)}, u32[]{:S(2)}) collective-permute-start(bf16[256,2048]{1,0:T(8,128)(2,1)} %get-tuple-element.88), channel_id=1, source_target_pairs={{0,1},{1,0},{2,3},{3,2},{4,5},{5,4},{6,7},{7,6},{8,9},{9,8},{10,11... | collective-permute-start | bytes 3145736 | tf_op jit(solution)/shard_map/ppermute | solution.py:33
  382.8 97.3 %collective-permute-start.85 = (bf16[256,2048]{1,0:T(8,128)(2,1)}, bf16[256,2048]{1,0:T(8,128)(2,1)}, u32[]{:S(2)}, u32[]{:S(2)}) collective-permute-start(bf16[256,2048]{1,0:T(8,128)(2,1)} %get-tuple-element.104), channel_id=1, source_target_pairs={{0,1},{1,0},{2,3},{3,2},{4,5},{5,4},{6,7},{7,6},{8,9},{9,8},{10,11... | collective-permute-start | bytes 3145736 | tf_op jit(solution)/shard_map/ppermute | solution.py:33
  464.8 28.1 %collective-permute-start.87 = (bf16[256,2048]{1,0:T(8,128)(2,1)}, bf16[256,2048]{1,0:T(8,128)(2,1)S(1)}, u32[]{:S(2)}, u32[]{:S(2)}) collective-permute-start(bf16[256,2048]{1,0:T(8,128)(2,1)} %get-tuple-element.106), channel_id=1, source_target_pairs={{0,1},{1,0},{2,3},{3,2},{4,5},{5,4},{6,7},{7,6},{8,9},{9,8},{10,11... | collective-permute-start | bytes 3145736 | tf_op jit(solution)/shard_map/ppermute | solution.py:33
  491.7 27.0 %collective-permute-start.91 = (bf16[256,2048]{1,0:T(8,128)(2,1)S(1)}, bf16[256,2048]{1,0:T(8,128)(2,1)S(1)}, u32[]{:S(2)}, u32[]{:S(2)}) collective-permute-start(bf16[256,2048]{1,0:T(8,128)(2,1)S(1)} %copy-done.120), channel_id=1, source_target_pairs={{0,1},{1,0},{2,3},{3,2},{4,5},{5,4},{6,7},{7,6},{8,9},{9,8},{10,11... | collective-permute-start | bytes 3145736 | tf_op jit(solution)/shard_map/ppermute | solution.py:33
  493.2 27.0 %collective-permute-start.55 = (bf16[256,2048]{1,0:T(8,128)(2,1)S(1)}, bf16[256,2048]{1,0:T(8,128)(2,1)S(1)}, u32[]{:S(2)}, u32[]{:S(2)}) collective-permute-start(bf16[256,2048]{1,0:T(8,128)(2,1)S(1)} %copy-done.123), channel_id=1, source_target_pairs={{0,1},{1,0},{2,3},{3,2},{4,5},{5,4},{6,7},{7,6},{8,9},{9,8},{10,11... | collective-permute-start | bytes 3145736 | tf_op jit(solution)/shard_map/ppermute | solution.py:33
  519.4 65.3 %collective-permute-start.84 = (bf16[256,2048]{1,0:T(8,128)(2,1)S(1)}, bf16[256,2048]{1,0:T(8,128)(2,1)S(1)}, u32[]{:S(2)}, u32[]{:S(2)}) collective-permute-start(bf16[256,2048]{1,0:T(8,128)(2,1)S(1)} %copy-done.119), channel_id=1, source_target_pairs={{0,1},{1,0},{2,3},{3,2},{4,5},{5,4},{6,7},{7,6},{8,9},{9,8},{10,11... | collective-permute-start | bytes 3145736 | tf_op jit(solution)/shard_map/ppermute | solution.py:33
  519.4 42.4 %collective-permute-start.93 = (bf16[256,2048]{1,0:T(8,128)(2,1)S(1)}, bf16[256,2048]{1,0:T(8,128)(2,1)S(1)}, u32[]{:S(2)}, u32[]{:S(2)}) collective-permute-start(bf16[256,2048]{1,0:T(8,128)(2,1)S(1)} %add_convert_fusion.4), channel_id=1, source_target_pairs={{0,2},{1,3},{2,0},{3,1},{4,6},{5,7},{6,4},{7,5},{8,10},{9,11},{10,... | collective-permute-start | bytes 3145736 | tf_op jit(solution)/shard_map/ppermute | solution.py:33
  520.2 65.7 %collective-permute-start.86 = (bf16[256,2048]{1,0:T(8,128)(2,1)S(1)}, bf16[256,2048]{1,0:T(8,128)(2,1)S(1)}, u32[]{:S(2)}, u32[]{:S(2)}) collective-permute-start(bf16[256,2048]{1,0:T(8,128)(2,1)S(1)} %add_convert_fusion.10), channel_id=1, source_target_pairs={{0,4},{1,5},{2,6},{3,7},{4,0},{5,1},{6,2},{7,3},{8,12},{9,13},{10,... | collective-permute-start | bytes 3145736 | tf_op jit(solution)/shard_map/ppermute | solution.py:33
  539.3 44.7 %collective-permute-start.97 = (bf16[256,2048]{1,0:T(8,128)(2,1)S(1)}, bf16[256,2048]{1,0:T(8,128)(2,1)S(1)}, u32[]{:S(2)}, u32[]{:S(2)}) collective-permute-start(bf16[256,2048]{1,0:T(8,128)(2,1)S(1)} %add_convert_fusion), channel_id=1, source_target_pairs={{0,4},{1,5},{2,6},{3,7},{4,0},{5,1},{6,2},{7,3},{8,12},{9,13},{10,... | collective-permute-start | bytes 3145736 | tf_op jit(solution)/shard_map/ppermute | solution.py:33
  541.0 46.5 %collective-permute-start.90 = (bf16[256,2048]{1,0:T(8,128)(2,1)S(1)}, bf16[256,2048]{1,0:T(8,128)(2,1)S(1)}, u32[]{:S(2)}, u32[]{:S(2)}) collective-permute-start(bf16[256,2048]{1,0:T(8,128)(2,1)S(1)} %add_convert_fusion.6), channel_id=1, source_target_pairs={{0,2},{1,3},{2,0},{3,1},{4,6},{5,7},{6,4},{7,5},{8,10},{9,11},{10,... | collective-permute-start | bytes 3145736 | tf_op jit(solution)/shard_map/ppermute | solution.py:33
  561.8 31.2 %collective-permute-start.65 = (bf16[256,2048]{1,0:T(8,128)(2,1)S(1)}, bf16[256,2048]{1,0:T(8,128)(2,1)}, u32[]{:S(2)}, u32[]{:S(2)}) collective-permute-start(bf16[256,2048]{1,0:T(8,128)(2,1)S(1)} %copy-done.118), channel_id=1, source_target_pairs={{0,1},{1,0},{2,3},{3,2},{4,5},{5,4},{6,7},{7,6},{8,9},{9,8},{10,11... | collective-permute-start | bytes 3145736 | tf_op jit(solution)/shard_map/ppermute | solution.py:33
  584.0 53.1 %collective-permute-start.44 = (bf16[256,2048]{1,0:T(8,128)(2,1)}, bf16[256,2048]{1,0:T(8,128)(2,1)}, u32[]{:S(2)}, u32[]{:S(2)}) collective-permute-start(bf16[256,2048]{1,0:T(8,128)(2,1)} %get-tuple-element.86), channel_id=1, source_target_pairs={{0,1},{1,0},{2,3},{3,2},{4,5},{5,4},{6,7},{7,6},{8,9},{9,8},{10,11... | collective-permute-start | bytes 3145736 | tf_op jit(solution)/shard_map/ppermute | solution.py:33
  585.9 51.1 %collective-permute-start.50 = (bf16[256,2048]{1,0:T(8,128)(2,1)}, bf16[256,2048]{1,0:T(8,128)(2,1)}, u32[]{:S(2)}, u32[]{:S(2)}) collective-permute-start(bf16[256,2048]{1,0:T(8,128)(2,1)} %add_convert_fusion.22), channel_id=1, source_target_pairs={{0,4},{1,5},{2,6},{3,7},{4,0},{5,1},{6,2},{7,3},{8,12},{9,13},{10,... | collective-permute-start | bytes 3145736 | tf_op jit(solution)/shard_map/ppermute | solution.py:33
  587.4 46.6 %collective-permute-start.83 = (bf16[256,2048]{1,0:T(8,128)(2,1)}, bf16[256,2048]{1,0:T(8,128)(2,1)}, u32[]{:S(2)}, u32[]{:S(2)}) collective-permute-start(bf16[256,2048]{1,0:T(8,128)(2,1)} %add_convert_fusion.12), channel_id=1, source_target_pairs={{0,4},{1,5},{2,6},{3,7},{4,0},{5,1},{6,2},{7,3},{8,12},{9,13},{10,... | collective-permute-start | bytes 3145736 | tf_op jit(solution)/shard_map/ppermute | solution.py:33
  592.9 44.1 %collective-permute-start.62 = (bf16[256,2048]{1,0:T(8,128)(2,1)}, bf16[256,2048]{1,0:T(8,128)(2,1)}, u32[]{:S(2)}, u32[]{:S(2)}) collective-permute-start(bf16[256,2048]{1,0:T(8,128)(2,1)} %add_convert_fusion.18), channel_id=1, source_target_pairs={{0,2},{1,3},{2,0},{3,1},{4,6},{5,7},{6,4},{7,5},{8,10},{9,11},{10,... | collective-permute-start | bytes 3145736 | tf_op jit(solution)/shard_map/ppermute | solution.py:33
  645.2 236.7 %collective-permute-start.119 = (f32[4,2048]{1,0:T(4,128)S(1)}, f32[4,2048]{1,0:T(4,128)S(1)}, u32[]{:S(2)}, u32[]{:S(2)}) collective-permute-start(f32[4,2048]{1,0:T(4,128)S(1)} %pad_maximum_fusion.3), channel_id=1, source_target_pairs={{0,1},{1,0},{2,3},{3,2},{4,5},{5,4},{6,7},{7,6},{8,9},{9,8},{10,11... | collective-permute-start | bytes 98312 | tf_op jit(solution)/shard_map/ppermute | solution.py:33
  (220 other events, 2990.0 us)
Sparse Core Ops, SparseCore 0:
  464.2 295.5 all-reduce.2

commit v3 on v2

--- a/solution.py
+++ b/solution.py
@@ -226,7 +226,7 @@
         ],
         compiler_params=pltpu.CompilerParams(vmem_limit_bytes=32 * MIB),
         cost_estimate=pl.CostEstimate(
-            flops=5 * rows * span * width * length, bytes_accessed=16 * MIB, transcendentals=rows * span * length
+            flops=1000, bytes_accessed=MIB, transcendentals=0
         ),
     )(low, at, q, do, o, lse, k, kt, v, dock, docq)
 
@@ -277,16 +277,6 @@
         fill(w_s, split_parts(parts), 0)
 
     o_ref[...] = dot_nt(g_ref[...], w_s[...]).astype(BF)
-
-
-def dh_kernel(g_ref, kv_ref, shared_ref, *refs):
-    *parts, o_ref, w_s = refs
-
-    @pl.when(pl.program_id(0) == 0)
-    def _():
-        fill(w_s, split_parts(parts), 1)
-
-    o_ref[...] = dot_nt(g_ref[...], w_s[...]) + dot_nt(kv_ref[...], shared_ref[...])
 
 
 def slot_product(kernel, tiled, fixed, parts, outs, shape):
@@ -310,103 +300,109 @@
     return result
 
 
-def weight_grad_kernel(*refs, units):
-    count = sum(len(a) + len(b) for a, b in units)
-    ins = refs[:count]
-    o_ref, a_s, b_s, acc, sem = refs[count:]
-    steps = len(units)
-    wide = a_s.shape[2]
-    tile = min(256, wide)
-
-    def copies(u):
-        slot, at, out = u % 2, sum(len(a) + len(b) for a, b in units[:u]), []
-        for which, (buf, rows) in enumerate(((a_s, units[u][0]), (b_s, units[u][1]))):
-            begin = 0
-            for j, size in enumerate(rows):
-                out.append(
-                    pltpu.make_async_copy(ins[at], buf.at[slot, pl.ds(begin, size)], sem.at[slot, which, j])
-                )
-                begin += size
-                at += 1
-        return out
-
-    for c in copies(0):
-        c.start()
-    for u in range(steps):
-        if u + 1 < steps:
-            for c in copies(u + 1):
-                c.start()
-        for c in copies(u):
-            c.wait()
-
-        @pl.loop(0, wide // tile)
-        def _(i, u=u):
-            here = pl.ds(pl.multiple_of(i * tile, tile), tile)
-            term = dot_tn(a_s[u % 2, :, here], b_s[u % 2])
-            if u == 0:
-                acc[here, :] = term
-            elif u + 1 < steps:
-                acc[here, :] += term
-            else:
-                o_ref[here, :] = (acc[here, :] + term).astype(BF)
-
-
-def weight_grad(a_units, b_units):
-    units = [([x.shape[0] for x in a], [x.shape[0] for x in b]) for a, b in zip(a_units, b_units)]
-    flat = [x for a, b in zip(a_units, b_units) for x in list(a) + list(b)]
-    tokens = sum(units[0][0])
-    wide, cols = a_units[0][0].shape[1], b_units[0][0].shape[1]
-    most = max(max(len(a), len(b)) for a, b in units)
+def after_kernel(x_ref, *refs):
+    refs[-1][...] = x_ref[...]
+
+
+def after(x, *first):
     return pl.pallas_call(
-        functools.partial(weight_grad_kernel, units=units),
-        in_specs=[pl.BlockSpec(memory_space=pl.ANY)] * len(flat),
+        after_kernel,
+        in_specs=[pl.BlockSpec(memory_space=pltpu.VMEM)] + [pl.BlockSpec(memory_space=pl.ANY)] * len(first),
         out_specs=pl.BlockSpec(memory_space=pltpu.VMEM),
-        out_shape=jax.ShapeDtypeStruct((wide, cols), BF),
-        scratch_shapes=[
-            pltpu.VMEM((2, tokens, wide), BF),
-            pltpu.VMEM((2, tokens, cols), BF),
-            pltpu.VMEM((wide, cols), F32),
-            pltpu.SemaphoreType.DMA((2, 2, most)),
-        ],
-        compiler_params=pltpu.CompilerParams(vmem_limit_bytes=48 * MIB),
-        cost_estimate=pl.CostEstimate(
-            flops=2 * tokens * len(units) * wide * cols, bytes_accessed=32 * MIB, transcendentals=0
-        ),
-    )(*flat)
-
-
-def sum_all(x, axes):
-    for axis in axes:
-        for bit in range(lax.axis_size(axis).bit_length() - 1):
-            x = x + swap(x, bit, axis)
-    return x
+        out_shape=jax.ShapeDtypeStruct(x.shape, x.dtype),
+    )(x, *first)
 
 
 MESH = pl.DeviceIdType.MESH
 
 
-def greet(bits, line):
+def greet(bits, line=False, dp_bits=()):
     me, z = lax.axis_index("tensor"), lax.axis_index("dp")
     barrier = pltpu.get_barrier_semaphore()
     for bit in bits:
         pl.semaphore_signal(barrier, inc=1, device_id={"tensor": me ^ (1 << bit)}, device_id_type=MESH)
     count = len(bits)
+    flips = {1 << bit for bit in dp_bits} | ({1} if line else set())
+    for flip in sorted(flips):
+        pl.semaphore_signal(barrier, inc=1, device_id={"dp": z ^ flip}, device_id_type=MESH)
+    count += len(flips)
     if line:
         inner = (z == 1) | (z == 2)
-        pl.semaphore_signal(barrier, inc=1, device_id={"dp": z ^ 1}, device_id_type=MESH)
 
         @pl.when(inner)
         def _():
             pl.semaphore_signal(barrier, inc=1, device_id={"dp": 3 - z}, device_id_type=MESH)
 
-        count = count + 1 + inner.astype(jnp.int32)
+        count = count + inner.astype(jnp.int32)
     pl.semaphore_wait(barrier, count)
 
 
+class Line:
+    def __init__(self, own, near, far, sem):
+        self.own, self.near, self.far, self.sem = own, near, far, sem
+        self.z = lax.axis_index("dp")
+        self.inner = (self.z == 1) | (self.z == 2)
+        self.outer = jnp.logical_not(self.inner)
+
+    def copy(self, i, hop):
+        src = (self.own, self.near, self.near)[hop].at[i]
+        dst = (self.near, self.far, self.near)[hop].at[i]
+        return pltpu.make_async_remote_copy(
+            src_ref=src, dst_ref=dst, send_sem=self.sem.at[0, hop, i], recv_sem=self.sem.at[1, hop, i],
+            device_id={"dp": 3 - self.z if hop == 1 else self.z ^ 1}, device_id_type=MESH,
+        )
+
+    def start(self, i):
+        @pl.when(self.outer)
+        def _():
+            self.copy(i, 0).start()
+
+    def middle(self, i, own):
+        @pl.when(self.inner)
+        def _():
+            self.copy(i, 0).wait_recv()
+            self.near[i] = (own().astype(F32) + self.near[i].astype(F32)).astype(BF)
+            self.copy(i, 1).start()
+
+    def back(self, i):
+        @pl.when(self.inner)
+        def _():
+            self.copy(i, 1).wait()
+            self.near[i] = (self.near[i].astype(F32) + self.far[i].astype(F32)).astype(BF)
+            self.copy(i, 2).start()
+
+    def close(self, i):
+        @pl.when(self.outer)
+        def _():
+            self.copy(i, 0).wait_send()
+            self.copy(i, 2).wait_recv()
+
+        @pl.when(self.inner)
+        def _():
+            self.copy(i, 2).wait_send()
+
+
 class Scatter:
-    def __init__(self, bits, send, recv, send_sem, recv_sem):
+    def __init__(self, bits, send, recv, send_sem, recv_sem, shared=0):
         self.bits, self.send, self.recv, self.send_sem, self.recv_sem = bits, send, recv, send_sem, recv_sem
         self.me = lax.axis_index("tensor")
+        self.shared = shared
+        self.busy = {}
+
+    def place(self, k):
+        if not self.shared:
+            return k
+        return k // 2 if k % 2 == 0 else (1 << len(self.bits)) // 2 + k // 2 % self.shared
+
+    def claim(self, k):
+        place = self.place(k)
+        if place in self.busy:
+            self.copy(self.busy.pop(place)).wait_send()
+        return self.send.at[place]
+
+    def launch(self, k):
+        self.copy(k).start()
+        self.busy[self.place(k)] = k
 
     def stage(self, k):
         return next((i for i, b in enumerate(self.bits) if k >> b & 1), len(self.bits))
@@ -414,7 +410,7 @@
     def copy(self, k):
         bit = self.bits[self.stage(k)]
         return pltpu.make_async_remote_copy(
-            src_ref=self.send.at[k],
+            src_ref=self.send.at[self.place(k)],
             dst_ref=self.recv.at[k - 1],
             send_sem=self.send_sem.at[k],
             recv_sem=self.recv_sem.at[k],
@@ -423,24 +419,25 @@
         )
 
     def put(self, k, value):
-        self.send[k] = value.astype(BF)
+        self.claim(k)[...] = value.astype(BF)
         if self.stage(k) == 0:
-            self.copy(k).start()
+            self.launch(k)
 
     def total(self, k):
-        value = self.send[k].astype(F32)
+        value = self.send[self.place(k)].astype(F32)
         for bit in self.bits[: self.stage(k)]:
             self.copy(k | (1 << bit)).wait_recv()
             value = value + self.recv[(k | (1 << bit)) - 1].astype(F32)
         return value
 
     def forward(self, k):
-        self.send[k] = self.total(k).astype(BF)
-        self.copy(k).start()
+        self.send[self.place(k)] = self.total(k).astype(BF)
+        self.launch(k)
 
     def drain(self):
-        for k in range(1, 1 << len(self.bits)):
+        for k in self.busy.values():
             self.copy(k).wait_send()
+        self.busy = {}
 
 
 def scatter_order(bits):
@@ -450,35 +447,30 @@
 
 
 def attention_grads_kernel(a_ref, gm_ref, dq_ref, h_ref, dkv_ref, wo_ref, wq_ref, kv_ref,
-                           send, recv, ksend, krecv, zbuf, ssem, rsem, ksem, krsem, zsem, *, orders, line, qw):
+                           send, recv, ksend, krecv, ssem, rsem, ksem, krsem, *, orders, qw):
     bits_of = [[0] + list(o)[::-1] for o in orders]
     count = len(bits_of[0])
     n = 1 << count
     half = gm_ref.shape[1] // 2
-    greet(range(count), line)
-    z = lax.axis_index("dp")
-
+    greet(range(count))
     kv = Scatter(bits_of[0], ksend, krecv, ksem, krsem)
     for k in list(range(1, n, 2)) + list(range(0, n, 2)):
         kv.put(k, dkv_ref[k])
 
     pairs = ((a_ref, gm_ref, wo_ref), (dq_ref, h_ref, wq_ref))
     work = [
-        [Scatter(bits_of[p], send.at[m, p], recv.at[m, p], ssem.at[m, p], rsem.at[m, p]) for p in range(2)]
+        [Scatter(bits_of[p], send.at[m, p], recv.at[m, p], ssem.at[m, p], rsem.at[m, p], shared=2) for p in range(2)]
         for m in range(2)
     ]
     sequence = [scatter_order(b) for b in bits_of]
 
-    def compute(m, p, k):
+    def products(m):
         x, y, _ = pairs[m]
-        work[m][p].put(k, dot_tn(x[:, k * qw : (k + 1) * qw], y[:, p * half : (p + 1) * half]))
-
-    def products(m):
         for i in range(n // 2):
             for p in range(2):
                 k = (sequence[p] + [0])[i]
-                compute(m, p, k + 1)
-                compute(m, p, k)
+                for j in (k + 1, k):
+                    work[m][p].put(j, dot_tn(x[:, j * qw : (j + 1) * qw], y[:, p * half : (p + 1) * half]))
 
     def stage(m, i):
         for at in range(n // 2 - 1):
@@ -487,70 +479,14 @@
                 if work[m][p].stage(k) == i:
                     work[m][p].forward(k)
 
-    def z_copy(m, p, hop, to):
-        return pltpu.make_async_remote_copy(
-            src_ref=zbuf.at[m, p, hop % 2],
-            dst_ref=zbuf.at[m, p, 2 + hop % 2],
-            send_sem=zsem.at[m, p, hop],
-            recv_sem=zsem.at[m, p, 3 + hop],
-            device_id={"dp": to},
-            device_id_type=MESH,
-        )
-
-    inner = (z == 1) | (z == 2)
-    outer = jnp.logical_not(inner)
-
-    def finish(m, p):
-        value = work[m][p].total(0)
-        if not line:
-            pairs[m][2][:, p * half : (p + 1) * half] = value
-            return
-        zbuf[m, p, 0] = value.astype(BF)
-
-        @pl.when(outer)
-        def _():
-            z_copy(m, p, 0, z ^ 1).start()
-
-    def middle(m, p):
-        @pl.when(inner)
-        def _():
-            z_copy(m, p, 0, z ^ 1).wait_recv()
-            zbuf[m, p, 1] = (zbuf[m, p, 0].astype(F32) + zbuf[m, p, 2].astype(F32)).astype(BF)
-            z_copy(m, p, 1, 3 - z).start()
-
-    def back(m, p):
-        here = pairs[m][2].at[:, p * half : (p + 1) * half]
-
-        @pl.when(inner)
-        def _():
-            z_copy(m, p, 1, 3 - z).wait_recv()
-            both = (zbuf[m, p, 1].astype(F32) + zbuf[m, p, 3].astype(F32)).astype(BF)
-            zbuf[m, p, 0] = both
-            z_copy(m, p, 2, z ^ 1).start()
-            here[...] = both.astype(F32)
-
-    def close(m, p):
-        here = pairs[m][2].at[:, p * half : (p + 1) * half]
-
-        @pl.when(outer)
-        def _():
-            z_copy(m, p, 0, z ^ 1).wait_send()
-            z_copy(m, p, 2, z ^ 1).wait_recv()
-            here[...] = zbuf[m, p, 2].astype(F32)
-
-        @pl.when(inner)
-        def _():
-            z_copy(m, p, 1, 3 - z).wait_send()
-            z_copy(m, p, 2, z ^ 1).wait_send()
-
     def kv_stage(i):
         for k in scatter_order(bits_of[0]):
             if kv.stage(k) == i:
                 kv.forward(k)
 
-    def both(step, m):
+    def finish(m):
         for p in range(2):
-            step(m, p)
+            pairs[m][2][p] = work[m][p].total(0).astype(BF)
 
     products(0)
     stage(0, 1)
@@ -560,18 +496,10 @@
         if i + 1 < count:
             stage(0, i + 1)
         else:
-            both(finish, 0)
+            finish(0)
         stage(1, i)
     kv_ref[...] = kv.total(0).astype(BF)
-    if line:
-        both(middle, 0)
-    both(finish, 1)
-    if line:
-        both(back, 0)
-        both(middle, 1)
-        both(close, 0)
-        both(back, 1)
-        both(close, 1)
+    finish(1)
     kv.drain()
     for m in range(2):
         for p in range(2):
@@ -579,118 +507,610 @@
 
 
 def attention_grads(a, gm, dq, h, dkv, orders):
-    n, line = lax.axis_size("tensor"), lax.axis_size("dp") == 4
+    n = lax.axis_size("tensor")
     tokens, d = gm.shape
     qw = a.shape[1] // n
     slot = dkv.shape[1:]
     dma = pltpu.SemaphoreType.DMA
     vmem = pl.BlockSpec(memory_space=pltpu.VMEM)
     return pl.pallas_call(
-        functools.partial(attention_grads_kernel, orders=orders, line=line, qw=qw),
+        functools.partial(attention_grads_kernel, orders=orders, qw=qw),
         in_specs=[vmem] * 5,
         out_specs=[vmem] * 3,
         out_shape=[
-            jax.ShapeDtypeStruct((qw, d), F32),
-            jax.ShapeDtypeStruct((qw, d), F32),
+            jax.ShapeDtypeStruct((2, qw, d // 2), BF),
+            jax.ShapeDtypeStruct((2, qw, d // 2), BF),
             jax.ShapeDtypeStruct(slot, BF),
         ],
         scratch_shapes=[
-            pltpu.VMEM((2, 2, n, qw, d // 2), BF),
+            pltpu.VMEM((2, 2, n // 2 + 2, qw, d // 2), BF),
             pltpu.VMEM((2, 2, n - 1, qw, d // 2), BF),
             pltpu.VMEM((n,) + slot, BF),
             pltpu.VMEM((n - 1,) + slot, BF),
-            pltpu.VMEM((2, 2, 4, qw, d // 2), BF),
-            dma((2, 2, n)), dma((2, 2, n)), dma((n,)), dma((n,)), dma((2, 2, 6)),
+            dma((2, 2, n)), dma((2, 2, n)), dma((n,)), dma((n,)),
         ],
         compiler_params=pltpu.CompilerParams(
             collective_id=1, has_side_effects=True, vmem_limit_bytes=60 * MIB
         ),
+        cost_estimate=pl.CostEstimate(flops=1000, bytes_accessed=MIB, transcendentals=0),
+    )(a, gm, dq, h, dkv)
+
+
+def last_kernel(wo_ref, wq_ref, dq_ref, kv_ref, shared_ref, h_ref, x_ref, gain_ref, mixed_ref, qb_ref, *refs,
+                order, line, eps_rows):
+    count = len(order) + 1
+    n = 1 << count
+    parts = refs[: 2 * n]
+    (wog_ref, wqg_ref, grad_ref, late_ref, sg_ref,
+     w_s, near, far, part, send, recv, dsend, drecv, piece_s, gathered, vsend, vrecv,
+     zsem, ssem, rsem, dsem, gsem, vsem) = refs[2 * n :]
+    me, z = lax.axis_index("tensor"), lax.axis_index("dp")
+    dp_bits = range(lax.axis_size("dp").bit_length() - 1)
+    tokens, d = x_ref.shape
+    hd = kv_ref.shape[1] // 2
+    piece = d // n
+    greet(range(count), line, dp_bits)
+
+    owns = [wo_ref.at[0], wo_ref.at[1], wq_ref.at[0], wq_ref.at[1]]
+    chains = []
+    if line:
+        for i, ref in enumerate((wo_ref, wq_ref)):
+            c = Line(ref, near.at[i], far.at[i], zsem.at[i])
+            c.values = [lambda ref=ref, p=p: ref[p] for p in range(2)]
+            chains.append(c)
+            for p in range(2):
+                c.start(p)
+
+    ahead = [0, 0]
+
+    def chain_to(middles, backs):
+        while line and ahead[0] < min(middles, 4):
+            i, p = divmod(ahead[0], 2)
+            chains[i].middle(p, chains[i].values[p])
+            ahead[0] += 1
+        while line and ahead[1] < min(backs, 4):
+            i, p = divmod(ahead[1], 2)
+            chains[i].back(p)
+            ahead[1] += 1
+
+    part[...] = dot_tn(h_ref[...], kv_ref[...])
+    scatter = Scatter([0] + list(order)[::-1], send, recv, ssem, rsem)
+    for k in list(range(1, n, 2)) + list(range(0, n, 2)):
+        scatter.put(k, part[pl.ds(pl.multiple_of((me ^ k) * piece, piece), piece), :])
+    fill(w_s, split_parts(parts), 1)
+    for i in range(1, count):
+        for k in scatter_order(scatter.bits):
+            if scatter.stage(k) == i:
+                scatter.forward(k)
+    chain_to(1, 0)
+
+    gain_part, shift_part = jnp.zeros((1, d), F32), jnp.zeros((1, d), F32)
+    for t in range(tokens // eps_rows):
+        rows = slice(t * eps_rows, (t + 1) * eps_rows)
+        grad = dot_nt(dq_ref[rows], w_s[...]) + dot_nt(kv_ref[rows], shared_ref[...])
+        unit, scale = norm_parts(x_ref[rows].astype(F32))
+        e = gain_ref[...] * grad
+        back = e - jnp.mean(e, axis=-1, keepdims=True) - unit * jnp.mean(e * unit, axis=-1, keepdims=True)
+        grad_ref[rows] = mixed_ref[rows] + scale * back
+        gain_part += jnp.sum(grad * unit, axis=0, keepdims=True)
+        shift_part += jnp.sum(grad, axis=0, keepdims=True)
+        chain_to(2 + t, 1 + t)
+    at = 0
+    for value in (gain_part, shift_part, jnp.sum(kv_ref[:, hd:].astype(F32), axis=0, keepdims=True), qb_ref[...]):
+        late_ref[:, at : at + value.shape[1]] = value
+        at += value.shape[1]
+
+    hops = [("tensor", me, b) for b in range(count)] + [("dp", z, b) for b in dp_bits]
+
+    def small(buffers, sems, i, axis, at, bit):
+        return pltpu.make_async_remote_copy(
+            src_ref=buffers[0].at[i], dst_ref=buffers[1].at[i], send_sem=sems.at[0, i], recv_sem=sems.at[1, i],
+            device_id={axis: at ^ (1 << bit)}, device_id_type=MESH,
+        )
+
+    piece_s[...] = scatter.total(0)
+    pending = []
+    for i, (axis, at, bit) in enumerate(hops):
+        vsend[i] = late_ref[...]
+        c = small((vsend, vrecv), vsem, i, axis, at, bit)
+        c.start()
+        j = i if i < len(dp_bits) else None
+        if j is not None:
+            dsend[j] = piece_s[...]
+            e = small((dsend, drecv), dsem, j, "dp", z, dp_bits[j])
+            e.start()
+        if i:
+            chain_to(3 + i, 2 + i)
+        c.wait_recv()
+        late_ref[...] = late_ref[...] + vrecv[i]
+        pending.append(c)
+        if j is not None:
+            e.wait_recv()
+            piece_s[...] = piece_s[...] + drecv[j]
+            pending.append(e)
+        if j == len(dp_bits) - 1:
+            gathered[me] = piece_s[...].astype(BF)
+            held = [0]
+    sent = []
+    for bit in list(order) + [0]:
+        new = []
+        for k in held:
+            c = pltpu.make_async_remote_copy(
+                src_ref=gathered.at[me ^ k], dst_ref=gathered.at[me ^ k], send_sem=gsem.at[0, k | (1 << bit)],
+                recv_sem=gsem.at[1, k | (1 << bit)], device_id={"tensor": me ^ (1 << bit)}, device_id_type=MESH,
+            )
+            c.start()
+            sent.append(c)
+            new.append(c)
+        for c in new:
+            c.wait_recv()
+        held = held + [k | (1 << bit) for k in held]
+    chain_to(4, 4)
+    for k in range(n):
+        sg_ref[k * piece : (k + 1) * piece] = gathered[k].astype(F32)
+    if line:
+        for c in chains:
+            for p in range(2):
+                c.close(p)
+    half = d // 2
+    for i, ref in enumerate((wog_ref, wqg_ref)):
+        for p in range(2):
+            value = near[i, p] if line else (wo_ref, wq_ref)[i][p]
+            ref[:, p * half : (p + 1) * half] = value.astype(F32)
+    for c in pending + sent:
+        c.wait_send()
+    scatter.drain()
+
+
+def last(wo, wq, dq, kv, shared, h, x, gain, mixed, qb, parts, order):
+    n, dp = lax.axis_size("tensor"), lax.axis_size("dp")
+    line = dp == 4
+    tokens, d = x.shape
+    qw = wo.shape[1]
+    flat = parts[0] + parts[1]
+    piece, width = d // n, kv.shape[1]
+    size = 2 * d + qb.shape[1] + width // 2
+    bits = n.bit_length() - 1
+    dbits = dp.bit_length() - 1
+    dma = pltpu.SemaphoreType.DMA
+    vmem = pl.BlockSpec(memory_space=pltpu.VMEM)
+    item = (2, 2, qw, d // 2)
+    return pl.pallas_call(
+        functools.partial(last_kernel, order=order, line=line, eps_rows=tokens // 2),
+        in_specs=[vmem] * (10 + len(flat)),
+        out_specs=[vmem] * 5,
+        out_shape=[
+            jax.ShapeDtypeStruct((qw, d), F32),
+            jax.ShapeDtypeStruct((qw, d), F32),
+            jax.ShapeDtypeStruct((tokens, d), F32),
+            jax.ShapeDtypeStruct((1, size), F32),
+            jax.ShapeDtypeStruct((d, width), F32),
+        ],
+        scratch_shapes=[
+            pltpu.VMEM((d, n * qw), BF),
+            pltpu.VMEM(item, BF),
+            pltpu.VMEM(item, BF),
+            pltpu.VMEM((d, width), F32),
+            pltpu.VMEM((n, piece, width), BF),
+            pltpu.VMEM((n - 1, piece, width), BF),
+            pltpu.VMEM((dbits, piece, width), F32),
+            pltpu.VMEM((dbits, piece, width), F32),
+            pltpu.VMEM((piece, width), F32),
+            pltpu.VMEM((n, piece, width), BF),
+            pltpu.VMEM((bits + dbits, 1, size), F32),
+            pltpu.VMEM((bits + dbits, 1, size), F32),
+            dma((2, 2, 3, 2)), dma((n,)), dma((n,)), dma((2, dbits)), dma((2, n)), dma((2, bits + dbits)),
+        ],
+        compiler_params=pltpu.CompilerParams(
+            collective_id=4, has_side_effects=True, vmem_limit_bytes=60 * MIB
+        ),
+        cost_estimate=pl.CostEstimate(flops=1000, bytes_accessed=MIB, transcendentals=0),
+    )(wo, wq, dq, kv, shared, h, x, gain, mixed, qb, *flat)
+
+
+def mlp_kernel(x_ref, cot_ref, up_ref, bias_ref, down_ref, gn_ref, gb_ref, xg_ref, act_ref, gr_ref, *rest, orders):
+    n, seqs, span, d = cot_ref.shape
+    (ff_ref, x_s, c_s, act_s, gr_s, ff_s, send, recv, gsend, grecv, ssem, rsem, load, own, out) = rest
+    hidden = up_ref.shape[1]
+    tile, wide = min(512, hidden), 512
+    me = lax.axis_index("tensor")
+    paths = [list(o) + [0] for o in orders]
+    bits_of = [[0] + list(o)[::-1] for o in orders]
+    work = [Scatter(bits_of[p], send.at[p], recv.at[p], ssem.at[p], rsem.at[p], shared=2) for p in range(seqs)]
+
+    def last_bit(p, k):
+        return max((b for b in paths[p] if k >> b & 1), key=paths[p].index)
+
+    def hop(p, k, bit):
+        to = k | (1 << bit)
+        src = x_ref.at[p] if k == 0 else xg_ref.at[me ^ k, p]
+        return pltpu.make_async_remote_copy(
+            src_ref=src, dst_ref=xg_ref.at[me ^ k, p], send_sem=gsend.at[p, to], recv_sem=grecv.at[p, to],
+            device_id={"tensor": me ^ (1 << bit)}, device_id_type=MESH,
+        )
+
+    def arrival(p, k):
+        bit = last_bit(p, k)
+        return pltpu.make_async_remote_copy(
+            src_ref=x_ref.at[p], dst_ref=xg_ref.at[me ^ k, p], send_sem=gsend.at[p, k], recv_sem=grecv.at[p, k],
+            device_id={"tensor": me ^ (1 << bit)}, device_id_type=MESH,
+        )
+
+    def slots_at(p, t):
+        if t == 0:
+            return [0]
+        return sorted((k for k in range(2, n, 2) if last_bit(p, k) == paths[p][t - 1]), reverse=True)
+
+    steps = len(paths[0])
+    units = [(p, k) for t in range(steps) for i in range(len(slots_at(0, t))) for p in range(seqs) for k in [slots_at(p, t)[i]]]
+
+    def cot_loads(u):
+        p, e = units[u]
+        return [
+            pltpu.make_async_copy(
+                cot_ref.at[me ^ (e + j), p], c_s.at[u % 2, j * span : (j + 1) * span], load.at[u % 2, j]
+            )
+            for j in range(2)
+        ]
+
+    def x_loads(u):
+        p, e = units[u]
+        return [
+            pltpu.make_async_copy(
+                x_ref.at[p] if e + j == 0 else xg_ref.at[me ^ (e + j), p],
+                x_s.at[j * span : (j + 1) * span], load.at[2, j],
+            )
+            for j in range(2)
+        ]
+
+    def hidden_stores(u):
+        p, e = units[u]
+        return [
+            pltpu.make_async_copy(
+                buf.at[j * span : (j + 1) * span], ref.at[me ^ (e + j), p], out.at[i, j]
+            )
+            for i, (buf, ref) in enumerate(((act_s, act_ref), (gr_s, gr_ref)))
+            for j in range(2)
+        ]
+
+    def ff_stores(u):
+        p, e = units[u]
+        return [
+            pltpu.make_async_copy(ff_s.at[j * span : (j + 1) * span], ff_ref.at[p, e + j], out.at[2, j])
+            for j in range(2)
+        ]
+
+    waiting = []
+
+    def run(u):
+        p, e = units[u]
+        for j in range(2):
+            if e + j and (e + j) % 2 == 1:
+                arrival(p, e + j).wait_recv()
+        for c in x_loads(u):
+            c.start()
+        if u + 1 < len(units):
+            for c in cot_loads(u + 1):
+                c.start()
+        if u:
+            for c in hidden_stores(u - 1):
+                c.wait()
+        for c in x_loads(u) + cot_loads(u):
+            c.wait()
+
+        @pl.loop(0, hidden // tile)
+        def _(i):
+            here = pl.ds(pl.multiple_of(i * tile, tile), tile)
+            raised = dot(x_s[...], up_ref[:, here]) + bias_ref[:, here]
+            square = raised * raised
+            th = jnp.tanh(0.7978845608028654 * raised * (1.0 + 0.044715 * square))
+            act_s[:, here] = (0.5 * raised * (1.0 + th)).astype(BF)
+            slope = 0.5 * (1.0 + th) + 0.5 * raised * (1.0 - th * th) * (
+                0.7978845608028654 * (1.0 + 3 * 0.044715 * square)
+            )
+            gr = (dot_nt(c_s[u % 2], down_ref[here, :]) * slope).astype(BF)
+            gr_s[:, here] = gr
+            gb = jnp.sum(gr.astype(F32), axis=0, keepdims=True)
+            gb_ref[:, here] = gb if u == 0 else gb_ref[:, here] + gb
+
+        for c in hidden_stores(u):
+            c.start()
+        while waiting:
+            q, k = waiting.pop(0)
+            work[q].forward(k)
+        if u:
+            for c in ff_stores(u - 1):
+                c.wait()
+        odd, even = work[p].claim(e + 1), work[p].claim(e)
+
+        @pl.loop(0, d // wide)
+        def _(i):
+            here = pl.ds(pl.multiple_of(i * wide, wide), wide)
+            gn = dot_nt(gr_s[...], up_ref[here, :]).astype(BF)
+            even[:, here] = gn[:span]
+            odd[:, here] = gn[span:]
+            ff_s[:, here] = dot(act_s[...], down_ref[:, here]).astype(BF)
+
+        work[p].launch(e + 1)
+        for c in ff_stores(u):
+            c.start()
+
+    keep = [pltpu.make_async_copy(x_ref.at[p], xg_ref.at[me, p], own.at[p]) for p in range(seqs)]
+    greet(range(steps))
+    for p in range(seqs):
+        hop(p, 0, paths[p][0]).start()
+    for p in range(seqs):
+        hop(p, 0, 0).start()
+        keep[p].start()
+    for c in cot_loads(0):
+        c.start()
+    sent = [(p, 0, b) for p in range(seqs) for b in (paths[p][0], 0)]
+    u = 0
+    for t in range(steps):
+        while u < len(units) and units[u][1] in slots_at(units[u][0], t):
+            if t and units[u][0] == 0:
+                for p in range(seqs):
+                    k = units[u + p][1]
+                    arrival(p, k).wait_recv()
+                    if t < steps - 1:
+                        hop(p, k, paths[p][t]).start()
+                        sent.append((p, k, paths[p][t]))
+                    hop(p, k, 0).start()
+                    sent.append((p, k, 0))
+            run(u)
+            p, k = units[u]
+            if work[p].stage(k) == 1:
+                waiting.append((p, k))
+            u += 1
+        if 0 < t < steps - 1:
+            for p in range(seqs):
+                for before in range(t - 1, -1, -1):
+                    for k in slots_at(p, before):
+                        hop(p, k, paths[p][t]).start()
+                        sent.append((p, k, paths[p][t]))
+    for p, k in waiting:
+        work[p].forward(k)
+    for i in range(2, steps):
+        for at in range(n // 2 - 1):
+            for p in range(seqs):
+                k = scatter_order(bits_of[p])[at]
+                if work[p].stage(k) == i:
+                    work[p].forward(k)
+    for p in range(seqs):
+        gn_ref[p] = work[p].total(0)
+    for c in hidden_stores(len(units) - 1) + ff_stores(len(units) - 1) + keep:
+        c.wait()
+    for p, k, b in sent:
+        hop(p, k, b).wait_send()
+    for p in range(seqs):
+        work[p].drain()
+
+
+def mlp(normed, cot, up, bias, down, orders):
+    n, seqs, span, d = cot.shape
+    ff = up.shape[1]
+    dma = pltpu.SemaphoreType.DMA
+    hbm, vmem = pl.BlockSpec(memory_space=pl.ANY), pl.BlockSpec(memory_space=pltpu.VMEM)
+    return pl.pallas_call(
+        functools.partial(mlp_kernel, orders=orders),
+        in_specs=[hbm, hbm, vmem, vmem, vmem],
+        out_specs=[vmem, vmem, hbm, hbm, hbm, hbm],
+        out_shape=[
+            jax.ShapeDtypeStruct((seqs, span, d), F32),
+            jax.ShapeDtypeStruct((1, ff), F32),
+            jax.ShapeDtypeStruct((n, seqs, span, d), BF),
+            jax.ShapeDtypeStruct((n, seqs, span, ff), BF),
+            jax.ShapeDtypeStruct((n, seqs, span, ff), BF),
+            jax.ShapeDtypeStruct((seqs, n, span, d), BF),
+        ],
+        scratch_shapes=[
+            pltpu.VMEM((2 * span, d), BF),
+            pltpu.VMEM((2, 2 * span, d), BF),
+            pltpu.VMEM((2 * span, ff), BF),
+            pltpu.VMEM((2 * span, ff), BF),
+            pltpu.VMEM((2 * span, d), BF),
+            pltpu.VMEM((seqs, n // 2 + 2, span, d), BF),
+            pltpu.VMEM((seqs, n - 1, span, d), BF),
+            dma((seqs, n)), dma((seqs, n)), dma((seqs, n)), dma((seqs, n)), dma((3, 2)), dma((seqs,)), dma((3, 2)),
+        ],
+        compiler_params=pltpu.CompilerParams(collective_id=2, has_side_effects=True, vmem_limit_bytes=60 * MIB),
         cost_estimate=pl.CostEstimate(
-            flops=4 * tokens * n * qw * d, bytes_accessed=64 * MIB, transcendentals=0
+            flops=8 * n * seqs * span * d * ff, bytes_accessed=100 * MIB, transcendentals=n * seqs * span * ff
         ),
-    )(a, gm, dq, h, dkv)
-
-
-def mlp_kernel(xa_ref, xb_ref, ca_ref, cb_ref, up_ref, bias_ref, down_ref,
-               ffa_ref, ffb_ref, gna_ref, gnb_ref, act_ref, gr_ref, gb_ref, x_s, c_s, ff_s, gn_s):
-    step = pl.program_id(0)
-    half = xa_ref.shape[0]
-
-    @pl.when(step == 0)
-    def _():
-        x_s[:half] = xa_ref[...]
-        x_s[half:] = xb_ref[...]
-        c_s[:half] = ca_ref[...]
-        c_s[half:] = cb_ref[...]
-
-    raised = dot(x_s[...], up_ref[...]) + bias_ref[...]
-    square = raised * raised
-    th = jnp.tanh(0.7978845608028654 * raised * (1.0 + 0.044715 * square))
-    act = (0.5 * raised * (1.0 + th)).astype(BF)
-    act_ref[...] = act
-    ff = dot(act, down_ref[...])
-    slope = 0.5 * (1.0 + th) + 0.5 * raised * (1.0 - th * th) * (
-        0.7978845608028654 * (1.0 + 3 * 0.044715 * square)
-    )
-    gr32 = dot_nt(c_s[...], down_ref[...]) * slope
-    gr = gr32.astype(BF)
-    gr_ref[...] = gr
-    gb_ref[...] = jnp.sum(gr.astype(F32), axis=0, keepdims=True)
-    gn = dot_nt(gr, up_ref[...])
-
-    @pl.when(step == 0)
-    def _():
-        ff_s[...] = ff
-        gn_s[...] = gn
-
-    @pl.when(step != 0)
-    def _():
-        ff_s[...] += ff
-        gn_s[...] += gn
-
-    @pl.when(step == pl.num_programs(0) - 1)
-    def _():
-        ffa_ref[...] = ff_s[:half].astype(BF)
-        ffb_ref[...] = ff_s[half:].astype(BF)
-        gna_ref[...] = gn_s[:half].astype(BF)
-        gnb_ref[...] = gn_s[half:].astype(BF)
-
-
-def mlp_unit(xa, xb, ca, cb, up, bias, down):
-    half, d = xa.shape
-    ff = up.shape[1]
-    tile = min(512, ff)
-    tokens = 2 * half
-    whole = pl.BlockSpec((half, d), lambda j: (0, 0))
+    )(normed, cot, up, bias, down)
+
+
+class ScatterParts(Scatter):
+    def copy(self, k):
+        if self.stage(k):
+            return super().copy(k)
+        return pltpu.make_async_remote_copy(
+            src_ref=self.source.at[k],
+            dst_ref=self.recv.at[k - 1],
+            send_sem=self.send_sem.at[k],
+            recv_sem=self.recv_sem.at[k],
+            device_id={"tensor": self.me ^ (1 << self.bits[0])},
+            device_id_type=MESH,
+        )
+
+    def place(self, k):
+        return k // 2 if k % 2 == 0 else -k
+
+
+def mlp_grads_kernel(gr_ref, x_ref, part_ref, down_ref, up_ref, ff_ref, sum_ref,
+                     a_s, b_s, acc, send, recv, far, piece, ssem, rsem, load, own, zsem, psem, *, orders, line):
+    seqs, n = part_ref.shape[:2]
+    bits_of = [[0] + list(o)[::-1] for o in orders]
+    work = []
+    for p in range(seqs):
+        w = ScatterParts(bits_of[p], send.at[p], recv.at[p], ssem.at[p], rsem.at[p])
+        w.source = part_ref.at[p]
+        work.append(w)
+    evens = [
+        pltpu.make_async_copy(part_ref.at[p, k], send.at[p, k // 2], own.at[p, k // 2])
+        for p in range(seqs) for k in range(0, n, 2)
+    ]
+    wide = acc.shape[0]
+    tile = min(256, wide)
+    steps = n
+
+    def loads(u):
+        return [
+            pltpu.make_async_copy(x_ref.at[u], a_s.at[u % 2], load.at[u % 2, 0]),
+            pltpu.make_async_copy(gr_ref.at[u], b_s.at[u % 2], load.at[u % 2, 1]),
+        ]
+
+    greet(range(len(bits_of[0])), line)
+    chain = Line(down_ref, sum_ref, far, zsem)
+    pieces = down_ref.shape[0]
+    for k in range(n - 1, 0, -2):
+        for p in range(seqs):
+            work[p].launch(k)
+    if line:
+        for i in range(pieces):
+            chain.start(i)
+
+    def own_piece(i):
+        def value():
+            c = pltpu.make_async_copy(down_ref.at[i], piece, psem)
+            c.start()
+            c.wait()
+            return piece[...]
+
+        return value
+
+    ahead = [0, 0]
+
+    def chain_to(middles):
+        while line and ahead[0] < min(middles, pieces):
+            chain.middle(ahead[0], own_piece(ahead[0]))
+            ahead[0] += 1
+            if ahead[0] > 1:
+                chain.back(ahead[0] - 2)
+
+    for c in loads(0) + evens:
+        c.start()
+
+    def forwards(i):
+        for at in range(n // 2 - 1):
+            for p in range(seqs):
+                k = scatter_order(bits_of[p])[at]
+                if work[p].stage(k) == i:
+                    work[p].forward(k)
+
+    stages = len(bits_of[0])
+    when = {(i - 1) * (steps // (stages - 1)) + 1: i for i in range(1, stages)} if stages > 1 else {}
+    when = {min(u + 2 * (i - 1), steps - 1): i for u, i in when.items()}
+    for u in range(steps):
+        if u + 1 < steps:
+            for c in loads(u + 1):
+                c.start()
+        for c in loads(u):
+            c.wait()
+
+        @pl.loop(0, wide // tile)
+        def _(i, u=u):
+            here = pl.ds(pl.multiple_of(i * tile, tile), tile)
+            term = dot_tn(a_s[u % 2, :, here], b_s[u % 2])
+            if u == 0:
+                acc[here, :] = term
+            elif u < n - 1:
+                acc[here, :] += term
+            else:
+                up_ref[here, :] = (acc[here, :] + term).astype(BF)
+
+        if u == 0:
+            for c in evens:
+                c.wait()
+        if u in when:
+            forwards(when[u])
+        chain_to((u + 1) // 3)
+    chain_to(5)
+    for p in range(seqs):
+        ff_ref[p] = work[p].total(0)
+        work[p].drain()
+    if line:
+        chain_to(pieces)
+        chain.back(pieces - 1)
+        for i in range(pieces):
+            chain.close(i)
+
+
+def weight_grad_kernel(a_ref, b_ref, o_ref, acc):
+    step, last = pl.program_id(0), pl.num_programs(0) - 1
+    wide = acc.shape[0]
+    tile = min(256, wide)
+
+    @pl.loop(0, wide // tile)
+    def _(i):
+        here = pl.ds(pl.multiple_of(i * tile, tile), tile)
+        term = dot_tn(a_ref[:, here], b_ref[...])
+
+        @pl.when(step == 0)
+        def _():
+            acc[here, :] = term
+
+        @pl.when((step > 0) & (step < last))
+        def _():
+            acc[here, :] += term
+
+        @pl.when(step == last)
+        def _():
+            o_ref[here, :] = (acc[here, :] + term).astype(BF)
+
+
+def weight_grad(a, b):
+    tokens, wide = a.shape
+    cols = b.shape[1]
+    tile = min(512, tokens // 2)
     return pl.pallas_call(
-        mlp_kernel,
-        grid=(ff // tile,),
-        in_specs=[
-            whole, whole, whole, whole,
-            pl.BlockSpec((d, tile), lambda j: (0, j)),
-            pl.BlockSpec((1, tile), lambda j: (0, j)),
-            pl.BlockSpec((tile, d), lambda j: (j, 0)),
+        weight_grad_kernel,
+        grid=(tokens // tile,),
+        in_specs=[pl.BlockSpec((tile, wide), lambda i: (i, 0)), pl.BlockSpec((tile, cols), lambda i: (i, 0))],
+        out_specs=pl.BlockSpec((wide, cols), lambda i: (0, 0)),
+        out_shape=jax.ShapeDtypeStruct((wide, cols), BF),
+        scratch_shapes=[pltpu.VMEM((wide, cols), F32)],
+        compiler_params=pltpu.CompilerParams(vmem_limit_bytes=40 * MIB),
+        cost_estimate=pl.CostEstimate(flops=1000, bytes_accessed=MIB, transcendentals=0),
+    )(a, b)
+
+
+def mlp_grads(gr, x, parts, down, orders):
+    line = lax.axis_size("dp") == 4
+    seqs, n, span, d = parts.shape
+    tokens, cols = seqs * span, gr.shape[-1]
+    rows = down.shape[0] // 8
+    down = down.reshape(8, rows, d)
+    wait = down.shape if line else (1, 16, 128)
+    dma = pltpu.SemaphoreType.DMA
+    hbm, vmem = pl.BlockSpec(memory_space=pl.ANY), pl.BlockSpec(memory_space=pltpu.VMEM)
+    flat = lambda v: v.reshape(n, tokens, v.shape[-1])
+    up, ff, total = pl.pallas_call(
+        functools.partial(mlp_grads_kernel, orders=orders, line=line),
+        in_specs=[hbm] * 4,
+        out_specs=[vmem] * 3,
+        out_shape=[
+            jax.ShapeDtypeStruct((d, cols), BF),
+            jax.ShapeDtypeStruct((seqs, span, d), F32),
+            jax.ShapeDtypeStruct(wait, BF),
         ],
-        out_specs=[
-            whole, whole, whole, whole,
-            pl.BlockSpec((tokens, tile), lambda j: (0, j)),
-            pl.BlockSpec((tokens, tile), lambda j: (0, j)),
-            pl.BlockSpec((1, tile), lambda j: (0, j)),
+        scratch_shapes=[
+            pltpu.VMEM((2, tokens, d), BF),
+            pltpu.VMEM((2, tokens, cols), BF),
+            pltpu.VMEM((d, cols), F32),
+            pltpu.VMEM((seqs, n // 2, span, d), BF),
+            pltpu.VMEM((seqs, n - 1, span, d), BF),
+            pltpu.VMEM(wait, BF),
+            pltpu.VMEM((rows, d), BF),
+            dma((seqs, n)), dma((seqs, n)), dma((2, 2)), dma((seqs, n // 2)), dma((2, 3, 8)), dma,
         ],
-        out_shape=[jax.ShapeDtypeStruct((half, d), BF)] * 4
-        + [jax.ShapeDtypeStruct((tokens, ff), BF)] * 2
-        + [jax.ShapeDtypeStruct((1, ff), F32)],
-        scratch_shapes=[
-            pltpu.VMEM((tokens, d), BF),
-            pltpu.VMEM((tokens, d), BF),
-            pltpu.VMEM((tokens, d), F32),
-            pltpu.VMEM((tokens, d), F32),
-        ],
-        compiler_params=pltpu.CompilerParams(vmem_limit_bytes=56 * MIB),
+        compiler_params=pltpu.CompilerParams(collective_id=3, has_side_effects=True, vmem_limit_bytes=60 * MIB),
         cost_estimate=pl.CostEstimate(
-            flops=8 * tokens * d * ff, bytes_accessed=20 * MIB, transcendentals=tokens * ff
+            flops=1000, bytes_accessed=256 * MIB, transcendentals=0
         ),
-    )(xa, xb, ca, cb, up, bias, down)
+    )(flat(gr), flat(x), parts, down)
+    down = down.reshape(8 * rows, d)
+    return up, ff, total.reshape(down.shape) if line else lax.psum(down, "dp")
 
 
 def norm_parts(values):
@@ -721,7 +1141,7 @@
     tokens = seqs * span
 
     x32 = inputs.astype(F32)
-    unit1, scale1 = norm_parts(x32)
+    unit1, _ = norm_parts(x32)
     hidden = (unit1 * attn_gain + attn_shift).astype(BF)
     h2 = hidden.reshape(tokens, d)
     shared = dot(h2, shared_matrix)
@@ -758,29 +1178,14 @@
     mixed, normed = mixed.reshape(seqs, span, d), normed.reshape(seqs, span, d)
     unit2, scale2 = norm_parts(mixed)
 
-    cot_slots = [gather_slots(cotangent[r], paths[r % 2]) for r in range(seqs)]
-    normed_slots = [gather_slots(normed[r], paths[r % 2]) for r in range(seqs)]
-    ff_slots = [[None] * n for _ in range(seqs)]
-    gn_slots = [[None] * n for _ in range(seqs)]
-    acts, grs, xs, cs = [], [], [], []
-    up_bias_part = jnp.zeros((1, up_bias.shape[0]), F32)
-    for k in range(0, n, 2):
-        for r in range(seqs):
-            xa, xb, ca, cb = normed_slots[r][k], normed_slots[r][k + 1], cot_slots[r][k], cot_slots[r][k + 1]
-            ffa, ffb, gna, gnb, act, gr, gb = mlp_unit(
-                xa, xb, ca, cb, expansion_weights, up_bias[None], down_matrix
-            )
-            ff_slots[r][k], ff_slots[r][k + 1] = ffa, ffb
-            gn_slots[r][k], gn_slots[r][k + 1] = gna, gnb
-            acts.append(act)
-            grs.append(gr)
-            xs.append([xa, xb])
-            cs.append([ca, cb])
-            up_bias_part = up_bias_part + gb
-    grad_normed = jnp.stack([scatter_slots(gn_slots[r], paths[r % 2]) for r in range(seqs)])
-    down_gradient = weight_grad([[a] for a in acts], cs)
-    up_gradient = weight_grad(xs, [[g] for g in grs])
-    mlp_branch = jnp.stack([scatter_slots(ff_slots[r], paths[r % 2]) for r in range(seqs)])
+    cot_every = lax.all_gather(cotangent, "tensor")
+    grad_normed, up_bias_part, normed_every, acts, grs, ff_parts = mlp(
+        normed, cot_every, expansion_weights, up_bias[None], down_matrix, paths
+    )
+    every = lambda v: v.reshape(n * tokens, v.shape[-1])
+    down_part = weight_grad(every(acts), every(cot_every))
+    up_part, mlp_branch, down_gradient = mlp_grads(grs, normed_every, ff_parts, down_part, paths)
+    up_gradient = lax.psum(up_part, "dp")
     block_out = (mixed + mlp_branch + down_bias).astype(BF)
 
     cot_wide = cotangent.astype(F32)
@@ -795,47 +1200,31 @@
     dq2 = dq.reshape(tokens, n * qw)
 
     dkv = jnp.concatenate([dk * LN2, dv], axis=-1).astype(BF).reshape(seqs, n, span, 2 * hd).swapaxes(0, 1)
-    output_gradient, query_gradient, dkv_own = attention_grads(
-        a2, gm2, dq2, h2, dkv.reshape(n, tokens, 2 * hd), paths
+    wo_own, wq_own, dkv_own = attention_grads(a2, gm2, dq2, h2, dkv.reshape(n, tokens, 2 * hd), paths)
+    query_bias_part = xor_order(jnp.sum(dq2.astype(F32), axis=0).reshape(n, qw), me).reshape(-1)
+    ff = up_bias.shape[0]
+    up_bias_every = lax.dynamic_update_slice_in_dim(jnp.zeros((n * ff,), F32), up_bias_part[0], me * ff, 0)
+    vector = jnp.concatenate(
+        [query_bias_part, mlp_gain_part, mlp_shift_part, jnp.sum(grad_mixed, axis=(0, 1)),
+         jnp.sum(cot_wide, axis=(0, 1)), up_bias_every]
+    )[None]
+    output_gradient, query_gradient, input_grad, late, shared_grad = last(
+        wo_own, wq_own, dq2, dkv_own, shared_matrix, h2, inputs.reshape(tokens, d), attn_gain[None],
+        grad_mixed.reshape(tokens, d), vector, wq, paths[0],
     )
+    input_grad = input_grad.reshape(seqs, span, d)
     if lax.axis_size("dp") != 4:
-        output_gradient, query_gradient = lax.psum((output_gradient.astype(BF), query_gradient.astype(BF)), "dp")
-    dkv_own = dkv_own.reshape(seqs, span, 2 * hd)
-
-    (grad_hidden,) = slot_product(
-        dh_kernel, [dq2, dkv_own.reshape(tokens, 2 * hd)], [shared_matrix], wq, [like(F32, d)], (d, n * qw)
-    )
-    grad_hidden = grad_hidden.reshape(seqs, span, d)
-    back1, attn_gain_part, attn_shift_part = norm_back(unit1, scale1, attn_gain, grad_hidden)
-    input_grad = grad_mixed + back1
-    shared_part = dot_tn(h2, dkv_own.reshape(tokens, 2 * hd))
-    value_bias_part = jnp.sum(dkv_own[..., hd:].astype(F32), axis=(0, 1))
-    query_bias_part = xor_order(jnp.sum(dq2.astype(F32), axis=0).reshape(n, qw), me).reshape(-1)
-
-    everywhere = ("tensor", "dp")
-    down_gradient, up_gradient = lax.psum((down_gradient, up_gradient), "dp")
-    up_bias_grad = sum_all(up_bias_part, ("dp",))[0]
-    early = sum_all(
-        jnp.stack([mlp_gain_part, mlp_shift_part, jnp.sum(grad_mixed, axis=(0, 1)), jnp.sum(cot_wide, axis=(0, 1))]),
-        everywhere,
-    )
-    mlp_gain_grad, mlp_shift_grad, output_bias_grad, down_bias_grad = early
-    late = sum_all(
-        jnp.concatenate([attn_gain_part, attn_shift_part, query_bias_part, value_bias_part])[None], everywhere
-    )[0]
-    attn_gain_grad, attn_shift_grad = late[:d], late[d : 2 * d]
-    query_bias_grad = lax.dynamic_slice_in_dim(late, 2 * d + me * qw, qw, 0)
-    value_bias_grad = late[2 * d + n * qw :]
-    piece = d // n
-    shared_slots = [
-        lax.dynamic_slice_in_dim(shared_part, (me ^ k) * piece, piece, 0).astype(BF) for k in range(n)
-    ]
-    shared_sum = sum_all(scatter_slots(shared_slots, paths[0]), ("dp",)).astype(BF)
-    shared_slots = jnp.concatenate(gather_slots(shared_sum, paths[0]), axis=0)
-    shared_grad = xor_order(shared_slots.reshape(n, piece, 2 * hd), me).reshape(d, 2 * hd).astype(F32)
-    output_gradient, query_gradient, up_gradient, down_gradient = (
-        g.astype(F32) for g in (output_gradient, query_gradient.T, up_gradient, down_gradient)
-    )
+        output_gradient, query_gradient = (
+            g.astype(F32) for g in lax.psum((output_gradient.astype(BF), query_gradient.astype(BF)), "dp")
+        )
+    late = after(late, up_gradient)[0]
+    ends = [d, 2 * d, 2 * d + hd, 2 * d + hd + n * qw]
+    ends += [ends[-1] + d * (i + 1) for i in range(4)]
+    (attn_gain_grad, attn_shift_grad, value_bias_grad, query_bias_all, mlp_gain_grad, mlp_shift_grad,
+     output_bias_grad, down_bias_grad, up_bias_all) = jnp.split(late, ends)
+    query_bias_grad = lax.dynamic_slice_in_dim(query_bias_all, me * qw, qw, 0)
+    up_bias_grad = lax.dynamic_slice_in_dim(up_bias_all, me * ff, ff, 0)
+    query_gradient, up_gradient, down_gradient = query_gradient.T, up_gradient.astype(F32), down_gradient.astype(F32)
     return (
         block_out, input_grad, attn_gain_grad, attn_shift_grad, query_gradient, query_bias_grad, shared_grad,
         value_bias_grad, output_gradient, output_bias_grad, mlp_gain_grad, mlp_shift_grad, up_gradient, up_bias_grad,

time: 965 us -> 945 us (0.979)
  Pallas kernels: 441 us -> 675 us
  waiting for transfers between devices: 252 us -> 123 us
  starting transfers between devices: 108 us -> 22.2 us
  other arithmetic: 69.9 us -> 37.3 us
    pallas_call x11 -> x6, Pallas kernels: 375 us -> 619 us  [the longest x1 201 us: mlp(): pl.pallas_call(functools.partial(mlp_kernel, orders=orders), in_specs=[hb...]
    ppermute x126 -> x42, waiting for transfers between devices: 252 us -> 122 us  [swap(): return lax.ppermute(x, axis, [(i, i ^ 1 << bit) for i in range(n)])]
    ppermute x126 -> x42, starting transfers between devices: 107 us -> 22.1 us  [swap(): return lax.ppermute(x, axis, [(i, i ^ 1 << bit) for i in range(n)])]
    convert_element_type x17 -> x2, other arithmetic: 29.1 us -> 13.4 us  [the longest x1 6.79 us: body(): up_gradient.astype(F32)]
    pallas_call x4 -> x3, Pallas kernels: 40.7 us -> 29.6 us  [slot_product(): pl.pallas_call(kernel, grid=(2,), in_specs=[flow(a) for a in tiled] + [st...]
    unnamed x305 -> x172, local copies, waits for them, and re-layouts: 48.8 us -> 44.4 us
  transfers between devices with their start and end apart: 127 -> 44, of which waited for: 35 -> 12; matrix products, arithmetic and copies ran while one was open for 10% -> 6% of each run, Pallas kernels for 46% -> 32%
where the time goes in v3:
time: 945 us; the launch traced here: 936 us
  Pallas kernels  675 us (71%)
  waiting for transfers between devices  123 us (13%)
  local copies, waits for them, and re-layouts  63.2 us (7%)
  other arithmetic  37.3 us (4%)
  starting transfers between devices  22.2 us (2%)
  between operations  15.2 us (2%)
    pallas_call x1, Pallas kernels, mlp(): pl.pallas_call(functools.partial(mlp_kernel, orders=orders), in_specs=[hb...  201 us
    pallas_call x1, Pallas kernels, mlp_grads(): pl.pallas_call(functools.partial(mlp_grads_kernel, orders=orders, line=li...  138 us
    pallas_call x1, Pallas kernels, attention_grads(): pl.pallas_call(functools.partial(attention_grads_kernel, orders=orders, q...  126 us
    ppermute x42, waiting for transfers between devices, swap(): return lax.ppermute(x, axis, [(i, i ^ 1 << bit) for i in range(n)])  122 us
    pallas_call x1, Pallas kernels, last(): pl.pallas_call(functools.partial(last_kernel, order=order, line=line, eps...  120 us
    unnamed x172, local copies, waits for them, and re-layouts  44.4 us
    pallas_call x1, Pallas kernels, weight_grad(): pl.pallas_call(weight_grad_kernel, grid=(tokens // tile,), in_specs=[pl.B...  31.8 us
    pallas_call x3, Pallas kernels, slot_product(): pl.pallas_call(kernel, grid=(2,), in_specs=[flow(a) for a in tiled] + [st...  29.6 us
  transfers between devices with their start and end apart: 44, of which 12 were waited for; matrix products, arithmetic and copies ran while one was open for 6% of the time, Pallas kernels for 32%

profile of v3, /device:TPU:0, one launch (start us, length us, event | category | flops | bytes accessed | tf_op | source)
XLA Modules:
  0.0 936.2 jit_solution(643588293896587246)
XLA Ops:
  8.5 2.6 collective-permute-start.1
  11.1 1.5 collective-permute-start.3
  12.6 1.9 convert_reduce_fusion.1
  22.7 1.9 collective-permute-start.8
  25.8 1.5 collective-permute-start.24
  27.8 1.6 collective-permute-start.10
  29.4 7.9 collective-permute-done.22
  37.4 3.1 collective-permute-done.24
  40.5 19.2 %collective-permute-done.8.refs_2_ = bf16[1024,256]{1,0:T(8,128)(2,1)S(1)} collective-permute-done((bf16[1024,256]{1,0:T(8,128)(2,1)S(1)}, bf16[1024,256]{1,0:T(8,128)(2,1)S(1)}, u32[]{:S(2)}, u32[]{:S(2)}) %collective-permute-start.8) | collective-permute-done | bytes 524320 | tf_op jit(solution)/shard_map/ppermute | solution.py:33
  59.7 3.3 collective-permute-done.17.refs_12_
  63.8 1.9 reshape.202.dock_ref
  65.7 10.0 %collective-permute-done.10.refs_4_ = bf16[1024,256]{1,0:T(8,128)(2,1)} collective-permute-done((bf16[1024,256]{1,0:T(8,128)(2,1)S(1)}, bf16[1024,256]{1,0:T(8,128)(2,1)}, u32[]{:S(2)}, u32[]{:S(2)}) %collective-permute-start.10) | collective-permute-done | bytes 524320 | tf_op jit(solution)/shard_map/ppermute | solution.py:33
  77.6 1.5 collective-permute-start.31
  79.7 1.7 collective-permute-done.25
  82.1 54.4 %collective-permute-done.26 = bf16[2,256,256]{2,1,0:T(8,128)(2,1)S(1)} collective-permute-done((bf16[2,256,256]{2,1,0:T(8,128)(2,1)}, bf16[2,256,256]{2,1,0:T(8,128)(2,1)S(1)}, u32[]{:S(2)}, u32[]{:S(2)}) %collective-permute-start.26) | collective-permute-done | bytes 262176 | tf_op jit(solution)/shard_map/ppermute | solution.py:33
  137.7 1.8 constant_dynamic-update-slice_fusion.14
  139.4 1.7 constant_dynamic-update-slice_fusion.13
  142.3 18.4 %collective-permute-done.12.refs_6_ = bf16[1024,256]{1,0:T(8,128)(2,1)} collective-permute-done((bf16[1024,256]{1,0:T(8,128)(2,1)}, bf16[1024,256]{1,0:T(8,128)(2,1)}, u32[]{:S(2)}, u32[]{:S(2)}) %collective-permute-start.12) | collective-permute-done | bytes 524320 | tf_op jit(solution)/shard_map/ppermute | solution.py:33
  161.4 1.7 constant_dynamic-update-slice_fusion.11
  166.7 1.7 collective-permute-start.40
  170.5 3.8 fusion.11
  174.3 2.3 copy.46.vt_ref
  176.5 1.5 copy.48.kt_ref
  178.0 1.9 collective-permute-done.33.refs_6_
  187.3 9.9 %shard_map.297 = bf16[512,2048]{1,0:T(8,128)(2,1)} custom-call(bf16[512,2048]{1,0:T(8,128)(2,1)} %bitcast.99, f32[1,2048]{1,0:T(1,128)S(1)} %constant_dynamic-update-slice_fusion.b_ref, bf16[1024,256]{1,0:T(8,128)(2,1)S(1)} %copy-done.12, bf16[1024,256]{1,0:T(8,128)(2,1)} %collective-permute-done.7.refs_1_, bf16[1024,256]{1,0:T(8,128)(2,1)S(1)} %copy-done.18, ...), custom_call_target="tpu_custom_call" | custom-call | flops 4294967296 | bytes 16777216 | tf_op jit(solution)/shard_map/pallas_call | solution.py:288
  197.2 1.6 copy-done.13
  198.8 11.2 %shard_map.298 = (bf16[2,256,2048]{2,1,0:T(8,128)(2,1)S(1)}, f32[2,8,1,512]{3,2,1,0:T(1,128)S(1)}) custom-call(s32[2]{0:T(128)S(1)} %fusion.9.low_ref, s32[1]{0:T(128)} %bitcast.at_ref, bf16[2,256,2048]{2,1,0:T(8,128)(2,1)S(1)} %bitcast.88, bf16[2,2048,128]{2,1,0:T(8,128)(2,1)S(1)} %copy-done.7, bf16[2,128,2048]{2,1,0:T(8,128)(2,1)S(1)} %copy-done.16, ...), custom_call_target="tpu_custom_call" | custom-call | flops 4294967296 | bytes 8388608 | tf_op jit(solution)/shard_map/pallas_call | solution.py:169
  212.7 10.8 %shard_map.299 = (f32[512,2048]{1,0:T(8,128)}, bf16[512,2048]{1,0:T(8,128)(2,1)}) custom-call(bf16[512,2048]{1,0:T(8,128)(2,1)} %bitcast.86, bf16[512,2048]{1,0:T(8,128)(2,1)} %bitcast.96, f32[1,2048]{1,0:T(1,128)S(1)} %bitcast.92, f32[1,2048]{1,0:T(1,128)S(1)} %bitcast.91, f32[1,2048]{1,0:T(1,128)S(1)} %bitcast.93, bf16[256,1024]{1,0:T(8,128)(2,1)S(1)} %copy-done.25, ...), custom_call_target="tpu_custom_call" | custom-call | flops 4294967296 | bytes 16777216 | tf_op jit(solution)/shard_map/pallas_call | solution.py:288
  223.4 2.5 reduce_sum.111
  225.9 2.7 multiply_reduce_fusion.2
  228.7 201.3 %shard_map.300 = (f32[2,256,2048]{2,1,0:T(8,128)}, f32[1,1024]{1,0:T(1,128)}, bf16[8,2,256,2048]{3,2,1,0:T(8,128)(2,1)}, bf16[8,2,256,1024]{3,2,1,0:T(8,128)(2,1...) custom-call(bf16[2,256,2048]{2,1,0:T(8,128)(2,1)} %bitcast.141, ...), custom_call_target="tpu_custom_call" | custom-call | flops 68719476736 | bytes 104857600 | tf_op jit(solution)/shard_map/pallas_call | solution.py:894
  430.1 3.4 copy-done.3
  433.5 31.8 %shard_map.301 = bf16[1024,2048]{1,0:T(8,128)(2,1)S(1)} custom-call(bf16[4096,1024]{1,0:T(8,128)(2,1)S(1)} %bitcast.85, bf16[4096,2048]{1,0:T(8,128)(2,1)} %bitcast.103), custom_call_target="tpu_custom_call" | custom-call | flops 1000 | bytes 1048576 | tf_op jit(solution)/shard_map/pallas_call | solution.py:1066
  465.3 2.0 copy-done.2
  467.3 138.1 %shard_map.302 = (bf16[2048,1024]{1,0:T(8,128)(2,1)}, f32[2,256,2048]{2,1,0:T(8,128)}, bf16[8,128,2048]{2,1,0:T(8,128)(2,1)}) custom-call(bf16[8,512,1024]{2,1,0:T(8,128)(2,1)} %bitcast.108, bf16[8,512,2048]{2,1,0:T(8,128)(2,1)} %bitcast.104, bf16[2,8,256,2048]{3,2,1,0:T(8,128)(2,1)} %get-tuple-element.45.part_ref, bf16[8,128,2048]{2,1,0:T(8,128)(2,1)} %bitcast.84), custom_call_target="tpu_custom_call" | custom-call | flops 1000 | bytes 268435456 | tf_op jit(solution)/shard_map/pallas_call | solution.py:1088
  605.5 5.8 multiply_reduce_fusion.3
  614.0 5.7 fusion.10
  619.7 1.7 convert_element_type.40
  624.1 8.9 shard_map.303
  633.0 1.6 copy-done.15
  634.6 14.9 %shard_map.304 = (bf16[2,256,2048]{2,1,0:T(8,128)(2,1)S(1)}, f32[2,2048,128]{2,1,0:T(8,128)S(1)}, f32[2,2048,128]{2,1,0:T(8,128)S(1)}) custom-call(s32[2]{0:T(128)S(1)} %fusion.9.low_ref, s32[1]{0:T(128)} %bitcast.at_ref, bf16[2,256,2048]{2,1,0:T(8,128)(2,1)S(1)} %bitcast.89, bf16[2,256,2048]{2,1,0:T(8,128)(2,1)S(1)} %bitcast.90, ...), custom_call_target="tpu_custom_call" | custom-call | flops 1000 | bytes 1048576 | tf_op jit(solution)/shard_map/pallas_call | solution.py:204
  652.3 126.1 %shard_map.305 = (bf16[2,256,1024]{2,1,0:T(8,128)(2,1)}, bf16[2,256,1024]{2,1,0:T(8,128)(2,1)}, bf16[512,256]{1,0:T(8,128)(2,1)}) custom-call(bf16[512,2048]{1,0:T(8,128)(2,1)} %bitcast.87, bf16[512,2048]{1,0:T(8,128)(2,1)} %bitcast.106, bf16[512,2048]{1,0:T(8,128)(2,1)} %bitcast.82, bf16[512,2048]{1,0:T(8,128)(2,1)} %bitcast.100, bf16[8,512,256]{2,1,0:T(8,128)(2,1)} %bitcast.107), custom_call_target="tpu_custom_call" | custom-call | flops 1000 | bytes 1048576 | tf_op jit(solution)/shard_map/pallas_call | solution.py:516
  780.0 120.0 %shard_map.306 = (f32[256,2048]{1,0:T(8,128)}, f32[256,2048]{1,0:T(8,128)}, f32[512,2048]{1,0:T(8,128)}, f32[1,22656]{1,0:T(1,128)}, f32[2048,256]{1,0:T(8,128)}) custom-call(bf16[2,256,1024]{2,1,0:T(8,128)(2,1)} %get-tuple-element.53.wo_ref, bf16[2,256,1024]{2,1,0:T(8,128)(2,1)} %get-tuple-element.54.wq_ref, bf16[512,2048]{1,0:T(8,128)(2,1)} %bitcast.83, ...), custom_call_target="tpu_custom_call" | custom-call | flops 1000 | bytes 1048576 | tf_op jit(solution)/shard_map/pallas_call | solution.py:678
  900.0 2.9 copy.52
  902.9 6.7 bitcast_convert_fusion
  909.6 1.5 shard_map.307
  915.6 6.8 convert_element_type.42
  922.4 2.1 copy.82
  (286 shorter events, 52.2 us)
Async XLA Ops:
  7.2 221.5 %all-gather.3.cloned.1.call-start = ((), (), s32[]{:S(2)}) async-start(), calls=%async_computation.1 | async-start | bytes 18874368 | tf_op jit(solution)/shard_map/all_gather | solution.py:1181
  7.9 901.6 %all-reduce.2.cloned.1.call-start = ((), (), s32[]{:S(2)}) async-start(), calls=%async_computation | async-start | bytes 8388608 | tf_op jit(solution)/shard_map/psum | solution.py:1188
  8.0 14.5 %collective-permute-start = (f32[1,256]{1,0:T(1,128)}, f32[1,256]{1,0:T(1,128)S(1)}, u32[]{:S(2)}, u32[]{:S(2)}) collective-permute-start(f32[1,256]{1,0:T(1,128)} %bitcast.135), channel_id=1, source_target_pairs={{0,1},{1,0},{2,3},{3,2},{4,5},{5,4},{6,7},{7,6},{8,9},{9,8},{10,11... | collective-permute-start | bytes 3080 | tf_op jit(solution)/shard_map/ppermute | solution.py:33
  8.5 12.9 %collective-permute-start.1 = (f32[1,256]{1,0:T(1,128)}, f32[1,256]{1,0:T(1,128)S(1)}, u32[]{:S(2)}, u32[]{:S(2)}) collective-permute-start(f32[1,256]{1,0:T(1,128)} %bitcast.136), channel_id=1, source_target_pairs={{0,2},{1,3},{2,0},{3,1},{4,6},{5,7},{6,4},{7,5},{8,10},{9,11},{10,... | collective-permute-start | bytes 3080 | tf_op jit(solution)/shard_map/ppermute | solution.py:33
  11.1 11.6 %collective-permute-start.3 = (f32[1,256]{1,0:T(1,128)}, f32[1,256]{1,0:T(1,128)S(1)}, u32[]{:S(2)}, u32[]{:S(2)}) collective-permute-start(f32[1,256]{1,0:T(1,128)} %bitcast.137), channel_id=1, source_target_pairs={{0,4},{1,5},{2,6},{3,7},{4,0},{5,1},{6,2},{7,3},{8,12},{9,13},{10,... | collective-permute-start | bytes 3080 | tf_op jit(solution)/shard_map/ppermute | solution.py:33
  19.0 8.8 collective-permute-start.21
  19.3 155.0 %copy-start.9 = (bf16[1024,256]{1,0:T(8,128)(2,1)}, bf16[1024,256]{1,0:T(8,128)(2,1)S(1)}, u32[]{:S(2)}) copy-start(bf16[1024,256]{1,0:T(8,128)(2,1)S(1)} %get-tuple-element.126.refs_8_) | copy-start | bytes 1572868
  19.3 155.0 %copy-start.11 = (bf16[1024,256]{1,0:T(8,128)(2,1)}, bf16[1024,256]{1,0:T(8,128)(2,1)S(1)}, u32[]{:S(2)}) copy-start(bf16[1024,256]{1,0:T(8,128)(2,1)S(1)} %get-tuple-element.127.refs_0_) | copy-start | bytes 1572868
  21.4 3.2 collective-permute-start.2
  22.0 3.6 collective-permute-start.5
  22.5 14.8 %collective-permute-start.22 = (bf16[2,256,256]{2,1,0:T(8,128)(2,1)S(1)}, bf16[2,256,256]{2,1,0:T(8,128)(2,1)}, u32[]{:S(2)}, u32[]{:S(2)}) collective-permute-start(bf16[2,256,256]{2,1,0:T(8,128)(2,1)S(1)} %get-tuple-element.128), channel_id=1, source_target_pairs={{0,2},{1,3},{2,0},{3,1},{4,6},{5,7},{6,4},{7,5},{8,10},{9,11},{10,... | collective-permute-start | bytes 786440 | tf_op jit(solution)/shard_map/ppermute | solution.py:33
  22.7 37.0 %collective-permute-start.8 = (bf16[1024,256]{1,0:T(8,128)(2,1)S(1)}, bf16[1024,256]{1,0:T(8,128)(2,1)S(1)}, u32[]{:S(2)}, u32[]{:S(2)}) collective-permute-start(bf16[1024,256]{1,0:T(8,128)(2,1)S(1)} %get-tuple-element.127.refs_0_), channel_id=1, source_target_pairs={{0,2},{1,3},{2,0},{3,1},{4,6},{5,7},{6,4},{7,5},{8,10},{9,11},{10,... | collective-permute-start | bytes 1572872 | tf_op jit(solution)/shard_map/ppermute | solution.py:33
  24.6 1.1 collective-permute-start.4
  25.6 1.7 collective-permute-start.6
  25.8 14.8 %collective-permute-start.24 = (bf16[2,256,256]{2,1,0:T(8,128)(2,1)S(1)}, bf16[2,256,256]{2,1,0:T(8,128)(2,1)S(1)}, u32[]{:S(2)}, u32[]{:S(2)}) collective-permute-start(bf16[2,256,256]{2,1,0:T(8,128)(2,1)S(1)} %get-tuple-element.128), channel_id=1, source_target_pairs={{0,4},{1,5},{2,6},{3,7},{4,0},{5,1},{6,2},{7,3},{8,12},{9,13},{10,... | collective-permute-start | bytes 786440 | tf_op jit(solution)/shard_map/ppermute | solution.py:33
  27.3 35.7 %collective-permute-start.17 = (bf16[1024,256]{1,0:T(8,128)(2,1)S(1)}, bf16[1024,256]{1,0:T(8,128)(2,1)S(1)}, u32[]{:S(2)}, u32[]{:S(2)}) collective-permute-start(bf16[1024,256]{1,0:T(8,128)(2,1)S(1)} %get-tuple-element.126.refs_8_), channel_id=1, source_target_pairs={{0,4},{1,5},{2,6},{3,7},{4,0},{5,1},{6,2},{7,3},{8,12},{9,13},{10,... | collective-permute-start | bytes 1572872 | tf_op jit(solution)/shard_map/ppermute | solution.py:33
  27.8 47.9 %collective-permute-start.10 = (bf16[1024,256]{1,0:T(8,128)(2,1)S(1)}, bf16[1024,256]{1,0:T(8,128)(2,1)}, u32[]{:S(2)}, u32[]{:S(2)}) collective-permute-start(bf16[1024,256]{1,0:T(8,128)(2,1)S(1)} %get-tuple-element.127.refs_0_), channel_id=1, source_target_pairs={{0,4},{1,5},{2,6},{3,7},{4,0},{5,1},{6,2},{7,3},{8,12},{9,13},{10,... | collective-permute-start | bytes 1572872 | tf_op jit(solution)/shard_map/ppermute | solution.py:33
  37.3 39.7 %collective-permute-start.15 = (bf16[1024,256]{1,0:T(8,128)(2,1)S(1)}, bf16[1024,256]{1,0:T(8,128)(2,1)}, u32[]{:S(2)}, u32[]{:S(2)}) collective-permute-start(bf16[1024,256]{1,0:T(8,128)(2,1)S(1)} %get-tuple-element.126.refs_8_), channel_id=1, source_target_pairs={{0,2},{1,3},{2,0},{3,1},{4,6},{5,7},{6,4},{7,5},{8,10},{9,11},{10,... | collective-permute-start | bytes 1572872 | tf_op jit(solution)/shard_map/ppermute | solution.py:33
  40.5 37.1 %collective-permute-start.14 = (bf16[1024,256]{1,0:T(8,128)(2,1)S(1)}, bf16[1024,256]{1,0:T(8,128)(2,1)}, u32[]{:S(2)}, u32[]{:S(2)}) collective-permute-start(bf16[1024,256]{1,0:T(8,128)(2,1)S(1)} %get-tuple-element.126.refs_8_), channel_id=1, source_target_pairs={{0,1},{1,0},{2,3},{3,2},{4,5},{5,4},{6,7},{7,6},{8,9},{9,8},{10,11... | collective-permute-start | bytes 1572872 | tf_op jit(solution)/shard_map/ppermute | solution.py:33
  59.7 19.4 %collective-permute-start.7 = (bf16[1024,256]{1,0:T(8,128)(2,1)S(1)}, bf16[1024,256]{1,0:T(8,128)(2,1)}, u32[]{:S(2)}, u32[]{:S(2)}) collective-permute-start(bf16[1024,256]{1,0:T(8,128)(2,1)S(1)} %get-tuple-element.127.refs_0_), channel_id=1, source_target_pairs={{0,1},{1,0},{2,3},{3,2},{4,5},{5,4},{6,7},{7,6},{8,9},{9,8},{10,11... | collective-permute-start | bytes 1572872 | tf_op jit(solution)/shard_map/ppermute | solution.py:33
  63.0 16.7 %collective-permute-start.23 = (bf16[2,256,256]{2,1,0:T(8,128)(2,1)}, bf16[2,256,256]{2,1,0:T(8,128)(2,1)S(1)}, u32[]{:S(2)}, u32[]{:S(2)}) collective-permute-start(bf16[2,256,256]{2,1,0:T(8,128)(2,1)} %collective-permute-done.22), channel_id=1, source_target_pairs={{0,1},{1,0},{2,3},{3,2},{4,5},{5,4},{6,7},{7,6},{8,9},{9,8},{10,11... | collective-permute-start | bytes 786440 | tf_op jit(solution)/shard_map/ppermute | solution.py:33
  75.7 60.8 %collective-permute-start.29 = (bf16[256,1024]{1,0:T(8,128)(2,1)}, bf16[256,1024]{1,0:T(8,128)(2,1)}, u32[]{:S(2)}, u32[]{:S(2)}) collective-permute-start(bf16[256,1024]{1,0:T(8,128)(2,1)} %get-tuple-element.125.refs_0_), channel_id=1, source_target_pairs={{0,2},{1,3},{2,0},{3,1},{4,6},{5,7},{6,4},{7,5},{8,10},{9,11},{10,... | collective-permute-start | bytes 1572872 | tf_op jit(solution)/shard_map/ppermute | solution.py:33
  77.0 60.0 %collective-permute-start.38 = (bf16[256,1024]{1,0:T(8,128)(2,1)}, bf16[256,1024]{1,0:T(8,128)(2,1)}, u32[]{:S(2)}, u32[]{:S(2)}) collective-permute-start(bf16[256,1024]{1,0:T(8,128)(2,1)} %get-tuple-element.124.refs_8_), channel_id=1, source_target_pairs={{0,4},{1,5},{2,6},{3,7},{4,0},{5,1},{6,2},{7,3},{8,12},{9,13},{10,... | collective-permute-start | bytes 1572872 | tf_op jit(solution)/shard_map/ppermute | solution.py:33
  77.6 60.0 %collective-permute-start.31 = (bf16[256,1024]{1,0:T(8,128)(2,1)}, bf16[256,1024]{1,0:T(8,128)(2,1)S(1)}, u32[]{:S(2)}, u32[]{:S(2)}) collective-permute-start(bf16[256,1024]{1,0:T(8,128)(2,1)} %get-tuple-element.125.refs_0_), channel_id=1, source_target_pairs={{0,4},{1,5},{2,6},{3,7},{4,0},{5,1},{6,2},{7,3},{8,12},{9,13},{10,... | collective-permute-start | bytes 1572872 | tf_op jit(solution)/shard_map/ppermute | solution.py:33
  79.1 57.4 %collective-permute-start.26 = (bf16[2,256,256]{2,1,0:T(8,128)(2,1)}, bf16[2,256,256]{2,1,0:T(8,128)(2,1)S(1)}, u32[]{:S(2)}, u32[]{:S(2)}) collective-permute-start(bf16[2,256,256]{2,1,0:T(8,128)(2,1)} %collective-permute-done.22), channel_id=1, source_target_pairs={{0,4},{1,5},{2,6},{3,7},{4,0},{5,1},{6,2},{7,3},{8,12},{9,13},{10,... | collective-permute-start | bytes 786440 | tf_op jit(solution)/shard_map/ppermute | solution.py:33
  79.7 1.7 collective-permute-start.25
  81.4 59.7 %collective-permute-start.36 = (bf16[256,1024]{1,0:T(8,128)(2,1)}, bf16[256,1024]{1,0:T(8,128)(2,1)S(1)}, u32[]{:S(2)}, u32[]{:S(2)}) collective-permute-start(bf16[256,1024]{1,0:T(8,128)(2,1)} %get-tuple-element.124.refs_8_), channel_id=1, source_target_pairs={{0,2},{1,3},{2,0},{3,1},{4,6},{5,7},{6,4},{7,5},{8,10},{9,11},{10,... | collective-permute-start | bytes 1572872 | tf_op jit(solution)/shard_map/ppermute | solution.py:33
  136.5 5.0 collective-permute-start.28
  136.5 5.2 collective-permute-start.35
  137.0 23.7 %collective-permute-start.12 = (bf16[1024,256]{1,0:T(8,128)(2,1)}, bf16[1024,256]{1,0:T(8,128)(2,1)}, u32[]{:S(2)}, u32[]{:S(2)}) collective-permute-start(bf16[1024,256]{1,0:T(8,128)(2,1)} %copy-done.17), channel_id=1, source_target_pairs={{0,4},{1,5},{2,6},{3,7},{4,0},{5,1},{6,2},{7,3},{8,12},{9,13},{10,... | collective-permute-start | bytes 1572872 | tf_op jit(solution)/shard_map/ppermute | solution.py:33
  137.6 4.5 collective-permute-start.27
  141.1 24.2 %collective-permute-start.19 = (bf16[1024,256]{1,0:T(8,128)(2,1)}, bf16[1024,256]{1,0:T(8,128)(2,1)}, u32[]{:S(2)}, u32[]{:S(2)}) collective-permute-start(bf16[1024,256]{1,0:T(8,128)(2,1)} %copy-done.58), channel_id=1, source_target_pairs={{0,2},{1,3},{2,0},{3,1},{4,6},{5,7},{6,4},{7,5},{8,10},{9,11},{10,... | collective-permute-start | bytes 1572872 | tf_op jit(solution)/shard_map/ppermute | solution.py:33
  141.5 24.1 %collective-permute-start.18 = (bf16[1024,256]{1,0:T(8,128)(2,1)}, bf16[1024,256]{1,0:T(8,128)(2,1)S(1)}, u32[]{:S(2)}, u32[]{:S(2)}) collective-permute-start(bf16[1024,256]{1,0:T(8,128)(2,1)} %copy-done.58), channel_id=1, source_target_pairs={{0,1},{1,0},{2,3},{3,2},{4,5},{5,4},{6,7},{7,6},{8,9},{9,8},{10,11... | collective-permute-start | bytes 1572872 | tf_op jit(solution)/shard_map/ppermute | solution.py:33
  141.7 24.2 %collective-permute-start.9 = (bf16[1024,256]{1,0:T(8,128)(2,1)}, bf16[1024,256]{1,0:T(8,128)(2,1)S(1)}, u32[]{:S(2)}, u32[]{:S(2)}) collective-permute-start(bf16[1024,256]{1,0:T(8,128)(2,1)} %copy-done.17), channel_id=1, source_target_pairs={{0,1},{1,0},{2,3},{3,2},{4,5},{5,4},{6,7},{7,6},{8,9},{9,8},{10,11... | collective-permute-start | bytes 1572872 | tf_op jit(solution)/shard_map/ppermute | solution.py:33
  142.1 26.2 %collective-permute-start.11 = (bf16[1024,256]{1,0:T(8,128)(2,1)}, bf16[1024,256]{1,0:T(8,128)(2,1)S(1)}, u32[]{:S(2)}, u32[]{:S(2)}) collective-permute-start(bf16[1024,256]{1,0:T(8,128)(2,1)} %collective-permute-done.10.refs_4_), channel_id=1, source_target_pairs={{0,1},{1,0},{2,3},{3,2},{4,5},{5,4},{6,7},{7,6},{8,9},{9,8},{10,11... | collective-permute-start | bytes 1572872 | tf_op jit(solution)/shard_map/ppermute | solution.py:33
  160.7 8.4 collective-permute-start.16
  165.3 14.7 %collective-permute-start.33 = (bf16[256,1024]{1,0:T(8,128)(2,1)}, bf16[256,1024]{1,0:T(8,128)(2,1)}, u32[]{:S(2)}, u32[]{:S(2)}) collective-permute-start(bf16[256,1024]{1,0:T(8,128)(2,1)} %collective-permute-done.29.refs_2_), channel_id=1, source_target_pairs={{0,4},{1,5},{2,6},{3,7},{4,0},{5,1},{6,2},{7,3},{8,12},{9,13},{10,... | collective-permute-start | bytes 1572872 | tf_op jit(solution)/shard_map/ppermute | solution.py:33
  165.6 15.5 %collective-permute-start.30 = (bf16[256,1024]{1,0:T(8,128)(2,1)}, bf16[256,1024]{1,0:T(8,128)(2,1)}, u32[]{:S(2)}, u32[]{:S(2)}) collective-permute-start(bf16[256,1024]{1,0:T(8,128)(2,1)} %collective-permute-done.29.refs_2_), channel_id=1, source_target_pairs={{0,1},{1,0},{2,3},{3,2},{4,5},{5,4},{6,7},{7,6},{8,9},{9,8},{10,11... | collective-permute-start | bytes 1572872 | tf_op jit(solution)/shard_map/ppermute | solution.py:33
  166.7 14.4 %collective-permute-start.40 = (bf16[256,1024]{1,0:T(8,128)(2,1)}, bf16[256,1024]{1,0:T(8,128)(2,1)}, u32[]{:S(2)}, u32[]{:S(2)}) collective-permute-start(bf16[256,1024]{1,0:T(8,128)(2,1)} %collective-permute-done.38.refs_12_), channel_id=1, source_target_pairs={{0,2},{1,3},{2,0},{3,1},{4,6},{5,7},{6,4},{7,5},{8,10},{9,11},{10,... | collective-permute-start | bytes 1572872 | tf_op jit(solution)/shard_map/ppermute | solution.py:33
  169.1 12.4 %collective-permute-start.13 = (bf16[1024,256]{1,0:T(8,128)(2,1)}, bf16[1024,256]{1,0:T(8,128)(2,1)}, u32[]{:S(2)}, u32[]{:S(2)}) collective-permute-start(bf16[1024,256]{1,0:T(8,128)(2,1)} %collective-permute-done.12.refs_6_), channel_id=1, source_target_pairs={{0,1},{1,0},{2,3},{3,2},{4,5},{5,4},{6,7},{7,6},{8,9},{9,8},{10,11... | collective-permute-start | bytes 1572872 | tf_op jit(solution)/shard_map/ppermute | solution.py:33
  170.0 11.7 %collective-permute-start.20 = (bf16[1024,256]{1,0:T(8,128)(2,1)}, bf16[1024,256]{1,0:T(8,128)(2,1)}, u32[]{:S(2)}, u32[]{:S(2)}) collective-permute-start(bf16[1024,256]{1,0:T(8,128)(2,1)} %collective-permute-done.19.refs_14_), channel_id=1, source_target_pairs={{0,1},{1,0},{2,3},{3,2},{4,5},{5,4},{6,7},{7,6},{8,9},{9,8},{10,11... | collective-permute-start | bytes 1572872 | tf_op jit(solution)/shard_map/ppermute | solution.py:33
  179.9 31.5 %collective-permute-start.39 = (bf16[256,1024]{1,0:T(8,128)(2,1)}, bf16[256,1024]{1,0:T(8,128)(2,1)S(1)}, u32[]{:S(2)}, u32[]{:S(2)}) collective-permute-start(bf16[256,1024]{1,0:T(8,128)(2,1)} %collective-permute-done.38.refs_12_), channel_id=1, source_target_pairs={{0,1},{1,0},{2,3},{3,2},{4,5},{5,4},{6,7},{7,6},{8,9},{9,8},{10,11... | collective-permute-start | bytes 1572872 | tf_op jit(solution)/shard_map/ppermute | solution.py:33
  181.1 30.3 %collective-permute-start.32 = (bf16[256,1024]{1,0:T(8,128)(2,1)}, bf16[256,1024]{1,0:T(8,128)(2,1)S(1)}, u32[]{:S(2)}, u32[]{:S(2)}) collective-permute-start(bf16[256,1024]{1,0:T(8,128)(2,1)} %copy-done.28), channel_id=1, source_target_pairs={{0,1},{1,0},{2,3},{3,2},{4,5},{5,4},{6,7},{7,6},{8,9},{9,8},{10,11... | collective-permute-start | bytes 1572872 | tf_op jit(solution)/shard_map/ppermute | solution.py:33
  181.1 30.4 %collective-permute-start.37 = (bf16[256,1024]{1,0:T(8,128)(2,1)}, bf16[256,1024]{1,0:T(8,128)(2,1)S(1)}, u32[]{:S(2)}, u32[]{:S(2)}) collective-permute-start(bf16[256,1024]{1,0:T(8,128)(2,1)} %copy-done.31), channel_id=1, source_target_pairs={{0,1},{1,0},{2,3},{3,2},{4,5},{5,4},{6,7},{7,6},{8,9},{9,8},{10,11... | collective-permute-start | bytes 1572872 | tf_op jit(solution)/shard_map/ppermute | solution.py:33
  181.6 29.9 %collective-permute-start.34 = (bf16[256,1024]{1,0:T(8,128)(2,1)}, bf16[256,1024]{1,0:T(8,128)(2,1)S(1)}, u32[]{:S(2)}, u32[]{:S(2)}) collective-permute-start(bf16[256,1024]{1,0:T(8,128)(2,1)} %collective-permute-done.33.refs_6_), channel_id=1, source_target_pairs={{0,1},{1,0},{2,3},{3,2},{4,5},{5,4},{6,7},{7,6},{8,9},{9,8},{10,11... | collective-permute-start | bytes 1572872 | tf_op jit(solution)/shard_map/ppermute | solution.py:33
  181.6 29.8 %collective-permute-start.41 = (bf16[256,1024]{1,0:T(8,128)(2,1)}, bf16[256,1024]{1,0:T(8,128)(2,1)S(1)}, u32[]{:S(2)}, u32[]{:S(2)}) collective-permute-start(bf16[256,1024]{1,0:T(8,128)(2,1)} %collective-permute-done.40.refs_14_), channel_id=1, source_target_pairs={{0,1},{1,0},{2,3},{3,2},{4,5},{5,4},{6,7},{7,6},{8,9},{9,8},{10,11... | collective-permute-start | bytes 1572872 | tf_op jit(solution)/shard_map/ppermute | solution.py:33
  652.3 126.1 %copy-start.1 = (bf16[2,256,2048]{2,1,0:T(8,128)(2,1)S(1)}, bf16[2,256,2048]{2,1,0:T(8,128)(2,1)}, u32[]{:S(2)}) copy-start(bf16[2,256,2048]{2,1,0:T(8,128)(2,1)} %copy-done) | copy-start | bytes 6291460
  652.3 126.7 %copy-start.68 = (f32[1,1024]{1,0:T(1,128)S(1)}, f32[1,1024]{1,0:T(1,128)}, u32[]{:S(2)}) copy-start(f32[1,1024]{1,0:T(1,128)} %get-tuple-element.56) | copy-start | bytes 12292
  (70 other events, 511.0 us)
Sparse Core Ops, SparseCore 0:
  9.9 151.3 all-gather.2
  605.6 154.5 all-reduce.1

commit v4 on v3

--- a/solution.py
+++ b/solution.py
@@ -28,33 +28,9 @@
     return lax.dot_general(a, b, (((0,), (0,)), ((), ())), preferred_element_type=F32)
 
 
-def swap(x, bit, axis="tensor"):
-    n = lax.axis_size(axis)
-    return lax.ppermute(x, axis, [(i, i ^ (1 << bit)) for i in range(n)])
-
-
 def bit_orders(n):
     bits = list(range(1, n.bit_length() - 1))
     return bits, bits[::-1]
-
-
-def gather_slots(block, order):
-    held = {0: block}
-    for bit in list(order) + [0]:
-        held.update({k | (1 << bit): swap(v, bit) for k, v in list(held.items())})
-    return [held[k] for k in range(len(held))]
-
-
-def scatter_slots(slots, order):
-    held = dict(enumerate(slots))
-    for bit in [0] + list(order)[::-1]:
-        for k in sorted(held, reverse=True):
-            if k & (1 << bit):
-                arrived = swap(held.pop(k).astype(BF), bit)
-                low = k ^ (1 << bit)
-                held[low] = held[low].astype(F32) + arrived.astype(F32)
-        held = {k: (v if len(held) == 1 else v.astype(BF)) for k, v in held.items()}
-    return held[0].astype(F32)
 
 
 def xor_order(x, me):
@@ -231,37 +207,17 @@
     )(low, at, q, do, o, lse, k, kt, v, dock, docq)
 
 
-def fill(whole_ref, parts, axis):
-    for i, slots in enumerate(parts):
-        for k, part in enumerate(slots):
-            rows, cols = part.shape
-            if axis == 1:
-                whole_ref[i * rows : (i + 1) * rows, k * cols : (k + 1) * cols] = part[...]
-            else:
-                whole_ref[k * rows : (k + 1) * rows, i * cols : (i + 1) * cols] = part[...]
-
-
-def split_parts(refs):
-    count = len(refs) // 2
-    return [refs[:count], refs[count:]]
-
-
-def q_kernel(x_ref, b_ref, *refs, factor):
-    *parts, o_ref, w_s = refs
-
+def fill_rows(whole_ref, every_ref):
+    n, rows, _ = every_ref.shape
+    me = lax.axis_index("tensor")
+    for k in range(n):
+        whole_ref[k * rows : (k + 1) * rows, :] = every_ref[me ^ k]
+
+
+def o_kernel(a_ref, x_ref, w_ref, b_ref, gain_ref, shift_ref, mixed_ref, normed_ref, w_s):
     @pl.when(pl.program_id(0) == 0)
     def _():
-        fill(w_s, split_parts(parts), 1)
-
-    o_ref[...] = ((dot(x_ref[...], w_s[...]) + b_ref[...]) * factor).astype(BF)
-
-
-def o_kernel(a_ref, x_ref, b_ref, gain_ref, shift_ref, *refs):
-    *parts, mixed_ref, normed_ref, w_s = refs
-
-    @pl.when(pl.program_id(0) == 0)
-    def _():
-        fill(w_s, split_parts(parts), 0)
+        fill_rows(w_s, w_ref)
 
     mixed = x_ref[...].astype(F32) + dot(a_ref[...], w_s[...]) + b_ref[...]
     mixed_ref[...] = mixed
@@ -269,48 +225,32 @@
     normed_ref[...] = (unit * gain_ref[...] + shift_ref[...]).astype(BF)
 
 
-def do_kernel(g_ref, *refs):
-    *parts, o_ref, w_s = refs
-
+def do_kernel(g_ref, w_ref, o_ref, w_s):
     @pl.when(pl.program_id(0) == 0)
     def _():
-        fill(w_s, split_parts(parts), 0)
+        fill_rows(w_s, w_ref)
 
     o_ref[...] = dot_nt(g_ref[...], w_s[...]).astype(BF)
 
 
-def slot_product(kernel, tiled, fixed, parts, outs, shape):
-    flat = parts[0] + parts[1]
+def slot_product(kernel, tiled, weights, fixed, outs):
+    n, rows, cols = weights.shape
     tokens = tiled[0].shape[0]
     tile = tokens // 2
-    still = lambda a: pl.BlockSpec(a.shape, lambda i: (0, 0), pipeline_mode=pl.Buffered(1))
+    still = lambda a: pl.BlockSpec(a.shape, lambda i: (0,) * a.ndim, pipeline_mode=pl.Buffered(1))
     flow = lambda a: pl.BlockSpec((tile, a.shape[1]), lambda i: (i, 0))
-    result = pl.pallas_call(
+    return pl.pallas_call(
         kernel,
         grid=(2,),
-        in_specs=[flow(a) for a in tiled] + [still(a) for a in fixed] + [still(a) for a in flat],
+        in_specs=[flow(a) for a in tiled] + [still(weights)] + [still(a) for a in fixed],
         out_specs=[flow(o) for o in outs],
         out_shape=outs,
-        scratch_shapes=[pltpu.VMEM(shape, BF)],
+        scratch_shapes=[pltpu.VMEM((n * rows, cols), BF)],
         compiler_params=pltpu.CompilerParams(vmem_limit_bytes=48 * MIB),
         cost_estimate=pl.CostEstimate(
-            flops=2 * tokens * shape[0] * shape[1], bytes_accessed=2 * shape[0] * shape[1] + 8 * MIB, transcendentals=0
+            flops=2 * tokens * n * rows * cols, bytes_accessed=2 * n * rows * cols + 8 * MIB, transcendentals=0
         ),
-    )(*tiled, *fixed, *flat)
-    return result
-
-
-def after_kernel(x_ref, *refs):
-    refs[-1][...] = x_ref[...]
-
-
-def after(x, *first):
-    return pl.pallas_call(
-        after_kernel,
-        in_specs=[pl.BlockSpec(memory_space=pltpu.VMEM)] + [pl.BlockSpec(memory_space=pl.ANY)] * len(first),
-        out_specs=pl.BlockSpec(memory_space=pltpu.VMEM),
-        out_shape=jax.ShapeDtypeStruct(x.shape, x.dtype),
-    )(x, *first)
+    )(*tiled, weights, *fixed)
 
 
 MESH = pl.DeviceIdType.MESH
@@ -446,13 +386,38 @@
     return sorted(range(2, n, 2), key=lambda k: (rank(k), -k))
 
 
-def attention_grads_kernel(a_ref, gm_ref, dq_ref, h_ref, dkv_ref, wo_ref, wq_ref, kv_ref,
-                           send, recv, ksend, krecv, ssem, rsem, ksem, krsem, *, orders, qw):
+def attention_grads_kernel(a_ref, gm_ref, dq_ref, h_ref, dkv_ref, up_ref, after_ref, wo_ref, wq_ref, kv_ref, sum_ref,
+                           send, recv, ksend, krecv, far, own, ssem, rsem, ksem, krsem, zsem, psem,
+                           *, orders, line, qw):
     bits_of = [[0] + list(o)[::-1] for o in orders]
     count = len(bits_of[0])
     n = 1 << count
     half = gm_ref.shape[1] // 2
-    greet(range(count))
+    greet(range(count), line)
+    chain = Line(up_ref, sum_ref, far, zsem)
+    pieces = up_ref.shape[0]
+    if line:
+        for i in range(pieces):
+            chain.start(i)
+
+    def own_piece(i):
+        def value():
+            c = pltpu.make_async_copy(up_ref.at[i], own, psem)
+            c.start()
+            c.wait()
+            return own[...]
+
+        return value
+
+    ahead = [0]
+
+    def chain_to(middles):
+        while line and ahead[0] < min(middles, pieces):
+            chain.middle(ahead[0], own_piece(ahead[0]))
+            ahead[0] += 1
+            if ahead[0] > 1:
+                chain.back(ahead[0] - 2)
+
     kv = Scatter(bits_of[0], ksend, krecv, ksem, krsem)
     for k in list(range(1, n, 2)) + list(range(0, n, 2)):
         kv.put(k, dkv_ref[k])
@@ -491,59 +456,77 @@
     products(0)
     stage(0, 1)
     products(1)
+    chain_to(1)
     for i in range(1, count):
         kv_stage(i)
         if i + 1 < count:
             stage(0, i + 1)
+            chain_to(i + 1)
         else:
+            chain_to(3)
             finish(0)
         stage(1, i)
+    chain_to(4)
     kv_ref[...] = kv.total(0).astype(BF)
+    chain_to(5)
     finish(1)
+    if line:
+        chain_to(pieces)
+        chain.back(pieces - 1)
+        for i in range(pieces):
+            chain.close(i)
     kv.drain()
     for m in range(2):
         for p in range(2):
             work[m][p].drain()
 
 
-def attention_grads(a, gm, dq, h, dkv, orders):
-    n = lax.axis_size("tensor")
+def attention_grads(a, gm, dq, h, dkv, up, early, orders):
+    n, line = lax.axis_size("tensor"), lax.axis_size("dp") == 4
     tokens, d = gm.shape
     qw = a.shape[1] // n
     slot = dkv.shape[1:]
+    rows, cols = up.shape
+    pieces = 8
+    up = up.reshape(pieces, rows // pieces, cols)
+    wait = up.shape if line else (1, 16, 128)
     dma = pltpu.SemaphoreType.DMA
-    vmem = pl.BlockSpec(memory_space=pltpu.VMEM)
-    return pl.pallas_call(
-        functools.partial(attention_grads_kernel, orders=orders, qw=qw),
-        in_specs=[vmem] * 5,
-        out_specs=[vmem] * 3,
+    vmem, hbm = pl.BlockSpec(memory_space=pltpu.VMEM), pl.BlockSpec(memory_space=pl.ANY)
+    wo, wq, kv, total = pl.pallas_call(
+        functools.partial(attention_grads_kernel, orders=orders, line=line, qw=qw),
+        in_specs=[vmem] * 5 + [hbm] * 2,
+        out_specs=[vmem] * 4,
         out_shape=[
             jax.ShapeDtypeStruct((2, qw, d // 2), BF),
             jax.ShapeDtypeStruct((2, qw, d // 2), BF),
             jax.ShapeDtypeStruct(slot, BF),
+            jax.ShapeDtypeStruct(wait, BF),
         ],
         scratch_shapes=[
             pltpu.VMEM((2, 2, n // 2 + 2, qw, d // 2), BF),
             pltpu.VMEM((2, 2, n - 1, qw, d // 2), BF),
             pltpu.VMEM((n,) + slot, BF),
             pltpu.VMEM((n - 1,) + slot, BF),
-            dma((2, 2, n)), dma((2, 2, n)), dma((n,)), dma((n,)),
+            pltpu.VMEM(wait, BF),
+            pltpu.VMEM(up.shape[1:], BF),
+            dma((2, 2, n)), dma((2, 2, n)), dma((n,)), dma((n,)), dma((2, 3, pieces)), dma,
         ],
         compiler_params=pltpu.CompilerParams(
             collective_id=1, has_side_effects=True, vmem_limit_bytes=60 * MIB
         ),
         cost_estimate=pl.CostEstimate(flops=1000, bytes_accessed=MIB, transcendentals=0),
-    )(a, gm, dq, h, dkv)
-
-
-def last_kernel(wo_ref, wq_ref, dq_ref, kv_ref, shared_ref, h_ref, x_ref, gain_ref, mixed_ref, qb_ref, *refs,
+    )(a, gm, dq, h, dkv, up, early)
+    up = up.reshape(rows, cols)
+    return wo, wq, kv, total.reshape(rows, cols) if line else lax.psum(up, "dp")
+
+
+def last_kernel(wo_ref, wq_ref, dq_ref, kv_ref, shared_ref, h_ref, x_ref, gain_ref, mixed_ref, qb_ref, w_ref, *refs,
                 order, line, eps_rows):
     count = len(order) + 1
     n = 1 << count
-    parts = refs[: 2 * n]
     (wog_ref, wqg_ref, grad_ref, late_ref, sg_ref,
      w_s, near, far, part, send, recv, dsend, drecv, piece_s, gathered, vsend, vrecv,
-     zsem, ssem, rsem, dsem, gsem, vsem) = refs[2 * n :]
+     zsem, ssem, rsem, dsem, gsem, vsem) = refs
     me, z = lax.axis_index("tensor"), lax.axis_index("dp")
     dp_bits = range(lax.axis_size("dp").bit_length() - 1)
     tokens, d = x_ref.shape
@@ -577,7 +560,8 @@
     scatter = Scatter([0] + list(order)[::-1], send, recv, ssem, rsem)
     for k in list(range(1, n, 2)) + list(range(0, n, 2)):
         scatter.put(k, part[pl.ds(pl.multiple_of((me ^ k) * piece, piece), piece), :])
-    fill(w_s, split_parts(parts), 1)
+    for k in range(n):
+        w_s[:, k * w_ref.shape[2] : (k + 1) * w_ref.shape[2]] = w_ref[k]
     for i in range(1, count):
         for k in scatter_order(scatter.bits):
             if scatter.stage(k) == i:
@@ -662,12 +646,11 @@
     scatter.drain()
 
 
-def last(wo, wq, dq, kv, shared, h, x, gain, mixed, qb, parts, order):
+def last(wo, wq, dq, kv, shared, h, x, gain, mixed, qb, w, order):
     n, dp = lax.axis_size("tensor"), lax.axis_size("dp")
     line = dp == 4
     tokens, d = x.shape
     qw = wo.shape[1]
-    flat = parts[0] + parts[1]
     piece, width = d // n, kv.shape[1]
     size = 2 * d + qb.shape[1] + width // 2
     bits = n.bit_length() - 1
@@ -677,7 +660,7 @@
     item = (2, 2, qw, d // 2)
     return pl.pallas_call(
         functools.partial(last_kernel, order=order, line=line, eps_rows=tokens // 2),
-        in_specs=[vmem] * (10 + len(flat)),
+        in_specs=[vmem] * 11,
         out_specs=[vmem] * 5,
         out_shape=[
             jax.ShapeDtypeStruct((qw, d), F32),
@@ -705,12 +688,147 @@
             collective_id=4, has_side_effects=True, vmem_limit_bytes=60 * MIB
         ),
         cost_estimate=pl.CostEstimate(flops=1000, bytes_accessed=MIB, transcendentals=0),
-    )(wo, wq, dq, kv, shared, h, x, gain, mixed, qb, *flat)
+    )(wo, wq, dq, kv, shared, h, x, gain, mixed, qb, w)
+
+
+class Gather:
+    def __init__(self, orders, refs, send_sem, recv_sem):
+        self.paths = [list(o) + [0] for o in orders]
+        self.refs, self.send_sem, self.recv_sem = refs, send_sem, recv_sem
+        self.me = lax.axis_index("tensor")
+        self.n = 1 << len(self.paths[0])
+        self.sent = []
+
+    def last_bit(self, p, k):
+        return max((b for b in self.paths[p] if k >> b & 1), key=self.paths[p].index)
+
+    def copies(self, p, k, bit):
+        to = k | (1 << bit)
+        return [
+            pltpu.make_async_remote_copy(
+                src_ref=ref(p, k), dst_ref=ref(p, to), send_sem=self.send_sem.at[i, p, to],
+                recv_sem=self.recv_sem.at[i, p, to], device_id={"tensor": self.me ^ (1 << bit)}, device_id_type=MESH,
+            )
+            for i, ref in enumerate(self.refs)
+        ]
+
+    def hop(self, p, k, bit):
+        for c in self.copies(p, k, bit):
+            c.start()
+            self.sent.append(c)
+
+    def arrived(self, p, k):
+        bit = self.last_bit(p, k)
+        for c in self.copies(p, k ^ (1 << bit), bit):
+            c.wait_recv()
+
+    def at_step(self, p, t):
+        if t == 0:
+            return [0]
+        return sorted((k for k in range(2, self.n, 2) if self.last_bit(p, k) == self.paths[p][t - 1]), reverse=True)
+
+    def drain(self):
+        for c in self.sent:
+            c.wait_send()
+
+
+def first_kernel(x_ref, gain_ref, shift_ref, shared_ref, vb_ref, wq_ref, bq_ref, h_ref, kv_ref, w_ref, q_ref,
+                 bias, send_sem, recv_sem, *, orders, factor, rows):
+    n, d, qw = w_ref.shape
+    seqs, span = kv_ref.shape[1:3]
+    hd = vb_ref.shape[1]
+    half = d // 2
+    tokens = x_ref.shape[0]
+    greet(range(len(orders[0]) + 1))
+    weights = Gather(
+        orders, [lambda p, k: w_ref.at[k, p * half : (p + 1) * half], lambda p, k: bias.at[p, k]],
+        send_sem.at[0], recv_sem.at[0],
+    )
+    shared = Gather(orders, [lambda p, k: kv_ref.at[k, p]], send_sem.at[1], recv_sem.at[1])
+    steps = len(weights.paths[0])
+    w_ref[0] = wq_ref[...]
+    for p in range(2):
+        bias[p, 0] = bq_ref[...]
+    for p in range(2):
+        weights.hop(p, 0, weights.paths[p][0])
+    for p in range(2):
+        weights.hop(p, 0, 0)
+    for t in range(tokens // rows):
+        here = slice(t * rows, (t + 1) * rows)
+        unit, _ = norm_parts(x_ref[here].astype(F32))
+        h_ref[here] = (unit * gain_ref[...] + shift_ref[...]).astype(BF)
+    kv = dot(h_ref[...], shared_ref[...])
+    for r in range(seqs):
+        here = slice(r * span, (r + 1) * span)
+        kv_ref[0, r, :, :hd] = kv[here, :hd].astype(BF)
+        kv_ref[0, r, :, hd:] = (kv[here, hd:] + vb_ref[...]).astype(BF)
+    for p in range(2):
+        shared.hop(p, 0, shared.paths[p][0])
+    for p in range(2):
+        shared.hop(p, 0, 0)
+
+    def product(k):
+        q_ref[:, k * qw : (k + 1) * qw] = ((dot(h_ref[...], w_ref[k]) + bias[0, k]) * factor).astype(BF)
+
+    product(0)
+    ready = [1]
+    for t in range(1, steps):
+        for g in (weights, shared):
+            for p in range(2):
+                for k in g.at_step(p, t):
+                    g.arrived(p, k)
+                    if t < steps - 1:
+                        g.hop(p, k, g.paths[p][t])
+                    g.hop(p, k, 0)
+            if t < steps - 1:
+                for p in range(2):
+                    for before in range(t - 1, -1, -1):
+                        for k in g.at_step(p, before):
+                            g.hop(p, k, g.paths[p][t])
+    for k in range(1, n, 2):
+        for p in range(2):
+            weights.arrived(p, k)
+        product(k)
+        if k > 1:
+            product(k - 1)
+    for k in range(1, n, 2):
+        for p in range(2):
+            shared.arrived(p, k)
+    weights.drain()
+    shared.drain()
+
+
+def first(x, gain, shift, shared, vb, wq, bq, seqs, factor, orders):
+    n = lax.axis_size("tensor")
+    tokens, d = x.shape
+    qw = wq.shape[1]
+    dma = pltpu.SemaphoreType.DMA
+    vmem = pl.BlockSpec(memory_space=pltpu.VMEM)
+    return pl.pallas_call(
+        functools.partial(first_kernel, orders=orders, factor=factor, rows=tokens // 4),
+        in_specs=[vmem] * 7,
+        out_specs=[vmem] * 4,
+        out_shape=[
+            jax.ShapeDtypeStruct((tokens, d), BF),
+            jax.ShapeDtypeStruct((n, seqs, tokens // seqs, shared.shape[1]), BF),
+            jax.ShapeDtypeStruct((n, d, qw), BF),
+            jax.ShapeDtypeStruct((tokens, n * qw), BF),
+        ],
+        scratch_shapes=[
+            pltpu.VMEM((2, n, 1, qw), F32),
+            dma((2, 2, 2, n)), dma((2, 2, 2, n)),
+        ],
+        compiler_params=pltpu.CompilerParams(collective_id=5, has_side_effects=True, vmem_limit_bytes=48 * MIB),
+        cost_estimate=pl.CostEstimate(
+            flops=2 * tokens * d * n * qw, bytes_accessed=64 * MIB, transcendentals=0
+        ),
+    )(x, gain, shift, shared, vb, wq, bq)
 
 
 def mlp_kernel(x_ref, cot_ref, up_ref, bias_ref, down_ref, gn_ref, gb_ref, xg_ref, act_ref, gr_ref, *rest, orders):
     n, seqs, span, d = cot_ref.shape
-    (ff_ref, x_s, c_s, act_s, gr_s, ff_s, send, recv, gsend, grecv, ssem, rsem, load, own, out) = rest
+    (ff_ref, down_grad_ref, x_s, c_s, act_s, gr_s, ff_s, send, recv, a_s, acc,
+     gsend, grecv, ssem, rsem, load, own, out, aload, gout) = rest
     hidden = up_ref.shape[1]
     tile, wide = min(512, hidden), 512
     me = lax.axis_index("tensor")
@@ -870,15 +988,76 @@
                         sent.append((p, k, paths[p][t]))
     for p, k in waiting:
         work[p].forward(k)
+    for c in hidden_stores(len(units) - 1) + ff_stores(len(units) - 1):
+        c.wait()
+
+    strip = a_s.shape[2]
+    strips = hidden // strip
+
+    def grad_loads(q, j, slot):
+        return [
+            c
+            for r in range(seqs)
+            for c in (
+                pltpu.make_async_copy(
+                    act_ref.at[j, r, :, q * strip : (q + 1) * strip], a_s.at[slot, r * span : (r + 1) * span],
+                    aload.at[slot, r],
+                ),
+                pltpu.make_async_copy(
+                    cot_ref.at[j, r], c_s.at[slot, r * span : (r + 1) * span], load.at[slot, r]
+                ),
+            )
+        ]
+
+    def grad_store(q):
+        return pltpu.make_async_copy(
+            ff_s.at[:strip], down_grad_ref.at[q * strip : (q + 1) * strip], gout
+        )
+
+    def grad_strip(q):
+        for c in grad_loads(q, 0, 0):
+            c.start()
+
+        @pl.loop(0, n)
+        def _(j):
+            slot = lax.rem(j, 2)
+
+            @pl.when(j + 1 < n)
+            def _():
+                for c in grad_loads(q, j + 1, 1 - slot):
+                    c.start()
+
+            for c in grad_loads(q, j, slot):
+                c.wait()
+            term = dot_tn(a_s[slot], c_s[slot])
+
+            @pl.when(j == 0)
+            def _():
+                acc[...] = term
+
+            @pl.when(j > 0)
+            def _():
+                acc[...] += term
+
+        if q:
+            grad_store(q - 1).wait()
+        ff_s[:strip] = acc[...].astype(BF)
+        grad_store(q).start()
+
+    for q in range(strips // 2):
+        grad_strip(q)
     for i in range(2, steps):
         for at in range(n // 2 - 1):
             for p in range(seqs):
                 k = scatter_order(bits_of[p])[at]
                 if work[p].stage(k) == i:
                     work[p].forward(k)
+    for q in range(strips // 2, strips):
+        grad_strip(q)
+    grad_store(strips - 1).wait()
     for p in range(seqs):
         gn_ref[p] = work[p].total(0)
-    for c in hidden_stores(len(units) - 1) + ff_stores(len(units) - 1) + keep:
+    for c in keep:
         c.wait()
     for p, k, b in sent:
         hop(p, k, b).wait_send()
@@ -889,12 +1068,13 @@
 def mlp(normed, cot, up, bias, down, orders):
     n, seqs, span, d = cot.shape
     ff = up.shape[1]
+    strip = min(2 * span, ff // 2, 256)
     dma = pltpu.SemaphoreType.DMA
     hbm, vmem = pl.BlockSpec(memory_space=pl.ANY), pl.BlockSpec(memory_space=pltpu.VMEM)
     return pl.pallas_call(
         functools.partial(mlp_kernel, orders=orders),
         in_specs=[hbm, hbm, vmem, vmem, vmem],
-        out_specs=[vmem, vmem, hbm, hbm, hbm, hbm],
+        out_specs=[vmem, vmem, hbm, hbm, hbm, hbm, hbm],
         out_shape=[
             jax.ShapeDtypeStruct((seqs, span, d), F32),
             jax.ShapeDtypeStruct((1, ff), F32),
@@ -902,6 +1082,7 @@
             jax.ShapeDtypeStruct((n, seqs, span, ff), BF),
             jax.ShapeDtypeStruct((n, seqs, span, ff), BF),
             jax.ShapeDtypeStruct((seqs, n, span, d), BF),
+            jax.ShapeDtypeStruct((ff, d), BF),
         ],
         scratch_shapes=[
             pltpu.VMEM((2 * span, d), BF),
@@ -911,7 +1092,10 @@
             pltpu.VMEM((2 * span, d), BF),
             pltpu.VMEM((seqs, n // 2 + 2, span, d), BF),
             pltpu.VMEM((seqs, n - 1, span, d), BF),
+            pltpu.VMEM((2, seqs * span, strip), BF),
+            pltpu.VMEM((strip, d), F32),
             dma((seqs, n)), dma((seqs, n)), dma((seqs, n)), dma((seqs, n)), dma((3, 2)), dma((seqs,)), dma((3, 2)),
+            dma((2, seqs)), dma,
         ],
         compiler_params=pltpu.CompilerParams(collective_id=2, has_side_effects=True, vmem_limit_bytes=60 * MIB),
         cost_estimate=pl.CostEstimate(
@@ -937,8 +1121,8 @@
         return k // 2 if k % 2 == 0 else -k
 
 
-def mlp_grads_kernel(gr_ref, x_ref, part_ref, down_ref, up_ref, ff_ref, sum_ref,
-                     a_s, b_s, acc, send, recv, far, piece, ssem, rsem, load, own, zsem, psem, *, orders, line):
+def mlp_grads_kernel(gr_ref, x_ref, part_ref, after_ref, up_ref, ff_ref,
+                     a_s, b_s, acc, send, recv, ssem, rsem, load, own, *, orders):
     seqs, n = part_ref.shape[:2]
     bits_of = [[0] + list(o)[::-1] for o in orders]
     work = []
@@ -960,34 +1144,10 @@
             pltpu.make_async_copy(gr_ref.at[u], b_s.at[u % 2], load.at[u % 2, 1]),
         ]
 
-    greet(range(len(bits_of[0])), line)
-    chain = Line(down_ref, sum_ref, far, zsem)
-    pieces = down_ref.shape[0]
+    greet(range(len(bits_of[0])))
     for k in range(n - 1, 0, -2):
         for p in range(seqs):
             work[p].launch(k)
-    if line:
-        for i in range(pieces):
-            chain.start(i)
-
-    def own_piece(i):
-        def value():
-            c = pltpu.make_async_copy(down_ref.at[i], piece, psem)
-            c.start()
-            c.wait()
-            return piece[...]
-
-        return value
-
-    ahead = [0, 0]
-
-    def chain_to(middles):
-        while line and ahead[0] < min(middles, pieces):
-            chain.middle(ahead[0], own_piece(ahead[0]))
-            ahead[0] += 1
-            if ahead[0] > 1:
-                chain.back(ahead[0] - 2)
-
     for c in loads(0) + evens:
         c.start()
 
@@ -1024,75 +1184,24 @@
                 c.wait()
         if u in when:
             forwards(when[u])
-        chain_to((u + 1) // 3)
-    chain_to(5)
     for p in range(seqs):
         ff_ref[p] = work[p].total(0)
         work[p].drain()
-    if line:
-        chain_to(pieces)
-        chain.back(pieces - 1)
-        for i in range(pieces):
-            chain.close(i)
-
-
-def weight_grad_kernel(a_ref, b_ref, o_ref, acc):
-    step, last = pl.program_id(0), pl.num_programs(0) - 1
-    wide = acc.shape[0]
-    tile = min(256, wide)
-
-    @pl.loop(0, wide // tile)
-    def _(i):
-        here = pl.ds(pl.multiple_of(i * tile, tile), tile)
-        term = dot_tn(a_ref[:, here], b_ref[...])
-
-        @pl.when(step == 0)
-        def _():
-            acc[here, :] = term
-
-        @pl.when((step > 0) & (step < last))
-        def _():
-            acc[here, :] += term
-
-        @pl.when(step == last)
-        def _():
-            o_ref[here, :] = (acc[here, :] + term).astype(BF)
-
-
-def weight_grad(a, b):
-    tokens, wide = a.shape
-    cols = b.shape[1]
-    tile = min(512, tokens // 2)
-    return pl.pallas_call(
-        weight_grad_kernel,
-        grid=(tokens // tile,),
-        in_specs=[pl.BlockSpec((tile, wide), lambda i: (i, 0)), pl.BlockSpec((tile, cols), lambda i: (i, 0))],
-        out_specs=pl.BlockSpec((wide, cols), lambda i: (0, 0)),
-        out_shape=jax.ShapeDtypeStruct((wide, cols), BF),
-        scratch_shapes=[pltpu.VMEM((wide, cols), F32)],
-        compiler_params=pltpu.CompilerParams(vmem_limit_bytes=40 * MIB),
-        cost_estimate=pl.CostEstimate(flops=1000, bytes_accessed=MIB, transcendentals=0),
-    )(a, b)
-
-
-def mlp_grads(gr, x, parts, down, orders):
-    line = lax.axis_size("dp") == 4
+
+
+def mlp_grads(gr, x, parts, early, orders):
     seqs, n, span, d = parts.shape
     tokens, cols = seqs * span, gr.shape[-1]
-    rows = down.shape[0] // 8
-    down = down.reshape(8, rows, d)
-    wait = down.shape if line else (1, 16, 128)
     dma = pltpu.SemaphoreType.DMA
     hbm, vmem = pl.BlockSpec(memory_space=pl.ANY), pl.BlockSpec(memory_space=pltpu.VMEM)
     flat = lambda v: v.reshape(n, tokens, v.shape[-1])
-    up, ff, total = pl.pallas_call(
-        functools.partial(mlp_grads_kernel, orders=orders, line=line),
+    return pl.pallas_call(
+        functools.partial(mlp_grads_kernel, orders=orders),
         in_specs=[hbm] * 4,
-        out_specs=[vmem] * 3,
+        out_specs=[vmem] * 2,
         out_shape=[
             jax.ShapeDtypeStruct((d, cols), BF),
             jax.ShapeDtypeStruct((seqs, span, d), F32),
-            jax.ShapeDtypeStruct(wait, BF),
         ],
         scratch_shapes=[
             pltpu.VMEM((2, tokens, d), BF),
@@ -1100,17 +1209,11 @@
             pltpu.VMEM((d, cols), F32),
             pltpu.VMEM((seqs, n // 2, span, d), BF),
             pltpu.VMEM((seqs, n - 1, span, d), BF),
-            pltpu.VMEM(wait, BF),
-            pltpu.VMEM((rows, d), BF),
-            dma((seqs, n)), dma((seqs, n)), dma((2, 2)), dma((seqs, n // 2)), dma((2, 3, 8)), dma,
+            dma((seqs, n)), dma((seqs, n)), dma((2, 2)), dma((seqs, n // 2)),
         ],
         compiler_params=pltpu.CompilerParams(collective_id=3, has_side_effects=True, vmem_limit_bytes=60 * MIB),
-        cost_estimate=pl.CostEstimate(
-            flops=1000, bytes_accessed=256 * MIB, transcendentals=0
-        ),
-    )(flat(gr), flat(x), parts, down)
-    down = down.reshape(8 * rows, d)
-    return up, ff, total.reshape(down.shape) if line else lax.psum(down, "dp")
+        cost_estimate=pl.CostEstimate(flops=1000, bytes_accessed=MIB, transcendentals=0),
+    )(flat(gr), flat(x), parts, early)
 
 
 def norm_parts(values):
@@ -1139,30 +1242,23 @@
     scale = hd**-0.5
     paths = bit_orders(n)
     tokens = seqs * span
+    ff = up_bias.shape[0]
 
     x32 = inputs.astype(F32)
-    unit1, _ = norm_parts(x32)
-    hidden = (unit1 * attn_gain + attn_shift).astype(BF)
-    h2 = hidden.reshape(tokens, d)
-    shared = dot(h2, shared_matrix)
-    kv_own = jnp.concatenate([shared[:, :hd], shared[:, hd:] + value_bias], axis=1).astype(BF)
-    kv_own = kv_own.reshape(seqs, span, 2 * hd)
-    kv = jnp.concatenate(gather_slots(kv_own, paths[0]), axis=1)
+    output_every = lax.all_gather(output_matrix, "tensor")
+    cot_every = lax.all_gather(cotangent, "tensor")
+    h2, kv, wq, query = first(
+        inputs.reshape(tokens, d), attn_gain[None], attn_shift[None], shared_matrix, value_bias[None], query_matrix,
+        query_bias[None], seqs, scale * LOG2E, paths,
+    )
+    kv = kv.swapaxes(0, 1).reshape(seqs, length, 2 * hd)
     keys, values = kv[..., :hd], kv[..., hd:]
     keys_t, values_t = keys.swapaxes(1, 2), values.swapaxes(1, 2)
-
-    half = d // 2
-    wq = [gather_slots(query_matrix[i * half : (i + 1) * half], paths[i]) for i in range(2)]
-    wo = [gather_slots(output_matrix[:, i * half : (i + 1) * half], paths[i]) for i in range(2)]
-    bq = jnp.concatenate(gather_slots(query_bias[None], paths[0]), axis=1)
-
+    query = query.reshape(seqs, span, n * qw)
     like = lambda t, cols: jax.ShapeDtypeStruct((tokens, cols), t)
-    (query,) = slot_product(
-        functools.partial(q_kernel, factor=scale * LOG2E), [h2], [bq], wq, [like(BF, n * qw)], (d, n * qw)
-    )
-    query = query.reshape(seqs, span, n * qw)
-    first = lax.dynamic_slice_in_dim(documents, me * span, 1, 1)
-    low = (jnp.sum((documents < first).astype(jnp.int32), axis=1) // span).astype(jnp.int32)
+
+    begin = lax.dynamic_slice_in_dim(documents, me * span, 1, 1)
+    low = (jnp.sum((documents < begin).astype(jnp.int32), axis=1) // span).astype(jnp.int32)
     low = jnp.minimum(low, me)
     at = me.reshape(1).astype(jnp.int32)
     dock = jnp.where(padding == 1, documents, -1)
@@ -1172,37 +1268,35 @@
     attended, lse = attention_fwd(query, keys, values_t, low, at, dock, docq, heads, hd)
     a2 = attended.reshape(tokens, n * qw)
     mixed, normed = slot_product(
-        o_kernel, [a2, inputs.reshape(tokens, d)], [output_bias[None], mlp_gain[None], mlp_shift[None]], wo,
-        [like(F32, d), like(BF, d)], (n * qw, d),
+        o_kernel, [a2, inputs.reshape(tokens, d)], output_every, [output_bias[None], mlp_gain[None], mlp_shift[None]],
+        [like(F32, d), like(BF, d)],
     )
     mixed, normed = mixed.reshape(seqs, span, d), normed.reshape(seqs, span, d)
     unit2, scale2 = norm_parts(mixed)
 
-    cot_every = lax.all_gather(cotangent, "tensor")
-    grad_normed, up_bias_part, normed_every, acts, grs, ff_parts = mlp(
+    grad_normed, up_bias_part, normed_every, acts, grs, ff_parts, down_part = mlp(
         normed, cot_every, expansion_weights, up_bias[None], down_matrix, paths
     )
-    every = lambda v: v.reshape(n * tokens, v.shape[-1])
-    down_part = weight_grad(every(acts), every(cot_every))
-    up_part, mlp_branch, down_gradient = mlp_grads(grs, normed_every, ff_parts, down_part, paths)
-    up_gradient = lax.psum(up_part, "dp")
-    block_out = (mixed + mlp_branch + down_bias).astype(BF)
+    down_gradient = lax.psum(down_part, "dp")
 
     cot_wide = cotangent.astype(F32)
     back2, mlp_gain_part, mlp_shift_part = norm_back(unit2, scale2, mlp_gain, grad_normed)
     grad_mixed = cot_wide + back2
     gm2 = grad_mixed.astype(BF).reshape(tokens, d)
-    (grad_attended,) = slot_product(do_kernel, [gm2], [], wo, [like(BF, n * qw)], (n * qw, d))
+    (grad_attended,) = slot_product(do_kernel, [gm2], output_every, [], [like(BF, n * qw)])
     grad_attended = grad_attended.reshape(seqs, span, n * qw)
     dq, dk, dv = attention_bwd(
         query, grad_attended, attended, lse, keys, keys_t, values, low, at, dock, docq, heads, hd, scale
     )
     dq2 = dq.reshape(tokens, n * qw)
+    up_part, mlp_branch = mlp_grads(grs, normed_every, ff_parts, dq2, paths)
+    block_out = (mixed + mlp_branch + down_bias).astype(BF)
 
     dkv = jnp.concatenate([dk * LN2, dv], axis=-1).astype(BF).reshape(seqs, n, span, 2 * hd).swapaxes(0, 1)
-    wo_own, wq_own, dkv_own = attention_grads(a2, gm2, dq2, h2, dkv.reshape(n, tokens, 2 * hd), paths)
+    wo_own, wq_own, dkv_own, up_gradient = attention_grads(
+        a2, gm2, dq2, h2, dkv.reshape(n, tokens, 2 * hd), up_part, down_gradient, paths
+    )
     query_bias_part = xor_order(jnp.sum(dq2.astype(F32), axis=0).reshape(n, qw), me).reshape(-1)
-    ff = up_bias.shape[0]
     up_bias_every = lax.dynamic_update_slice_in_dim(jnp.zeros((n * ff,), F32), up_bias_part[0], me * ff, 0)
     vector = jnp.concatenate(
         [query_bias_part, mlp_gain_part, mlp_shift_part, jnp.sum(grad_mixed, axis=(0, 1)),
@@ -1217,7 +1311,7 @@
         output_gradient, query_gradient = (
             g.astype(F32) for g in lax.psum((output_gradient.astype(BF), query_gradient.astype(BF)), "dp")
         )
-    late = after(late, up_gradient)[0]
+    late = late[0]
     ends = [d, 2 * d, 2 * d + hd, 2 * d + hd + n * qw]
     ends += [ends[-1] + d * (i + 1) for i in range(4)]
     (attn_gain_grad, attn_shift_grad, value_bias_grad, query_bias_all, mlp_gain_grad, mlp_shift_grad,

time: 945 us -> 847 us (0.90)
  waiting for transfers between devices: 123 us -> 40.2 us
  Pallas kernels: 675 us -> 701 us
  starting transfers between devices: 22.2 us -> 0.11 us
  local copies, waits for them, and re-layouts: 63.2 us -> 48.5 us
    ppermute x42 -> x0, waiting for transfers between devices: 122 us -> none  [swap(): return lax.ppermute(x, axis, [(i, i ^ 1 << bit) for i in range(n)])]
    pallas_call x4 -> x3, Pallas kernels: 298 us -> 360 us  [the longest x1 159 us: attention_grads(): pl.pallas_call(functools.partial(attention_grads_kernel, orders=orders, l...]
    all_gather x1, waiting for transfers between devices: 0.02 us -> 38.8 us  [body(): cot_every = lax.all_gather(cotangent, 'tensor')]
    pallas_call x1, Pallas kernels: 201 us -> 178 us  [mlp(): pl.pallas_call(functools.partial(mlp_kernel, orders=orders), in_specs=[hb...]
    ppermute x42 -> x0, starting transfers between devices: 22.1 us -> none  [swap(): return lax.ppermute(x, axis, [(i, i ^ 1 << bit) for i in range(n)])]
    unnamed x172 -> x91, local copies, waits for them, and re-layouts: 44.4 us -> 31.7 us
    pallas_call x3 -> x2, Pallas kernels: 29.6 us -> 21.4 us  [slot_product(): pl.pallas_call(kernel, grid=(2,), in_specs=[flow(a) for a in tiled] + [st...]
  transfers between devices with their start and end apart: 44 -> 3, of which waited for: 12 -> 1; matrix products, arithmetic and copies ran while one was open for 6% -> 4% of each run, Pallas kernels for 32% -> 30%
where the time goes in v4:
time: 847 us; the launch traced here: 837 us
  Pallas kernels  701 us (83%)
  local copies, waits for them, and re-layouts  48.5 us (6%)
  waiting for transfers between devices  40.2 us (5%)
  other arithmetic  32.4 us (4%)
  between operations  14.8 us (2%)
    pallas_call x1, Pallas kernels, mlp(): pl.pallas_call(functools.partial(mlp_kernel, orders=orders), in_specs=[hb...  178 us
    pallas_call x1, Pallas kernels, attention_grads(): pl.pallas_call(functools.partial(attention_grads_kernel, orders=orders, l...  159 us
    pallas_call x1, Pallas kernels, last(): pl.pallas_call(functools.partial(last_kernel, order=order, line=line, eps...  116 us
    pallas_call x1, Pallas kernels, mlp_grads(): pl.pallas_call(functools.partial(mlp_grads_kernel, orders=orders), in_spe...  108 us
    pallas_call x1, Pallas kernels, first(): pl.pallas_call(functools.partial(first_kernel, orders=orders, factor=fact...  91.6 us
    all_gather x1, waiting for transfers between devices, body(): cot_every = lax.all_gather(cotangent, 'tensor')  38.8 us
    unnamed x91, local copies, waits for them, and re-layouts  31.7 us
    pallas_call x2, Pallas kernels, slot_product(): pl.pallas_call(kernel, grid=(2,), in_specs=[flow(a) for a in tiled] + [st...  21.4 us
  transfers between devices with their start and end apart: 3, of which 1 were waited for; matrix products, arithmetic and copies ran while one was open for 4% of the time, Pallas kernels for 30%

profile of v4, /device:TPU:0, one launch (start us, length us, event | category | flops | bytes accessed | tf_op | source)
XLA Modules:
  0.0 836.8 jit_solution(2709684573595321794)
XLA Ops:
  7.2 0.7 all-gather.5.cloned.1.call-update
  8.0 0.7 all-gather.7.cloned.1.call-update
  8.7 1.2 copy-done.16
  9.9 0.7 copy-done.19
  10.6 1.2 copy-done.20
  11.9 0.7 copy-done.21
  13.9 91.6 %shard_map.297 = (bf16[512,2048]{1,0:T(8,128)(2,1)S(1)}, bf16[8,2,256,256]{3,2,1,0:T(8,128)(2,1)}, bf16[8,2048,256]{2,1,0:T(8,128)(2,1)}, bf16[512,2048]{1,0:T(8,128)(2,1)}) custom-call(bf16[512,2048]{1,0:T(8,128)(2,1)} %bitcast.109, f32[1,2048]{1,0:T(1,128)S(1)} %bitcast.92, f32[1,2048]{1,0:T(1,128)S(1)} %bitcast.93, bf16[2048,256]{1,0:T(8,128)(2,1)S(1)} %copy-done.16, ...), custom_call_target="tpu_custom_call" | custom-call | flops 4294967296 | bytes 67108864 | tf_op jit(solution)/shard_map/pallas_call | solution.py:807
  105.6 2.7 copy.48
  108.3 1.9 fusion.4
  110.2 1.5 copy.49.vt_ref
  112.4 3.3 reshape.175.dock_ref
  116.2 1.6 copy-done.5
  117.8 1.2 copy-done.8
  119.0 1.6 copy-done.14
  120.6 1.2 copy-done.17
  121.9 11.2 %shard_map.298 = (bf16[2,256,2048]{2,1,0:T(8,128)(2,1)S(1)}, f32[2,8,1,512]{3,2,1,0:T(1,128)S(1)}) custom-call(s32[2]{0:T(128)S(1)} %fusion.2.low_ref, s32[1]{0:T(128)} %bitcast.at_ref, bf16[2,256,2048]{2,1,0:T(8,128)(2,1)S(1)} %bitcast.87, bf16[2,2048,128]{2,1,0:T(8,128)(2,1)S(1)} %copy-done.8, bf16[2,128,2048]{2,1,0:T(8,128)(2,1)S(1)} %copy-done.17, ...), custom_call_target="tpu_custom_call" | custom-call | flops 4294967296 | bytes 8388608 | tf_op jit(solution)/shard_map/pallas_call | solution.py:145
  133.2 11.8 %shard_map.299 = (f32[512,2048]{1,0:T(8,128)}, bf16[512,2048]{1,0:T(8,128)(2,1)S(1)}) custom-call(bf16[512,2048]{1,0:T(8,128)(2,1)S(1)} %bitcast.85, bf16[512,2048]{1,0:T(8,128)(2,1)} %bitcast.110, bf16[8,256,2048]{2,1,0:T(8,128)(2,1)} %bitcast.135, f32[1,2048]{1,0:T(1,128)S(1)} %bitcast.94, f32[1,2048]{1,0:T(1,128)S(1)} %bitcast.90, f32[1,2048]{1,0:T(1,128)S(1)} %bitcast.95), custom_call_target="tpu_custom_call" | custom-call | flops 4294967296 | bytes 16777216 | tf_op jit(solution)/shard_map/pallas_call | solution.py:242
  145.0 1.3 copy-done.26
  146.3 2.5 reduce_sum.91
  148.8 2.8 multiply_reduce_fusion.2
  151.6 38.8 %all-gather.7.cloned.1.call-done = bf16[16,256,2048]{2,1,0:T(8,128)(2,1)} async-done(((bf16[2,256,2048]{2,1,0:T(8,128)(2,1)}), bf16[16,256,2048]{2,1,0:T(8,128)(2,1)}) %all-gather.7.cloned.1.call-update) | async-done | bytes 16777232 | tf_op jit(solution)/shard_map/all_gather | solution.py:1249
  190.4 178.5 %shard_map.300 = (f32[2,256,2048]{2,1,0:T(8,128)}, f32[1,1024]{1,0:T(1,128)}, bf16[8,2,256,2048]{3,2,1,0:T(8,128)(2,1)}, bf16[8,2,256,1024]{3,2,1,0:T(8,128)(2,1...) custom-call(bf16[2,256,2048]{2,1,0:T(8,128)(2,1)} %bitcast.98, ...), custom_call_target="tpu_custom_call" | custom-call | flops 68719476736 | bytes 104857600 | tf_op jit(solution)/shard_map/pallas_call | solution.py:1074
  369.0 5.8 multiply_reduce_fusion.3
  375.0 1.8 copy-done.29
  377.5 2.6 fusion.3
  380.4 1.7 copy-done.28
  382.1 9.6 %shard_map.301 = bf16[512,2048]{1,0:T(8,128)(2,1)S(1)} custom-call(bf16[512,2048]{1,0:T(8,128)(2,1)S(1)} %bitcast.83, bf16[8,256,2048]{2,1,0:T(8,128)(2,1)} %bitcast.136), custom_call_target="tpu_custom_call" | custom-call | flops 4294967296 | bytes 16777216 | tf_op jit(solution)/shard_map/pallas_call | solution.py:242
  391.7 14.6 %shard_map.302 = (bf16[2,256,2048]{2,1,0:T(8,128)(2,1)S(1)}, f32[2,2048,128]{2,1,0:T(8,128)S(1)}, f32[2,2048,128]{2,1,0:T(8,128)S(1)}) custom-call(s32[2]{0:T(128)S(1)} %fusion.2.low_ref, s32[1]{0:T(128)} %bitcast.at_ref, bf16[2,256,2048]{2,1,0:T(8,128)(2,1)S(1)} %bitcast.88, bf16[2,256,2048]{2,1,0:T(8,128)(2,1)S(1)} %bitcast.89, ...), custom_call_target="tpu_custom_call" | custom-call | flops 1000 | bytes 1048576 | tf_op jit(solution)/shard_map/pallas_call | solution.py:180
  406.3 1.3 copy-done
  407.7 1.3 copy-done.10
  409.0 1.3 copy-done.12
  410.3 108.5 %shard_map.303 = (bf16[2048,1024]{1,0:T(8,128)(2,1)}, f32[2,256,2048]{2,1,0:T(8,128)}) custom-call(bf16[8,512,1024]{2,1,0:T(8,128)(2,1)} %bitcast.104, bf16[8,512,2048]{2,1,0:T(8,128)(2,1)} %bitcast.101, bf16[2,8,256,2048]{3,2,1,0:T(8,128)(2,1)} %get-tuple-element.51.part_ref, bf16[512,2048]{1,0:T(8,128)(2,1)} %bitcast.80), custom_call_target="tpu_custom_call" | custom-call | flops 1000 | bytes 1048576 | tf_op jit(solution)/shard_map/pallas_call | solution.py:1198
  519.0 1.4 copy-done.11
  521.0 1.5 copy.56
  523.5 5.8 add_convert_fusion
  529.4 159.4 %shard_map.304 = (bf16[2,256,1024]{2,1,0:T(8,128)(2,1)}, bf16[2,256,1024]{2,1,0:T(8,128)(2,1)}, bf16[512,256]{1,0:T(8,128)(2,1)}, bf16[8,256,1024]{2,1,0:T(8,128)(2,1)}) custom-call(bf16[512,2048]{1,0:T(8,128)(2,1)} %bitcast.86, bf16[512,2048]{1,0:T(8,128)(2,1)} %bitcast.84, bf16[512,2048]{1,0:T(8,128)(2,1)} %bitcast.81, bf16[512,2048]{1,0:T(8,128)(2,1)} %copy-done.2, ...), custom_call_target="tpu_custom_call" | custom-call | flops 1000 | bytes 1048576 | tf_op jit(solution)/shard_map/pallas_call | solution.py:495
  688.8 115.7 %shard_map.305 = (f32[256,2048]{1,0:T(8,128)}, f32[256,2048]{1,0:T(8,128)}, f32[512,2048]{1,0:T(8,128)}, f32[1,22656]{1,0:T(1,128)}, f32[2048,256]{1,0:T(8,128)}) custom-call(bf16[2,256,1024]{2,1,0:T(8,128)(2,1)} %get-tuple-element.61.wo_ref, bf16[2,256,1024]{2,1,0:T(8,128)(2,1)} %get-tuple-element.62.wq_ref, bf16[512,2048]{1,0:T(8,128)(2,1)} %bitcast.82, ...), custom_call_target="tpu_custom_call" | custom-call | flops 1000 | bytes 1048576 | tf_op jit(solution)/shard_map/pallas_call | solution.py:661
  804.4 1.4 fusion.5
  805.8 1.2 slice_bitcast_fusion
  807.0 0.8 split.54
  807.8 2.9 copy.55
  811.2 6.8 bitcast_convert_fusion
  818.6 4.4 convert_element_type.34
  823.1 2.1 copy.71
  825.2 1.0 copy-done.34
  826.2 1.3 copy.72
  827.5 1.0 copy-done.33
  828.5 1.3 copy.73
  (111 shorter events, 6.7 us)
Async XLA Ops:
  7.2 125.9 %all-gather.5.cloned.1.call-start = ((), (), s32[]{:S(2)}) async-start(), calls=%async_computation.1 | async-start | bytes 9437184 | tf_op jit(solution)/shard_map/all_gather | solution.py:1248
  7.9 182.5 %all-gather.7.cloned.1.call-start = ((), (), s32[]{:S(2)}) async-start(), calls=%async_computation.2 | async-start | bytes 18874368 | tf_op jit(solution)/shard_map/all_gather | solution.py:1249
  8.7 520.7 %all-reduce.2.cloned.1.call-start = ((), (), s32[]{:S(2)}) async-start(), calls=%async_computation | async-start | bytes 8388608 | tf_op jit(solution)/shard_map/psum | solution.py:1280
  8.7 1.2 copy-start.16
  9.9 0.7 copy-start.19
  10.6 1.2 copy-start.20
  11.9 0.7 copy-start.21
  12.6 0.7 copy-start.24
  13.2 0.7 copy-start.25
  105.5 4.7 copy-start.2
  108.3 3.4 copy-start.36
  108.3 3.6 copy-start.37
  116.2 1.6 copy-start.5
  117.8 1.2 copy-start.8
  119.0 1.6 copy-start.14
  120.6 1.2 copy-start.17
  121.9 11.3 %copy-start.18 = (f32[2048]{0:T(1024)S(1)}, f32[2048]{0:T(1024)}, u32[]{:S(2)}) copy-start(f32[2048]{0:T(1024)} %param.30) | copy-start | bytes 24580
  121.9 11.3 %copy-start.22 = (f32[2048]{0:T(1024)S(1)}, f32[2048]{0:T(1024)}, u32[]{:S(2)}) copy-start(f32[2048]{0:T(1024)} %param.29) | copy-start | bytes 24580
  121.9 11.3 %copy-start.23 = (f32[2048]{0:T(1024)S(1)}, f32[2048]{0:T(1024)}, u32[]{:S(2)}) copy-start(f32[2048]{0:T(1024)} %param.31) | copy-start | bytes 24580
  133.1 258.6 %copy-start.4 = (bf16[2,256,2048]{2,1,0:T(8,128)(2,1)}, bf16[2,256,2048]{2,1,0:T(8,128)(2,1)S(1)}, u32[]{:S(2)}) copy-start(bf16[2,256,2048]{2,1,0:T(8,128)(2,1)S(1)} %get-tuple-element.46.o_ref) | copy-start | bytes 6291460
  145.0 1.3 copy-start.26
  368.9 6.1 copy-start.27
  368.9 7.9 copy-start.29
  369.0 8.5 %copy-start.31 = (bf16[2,256,2048]{2,1,0:T(8,128)(2,1)S(1)}, bf16[2,256,2048]{2,1,0:T(8,128)(2,1)}, u32[]{:S(2)}) copy-start(bf16[2,256,2048]{2,1,0:T(8,128)(2,1)} %param.19) | copy-start | bytes 6291460
  380.0 2.0 copy-start.28
  382.1 9.6 %copy-start.3 = (bf16[2,256,2048]{2,1,0:T(8,128)(2,1)}, bf16[2,256,2048]{2,1,0:T(8,128)(2,1)S(1)}, u32[]{:S(2)}) copy-start(bf16[2,256,2048]{2,1,0:T(8,128)(2,1)S(1)} %convert_element_type.29) | copy-start | bytes 6291460
  382.1 9.6 %copy-start.6 = (s32[2,2048,1]{2,1,0:T(8,128)S(1)}, s32[2,2048,1]{2,1,0:T(8,128)}, u32[]{:S(2)}) copy-start(s32[2,2048,1]{2,1,0:T(8,128)} %reshape.175.dock_ref) | copy-start | bytes 49156
  382.1 9.6 %copy-start.7 = (bf16[2,2048,128]{2,1,0:T(8,128)(2,1)S(1)}, bf16[2,2048,128]{2,1,0:T(8,128)(2,1)}, u32[]{:S(2)}) copy-start(bf16[2,2048,128]{2,1,0:T(8,128)(2,1)} %get-tuple-element.127.v_ref) | copy-start | bytes 3145732
  382.1 9.6 %copy-start.9 = (bf16[2,2048,128]{2,1,0:T(8,128)(2,1)S(1)}, bf16[2,2048,128]{2,1,0:T(8,128)(2,1)}, u32[]{:S(2)}) copy-start(bf16[2,2048,128]{2,1,0:T(8,128)(2,1)} %get-tuple-element.130.k_ref) | copy-start | bytes 3145732
  382.1 9.6 %copy-start.15 = (bf16[512,2048]{1,0:T(8,128)(2,1)S(1)}, bf16[512,2048]{1,0:T(8,128)(2,1)}, u32[]{:S(2)}) copy-start(bf16[512,2048]{1,0:T(8,128)(2,1)} %get-tuple-element.44) | copy-start | bytes 6291460
  406.3 1.3 copy-start
  407.7 1.3 copy-start.10
  409.0 1.3 copy-start.12
  410.3 108.5 %copy-start.13 = (f32[2,2048,128]{2,1,0:T(8,128)S(1)}, f32[2,2048,128]{2,1,0:T(8,128)}, u32[]{:S(2)}) copy-start(f32[2,2048,128]{2,1,0:T(8,128)} %copy-done.12) | copy-start | bytes 6291460
  518.8 1.6 copy-start.11
  520.6 1.9 copy-start.1
  521.0 2.2 copy-start.39
  521.0 2.6 copy-start.38
  523.5 5.8 copy-start.35
  811.2 7.4 copy-start.30
  818.6 4.5 copy-start.32
  823.1 3.1 copy-start.34
  826.2 2.3 copy-start.33
Sparse Core Ops, SparseCore 0:
  9.9 88.3 all-gather.4
  100.2 90.1 all-gather.6
  369.1 155.1 all-reduce.1

commit v5 on v4

--- a/solution.py
+++ b/solution.py
@@ -455,23 +455,24 @@
 
     products(0)
     stage(0, 1)
+    chain_to(1)
     products(1)
-    chain_to(1)
+    chain_to(3)
     for i in range(1, count):
         kv_stage(i)
         if i + 1 < count:
             stage(0, i + 1)
-            chain_to(i + 1)
+            chain_to(2 * i + 2)
         else:
-            chain_to(3)
+            chain_to(7)
             finish(0)
+            chain_to(8)
         stage(1, i)
-    chain_to(4)
+    chain_to(10)
     kv_ref[...] = kv.total(0).astype(BF)
-    chain_to(5)
+    chain_to(pieces)
     finish(1)
     if line:
-        chain_to(pieces)
         chain.back(pieces - 1)
         for i in range(pieces):
             chain.close(i)
@@ -487,7 +488,7 @@
     qw = a.shape[1] // n
     slot = dkv.shape[1:]
     rows, cols = up.shape
-    pieces = 8
+    pieces = rows // 128
     up = up.reshape(pieces, rows // pieces, cols)
     wait = up.shape if line else (1, 16, 128)
     dma = pltpu.SemaphoreType.DMA
@@ -525,8 +526,8 @@
     count = len(order) + 1
     n = 1 << count
     (wog_ref, wqg_ref, grad_ref, late_ref, sg_ref,
-     w_s, near, far, part, send, recv, dsend, drecv, piece_s, gathered, vsend, vrecv,
-     zsem, ssem, rsem, dsem, gsem, vsem) = refs
+     w_s, near, far, part, send, recv, dsend, drecv, piece_s, gathered, vsend, vrecv, esend, erecv,
+     zsem, ssem, rsem, dsem, gsem, vsem, esem) = refs
     me, z = lax.axis_index("tensor"), lax.axis_index("dp")
     dp_bits = range(lax.axis_size("dp").bit_length() - 1)
     tokens, d = x_ref.shape
@@ -534,27 +535,28 @@
     piece = d // n
     greet(range(count), line, dp_bits)
 
-    owns = [wo_ref.at[0], wo_ref.at[1], wq_ref.at[0], wq_ref.at[1]]
+    pieces = wo_ref.shape[0]
+    owns = (wo_ref, wq_ref)
     chains = []
     if line:
-        for i, ref in enumerate((wo_ref, wq_ref)):
-            c = Line(ref, near.at[i], far.at[i], zsem.at[i])
-            c.values = [lambda ref=ref, p=p: ref[p] for p in range(2)]
-            chains.append(c)
-            for p in range(2):
-                c.start(p)
-
+        for i, ref in enumerate(owns):
+            chains.append(Line(ref, near.at[i], far.at[i], zsem.at[i]))
     ahead = [0, 0]
 
-    def chain_to(middles, backs):
-        while line and ahead[0] < min(middles, 4):
-            i, p = divmod(ahead[0], 2)
-            chains[i].middle(p, chains[i].values[p])
+    def chain_to(middles):
+        while line and ahead[1] < min(middles + 2, len(owns) * pieces):
+            i, p = divmod(ahead[1], pieces)
+            chains[i].start(p)
+            ahead[1] += 1
+        while line and ahead[0] < min(middles, len(owns) * pieces):
+            i, p = divmod(ahead[0], pieces)
+            chains[i].middle(p, lambda: owns[i][p])
             ahead[0] += 1
-        while line and ahead[1] < min(backs, 4):
-            i, p = divmod(ahead[1], 2)
-            chains[i].back(p)
-            ahead[1] += 1
+            if ahead[0] > 1:
+                i, p = divmod(ahead[0] - 2, pieces)
+                chains[i].back(p)
+
+    chain_to(0)
 
     part[...] = dot_tn(h_ref[...], kv_ref[...])
     scatter = Scatter([0] + list(order)[::-1], send, recv, ssem, rsem)
@@ -562,11 +564,58 @@
         scatter.put(k, part[pl.ds(pl.multiple_of((me ^ k) * piece, piece), piece), :])
     for k in range(n):
         w_s[:, k * w_ref.shape[2] : (k + 1) * w_ref.shape[2]] = w_ref[k]
+    hops = [("tensor", me, b) for b in range(count)] + [("dp", z, b) for b in dp_bits]
+    pending = []
+
+    def swap_start(buffers, sems, value, i, axis, at, bit):
+        buffers[0][i] = value
+        c = pltpu.make_async_remote_copy(
+            src_ref=buffers[0].at[i], dst_ref=buffers[1].at[i], send_sem=sems.at[0, i], recv_sem=sems.at[1, i],
+            device_id={axis: at ^ (1 << bit)}, device_id_type=MESH,
+        )
+        c.start()
+        pending.append(c)
+        return lambda value: (c.wait_recv(), value + buffers[1][i])[1]
+
+    size = 2 * d + hd
+    tail = late_ref.at[:, size:]
+    front = late_ref.at[:, :size]
+    early_done, last_done, piece_done = [None], [None], [None]
+
+    def early(i):
+        if early_done[0] is not None:
+            tail[...] = early_done[0](tail[...])
+            early_done[0] = None
+        if i < len(hops):
+            early_done[0] = swap_start((esend, erecv), esem, tail[...], i, *hops[i])
+
+    def late(i):
+        if last_done[0] is not None:
+            front[...] = last_done[0](front[...])
+            last_done[0] = None
+        if i < len(hops):
+            last_done[0] = swap_start((vsend, vrecv), vsem, front[...], i, *hops[i])
+
+    def shared_sum(i):
+        if piece_done[0] is not None:
+            piece_s[...] = piece_done[0](piece_s[...])
+            piece_done[0] = None
+        if i < len(dp_bits):
+            piece_done[0] = swap_start((dsend, drecv), dsem, piece_s[...], i, "dp", z, dp_bits[i])
+
+    tail[...] = qb_ref[...]
+    early(0)
+    at = 1
+    chain_to(at)
     for i in range(1, count):
         for k in scatter_order(scatter.bits):
             if scatter.stage(k) == i:
                 scatter.forward(k)
-    chain_to(1, 0)
+        early(i)
+        at += 1
+        chain_to(at)
+    piece_s[...] = scatter.total(0)
+    shared_sum(0)
 
     gain_part, shift_part = jnp.zeros((1, d), F32), jnp.zeros((1, d), F32)
     for t in range(tokens // eps_rows):
@@ -578,44 +627,24 @@
         grad_ref[rows] = mixed_ref[rows] + scale * back
         gain_part += jnp.sum(grad * unit, axis=0, keepdims=True)
         shift_part += jnp.sum(grad, axis=0, keepdims=True)
-        chain_to(2 + t, 1 + t)
-    at = 0
-    for value in (gain_part, shift_part, jnp.sum(kv_ref[:, hd:].astype(F32), axis=0, keepdims=True), qb_ref[...]):
-        late_ref[:, at : at + value.shape[1]] = value
-        at += value.shape[1]
-
-    hops = [("tensor", me, b) for b in range(count)] + [("dp", z, b) for b in dp_bits]
-
-    def small(buffers, sems, i, axis, at, bit):
-        return pltpu.make_async_remote_copy(
-            src_ref=buffers[0].at[i], dst_ref=buffers[1].at[i], send_sem=sems.at[0, i], recv_sem=sems.at[1, i],
-            device_id={axis: at ^ (1 << bit)}, device_id_type=MESH,
-        )
-
-    piece_s[...] = scatter.total(0)
-    pending = []
-    for i, (axis, at, bit) in enumerate(hops):
-        vsend[i] = late_ref[...]
-        c = small((vsend, vrecv), vsem, i, axis, at, bit)
-        c.start()
-        j = i if i < len(dp_bits) else None
-        if j is not None:
-            dsend[j] = piece_s[...]
-            e = small((dsend, drecv), dsem, j, "dp", z, dp_bits[j])
-            e.start()
-        if i:
-            chain_to(3 + i, 2 + i)
-        c.wait_recv()
-        late_ref[...] = late_ref[...] + vrecv[i]
-        pending.append(c)
-        if j is not None:
-            e.wait_recv()
-            piece_s[...] = piece_s[...] + drecv[j]
-            pending.append(e)
-        if j == len(dp_bits) - 1:
-            gathered[me] = piece_s[...].astype(BF)
-            held = [0]
-    sent = []
+        if t + 1 < len(dp_bits):
+            shared_sum(t + 1)
+        if count + t < len(hops):
+            early(count + t)
+        at += 2
+        chain_to(at)
+    late_ref[:, :d] = gain_part
+    late_ref[:, d : 2 * d] = shift_part
+    late_ref[:, 2 * d : size] = jnp.sum(kv_ref[:, hd:].astype(F32), axis=0, keepdims=True)
+    late(0)
+    for i in range(max(tokens // eps_rows + 1, 1), len(dp_bits) + 1):
+        shared_sum(i)
+    shared_sum(len(dp_bits))
+    for i in range(count + tokens // eps_rows, len(hops) + 1):
+        early(i)
+    early(len(hops))
+    gathered[me] = piece_s[...].astype(BF)
+    sent, held, step = [], [0], 0
     for bit in list(order) + [0]:
         new = []
         for k in held:
@@ -626,21 +655,33 @@
             c.start()
             sent.append(c)
             new.append(c)
+        step += 1
+        late(step)
+        at += 1
+        chain_to(at)
         for c in new:
             c.wait_recv()
         held = held + [k | (1 << bit) for k in held]
-    chain_to(4, 4)
+    while step < len(hops):
+        step += 1
+        late(step)
+        at += 1
+        chain_to(at)
+    chain_to(len(owns) * pieces)
+    if line:
+        chains[-1].back(pieces - 1)
     for k in range(n):
         sg_ref[k * piece : (k + 1) * piece] = gathered[k].astype(F32)
     if line:
         for c in chains:
-            for p in range(2):
+            for p in range(pieces):
                 c.close(p)
-    half = d // 2
-    for i, ref in enumerate((wog_ref, wqg_ref)):
-        for p in range(2):
-            value = near[i, p] if line else (wo_ref, wq_ref)[i][p]
-            ref[:, p * half : (p + 1) * half] = value.astype(F32)
+    half, high = d // 2, wo_ref.shape[1]
+    for j in range(pieces):
+        values = [near[i, j] if line else owns[i][j] for i in range(len(owns))]
+        p, q = divmod(j, pieces // 2)
+        for ref, value in zip((wog_ref, wqg_ref), values):
+            ref[q * high : (q + 1) * high, p * half : (p + 1) * half] = value.astype(F32)
     for c in pending + sent:
         c.wait_send()
     scatter.drain()
@@ -651,13 +692,15 @@
     line = dp == 4
     tokens, d = x.shape
     qw = wo.shape[1]
+    cuts = 4
+    wo, wq = (v.reshape(cuts, -1, d // 2) for v in (wo, wq))
     piece, width = d // n, kv.shape[1]
     size = 2 * d + qb.shape[1] + width // 2
     bits = n.bit_length() - 1
     dbits = dp.bit_length() - 1
     dma = pltpu.SemaphoreType.DMA
     vmem = pl.BlockSpec(memory_space=pltpu.VMEM)
-    item = (2, 2, qw, d // 2)
+    item = (2,) + wo.shape
     return pl.pallas_call(
         functools.partial(last_kernel, order=order, line=line, eps_rows=tokens // 2),
         in_specs=[vmem] * 11,
@@ -680,9 +723,11 @@
             pltpu.VMEM((dbits, piece, width), F32),
             pltpu.VMEM((piece, width), F32),
             pltpu.VMEM((n, piece, width), BF),
-            pltpu.VMEM((bits + dbits, 1, size), F32),
-            pltpu.VMEM((bits + dbits, 1, size), F32),
-            dma((2, 2, 3, 2)), dma((n,)), dma((n,)), dma((2, dbits)), dma((2, n)), dma((2, bits + dbits)),
+            pltpu.VMEM((bits + dbits, 1, size - qb.shape[1]), F32),
+            pltpu.VMEM((bits + dbits, 1, size - qb.shape[1]), F32),
+            pltpu.VMEM((bits + dbits,) + qb.shape, F32),
+            pltpu.VMEM((bits + dbits,) + qb.shape, F32),
+            dma((2, 2, 3, cuts)), dma((n,)), dma((n,)), dma((2, dbits)), dma((2, n)), dma((2, bits + dbits)), dma((2, bits + dbits)),
         ],
         compiler_params=pltpu.CompilerParams(
             collective_id=4, has_side_effects=True, vmem_limit_bytes=60 * MIB

time: 847 us -> 815 us (0.962)
  Pallas kernels: 701 us -> 666 us
    pallas_call x1, Pallas kernels: 159 us -> 131 us  [attention_grads(): pl.pallas_call(functools.partial(attention_grads_kernel, orders=orders, l...]
    pallas_call x1, Pallas kernels: 116 us -> 102 us  [last(): pl.pallas_call(functools.partial(last_kernel, order=order, line=line, eps...]
  transfers between devices with their start and end apart: 3 -> 3, of which waited for: 1 -> 1; matrix products, arithmetic and copies ran while one was open for 4% -> 4% of each run, Pallas kernels for 30% -> 32%
where the time goes in v5:
time: 815 us; the launch traced here: 802 us
  Pallas kernels  666 us (82%)
  local copies, waits for them, and re-layouts  48.5 us (6%)
  waiting for transfers between devices  40.2 us (5%)
  other arithmetic  32.4 us (4%)
  between operations  14.8 us (2%)
    pallas_call x1, Pallas kernels, mlp(): pl.pallas_call(functools.partial(mlp_kernel, orders=orders), in_specs=[hb...  178 us
    pallas_call x1, Pallas kernels, attention_grads(): pl.pallas_call(functools.partial(attention_grads_kernel, orders=orders, l...  131 us
    pallas_call x1, Pallas kernels, mlp_grads(): pl.pallas_call(functools.partial(mlp_grads_kernel, orders=orders), in_spe...  115 us
    pallas_call x1, Pallas kernels, last(): pl.pallas_call(functools.partial(last_kernel, order=order, line=line, eps...  102 us
    pallas_call x1, Pallas kernels, first(): pl.pallas_call(functools.partial(first_kernel, orders=orders, factor=fact...  91.6 us
    all_gather x1, waiting for transfers between devices, body(): cot_every = lax.all_gather(cotangent, 'tensor')  38.8 us
    unnamed x91, local copies, waits for them, and re-layouts  31.7 us
    pallas_call x2, Pallas kernels, slot_product(): pl.pallas_call(kernel, grid=(2,), in_specs=[flow(a) for a in tiled] + [st...  21.4 us
  transfers between devices with their start and end apart: 3, of which 1 were waited for; matrix products, arithmetic and copies ran while one was open for 4% of the time, Pallas kernels for 32%

profile of v5, /device:TPU:0, one launch (start us, length us, event | category | flops | bytes accessed | tf_op | source)
XLA Modules:
  0.0 801.7 jit_solution(8389673082651756862)
XLA Ops:
  7.2 0.7 all-gather.5.cloned.1.call-update
  8.0 0.7 all-gather.7.cloned.1.call-update
  8.7 1.2 copy-done.16
  9.9 0.7 copy-done.19
  10.6 1.2 copy-done.20
  11.9 0.7 copy-done.21
  13.9 91.6 %shard_map.297 = (bf16[512,2048]{1,0:T(8,128)(2,1)S(1)}, bf16[8,2,256,256]{3,2,1,0:T(8,128)(2,1)}, bf16[8,2048,256]{2,1,0:T(8,128)(2,1)}, bf16[512,2048]{1,0:T(8,128)(2,1)}) custom-call(bf16[512,2048]{1,0:T(8,128)(2,1)} %bitcast.111, f32[1,2048]{1,0:T(1,128)S(1)} %bitcast.94, f32[1,2048]{1,0:T(1,128)S(1)} %bitcast.95, bf16[2048,256]{1,0:T(8,128)(2,1)S(1)} %copy-done.16, ...), custom_call_target="tpu_custom_call" | custom-call | flops 4294967296 | bytes 67108864 | tf_op jit(solution)/shard_map/pallas_call | solution.py:852
  105.6 2.7 copy.48
  108.3 1.9 fusion.4
  110.2 1.5 copy.49.vt_ref
  112.4 3.3 reshape.183.dock_ref
  116.2 1.6 copy-done.5
  117.8 1.2 copy-done.8
  119.0 1.6 copy-done.14
  120.6 1.2 copy-done.17
  121.9 11.2 %shard_map.298 = (bf16[2,256,2048]{2,1,0:T(8,128)(2,1)S(1)}, f32[2,8,1,512]{3,2,1,0:T(1,128)S(1)}) custom-call(s32[2]{0:T(128)S(1)} %fusion.2.low_ref, s32[1]{0:T(128)} %bitcast.at_ref, bf16[2,256,2048]{2,1,0:T(8,128)(2,1)S(1)} %bitcast.89, bf16[2,2048,128]{2,1,0:T(8,128)(2,1)S(1)} %copy-done.8, bf16[2,128,2048]{2,1,0:T(8,128)(2,1)S(1)} %copy-done.17, ...), custom_call_target="tpu_custom_call" | custom-call | flops 4294967296 | bytes 8388608 | tf_op jit(solution)/shard_map/pallas_call | solution.py:145
  133.2 11.8 %shard_map.299 = (f32[512,2048]{1,0:T(8,128)}, bf16[512,2048]{1,0:T(8,128)(2,1)S(1)}) custom-call(bf16[512,2048]{1,0:T(8,128)(2,1)S(1)} %bitcast.87, bf16[512,2048]{1,0:T(8,128)(2,1)} %bitcast.112, bf16[8,256,2048]{2,1,0:T(8,128)(2,1)} %bitcast.139, f32[1,2048]{1,0:T(1,128)S(1)} %bitcast.96, f32[1,2048]{1,0:T(1,128)S(1)} %bitcast.92, f32[1,2048]{1,0:T(1,128)S(1)} %bitcast.97), custom_call_target="tpu_custom_call" | custom-call | flops 4294967296 | bytes 16777216 | tf_op jit(solution)/shard_map/pallas_call | solution.py:242
  145.0 1.3 copy-done.26
  146.3 2.5 reduce_sum.91
  148.8 2.8 multiply_reduce_fusion.2
  151.6 38.8 %all-gather.7.cloned.1.call-done = bf16[16,256,2048]{2,1,0:T(8,128)(2,1)} async-done(((bf16[2,256,2048]{2,1,0:T(8,128)(2,1)}), bf16[16,256,2048]{2,1,0:T(8,128)(2,1)}) %all-gather.7.cloned.1.call-update) | async-done | bytes 16777232 | tf_op jit(solution)/shard_map/all_gather | solution.py:1294
  190.4 178.5 %shard_map.300 = (f32[2,256,2048]{2,1,0:T(8,128)}, f32[1,1024]{1,0:T(1,128)}, bf16[8,2,256,2048]{3,2,1,0:T(8,128)(2,1)}, bf16[8,2,256,1024]{3,2,1,0:T(8,128)(2,1...) custom-call(bf16[2,256,2048]{2,1,0:T(8,128)(2,1)} %bitcast.100, ...), custom_call_target="tpu_custom_call" | custom-call | flops 68719476736 | bytes 104857600 | tf_op jit(solution)/shard_map/pallas_call | solution.py:1119
  369.0 5.8 multiply_reduce_fusion.3
  375.0 1.8 copy-done.29
  377.5 2.6 fusion.3
  380.4 1.7 copy-done.28
  382.1 9.6 %shard_map.301 = bf16[512,2048]{1,0:T(8,128)(2,1)S(1)} custom-call(bf16[512,2048]{1,0:T(8,128)(2,1)S(1)} %bitcast.85, bf16[8,256,2048]{2,1,0:T(8,128)(2,1)} %bitcast.140), custom_call_target="tpu_custom_call" | custom-call | flops 4294967296 | bytes 16777216 | tf_op jit(solution)/shard_map/pallas_call | solution.py:242
  391.7 14.6 %shard_map.302 = (bf16[2,256,2048]{2,1,0:T(8,128)(2,1)S(1)}, f32[2,2048,128]{2,1,0:T(8,128)S(1)}, f32[2,2048,128]{2,1,0:T(8,128)S(1)}) custom-call(s32[2]{0:T(128)S(1)} %fusion.2.low_ref, s32[1]{0:T(128)} %bitcast.at_ref, bf16[2,256,2048]{2,1,0:T(8,128)(2,1)S(1)} %bitcast.90, bf16[2,256,2048]{2,1,0:T(8,128)(2,1)S(1)} %bitcast.91, ...), custom_call_target="tpu_custom_call" | custom-call | flops 1000 | bytes 1048576 | tf_op jit(solution)/shard_map/pallas_call | solution.py:180
  406.3 1.3 copy-done
  407.7 1.3 copy-done.10
  409.0 1.3 copy-done.12
  410.3 114.7 %shard_map.303 = (bf16[2048,1024]{1,0:T(8,128)(2,1)}, f32[2,256,2048]{2,1,0:T(8,128)}) custom-call(bf16[8,512,1024]{2,1,0:T(8,128)(2,1)} %bitcast.106, bf16[8,512,2048]{2,1,0:T(8,128)(2,1)} %bitcast.103, bf16[2,8,256,2048]{3,2,1,0:T(8,128)(2,1)} %get-tuple-element.51.part_ref, bf16[512,2048]{1,0:T(8,128)(2,1)} %bitcast.82), custom_call_target="tpu_custom_call" | custom-call | flops 1000 | bytes 1048576 | tf_op jit(solution)/shard_map/pallas_call | solution.py:1243
  525.2 1.4 copy-done.11
  527.2 1.5 copy.56
  529.8 5.8 add_convert_fusion
  535.6 131.4 %shard_map.304 = (bf16[2,256,1024]{2,1,0:T(8,128)(2,1)}, bf16[2,256,1024]{2,1,0:T(8,128)(2,1)}, bf16[512,256]{1,0:T(8,128)(2,1)}, bf16[16,128,1024]{2,1,0:T(8,128)(2,1)}) custom-call(bf16[512,2048]{1,0:T(8,128)(2,1)} %bitcast.88, bf16[512,2048]{1,0:T(8,128)(2,1)} %bitcast.86, bf16[512,2048]{1,0:T(8,128)(2,1)} %bitcast.83, bf16[512,2048]{1,0:T(8,128)(2,1)} %copy-done.2, ...), custom_call_target="tpu_custom_call" | custom-call | flops 1000 | bytes 1048576 | tf_op jit(solution)/shard_map/pallas_call | solution.py:496
  667.1 102.2 %shard_map.305 = (f32[256,2048]{1,0:T(8,128)}, f32[256,2048]{1,0:T(8,128)}, f32[512,2048]{1,0:T(8,128)}, f32[1,22656]{1,0:T(1,128)}, f32[2048,256]{1,0:T(8,128)}) custom-call(bf16[4,128,1024]{2,1,0:T(8,128)(2,1)} %bitcast.116, bf16[4,128,1024]{2,1,0:T(8,128)(2,1)} %bitcast.117, bf16[512,2048]{1,0:T(8,128)(2,1)} %bitcast.84, ...), custom_call_target="tpu_custom_call" | custom-call | flops 1000 | bytes 1048576 | tf_op jit(solution)/shard_map/pallas_call | solution.py:704
  769.2 1.4 fusion.5
  770.7 1.2 slice_bitcast_fusion
  771.9 0.8 split.54
  772.6 2.9 copy.55
  776.1 6.8 bitcast_convert_fusion
  783.5 4.4 convert_element_type.34
  787.9 2.1 copy.71
  790.0 1.0 copy-done.34
  791.0 1.3 copy.72
  792.3 1.0 copy-done.33
  793.4 1.3 copy.73
  (111 shorter events, 6.7 us)
Async XLA Ops:
  7.2 125.9 %all-gather.5.cloned.1.call-start = ((), (), s32[]{:S(2)}) async-start(), calls=%async_computation.1 | async-start | bytes 9437184 | tf_op jit(solution)/shard_map/all_gather | solution.py:1293
  7.9 182.5 %all-gather.7.cloned.1.call-start = ((), (), s32[]{:S(2)}) async-start(), calls=%async_computation.2 | async-start | bytes 18874368 | tf_op jit(solution)/shard_map/all_gather | solution.py:1294
  8.7 526.9 %all-reduce.2.cloned.1.call-start = ((), (), s32[]{:S(2)}) async-start(), calls=%async_computation | async-start | bytes 8388608 | tf_op jit(solution)/shard_map/psum | solution.py:1325
  8.7 1.2 copy-start.16
  9.9 0.7 copy-start.19
  10.6 1.2 copy-start.20
  11.9 0.7 copy-start.21
  12.6 0.7 copy-start.24
  13.2 0.7 copy-start.25
  105.5 4.7 copy-start.2
  108.3 3.4 copy-start.36
  108.3 3.6 copy-start.37
  116.2 1.6 copy-start.5
  117.8 1.2 copy-start.8
  119.0 1.6 copy-start.14
  120.6 1.2 copy-start.17
  121.9 11.3 %copy-start.18 = (f32[2048]{0:T(1024)S(1)}, f32[2048]{0:T(1024)}, u32[]{:S(2)}) copy-start(f32[2048]{0:T(1024)} %param.30) | copy-start | bytes 24580
  121.9 11.3 %copy-start.22 = (f32[2048]{0:T(1024)S(1)}, f32[2048]{0:T(1024)}, u32[]{:S(2)}) copy-start(f32[2048]{0:T(1024)} %param.29) | copy-start | bytes 24580
  121.9 11.3 %copy-start.23 = (f32[2048]{0:T(1024)S(1)}, f32[2048]{0:T(1024)}, u32[]{:S(2)}) copy-start(f32[2048]{0:T(1024)} %param.31) | copy-start | bytes 24580
  133.1 258.6 %copy-start.4 = (bf16[2,256,2048]{2,1,0:T(8,128)(2,1)}, bf16[2,256,2048]{2,1,0:T(8,128)(2,1)S(1)}, u32[]{:S(2)}) copy-start(bf16[2,256,2048]{2,1,0:T(8,128)(2,1)S(1)} %get-tuple-element.46.o_ref) | copy-start | bytes 6291460
  145.0 1.3 copy-start.26
  368.9 6.1 copy-start.27
  368.9 7.9 copy-start.29
  369.0 8.5 %copy-start.31 = (bf16[2,256,2048]{2,1,0:T(8,128)(2,1)S(1)}, bf16[2,256,2048]{2,1,0:T(8,128)(2,1)}, u32[]{:S(2)}) copy-start(bf16[2,256,2048]{2,1,0:T(8,128)(2,1)} %param.19) | copy-start | bytes 6291460
  380.0 2.0 copy-start.28
  382.1 9.6 %copy-start.3 = (bf16[2,256,2048]{2,1,0:T(8,128)(2,1)}, bf16[2,256,2048]{2,1,0:T(8,128)(2,1)S(1)}, u32[]{:S(2)}) copy-start(bf16[2,256,2048]{2,1,0:T(8,128)(2,1)S(1)} %convert_element_type.29) | copy-start | bytes 6291460
  382.1 9.6 %copy-start.6 = (s32[2,2048,1]{2,1,0:T(8,128)S(1)}, s32[2,2048,1]{2,1,0:T(8,128)}, u32[]{:S(2)}) copy-start(s32[2,2048,1]{2,1,0:T(8,128)} %reshape.183.dock_ref) | copy-start | bytes 49156
  382.1 9.6 %copy-start.7 = (bf16[2,2048,128]{2,1,0:T(8,128)(2,1)S(1)}, bf16[2,2048,128]{2,1,0:T(8,128)(2,1)}, u32[]{:S(2)}) copy-start(bf16[2,2048,128]{2,1,0:T(8,128)(2,1)} %get-tuple-element.127.v_ref) | copy-start | bytes 3145732
  382.1 9.6 %copy-start.9 = (bf16[2,2048,128]{2,1,0:T(8,128)(2,1)S(1)}, bf16[2,2048,128]{2,1,0:T(8,128)(2,1)}, u32[]{:S(2)}) copy-start(bf16[2,2048,128]{2,1,0:T(8,128)(2,1)} %get-tuple-element.130.k_ref) | copy-start | bytes 3145732
  382.1 9.6 %copy-start.15 = (bf16[512,2048]{1,0:T(8,128)(2,1)S(1)}, bf16[512,2048]{1,0:T(8,128)(2,1)}, u32[]{:S(2)}) copy-start(bf16[512,2048]{1,0:T(8,128)(2,1)} %get-tuple-element.44) | copy-start | bytes 6291460
  406.3 1.3 copy-start
  407.7 1.3 copy-start.10
  409.0 1.3 copy-start.12
  410.3 114.8 %copy-start.13 = (f32[2,2048,128]{2,1,0:T(8,128)S(1)}, f32[2,2048,128]{2,1,0:T(8,128)}, u32[]{:S(2)}) copy-start(f32[2,2048,128]{2,1,0:T(8,128)} %copy-done.12) | copy-start | bytes 6291460
  525.1 1.6 copy-start.11
  526.9 1.9 copy-start.1
  527.2 2.2 copy-start.39
  527.2 2.6 copy-start.38
  529.8 5.8 copy-start.35
  776.1 7.4 copy-start.30
  783.5 4.5 copy-start.32
  787.9 3.1 copy-start.34
  791.0 2.3 copy-start.33
Sparse Core Ops, SparseCore 0:
  9.9 88.3 all-gather.4
  100.2 90.1 all-gather.6
  369.1 155.1 all-reduce.1

commit v6 on v5

--- a/solution.py
+++ b/solution.py
@@ -777,8 +777,8 @@
             c.wait_send()
 
 
-def first_kernel(x_ref, gain_ref, shift_ref, shared_ref, vb_ref, wq_ref, bq_ref, h_ref, kv_ref, w_ref, q_ref,
-                 bias, send_sem, recv_sem, *, orders, factor, rows):
+def first_kernel(x_ref, gain_ref, shift_ref, shared_ref, vb_ref, wq_ref, bq_ref, h_ref, k_ref, kt_ref, v_ref, vt_ref,
+                 w_ref, q_ref, kv_ref, bias, send_sem, recv_sem, *, orders, factor, rows):
     n, d, qw = w_ref.shape
     seqs, span = kv_ref.shape[1:3]
     hd = vb_ref.shape[1]
@@ -830,15 +830,22 @@
                     for before in range(t - 1, -1, -1):
                         for k in g.at_step(p, before):
                             g.hop(p, k, g.paths[p][t])
+    for k in range(n):
+        here = slice(k * span, (k + 1) * span)
+        for r in range(seqs):
+            if k % 2:
+                shared.arrived(r, k)
+            block = kv_ref[k, r]
+            k_ref[r, here, :] = block[:, :hd]
+            v_ref[r, here, :] = block[:, hd:]
+            kt_ref[r, :, here] = block[:, :hd].T
+            vt_ref[r, :, here] = block[:, hd:].T
     for k in range(1, n, 2):
         for p in range(2):
             weights.arrived(p, k)
         product(k)
         if k > 1:
             product(k - 1)
-    for k in range(1, n, 2):
-        for p in range(2):
-            shared.arrived(p, k)
     weights.drain()
     shared.drain()
 
@@ -846,20 +853,24 @@
 def first(x, gain, shift, shared, vb, wq, bq, seqs, factor, orders):
     n = lax.axis_size("tensor")
     tokens, d = x.shape
-    qw = wq.shape[1]
+    qw, hd = wq.shape[1], vb.shape[1]
+    span = tokens // seqs
+    plain = jax.ShapeDtypeStruct((seqs, n * span, hd), BF)
+    turned = jax.ShapeDtypeStruct((seqs, hd, n * span), BF)
     dma = pltpu.SemaphoreType.DMA
     vmem = pl.BlockSpec(memory_space=pltpu.VMEM)
     return pl.pallas_call(
         functools.partial(first_kernel, orders=orders, factor=factor, rows=tokens // 4),
         in_specs=[vmem] * 7,
-        out_specs=[vmem] * 4,
+        out_specs=[vmem] * 7,
         out_shape=[
             jax.ShapeDtypeStruct((tokens, d), BF),
-            jax.ShapeDtypeStruct((n, seqs, tokens // seqs, shared.shape[1]), BF),
+            plain, turned, plain, turned,
             jax.ShapeDtypeStruct((n, d, qw), BF),
             jax.ShapeDtypeStruct((tokens, n * qw), BF),
         ],
         scratch_shapes=[
+            pltpu.VMEM((n, seqs, span, 2 * hd), BF),
             pltpu.VMEM((2, n, 1, qw), F32),
             dma((2, 2, 2, n)), dma((2, 2, 2, n)),
         ],
@@ -1166,7 +1177,7 @@
         return k // 2 if k % 2 == 0 else -k
 
 
-def mlp_grads_kernel(gr_ref, x_ref, part_ref, after_ref, up_ref, ff_ref,
+def mlp_grads_kernel(gr_ref, x_ref, part_ref, mixed_ref, bias_ref, after_ref, up_ref, ff_ref,
                      a_s, b_s, acc, send, recv, ssem, rsem, load, own, *, orders):
     seqs, n = part_ref.shape[:2]
     bits_of = [[0] + list(o)[::-1] for o in orders]
@@ -1230,11 +1241,11 @@
         if u in when:
             forwards(when[u])
     for p in range(seqs):
-        ff_ref[p] = work[p].total(0)
+        ff_ref[p] = (mixed_ref[p] + work[p].total(0) + bias_ref[...]).astype(BF)
         work[p].drain()
 
 
-def mlp_grads(gr, x, parts, early, orders):
+def mlp_grads(gr, x, parts, mixed, bias, early, orders):
     seqs, n, span, d = parts.shape
     tokens, cols = seqs * span, gr.shape[-1]
     dma = pltpu.SemaphoreType.DMA
@@ -1242,11 +1253,11 @@
     flat = lambda v: v.reshape(n, tokens, v.shape[-1])
     return pl.pallas_call(
         functools.partial(mlp_grads_kernel, orders=orders),
-        in_specs=[hbm] * 4,
+        in_specs=[hbm] * 3 + [vmem] * 2 + [hbm],
         out_specs=[vmem] * 2,
         out_shape=[
             jax.ShapeDtypeStruct((d, cols), BF),
-            jax.ShapeDtypeStruct((seqs, span, d), F32),
+            jax.ShapeDtypeStruct((seqs, span, d), BF),
         ],
         scratch_shapes=[
             pltpu.VMEM((2, tokens, d), BF),
@@ -1258,7 +1269,7 @@
         ],
         compiler_params=pltpu.CompilerParams(collective_id=3, has_side_effects=True, vmem_limit_bytes=60 * MIB),
         cost_estimate=pl.CostEstimate(flops=1000, bytes_accessed=MIB, transcendentals=0),
-    )(flat(gr), flat(x), parts, early)
+    )(flat(gr), flat(x), parts, mixed, bias, early)
 
 
 def norm_parts(values):
@@ -1292,13 +1303,10 @@
     x32 = inputs.astype(F32)
     output_every = lax.all_gather(output_matrix, "tensor")
     cot_every = lax.all_gather(cotangent, "tensor")
-    h2, kv, wq, query = first(
+    h2, keys, keys_t, values, values_t, wq, query = first(
         inputs.reshape(tokens, d), attn_gain[None], attn_shift[None], shared_matrix, value_bias[None], query_matrix,
         query_bias[None], seqs, scale * LOG2E, paths,
     )
-    kv = kv.swapaxes(0, 1).reshape(seqs, length, 2 * hd)
-    keys, values = kv[..., :hd], kv[..., hd:]
-    keys_t, values_t = keys.swapaxes(1, 2), values.swapaxes(1, 2)
     query = query.reshape(seqs, span, n * qw)
     like = lambda t, cols: jax.ShapeDtypeStruct((tokens, cols), t)
 
@@ -1334,8 +1342,7 @@
         query, grad_attended, attended, lse, keys, keys_t, values, low, at, dock, docq, heads, hd, scale
     )
     dq2 = dq.reshape(tokens, n * qw)
-    up_part, mlp_branch = mlp_grads(grs, normed_every, ff_parts, dq2, paths)
-    block_out = (mixed + mlp_branch + down_bias).astype(BF)
+    up_part, block_out = mlp_grads(grs, normed_every, ff_parts, mixed, down_bias[None], dq2, paths)
 
     dkv = jnp.concatenate([dk * LN2, dv], axis=-1).astype(BF).reshape(seqs, n, span, 2 * hd).swapaxes(0, 1)
     wo_own, wq_own, dkv_own, up_gradient = attention_grads(

time: 815 us -> 815 us (level)
  local copies, waits for them, and re-layouts: 48.5 us -> 39.9 us
    unnamed x91 -> x88, local copies, waits for them, and re-layouts: 31.7 us -> 28.5 us
  transfers between devices with their start and end apart: 3 -> 3, of which waited for: 1 -> 1; matrix products, arithmetic and copies ran while one was open for 4% -> 3% of each run, Pallas kernels for 32% -> 32%
where the time goes in v6:
time: 815 us; the launch traced here: 802 us
  Pallas kernels  671 us (82%)
  waiting for transfers between devices  48 us (6%)
  local copies, waits for them, and re-layouts  39.9 us (5%)
  other arithmetic  28.5 us (3%)
  between operations  14.8 us (2%)
    pallas_call x1, Pallas kernels, mlp(): pl.pallas_call(functools.partial(mlp_kernel, orders=orders), in_specs=[hb...  178 us
    pallas_call x1, Pallas kernels, attention_grads(): pl.pallas_call(functools.partial(attention_grads_kernel, orders=orders, l...  134 us
    pallas_call x1, Pallas kernels, mlp_grads(): pl.pallas_call(functools.partial(mlp_grads_kernel, orders=orders), in_spe...  113 us
    pallas_call x1, Pallas kernels, last(): pl.pallas_call(functools.partial(last_kernel, order=order, line=line, eps...  103 us
    pallas_call x1, Pallas kernels, first(): pl.pallas_call(functools.partial(first_kernel, orders=orders, factor=fact...  94.8 us
    all_gather x1, waiting for transfers between devices, body(): cot_every = lax.all_gather(cotangent, 'tensor')  46.5 us
    unnamed x88, local copies, waits for them, and re-layouts  28.5 us
    pallas_call x2, Pallas kernels, slot_product(): pl.pallas_call(kernel, grid=(2,), in_specs=[flow(a) for a in tiled] + [st...  21.4 us
  transfers between devices with their start and end apart: 3, of which 1 were waited for; matrix products, arithmetic and copies ran while one was open for 3% of the time, Pallas kernels for 32%

profile of v6, /device:TPU:0, one launch (start us, length us, event | category | flops | bytes accessed | tf_op | source)
XLA Modules:
  0.0 801.9 jit_solution(4382559898108090073)
XLA Ops:
  7.3 0.7 all-gather.5.cloned.1.call-update
  8.0 0.7 all-gather.7.cloned.1.call-update
  8.8 0.9 dynamic-slice_reduce_fusion
  9.6 0.9 compare_select_fusion
  10.8 3.3 reshape.178.dock_ref
  14.1 0.7 constant_dynamic-slice_fusion.2
  14.9 94.8 %shard_map.297 = (bf16[512,2048]{1,0:T(8,128)(2,1)}, bf16[2,2048,128]{2,1,0:T(8,128)(2,1)S(1)}, bf16[2,128,2048]{2,1,0:T(8,128)(2,1)S(1)}, bf16[2,2048,128]{2,1,...) custom-call(bf16[512,2048]{1,0:T(8,128)(2,1)} %bitcast.105, ...), custom_call_target="tpu_custom_call" | custom-call | flops 4294967296 | bytes 67108864 | tf_op jit(solution)/shard_map/pallas_call | solution.py:862
  109.7 1.0 copy-done.15
  110.6 1.1 copy-done.17
  111.7 1.8 copy-done.10
  113.5 11.2 %shard_map.298 = (bf16[2,256,2048]{2,1,0:T(8,128)(2,1)S(1)}, f32[2,8,1,512]{3,2,1,0:T(1,128)S(1)}) custom-call(s32[2]{0:T(128)S(1)} %fusion.2.low_ref, s32[1]{0:T(128)} %bitcast.at_ref, bf16[2,256,2048]{2,1,0:T(8,128)(2,1)S(1)} %bitcast.83, bf16[2,2048,128]{2,1,0:T(8,128)(2,1)S(1)} %get-tuple-element.48.k_ref, ...), custom_call_target="tpu_custom_call" | custom-call | flops 4294967296 | bytes 8388608 | tf_op jit(solution)/shard_map/pallas_call | solution.py:145
  124.8 1.0 copy-done.13
  125.8 11.9 %shard_map.299 = (f32[512,2048]{1,0:T(8,128)}, bf16[512,2048]{1,0:T(8,128)(2,1)S(1)}) custom-call(bf16[512,2048]{1,0:T(8,128)(2,1)S(1)} %bitcast.81, bf16[512,2048]{1,0:T(8,128)(2,1)} %bitcast.106, bf16[8,256,2048]{2,1,0:T(8,128)(2,1)} %bitcast.133, f32[1,2048]{1,0:T(1,128)S(1)} %bitcast.90, f32[1,2048]{1,0:T(1,128)S(1)} %bitcast.86, f32[1,2048]{1,0:T(1,128)S(1)} %bitcast.91), custom_call_target="tpu_custom_call" | custom-call | flops 4294967296 | bytes 16777216 | tf_op jit(solution)/shard_map/pallas_call | solution.py:242
  137.6 1.3 copy-done.26
  139.0 2.5 reduce_sum.91
  141.4 3.9 multiply_reduce_fusion.2
  145.4 46.5 %all-gather.7.cloned.1.call-done = bf16[16,256,2048]{2,1,0:T(8,128)(2,1)} async-done(((bf16[2,256,2048]{2,1,0:T(8,128)(2,1)}), bf16[16,256,2048]{2,1,0:T(8,128)(2,1)}) %all-gather.7.cloned.1.call-update) | async-done | bytes 16777232 | tf_op jit(solution)/shard_map/all_gather | solution.py:1305
  191.9 178.4 %shard_map.300 = (f32[2,256,2048]{2,1,0:T(8,128)}, f32[1,1024]{1,0:T(1,128)}, bf16[8,2,256,2048]{3,2,1,0:T(8,128)(2,1)}, bf16[8,2,256,1024]{3,2,1,0:T(8,128)(2,1...) custom-call(bf16[2,256,2048]{2,1,0:T(8,128)(2,1)} %bitcast.94, ...), custom_call_target="tpu_custom_call" | custom-call | flops 68719476736 | bytes 104857600 | tf_op jit(solution)/shard_map/pallas_call | solution.py:1130
  370.4 6.0 multiply_reduce_fusion.3
  376.4 1.8 copy-done.29
  378.3 0.6 copy-done.31
  378.9 2.5 fusion.3
  381.8 1.7 copy-done.28
  383.5 9.6 %shard_map.301 = bf16[512,2048]{1,0:T(8,128)(2,1)S(1)} custom-call(bf16[512,2048]{1,0:T(8,128)(2,1)S(1)} %bitcast.79, bf16[8,256,2048]{2,1,0:T(8,128)(2,1)} %bitcast.134), custom_call_target="tpu_custom_call" | custom-call | flops 4294967296 | bytes 16777216 | tf_op jit(solution)/shard_map/pallas_call | solution.py:242
  393.1 14.6 %shard_map.302 = (bf16[2,256,2048]{2,1,0:T(8,128)(2,1)S(1)}, f32[2,2048,128]{2,1,0:T(8,128)S(1)}, f32[2,2048,128]{2,1,0:T(8,128)S(1)}) custom-call(s32[2]{0:T(128)S(1)} %fusion.2.low_ref, s32[1]{0:T(128)} %bitcast.at_ref, bf16[2,256,2048]{2,1,0:T(8,128)(2,1)S(1)} %bitcast.84, bf16[2,256,2048]{2,1,0:T(8,128)(2,1)S(1)} %bitcast.85, ...), custom_call_target="tpu_custom_call" | custom-call | flops 1000 | bytes 1048576 | tf_op jit(solution)/shard_map/pallas_call | solution.py:180
  407.8 1.3 copy-done
  409.1 1.3 copy-done.6
  410.4 1.3 copy-done.8
  411.7 113.0 %shard_map.303 = (bf16[2048,1024]{1,0:T(8,128)(2,1)}, bf16[2,256,2048]{2,1,0:T(8,128)(2,1)}) custom-call(bf16[8,512,1024]{2,1,0:T(8,128)(2,1)} %bitcast.99, bf16[8,512,2048]{2,1,0:T(8,128)(2,1)} %bitcast.98, bf16[2,8,256,2048]{3,2,1,0:T(8,128)(2,1)} %get-tuple-element.54.part_ref, f32[2,256,2048]{2,1,0:T(8,128)} %bitcast.96, f32[1,2048]{1,0:T(1,128)} %bitcast.122, ...), custom_call_target="tpu_custom_call" | custom-call | flops 1000 | bytes 1048576 | tf_op jit(solution)/shard_map/pallas_call | solution.py:1254
  524.9 1.4 copy-done.7
  526.9 1.5 copy.47
  529.5 133.7 %shard_map.304 = (bf16[2,256,1024]{2,1,0:T(8,128)(2,1)}, bf16[2,256,1024]{2,1,0:T(8,128)(2,1)}, bf16[512,256]{1,0:T(8,128)(2,1)}, bf16[16,128,1024]{2,1,0:T(8,128)(2,1)}) custom-call(bf16[512,2048]{1,0:T(8,128)(2,1)} %bitcast.82, bf16[512,2048]{1,0:T(8,128)(2,1)} %bitcast.80, bf16[512,2048]{1,0:T(8,128)(2,1)} %bitcast.77, ...), custom_call_target="tpu_custom_call" | custom-call | flops 1000 | bytes 1048576 | tf_op jit(solution)/shard_map/pallas_call | solution.py:496
  663.2 103.4 %shard_map.305 = (f32[256,2048]{1,0:T(8,128)}, f32[256,2048]{1,0:T(8,128)}, f32[512,2048]{1,0:T(8,128)}, f32[1,22656]{1,0:T(1,128)}, f32[2048,256]{1,0:T(8,128)}) custom-call(bf16[4,128,1024]{2,1,0:T(8,128)(2,1)} %bitcast.109, bf16[4,128,1024]{2,1,0:T(8,128)(2,1)} %bitcast.110, bf16[512,2048]{1,0:T(8,128)(2,1)} %bitcast.78, ...), custom_call_target="tpu_custom_call" | custom-call | flops 1000 | bytes 1048576 | tf_op jit(solution)/shard_map/pallas_call | solution.py:704
  766.7 1.4 fusion.4
  768.1 1.1 slice_bitcast_fusion
  769.2 0.8 split.54
  770.0 2.9 copy.46
  772.8 0.6 constant_dynamic-slice_fusion.1
  773.4 6.8 bitcast_convert_fusion
  780.2 0.6 constant_dynamic-slice_fusion
  780.8 4.4 convert_element_type.30
  785.3 1.3 copy.63
  786.6 1.6 copy-done.32
  788.2 2.1 copy.64
  790.3 1.0 copy-done.35
  791.3 1.3 copy.65
  792.6 1.0 copy-done.34
  793.6 1.3 copy.66
  (103 shorter events, 2.6 us)
Async XLA Ops:
  7.2 7.6 copy-start.20
  7.2 7.6 copy-start.21
  7.2 7.6 copy-start.12
  7.2 7.6 copy-start.25
  7.2 7.6 copy-start.24
  7.2 118.5 %all-gather.5.cloned.1.call-start = ((), (), s32[]{:S(2)}) async-start(), calls=%async_computation.1 | async-start | bytes 9437184 | tf_op jit(solution)/shard_map/all_gather | solution.py:1304
  8.0 183.9 %all-gather.7.cloned.1.call-start = ((), (), s32[]{:S(2)}) async-start(), calls=%async_computation.2 | async-start | bytes 18874368 | tf_op jit(solution)/shard_map/all_gather | solution.py:1305
  8.7 520.8 %all-reduce.2.cloned.1.call-start = ((), (), s32[]{:S(2)}) async-start(), calls=%async_computation | async-start | bytes 8388608 | tf_op jit(solution)/shard_map/psum | solution.py:1333
  14.8 96.8 %copy-start.4 = (s32[2,2048,1]{2,1,0:T(8,128)S(1)}, s32[2,2048,1]{2,1,0:T(8,128)}, u32[]{:S(2)}) copy-start(s32[2,2048,1]{2,1,0:T(8,128)} %reshape.178.dock_ref) | copy-start | bytes 49156
  109.7 1.0 copy-start.15
  110.6 1.1 copy-start.17
  111.7 1.8 copy-start.10
  113.5 12.2 %copy-start.19 = (f32[2048]{0:T(1024)S(1)}, f32[2048]{0:T(1024)}, u32[]{:S(2)}) copy-start(f32[2048]{0:T(1024)} %param.30) | copy-start | bytes 24580
  113.5 12.2 %copy-start.22 = (f32[2048]{0:T(1024)S(1)}, f32[2048]{0:T(1024)}, u32[]{:S(2)}) copy-start(f32[2048]{0:T(1024)} %param.29) | copy-start | bytes 24580
  113.5 12.2 %copy-start.23 = (f32[2048]{0:T(1024)S(1)}, f32[2048]{0:T(1024)}, u32[]{:S(2)}) copy-start(f32[2048]{0:T(1024)} %param.31) | copy-start | bytes 24580
  124.8 1.0 copy-start.13
  125.7 267.3 %copy-start.3 = (bf16[2,256,2048]{2,1,0:T(8,128)(2,1)}, bf16[2,256,2048]{2,1,0:T(8,128)(2,1)S(1)}, u32[]{:S(2)}) copy-start(bf16[2,256,2048]{2,1,0:T(8,128)(2,1)S(1)} %get-tuple-element.50.o_ref) | copy-start | bytes 6291460
  137.6 1.3 copy-start.26
  370.4 6.1 copy-start.27
  370.4 7.9 copy-start.29
  370.4 8.5 %copy-start.31 = (bf16[2,256,2048]{2,1,0:T(8,128)(2,1)S(1)}, bf16[2,256,2048]{2,1,0:T(8,128)(2,1)}, u32[]{:S(2)}) copy-start(bf16[2,256,2048]{2,1,0:T(8,128)(2,1)} %param.19) | copy-start | bytes 6291460
  381.4 2.0 copy-start.28
  383.5 9.6 %copy-start.2 = (bf16[2,256,2048]{2,1,0:T(8,128)(2,1)}, bf16[2,256,2048]{2,1,0:T(8,128)(2,1)S(1)}, u32[]{:S(2)}) copy-start(bf16[2,256,2048]{2,1,0:T(8,128)(2,1)S(1)} %convert_element_type.26) | copy-start | bytes 6291460
  383.5 9.6 %copy-start.5 = (s32[2,2048,1]{2,1,0:T(8,128)S(1)}, s32[2,2048,1]{2,1,0:T(8,128)}, u32[]{:S(2)}) copy-start(s32[2,2048,1]{2,1,0:T(8,128)} %reshape.178.dock_ref) | copy-start | bytes 49156
  383.5 9.6 %copy-start.11 = (bf16[512,2048]{1,0:T(8,128)(2,1)S(1)}, bf16[512,2048]{1,0:T(8,128)(2,1)}, u32[]{:S(2)}) copy-start(bf16[512,2048]{1,0:T(8,128)(2,1)} %get-tuple-element.47) | copy-start | bytes 6291460
  383.5 9.6 %copy-start.14 = (bf16[2,2048,128]{2,1,0:T(8,128)(2,1)S(1)}, bf16[2,2048,128]{2,1,0:T(8,128)(2,1)}, u32[]{:S(2)}) copy-start(bf16[2,2048,128]{2,1,0:T(8,128)(2,1)} %copy-done.13) | copy-start | bytes 3145732
  383.5 9.6 %copy-start.16 = (bf16[2,128,2048]{2,1,0:T(8,128)(2,1)S(1)}, bf16[2,128,2048]{2,1,0:T(8,128)(2,1)}, u32[]{:S(2)}) copy-start(bf16[2,128,2048]{2,1,0:T(8,128)(2,1)} %copy-done.15) | copy-start | bytes 3145732
  383.5 9.6 %copy-start.18 = (bf16[2,2048,128]{2,1,0:T(8,128)(2,1)S(1)}, bf16[2,2048,128]{2,1,0:T(8,128)(2,1)}, u32[]{:S(2)}) copy-start(bf16[2,2048,128]{2,1,0:T(8,128)(2,1)} %copy-done.17) | copy-start | bytes 3145732
  407.7 1.3 copy-start
  409.1 1.3 copy-start.6
  410.4 1.3 copy-start.8
  411.7 113.1 %copy-start.9 = (f32[2,2048,128]{2,1,0:T(8,128)S(1)}, f32[2,2048,128]{2,1,0:T(8,128)}, u32[]{:S(2)}) copy-start(f32[2,2048,128]{2,1,0:T(8,128)} %copy-done.8) | copy-start | bytes 6291460
  524.8 1.6 copy-start.7
  526.6 1.9 copy-start.1
  526.9 2.2 copy-start.37
  529.5 133.8 %copy-start.36 = (f32[18432]{0:T(1024)}, f32[18432]{0:T(1024)S(1)}, u32[]{:S(2)}) copy-start(f32[18432]{0:T(1024)S(1)} %constant_dynamic-update-slice_fusion) | copy-start | bytes 221188
  773.4 7.4 copy-start.30
  780.8 4.5 copy-start.33
  785.2 2.9 copy-start.32
  788.2 3.1 copy-start.35
  791.3 2.3 copy-start.34
Sparse Core Ops, SparseCore 0:
  10.0 89.7 all-gather.4
  101.6 90.2 all-gather.6
  370.5 155.2 all-reduce.1

commit v7 on v6

--- a/solution.py
+++ b/solution.py
@@ -631,7 +631,7 @@
             shared_sum(t + 1)
         if count + t < len(hops):
             early(count + t)
-        at += 2
+        at += 1
         chain_to(at)
     late_ref[:, :d] = gain_part
     late_ref[:, d : 2 * d] = shift_part
@@ -702,7 +702,7 @@
     vmem = pl.BlockSpec(memory_space=pltpu.VMEM)
     item = (2,) + wo.shape
     return pl.pallas_call(
-        functools.partial(last_kernel, order=order, line=line, eps_rows=tokens // 2),
+        functools.partial(last_kernel, order=order, line=line, eps_rows=tokens // 4),
         in_specs=[vmem] * 11,
         out_specs=[vmem] * 5,
         out_shape=[

time: 815 us -> 822 us (level)
  Pallas kernels: 671 us -> 683 us
    pallas_call x1, Pallas kernels: 113 us -> 122 us  [mlp_grads(): pl.pallas_call(functools.partial(mlp_grads_kernel, orders=orders), in_spe...]
where the time goes in v7:
time: 822 us; the launch traced here: 815 us
  Pallas kernels  683 us (83%)
  waiting for transfers between devices  48 us (6%)
  local copies, waits for them, and re-layouts  39.9 us (5%)
  other arithmetic  28.5 us (3%)
  between operations  14.8 us (2%)
    pallas_call x1, Pallas kernels, mlp(): pl.pallas_call(functools.partial(mlp_kernel, orders=orders), in_specs=[hb...  178 us
    pallas_call x1, Pallas kernels, attention_grads(): pl.pallas_call(functools.partial(attention_grads_kernel, orders=orders, l...  134 us
    pallas_call x1, Pallas kernels, mlp_grads(): pl.pallas_call(functools.partial(mlp_grads_kernel, orders=orders), in_spe...  122 us
    pallas_call x1, Pallas kernels, last(): pl.pallas_call(functools.partial(last_kernel, order=order, line=line, eps...  106 us
    pallas_call x1, Pallas kernels, first(): pl.pallas_call(functools.partial(first_kernel, orders=orders, factor=fact...  94.8 us
    all_gather x1, waiting for transfers between devices, body(): cot_every = lax.all_gather(cotangent, 'tensor')  46.5 us
    unnamed x88, local copies, waits for them, and re-layouts  28.5 us
    pallas_call x2, Pallas kernels, slot_product(): pl.pallas_call(kernel, grid=(2,), in_specs=[flow(a) for a in tiled] + [st...  21.4 us
  transfers between devices with their start and end apart: 3, of which 1 were waited for; matrix products, arithmetic and copies ran while one was open for 3% of the time, Pallas kernels for 32%

profile of v7, /device:TPU:0, one launch (start us, length us, event | category | flops | bytes accessed | tf_op | source)
XLA Modules:
  0.0 814.8 jit_solution(10257875416720219252)
XLA Ops:
  7.3 0.7 all-gather.5.cloned.1.call-update
  8.0 0.7 all-gather.7.cloned.1.call-update
  8.8 0.9 dynamic-slice_reduce_fusion
  9.6 0.9 compare_select_fusion
  10.8 3.3 reshape.178.dock_ref
  14.1 0.7 constant_dynamic-slice_fusion.2
  14.9 94.8 %shard_map.297 = (bf16[512,2048]{1,0:T(8,128)(2,1)}, bf16[2,2048,128]{2,1,0:T(8,128)(2,1)S(1)}, bf16[2,128,2048]{2,1,0:T(8,128)(2,1)S(1)}, bf16[2,2048,128]{2,1,...) custom-call(bf16[512,2048]{1,0:T(8,128)(2,1)} %bitcast.105, ...), custom_call_target="tpu_custom_call" | custom-call | flops 4294967296 | bytes 67108864 | tf_op jit(solution)/shard_map/pallas_call | solution.py:862
  109.7 1.0 copy-done.15
  110.6 1.1 copy-done.17
  111.7 1.8 copy-done.10
  113.5 11.2 %shard_map.298 = (bf16[2,256,2048]{2,1,0:T(8,128)(2,1)S(1)}, f32[2,8,1,512]{3,2,1,0:T(1,128)S(1)}) custom-call(s32[2]{0:T(128)S(1)} %fusion.2.low_ref, s32[1]{0:T(128)} %bitcast.at_ref, bf16[2,256,2048]{2,1,0:T(8,128)(2,1)S(1)} %bitcast.83, bf16[2,2048,128]{2,1,0:T(8,128)(2,1)S(1)} %get-tuple-element.48.k_ref, ...), custom_call_target="tpu_custom_call" | custom-call | flops 4294967296 | bytes 8388608 | tf_op jit(solution)/shard_map/pallas_call | solution.py:145
  124.8 1.0 copy-done.13
  125.8 11.9 %shard_map.299 = (f32[512,2048]{1,0:T(8,128)}, bf16[512,2048]{1,0:T(8,128)(2,1)S(1)}) custom-call(bf16[512,2048]{1,0:T(8,128)(2,1)S(1)} %bitcast.81, bf16[512,2048]{1,0:T(8,128)(2,1)} %bitcast.106, bf16[8,256,2048]{2,1,0:T(8,128)(2,1)} %bitcast.133, f32[1,2048]{1,0:T(1,128)S(1)} %bitcast.90, f32[1,2048]{1,0:T(1,128)S(1)} %bitcast.86, f32[1,2048]{1,0:T(1,128)S(1)} %bitcast.91), custom_call_target="tpu_custom_call" | custom-call | flops 4294967296 | bytes 16777216 | tf_op jit(solution)/shard_map/pallas_call | solution.py:242
  137.6 1.3 copy-done.26
  139.0 2.5 reduce_sum.91
  141.4 3.9 multiply_reduce_fusion.2
  145.4 46.5 %all-gather.7.cloned.1.call-done = bf16[16,256,2048]{2,1,0:T(8,128)(2,1)} async-done(((bf16[2,256,2048]{2,1,0:T(8,128)(2,1)}), bf16[16,256,2048]{2,1,0:T(8,128)(2,1)}) %all-gather.7.cloned.1.call-update) | async-done | bytes 16777232 | tf_op jit(solution)/shard_map/all_gather | solution.py:1305
  191.9 178.4 %shard_map.300 = (f32[2,256,2048]{2,1,0:T(8,128)}, f32[1,1024]{1,0:T(1,128)}, bf16[8,2,256,2048]{3,2,1,0:T(8,128)(2,1)}, bf16[8,2,256,1024]{3,2,1,0:T(8,128)(2,1...) custom-call(bf16[2,256,2048]{2,1,0:T(8,128)(2,1)} %bitcast.94, ...), custom_call_target="tpu_custom_call" | custom-call | flops 68719476736 | bytes 104857600 | tf_op jit(solution)/shard_map/pallas_call | solution.py:1130
  370.4 6.0 multiply_reduce_fusion.3
  376.4 1.8 copy-done.29
  378.3 0.6 copy-done.31
  378.9 2.5 fusion.3
  381.8 1.7 copy-done.28
  383.5 9.6 %shard_map.301 = bf16[512,2048]{1,0:T(8,128)(2,1)S(1)} custom-call(bf16[512,2048]{1,0:T(8,128)(2,1)S(1)} %bitcast.79, bf16[8,256,2048]{2,1,0:T(8,128)(2,1)} %bitcast.134), custom_call_target="tpu_custom_call" | custom-call | flops 4294967296 | bytes 16777216 | tf_op jit(solution)/shard_map/pallas_call | solution.py:242
  393.1 14.6 %shard_map.302 = (bf16[2,256,2048]{2,1,0:T(8,128)(2,1)S(1)}, f32[2,2048,128]{2,1,0:T(8,128)S(1)}, f32[2,2048,128]{2,1,0:T(8,128)S(1)}) custom-call(s32[2]{0:T(128)S(1)} %fusion.2.low_ref, s32[1]{0:T(128)} %bitcast.at_ref, bf16[2,256,2048]{2,1,0:T(8,128)(2,1)S(1)} %bitcast.84, bf16[2,256,2048]{2,1,0:T(8,128)(2,1)S(1)} %bitcast.85, ...), custom_call_target="tpu_custom_call" | custom-call | flops 1000 | bytes 1048576 | tf_op jit(solution)/shard_map/pallas_call | solution.py:180
  407.8 1.3 copy-done
  409.1 1.3 copy-done.6
  410.4 1.3 copy-done.8
  411.7 122.3 %shard_map.303 = (bf16[2048,1024]{1,0:T(8,128)(2,1)}, bf16[2,256,2048]{2,1,0:T(8,128)(2,1)}) custom-call(bf16[8,512,1024]{2,1,0:T(8,128)(2,1)} %bitcast.99, bf16[8,512,2048]{2,1,0:T(8,128)(2,1)} %bitcast.98, bf16[2,8,256,2048]{3,2,1,0:T(8,128)(2,1)} %get-tuple-element.54.part_ref, f32[2,256,2048]{2,1,0:T(8,128)} %bitcast.96, f32[1,2048]{1,0:T(1,128)} %bitcast.122, ...), custom_call_target="tpu_custom_call" | custom-call | flops 1000 | bytes 1048576 | tf_op jit(solution)/shard_map/pallas_call | solution.py:1254
  534.2 1.4 copy-done.7
  536.2 1.5 copy.47
  538.8 134.3 %shard_map.304 = (bf16[2,256,1024]{2,1,0:T(8,128)(2,1)}, bf16[2,256,1024]{2,1,0:T(8,128)(2,1)}, bf16[512,256]{1,0:T(8,128)(2,1)}, bf16[16,128,1024]{2,1,0:T(8,128)(2,1)}) custom-call(bf16[512,2048]{1,0:T(8,128)(2,1)} %bitcast.82, bf16[512,2048]{1,0:T(8,128)(2,1)} %bitcast.80, bf16[512,2048]{1,0:T(8,128)(2,1)} %bitcast.77, ...), custom_call_target="tpu_custom_call" | custom-call | flops 1000 | bytes 1048576 | tf_op jit(solution)/shard_map/pallas_call | solution.py:496
  673.1 106.3 %shard_map.305 = (f32[256,2048]{1,0:T(8,128)}, f32[256,2048]{1,0:T(8,128)}, f32[512,2048]{1,0:T(8,128)}, f32[1,22656]{1,0:T(1,128)}, f32[2048,256]{1,0:T(8,128)}) custom-call(bf16[4,128,1024]{2,1,0:T(8,128)(2,1)} %bitcast.109, bf16[4,128,1024]{2,1,0:T(8,128)(2,1)} %bitcast.110, bf16[512,2048]{1,0:T(8,128)(2,1)} %bitcast.78, ...), custom_call_target="tpu_custom_call" | custom-call | flops 1000 | bytes 1048576 | tf_op jit(solution)/shard_map/pallas_call | solution.py:704
  779.5 1.4 fusion.4
  780.9 1.1 slice_bitcast_fusion
  782.0 0.8 split.54
  782.8 2.9 copy.46
  785.7 0.6 constant_dynamic-slice_fusion.1
  786.2 6.8 bitcast_convert_fusion
  793.0 0.6 constant_dynamic-slice_fusion
  793.6 4.4 convert_element_type.30
  798.1 1.3 copy.63
  799.4 1.6 copy-done.32
  801.0 2.1 copy.64
  803.2 1.0 copy-done.35
  804.1 1.3 copy.65
  805.4 1.0 copy-done.34
  806.5 1.3 copy.66
  (103 shorter events, 2.6 us)
Async XLA Ops:
  7.2 7.6 copy-start.20
  7.2 7.6 copy-start.21
  7.2 7.6 copy-start.12
  7.2 7.6 copy-start.25
  7.2 7.6 copy-start.24
  7.2 118.5 %all-gather.5.cloned.1.call-start = ((), (), s32[]{:S(2)}) async-start(), calls=%async_computation.1 | async-start | bytes 9437184 | tf_op jit(solution)/shard_map/all_gather | solution.py:1304
  8.0 183.9 %all-gather.7.cloned.1.call-start = ((), (), s32[]{:S(2)}) async-start(), calls=%async_computation.2 | async-start | bytes 18874368 | tf_op jit(solution)/shard_map/all_gather | solution.py:1305
  8.7 530.1 %all-reduce.2.cloned.1.call-start = ((), (), s32[]{:S(2)}) async-start(), calls=%async_computation | async-start | bytes 8388608 | tf_op jit(solution)/shard_map/psum | solution.py:1333
  14.8 96.8 %copy-start.4 = (s32[2,2048,1]{2,1,0:T(8,128)S(1)}, s32[2,2048,1]{2,1,0:T(8,128)}, u32[]{:S(2)}) copy-start(s32[2,2048,1]{2,1,0:T(8,128)} %reshape.178.dock_ref) | copy-start | bytes 49156
  109.7 1.0 copy-start.15
  110.6 1.1 copy-start.17
  111.7 1.8 copy-start.10
  113.5 12.2 %copy-start.19 = (f32[2048]{0:T(1024)S(1)}, f32[2048]{0:T(1024)}, u32[]{:S(2)}) copy-start(f32[2048]{0:T(1024)} %param.30) | copy-start | bytes 24580
  113.5 12.2 %copy-start.22 = (f32[2048]{0:T(1024)S(1)}, f32[2048]{0:T(1024)}, u32[]{:S(2)}) copy-start(f32[2048]{0:T(1024)} %param.29) | copy-start | bytes 24580
  113.5 12.2 %copy-start.23 = (f32[2048]{0:T(1024)S(1)}, f32[2048]{0:T(1024)}, u32[]{:S(2)}) copy-start(f32[2048]{0:T(1024)} %param.31) | copy-start | bytes 24580
  124.8 1.0 copy-start.13
  125.7 267.3 %copy-start.3 = (bf16[2,256,2048]{2,1,0:T(8,128)(2,1)}, bf16[2,256,2048]{2,1,0:T(8,128)(2,1)S(1)}, u32[]{:S(2)}) copy-start(bf16[2,256,2048]{2,1,0:T(8,128)(2,1)S(1)} %get-tuple-element.50.o_ref) | copy-start | bytes 6291460
  137.6 1.3 copy-start.26
  370.4 6.1 copy-start.27
  370.4 7.9 copy-start.29
  370.4 8.5 %copy-start.31 = (bf16[2,256,2048]{2,1,0:T(8,128)(2,1)S(1)}, bf16[2,256,2048]{2,1,0:T(8,128)(2,1)}, u32[]{:S(2)}) copy-start(bf16[2,256,2048]{2,1,0:T(8,128)(2,1)} %param.19) | copy-start | bytes 6291460
  381.4 2.0 copy-start.28
  383.5 9.6 %copy-start.2 = (bf16[2,256,2048]{2,1,0:T(8,128)(2,1)}, bf16[2,256,2048]{2,1,0:T(8,128)(2,1)S(1)}, u32[]{:S(2)}) copy-start(bf16[2,256,2048]{2,1,0:T(8,128)(2,1)S(1)} %convert_element_type.26) | copy-start | bytes 6291460
  383.5 9.6 %copy-start.5 = (s32[2,2048,1]{2,1,0:T(8,128)S(1)}, s32[2,2048,1]{2,1,0:T(8,128)}, u32[]{:S(2)}) copy-start(s32[2,2048,1]{2,1,0:T(8,128)} %reshape.178.dock_ref) | copy-start | bytes 49156
  383.5 9.6 %copy-start.11 = (bf16[512,2048]{1,0:T(8,128)(2,1)S(1)}, bf16[512,2048]{1,0:T(8,128)(2,1)}, u32[]{:S(2)}) copy-start(bf16[512,2048]{1,0:T(8,128)(2,1)} %get-tuple-element.47) | copy-start | bytes 6291460
  383.5 9.6 %copy-start.14 = (bf16[2,2048,128]{2,1,0:T(8,128)(2,1)S(1)}, bf16[2,2048,128]{2,1,0:T(8,128)(2,1)}, u32[]{:S(2)}) copy-start(bf16[2,2048,128]{2,1,0:T(8,128)(2,1)} %copy-done.13) | copy-start | bytes 3145732
  383.5 9.6 %copy-start.16 = (bf16[2,128,2048]{2,1,0:T(8,128)(2,1)S(1)}, bf16[2,128,2048]{2,1,0:T(8,128)(2,1)}, u32[]{:S(2)}) copy-start(bf16[2,128,2048]{2,1,0:T(8,128)(2,1)} %copy-done.15) | copy-start | bytes 3145732
  383.5 9.6 %copy-start.18 = (bf16[2,2048,128]{2,1,0:T(8,128)(2,1)S(1)}, bf16[2,2048,128]{2,1,0:T(8,128)(2,1)}, u32[]{:S(2)}) copy-start(bf16[2,2048,128]{2,1,0:T(8,128)(2,1)} %copy-done.17) | copy-start | bytes 3145732
  407.7 1.3 copy-start
  409.1 1.3 copy-start.6
  410.4 1.3 copy-start.8
  411.7 122.4 %copy-start.9 = (f32[2,2048,128]{2,1,0:T(8,128)S(1)}, f32[2,2048,128]{2,1,0:T(8,128)}, u32[]{:S(2)}) copy-start(f32[2,2048,128]{2,1,0:T(8,128)} %copy-done.8) | copy-start | bytes 6291460
  534.0 1.6 copy-start.7
  535.9 1.9 copy-start.1
  536.2 2.2 copy-start.37
  538.8 134.4 %copy-start.36 = (f32[18432]{0:T(1024)}, f32[18432]{0:T(1024)S(1)}, u32[]{:S(2)}) copy-start(f32[18432]{0:T(1024)S(1)} %constant_dynamic-update-slice_fusion) | copy-start | bytes 221188
  786.2 7.4 copy-start.30
  793.6 4.5 copy-start.33
  798.1 2.9 copy-start.32
  801.0 3.1 copy-start.35
  804.1 2.3 copy-start.34
Sparse Core Ops, SparseCore 0:
  10.0 89.7 all-gather.4
  101.6 90.2 all-gather.6
  370.5 155.1 all-reduce.1
